TPU v7x, 32 devices: a whole 2x2x4 slice. The times are simulated.
32 devices in a mesh: row: 4 (over x, core), col: 8 (over z, y).
Axes of the slice: x: 2, y: 2, z: 4, core: 2. Of those that a mesh axis runs over, the one named last changes fastest.
Arguments:
- features: bfloat16 [16384, 1024], P(('row', 'col')), may hold values from -6 to 6
- neighbours: int32 [16384, 16], P(('row', 'col')), may hold values from 0 to 1279, as said below
- degrees: int32 [16384], P(('row', 'col')), may hold values from 1 to 16, as said below
- send_rows: int32 [32, 512], P(('row', 'col')), may hold values from 0 to 511
- send_count: int32 [32, 32], P(('row', 'col')), may hold values from 8 to 16, as said below
- hub_rows: int32 [256], P(('row', 'col')), may hold values from 0 to 511, as said below
- w_self: bfloat16 [1024, 1024], replicated, may hold values from -0.1875 to 0.1875
- w_neigh: bfloat16 [1024, 1024], replicated, may hold values from -0.1875 to 0.1875
- bias_term: float32 [1024], replicated, may hold values from -3 to 3
- cotangent: bfloat16 [16384, 1024], P(('row', 'col')), may hold values from -6 to 6
Outputs:
- hidden: bfloat16 [16384, 1024], P(('row', 'col'))
- grad_x: bfloat16 [16384, 1024], P(('row', 'col'))
- grad_self: bfloat16 [1024, 1024], replicated
- grad_neigh: bfloat16 [1024, 1024], replicated
Inputs may be any that keep to these rules, and one draw needn't show every extreme that they name: neighbours of partition d point to its own rows (below 512), to live slots of arrived_d only (row 512 + p * 16 + s with p != d and s < send_count[p, d]), or to hub rows; entries at j >= degrees[i] also lie in the table. `degrees`: every seed has at least one neighbour. `send_count`: each partition sends between 8 and 16 live rows to each partition, and exactly 16 to the next one. `hub_rows`: the 8 hub rows of a partition are distinct.
All inputs are finite; a program needn't handle non-finite values.
Results may differ from a plain program's by a relative error of at most 0.0064.
Values may be sent and summed in bfloat16 or wider, within the bound.
No kernel may reach another device: no remote copies, remote signals or barrier semaphores. Data moves between devices by JAX's collectives and lax.ppermute only.
A program may use at most 128 MiB of HBM per device.

v0:
```python
import jax
import jax.numpy as jnp
from jax import lax
from jax.sharding import PartitionSpec as P


def silu_slope(pre_act):
    sigmoid_val = jax.nn.sigmoid(pre_act)
    return sigmoid_val * (1.0 + pre_act * (1.0 - sigmoid_val))


def on_device(
    features,
    neighbours,
    degrees,
    send_rows,
    send_count,
    hub_rows,
    w_self,
    w_neigh,
    bias_term,
    cotangent,
):
    n_row = lax.axis_size("row")
    n_col = lax.axis_size("col")
    n_dev = n_row * n_col
    n_local, feat_width = features.shape
    fanout = neighbours.shape[1]
    capacity = send_rows.shape[1] // n_dev
    tile_size = min(512, n_local)
    n_tiles = n_local // tile_size
    slot_live = (
        jnp.arange(capacity, dtype=jnp.int32)[None, :] < send_count.reshape(n_dev, 1)
    ).reshape(-1, 1)
    outgoing = jnp.where(slot_live, features[send_rows[0]], jnp.zeros((), jnp.bfloat16))
    arrived = lax.all_to_all(outgoing, ("row", "col"), split_axis=0, concat_axis=0, tiled=True)
    own_hubs = features[hub_rows]
    by_column = lax.all_gather(own_hubs, "col", axis=0, tiled=True)
    all_hubs = lax.all_gather(by_column, "row", axis=0, tiled=True)
    src_table = jnp.concatenate([features, arrived, all_hubs], 0)
    table_len = src_table.shape[0]
    live_mask = jnp.arange(fanout, dtype=jnp.int32)[None, :] < degrees[:, None]
    inv_deg = 1.0 / degrees.astype(jnp.float32)

    def gather_tile(tile_index):
        tile_live = live_mask.astype(jnp.bfloat16)
        picked = src_table[neighbours]
        return jnp.einsum("nf,nfd->nd", tile_live, picked, preferred_element_type=jnp.float32)

    summed = lax.map(gather_tile, jnp.arange(n_tiles, dtype=jnp.int32)).reshape(n_local, feat_width)
    aggregate = (summed * inv_deg[:, None]).astype(jnp.bfloat16)
    pre_act = (
        jnp.dot(features, w_self, preferred_element_type=jnp.float32)
        + jnp.dot(aggregate, w_neigh, preferred_element_type=jnp.float32)
        + bias_term[None, :]
    )
    hidden = jax.nn.silu(pre_act).astype(jnp.bfloat16)
    d_pre = (cotangent.astype(jnp.float32) * silu_slope(pre_act)).astype(jnp.bfloat16)
    self_part = lax.dot_general(
        features, d_pre, (((0,), (0,)), ((), ())), preferred_element_type=jnp.float32
    )
    neigh_part = lax.dot_general(
        aggregate, d_pre, (((0,), (0,)), ((), ())), preferred_element_type=jnp.float32
    )
    grad_self, grad_neigh = lax.psum((self_part, neigh_part), ("row", "col"))
    d_agg = (
        lax.dot_general(
            d_pre, w_neigh, (((1,), (1,)), ((), ())), preferred_element_type=jnp.float32
        )
        * inv_deg[:, None]
    )
    d_own = lax.dot_general(
        d_pre, w_self, (((1,), (1,)), ((), ())), preferred_element_type=jnp.float32
    )

    def spread_tile(tile_index, d_table):
        target = jnp.where(live_mask, neighbours, table_len)
        updates = jnp.broadcast_to(d_agg[:, None, :], (tile_size, fanout, feat_width))
        return d_table.at[target.reshape(-1)].add(updates.reshape(-1, feat_width), mode="drop")

    d_table = lax.fori_loop(
        0, n_tiles, spread_tile, jnp.zeros((table_len, feat_width), jnp.float32)
    )
    n_slots = n_dev * capacity
    d_local = d_table[:n_local]
    d_arrived = d_table[n_local : n_local + n_slots]
    d_hubs = d_table[n_local + n_slots :]
    returned = lax.all_to_all(
        d_arrived.astype(jnp.bfloat16), ("row", "col"), split_axis=0, concat_axis=0, tiled=True
    ).astype(d_arrived.dtype)
    hub_back = lax.psum_scatter(d_hubs, ("row", "col"), scatter_dimension=0, tiled=True)
    grad_x = d_own + d_local
    grad_x = grad_x.at[send_rows[0]].add(jnp.where(slot_live, returned, 0.0))
    grad_x = grad_x.at[hub_rows].add(hub_back)
    return (
        hidden,
        grad_x.astype(jnp.bfloat16),
        grad_self.astype(jnp.bfloat16),
        grad_neigh.astype(jnp.bfloat16),
    )


def solution(mesh):
    in_specs = (
        P(("row", "col"), None),
        P(("row", "col"), None),
        P(("row", "col")),
        P(("row", "col"), None),
        P(("row", "col"), None),
        P(("row", "col")),
        P(),
        P(),
        P(),
        P(("row", "col"), None),
    )
    out_specs = (P(("row", "col"), None), P(("row", "col"), None), P(), P())
    return jax.shard_map(
        on_device, mesh=mesh, in_specs=in_specs, out_specs=out_specs, check_vma=False
    )
```

profile of v0, /device:TPU:0, one launch (start us, length us, event | category | flops | bytes accessed | tf_op | source)
XLA Modules:
  0.0 451.6 jit_solution(1332690763685159655)
XLA Ops:
  7.2 0.8 compare_select_fusion.2
  8.0 0.7 iota_compare_fusion.1
  8.8 4.8 %gather_fusion = bf16[512,1024]{1,0:T(8,128)(2,1)} fusion(bf16[512,1024]{1,0:T(8,128)(2,1)} %param.10, s32[1024]{0:T(1024)S(1)} %pad_clamp_fusion.1), kind=kCustom, calls=%fused_computation | custom fusion | bytes 2099200 | tf_op jit(solution)/shard_map/gather | solution.py:35
  13.6 2.4 broadcast_select_fusion
  16.0 7.4 %all-to-all-start = ((bf16[32,16,1024]{2,1,0:T(8,128)(2,1)}), bf16[32,16,1024]{2,1,0:T(8,128)(2,1)}, u32[]{:S(2)}, u32[]{:S(2)}) async-start(bf16[32,16,1024]{2,1,0:T(8,128)(2,1)} %broadcast_select_fusion), calls=%async_computation | async-start | bytes 2097152 | tf_op jit(solution)/shard_map/all_to_all | solution.py:36
  23.5 4.2 fusion.11
  27.7 0.6 gather_fusion.1
  28.3 41.4 %all-gather = bf16[64,1024]{1,0:T(8,128)(2,1)S(1)} all-gather(bf16[8,1024]{1,0:T(8,128)(2,1)S(1)} %gather_fusion.1), channel_id=2, replica_groups=mesh['row'=4,'col'=8] {'col'}, dimensions={0}, use_global_device_ids=true | all-gather | bytes 147456 | tf_op jit(solution)/shard_map/all_gather | solution.py:38
  69.7 7.7 %all-gather.1 = bf16[256,1024]{1,0:T(8,128)(2,1)} all-gather(bf16[64,1024]{1,0:T(8,128)(2,1)S(1)} %all-gather), channel_id=3, replica_groups=mesh['row'=4,'col'=8] {'row'}, dimensions={0}, use_global_device_ids=true | all-gather | bytes 655360 | tf_op jit(solution)/shard_map/all_gather | solution.py:39
  78.0 0.8 copy.15
  78.8 1.1 reshape.128
  79.9 0.8 copy.16
  80.7 1.1 reshape.107
  81.9 3.2 pad_maximum_fusion
  85.1 42.8 %gather_fusion.2 = bf16[8192,1024]{1,0:T(8,128)(2,1)} fusion(bf16[1280,1024]{1,0:T(8,128)(2,1)} %pad_maximum_fusion, s32[8192]{0:T(1024)S(1)} %broadcast_clamp_fusion), kind=kCustom, calls=%fused_computation.2 | custom fusion | bytes 33587200 | tf_op jit(solution)/shard_map/while/body/eval_jaxpr/gather | solution.py:47
  127.8 8.6 %fusion.12 = f32[512,1,1024]{2,1,0:T(1,128)S(1)} fusion(pred[512,16,1]{1,2,0:T(4,128)(4,1)S(1)} %copy.18, bf16[512,16,1024]{2,1,0:T(8,128)(2,1)} %bitcast.36), kind=kOutput, calls=%fused_computation.38 | convolution fusion | flops 16777216 | bytes 18882560 | tf_op jit(solution)/shard_map/while/body/eval_jaxpr/nf,nfd->nd/dot_general | solution.py:48
  136.5 3.0 multiply_convert_fusion
  139.6 1.3 convolution_multiply_fusion
  140.9 11.3 %broadcast_in_dim.67 = f32[512,16,1024]{2,1,0:T(8,128)} broadcast(f32[512,1024]{1,0:T(8,128)S(1)} %convolution_multiply_fusion), dimensions={0,2} | broadcast | bytes 35651584 | tf_op jit(solution)/shard_map/while/body/eval_jaxpr/broadcast_in_dim | solution.py:78
  152.2 73.6 %scatter_custom_fusion = f32[1280,1024]{1,0:T(8,128)} fusion(s32[8192]{0:T(1024)S(1)} %bitcast.40, f32[8192,1024]{1,0:T(8,128)} %bitcast.37, f32[]{:T(128)} %constant.13.clone.1), kind=kCustom, calls=%fused_computation.7 | custom fusion | flops 8388608 | bytes 5243392 | tf_op jit(solution)/shard_map/while/body/eval_jaxpr/scatter-add | solution.py:79
  225.8 2.8 slice.24
  228.6 2.3 slice.21
  230.9 5.4 %fusion.8 = f32[1024,1024]{1,0:T(8,128)} fusion(bf16[512,1024]{1,0:T(8,128)(2,1)} %copy-done.3, f32[512,1,1024]{2,1,0:T(1,128)} %copy-done.2, f32[512]{0:T(512)S(1)} %convert_divide_fusion), kind=kOutput, calls=%fused_computation.36 | convolution fusion | flops 1074790400 | bytes 7342080 | tf_op jit(solution)/shard_map/dot_general | solution.py:62
  236.3 3.4 all-to-all-start.1
  239.7 0.7 reduce-scatter.2.cloned.1.call-update
  240.4 4.5 convolution_bitcast_fusion
  244.9 176.1 %all-reduce.2 = (bf16[1024,1024]{0,1:T(8,128)(2,1)}, bf16[1024,1024]{1,0:T(8,128)(2,1)}) all-reduce(f32[1024,1024]{0,1:T(8,128)} %convolution_bitcast_fusion, f32[1024,1024]{1,0:T(8,128)} %fusion.8), channel_id=1, replica_groups=mesh['row'=4,'col'=8] {'row','col'}, use_global_device_ids=true, to_apply=%region_4.5 | all-reduce | flops 2097152 | bytes 12582912 | tf_op jit(solution)/shard_map/psum | solution.py:65
  421.0 4.0 copy.17
  425.0 4.9 %slice_add_fusion = f32[512,1024]{1,0:T(8,128)} fusion(f32[1280,1024]{1,0:T(8,128)} %scatter_custom_fusion, bf16[512,1024]{1,0:T(8,128)(2,1)S(1)} %copy-done.4, bf16[1024,1024]{1,0:T(8,128)(2,1)} %param.16), kind=kOutput, calls=%fused_computation.11 | convolution fusion | flops 1074266112 | bytes 7340032 | tf_op jit(solution)/shard_map/dot_general | solution.py:72
  429.9 8.4 %scatter_custom_fusion.1 = f32[512,1024]{1,0:T(8,128)} fusion(f32[512,1024]{1,0:T(8,128)} %slice_add_fusion, s32[512]{0:T(512)S(1)} %bitcast.42, bf16[512,1024]{1,0:T(8,128)(2,1)} %bitcast.13, f32[]{:T(128)} %constant.13.clone.1, pred[512]{0:T(512)(128)(4,1)S(1)} %lt.79), kind=kCustom, calls=%fused_computation.13 | custom fusion | flops 1572864 | bytes 3146752 | tf_op jit(solution)/shard_map/scatter-add | solution.py:93
  438.3 3.8 scatter_fusion
  442.1 2.7 convert_element_type.40
  (36 shorter events, 0.7 us)
Async XLA Ops:
  7.2 129.3 %copy-start = (bf16[1024,1024]{1,0:T(8,128)(2,1)S(1)}, bf16[1024,1024]{1,0:T(8,128)(2,1)}, u32[]{:S(2)}) copy-start(bf16[1024,1024]{1,0:T(8,128)(2,1)} %param.17) | copy-start | bytes 6291460
  13.6 9.9 %copy-start.6 = (s32[512]{0:T(512)S(1)}, s32[512]{0:T(512)}, u32[]{:S(2)}) copy-start(s32[512]{0:T(512)} %param.12) | copy-start | bytes 6148
  13.6 9.9 %copy-start.1 = (bf16[512,1024]{1,0:T(8,128)(2,1)S(1)}, bf16[512,1024]{1,0:T(8,128)(2,1)}, u32[]{:S(2)}) copy-start(bf16[512,1024]{1,0:T(8,128)(2,1)} %param.10) | copy-start | bytes 3145732
  16.0 65.9 %all-to-all-start = ((bf16[32,16,1024]{2,1,0:T(8,128)(2,1)}), bf16[32,16,1024]{2,1,0:T(8,128)(2,1)}, u32[]{:S(2)}, u32[]{:S(2)}) async-start(bf16[32,16,1024]{2,1,0:T(8,128)(2,1)} %broadcast_select_fusion), calls=%async_computation | async-start | bytes 2097152 | tf_op jit(solution)/shard_map/all_to_all | solution.py:36
  23.5 4.2 copy-start.9
  23.5 46.2 %copy-start.5 = (s32[512,16]{0,1:T(8,128)S(1)}, s32[512,16]{0,1:T(8,128)}, u32[]{:S(2)}) copy-start(s32[512,16]{0,1:T(8,128)} %param.11) | copy-start | bytes 98308
  127.8 8.7 %copy-start.7 = (bf16[512,1024]{1,0:T(8,128)(2,1)S(1)}, bf16[512,1024]{1,0:T(8,128)(2,1)}, u32[]{:S(2)}) copy-start(bf16[512,1024]{1,0:T(8,128)(2,1)} %param.19) | copy-start | bytes 3145732
  127.8 8.7 %copy-start.8 = (f32[1024]{0:T(1024)S(1)}, f32[1024]{0:T(1024)}, u32[]{:S(2)}) copy-start(f32[1024]{0:T(1024)} %param.18) | copy-start | bytes 12292
  127.8 8.7 %copy-start.10 = (f32[512,1024]{1,0:T(8,128)S(1)}, f32[512,1024]{1,0:T(8,128)}, u32[]{:S(2)}) copy-start(f32[512,1024]{1,0:T(8,128)} %fusion.11) | copy-start | bytes 6291460
  136.5 3.1 copy-start.2
  139.6 1.3 copy-start.3
  236.3 193.6 %all-to-all-start.1 = ((bf16[32,16,1024]{2,1,0:T(8,128)(2,1)}), bf16[32,16,1024]{2,1,0:T(8,128)(2,1)}, u32[]{:S(2)}, u32[]{:S(2)}) async-start(bf16[32,16,1024]{2,1,0:T(8,128)(2,1)} %bitcast.39), calls=%async_computation.1 | async-start | bytes 2097152 | tf_op jit(solution)/shard_map/all_to_all | solution.py:88
  239.7 198.6 %reduce-scatter.2.cloned.1.call-start = ((), (), s32[]{:S(2)}) async-start(), calls=%async_computation.3 | async-start | bytes 1081344 | tf_op jit(solution)/shard_map/reduce_scatter | solution.py:91
  421.0 4.0 copy-start.4
Sparse Core Ops, SparseCore 0:
  242.7 139.8 reduce-scatter.1
where the time goes:
time: 453 us; the launch traced here: 452 us
  blocking collectives  225 us (50%)
  other arithmetic  95.8 us (21%)
  local copies, waits for them, and re-layouts  73 us (16%)
  matrix products  31.9 us (7%)
  between operations  14.2 us (3%)
  starting transfers between devices  10.9 us (2%)
    psum x1, blocking collectives, on_device(): grad_self, grad_neigh = lax.psum((self_part, neigh_part), ('row', 'col'))  176 us
    scatter-add x1, other arithmetic, spread_tile(): d_table.at[target.reshape(-1)]  73.6 us
    gather x1, local copies, waits for them, and re-layouts, gather_tile(): picked = src_table[neighbours]  42.8 us
    all_gather x1, blocking collectives, on_device(): by_column = lax.all_gather(own_hubs, 'col', axis=0, tiled=True)  41.4 us
    broadcast_in_dim x1, local copies, waits for them, and re-layouts, spread_tile(): jnp.broadcast_to(d_agg[:, None, :], (tile_size, fanout, feat_width))  11.3 us
  transfers between devices with their start and end apart: 3, of which 0 were waited for; matrix products, arithmetic and copies ran while one was open for 7% of the time, Pallas kernels for 0%

commit v1 on v0

v1 whole, which is shorter than its diff:
```python
import jax
import jax.numpy as jnp
from jax import lax
from jax.sharding import PartitionSpec as P

AXES = ("row", "col")
BF16 = jnp.bfloat16
F32 = jnp.float32


def silu_slope(pre_act):
    sigmoid_val = jax.nn.sigmoid(pre_act)
    return sigmoid_val * (1.0 + pre_act * (1.0 - sigmoid_val))


def contract_rows(left, right):
    return lax.dot_general(left, right, (((0,), (0,)), ((), ())), preferred_element_type=F32)


def contract_cols(left, right):
    return lax.dot_general(left, right, (((1,), (1,)), ((), ())), preferred_element_type=F32)


def on_device(
    features,
    neighbours,
    degrees,
    send_rows,
    send_count,
    hub_rows,
    w_self,
    w_neigh,
    bias_term,
    cotangent,
):
    n_row = lax.axis_size("row")
    n_col = lax.axis_size("col")
    n_dev = n_row * n_col
    me = lax.axis_index("row") * n_col + lax.axis_index("col")
    n_local, width = features.shape
    fanout = neighbours.shape[1]
    n_slots = send_rows.shape[1]
    capacity = n_slots // n_dev
    n_hub = hub_rows.shape[0]
    half = width // 2

    core = n_col
    x_bits = [n_col << i for i in range(1, n_row.bit_length() - 1)]
    y_bits = [1]
    z_bits = [1 << i for i in range(1, n_col.bit_length() - 1)]

    def swap(value, mask):
        return lax.ppermute(value, AXES, [(i, i ^ mask) for i in range(n_dev)])

    def bit(mask):
        return (me & mask) // mask

    row_iota = jnp.arange(n_local, dtype=jnp.int32)
    slot_live = jnp.arange(capacity, dtype=jnp.int32)[None, :] < send_count.reshape(n_dev, 1)
    chosen = jnp.where(slot_live.reshape(-1), send_rows[0], -1)
    pick_send = (chosen[:, None] == row_iota[None, :]).astype(BF16)
    pick_hub = (hub_rows[:, None] == row_iota[None, :]).astype(BF16)
    own_hubs = jnp.dot(pick_hub, features, preferred_element_type=F32).astype(BF16)
    outgoing = jnp.dot(pick_send, features, preferred_element_type=F32).astype(BF16)
    arrived = lax.all_to_all(
        outgoing.reshape(n_dev, capacity, width), AXES, split_axis=0, concat_axis=0, tiled=True
    ).reshape(n_slots, width)

    hub_bits = z_bits + y_bits + x_bits + [core]
    hubs = own_hubs
    for mask in hub_bits:
        hubs = jnp.concatenate([hubs, swap(hubs, mask)], 0)
    peer_features = swap(features, core)

    hub_base = n_local + n_slots
    hub_id = neighbours - hub_base
    relative = (hub_id // n_hub) ^ me
    place = sum(((relative & mask) // mask) << i for i, mask in enumerate(hub_bits))
    where_to = jnp.where(hub_id >= 0, hub_base + place * n_hub + hub_id % n_hub, neighbours)
    where_to = jnp.where(jnp.arange(fanout, dtype=jnp.int32)[None, :] < degrees[:, None], where_to, -1)
    table_iota = jnp.arange(hub_base + n_dev * n_hub, dtype=jnp.int32)
    counts = sum((where_to[:, j : j + 1] == table_iota[None, :]).astype(F32) for j in range(fanout))
    counts = counts.astype(BF16)
    inv_deg = 1.0 / degrees.astype(F32)[:, None]

    summed = jnp.dot(counts[:, :n_local], features, preferred_element_type=F32)
    own_pre = jnp.dot(features, w_self, preferred_element_type=F32) + bias_term[None, :]
    summed = summed + jnp.dot(counts[:, n_local:hub_base], arrived, preferred_element_type=F32)
    summed = summed + jnp.dot(counts[:, hub_base:], hubs, preferred_element_type=F32)
    aggregate = (summed * inv_deg).astype(BF16)
    peer_aggregate = swap(aggregate, core)
    pre_act = own_pre + jnp.dot(aggregate, w_neigh, preferred_element_type=F32)
    hidden = jax.nn.silu(pre_act).astype(BF16)
    d_pre = (cotangent.astype(F32) * silu_slope(pre_act)).astype(BF16)

    d_agg = (contract_cols(d_pre, w_neigh) * inv_deg).astype(BF16)
    d_arrived = contract_rows(counts[:, n_local:hub_base], d_agg).astype(BF16)
    returned = lax.all_to_all(
        d_arrived.reshape(n_dev, capacity, width), AXES, split_axis=0, concat_axis=0, tiled=True
    ).reshape(n_slots, width)
    d_hubs = contract_rows(counts[:, hub_base:], d_agg)

    side = bit(core)
    mine = lax.dynamic_slice_in_dim(d_pre, side * half, half, 1)
    other = lax.dynamic_slice_in_dim(d_pre, (1 - side) * half, half, 1)
    peer_d_pre = swap(other, core)
    self_part = contract_rows(features, mine) + contract_rows(peer_features, peer_d_pre)
    neigh_part = contract_rows(aggregate, mine) + contract_rows(peer_aggregate, peer_d_pre)

    def keep_and_send(value, mask):
        size = value.shape[0] // 2
        b = bit(mask)
        keep = lax.dynamic_slice_in_dim(value, b * size, size, 0)
        send = lax.dynamic_slice_in_dim(value, (1 - b) * size, size, 0)
        return keep, send.astype(BF16)

    def fold_hubs(value):
        size = value.shape[0] // 2
        return value[:size], value[size:].astype(BF16)

    keep, send = fold_hubs(d_hubs)
    d_hubs = keep + swap(send, core).astype(F32)
    self_order = x_bits + y_bits
    neigh_order = y_bits + x_bits
    for self_mask, neigh_mask in zip(self_order, neigh_order):
        self_keep, self_send = keep_and_send(self_part, self_mask)
        neigh_keep, neigh_send = keep_and_send(neigh_part, neigh_mask)
        self_part = self_keep + swap(self_send, self_mask).astype(F32)
        neigh_part = neigh_keep + swap(neigh_send, neigh_mask).astype(F32)
    for mask in reversed(y_bits + x_bits):
        keep, send = fold_hubs(d_hubs)
        d_hubs = keep + swap(send, mask).astype(F32)

    n_z = 1 << len(z_bits)
    z_me = sum(bit(mask) << i for i, mask in enumerate(z_bits))
    piece = self_part.shape[0] // n_z
    total_self = lax.dynamic_slice_in_dim(self_part, z_me * piece, piece, 0)
    total_neigh = lax.dynamic_slice_in_dim(neigh_part, z_me * piece, piece, 0)
    hub_back = d_hubs[:n_hub]
    masks = [sum(mask for i, mask in enumerate(z_bits) if k >> i & 1) for k in range(n_z)]
    for k in range(1, n_z):
        to = z_me ^ k
        message = jnp.concatenate(
            [
                lax.dynamic_slice_in_dim(self_part, to * piece, piece, 0),
                lax.dynamic_slice_in_dim(neigh_part, to * piece, piece, 0),
                d_hubs[k * n_hub : (k + 1) * n_hub].reshape(2 * n_hub, half),
            ],
            0,
        ).astype(BF16)
        got = swap(message, masks[k]).astype(F32)
        total_self = total_self + got[:piece]
        total_neigh = total_neigh + got[piece : 2 * piece]
        hub_back = hub_back + got[2 * piece :].reshape(n_hub, width)

    own = jnp.stack([total_self, total_neigh]).astype(BF16)
    self_block = jnp.zeros((n_z * piece, half), BF16)
    neigh_block = jnp.zeros((n_z * piece, half), BF16)
    for k in range(n_z):
        got = own if k == 0 else swap(own, masks[k])
        at = (z_me ^ k) * piece
        self_block = lax.dynamic_update_slice_in_dim(self_block, got[0], at, 0)
        neigh_block = lax.dynamic_update_slice_in_dim(neigh_block, got[1], at, 0)

    def both(value, mask):
        got = swap(value, mask)
        b = bit(mask)
        return jnp.where(
            b == 0, jnp.concatenate([value, got], 0), jnp.concatenate([got, value], 0)
        )

    for self_mask, neigh_mask in zip(reversed(self_order), reversed(neigh_order)):
        self_block = both(self_block, self_mask)
        neigh_block = both(neigh_block, neigh_mask)

    def both_cols(value):
        got = swap(value, core)
        return jnp.where(
            side == 0, jnp.concatenate([value, got], 1), jnp.concatenate([got, value], 1)
        )

    grad_self = both_cols(self_block)
    grad_neigh = both_cols(neigh_block)

    d_local = contract_rows(counts[:, :n_local], d_agg)
    grad_x = contract_cols(d_pre, w_self) + d_local
    grad_x = grad_x + contract_rows(pick_send, returned)
    hub_high = hub_back.astype(BF16)
    hub_low = (hub_back - hub_high.astype(F32)).astype(BF16)
    grad_x = grad_x + contract_rows(
        jnp.concatenate([pick_hub, pick_hub], 0), jnp.concatenate([hub_high, hub_low], 0)
    )
    return hidden, grad_x.astype(BF16), grad_self, grad_neigh


def solution(mesh):
    split = P(AXES, None)
    in_specs = (split, split, P(AXES), split, split, P(AXES), P(), P(), P(), split)
    out_specs = (split, split, P(), P())
    return jax.shard_map(
        on_device, mesh=mesh, in_specs=in_specs, out_specs=out_specs, check_vma=False
    )
```

time: 453 us -> 217 us (0.48)
  blocking collectives: 225 us -> 0 us
  waiting for transfers between devices: 0.69 us -> 76.1 us
  other arithmetic: 95.8 us -> 32.4 us
  local copies, waits for them, and re-layouts: 73 us -> 15.9 us
  starting transfers between devices: 10.9 us -> 49.2 us
  between operations: 14.2 us -> 1.35 us
  matrix products: 31.9 us -> 41.6 us
    psum x1 -> x0, blocking collectives: 176 us -> none  [on_device(): grad_self, grad_neigh = lax.psum((self_part, neigh_part), ('row', 'col'))]
    scatter-add x3 -> x0, other arithmetic: 85.8 us -> none  [the longest x1 73.6 us: spread_tile(): d_table.at[target.reshape(-1)]]
    ppermute x0 -> x27, waiting for transfers between devices: none -> 76 us  [swap(): return lax.ppermute(value, AXES, [(i, i ^ mask) for i in range(n_dev)])]
    all_gather x2 -> x0, blocking collectives: 49.2 us -> none  [the longest x1 41.4 us: on_device(): by_column = lax.all_gather(own_hubs, 'col', axis=0, tiled=True)]
    gather x3 -> x0, local copies, waits for them, and re-layouts: 48.2 us -> none  [the longest x1 42.8 us: gather_tile(): picked = src_table[neighbours]]
    ppermute x0 -> x27, starting transfers between devices: none -> 40.7 us  [swap(): return lax.ppermute(value, AXES, [(i, i ^ mask) for i in range(n_dev)])]
    select_n x5 -> x8, other arithmetic: 3.31 us -> 16.4 us  [the longest x2 8.1 us: both_cols(): jnp.where(side == 0, jnp.concatenate([value, got], 1), jnp.concatenate([g...]
    broadcast_in_dim x2 -> x0, local copies, waits for them, and re-layouts: 12.4 us -> none  [the longest x1 11.3 us: spread_tile(): jnp.broadcast_to(d_agg[:, None, :], (tile_size, fanout, feat_width))]
  transfers between devices with their start and end apart: 3 -> 29, of which waited for: 0 -> 16; matrix products, arithmetic and copies ran while one was open for 7% -> 32% of each run, Pallas kernels for 0% -> 0%
where the time goes in v1:
time: 217 us; the launch traced here: 216 us
  waiting for transfers between devices  76.1 us (35%)
  starting transfers between devices  49.2 us (23%)
  matrix products  41.6 us (19%)
  other arithmetic  32.4 us (15%)
  local copies, waits for them, and re-layouts  15.9 us (7%)
    ppermute x27, waiting for transfers between devices, swap(): return lax.ppermute(value, AXES, [(i, i ^ mask) for i in range(n_dev)])  76 us
    ppermute x27, starting transfers between devices, swap(): return lax.ppermute(value, AXES, [(i, i ^ mask) for i in range(n_dev)])  40.7 us
    dot_general x9, matrix products, contract_rows(): lax.dot_general(left, right, (((0,), (0,)), ((), ())), preferred_element_...  17.1 us
    select_n x2, other arithmetic, both_cols(): jnp.where(side == 0, jnp.concatenate([value, got], 1), jnp.concatenate([g...  8.1 us
    select_n x4, other arithmetic, both(): jnp.where(b == 0, jnp.concatenate([value, got], 0), jnp.concatenate([got,...  7.5 us
    convert_element_type x1, other arithmetic, on_device(): counts = counts.astype(BF16)  5.77 us
    all_to_all x1, starting transfers between devices, on_device(): lax.all_to_all(outgoing.reshape(n_dev, capacity, width), AXES, split_axis...  4.97 us
  transfers between devices with their start and end apart: 29, of which 16 were waited for; matrix products, arithmetic and copies ran while one was open for 32% of the time, Pallas kernels for 0%

profile of v1, /device:TPU:0, one launch (start us, length us, event | category | flops | bytes accessed | tf_op | source)
XLA Modules:
  0.0 216.5 jit_solution(11857486865733873760)
XLA Ops:
  0.6 2.3 %constant_dynamic-update-slice_fusion.4 = (bf16[128,1024]{1,0:T(8,128)(2,1)S(1)}, bf16[256,1024]{1,0:T(8,128)(2,1)}, bf16[8,1024]{1,0:T(8,128)(2,1)S(1)}) fusion(bf16[512,1024]{1,0:T(8,128)(2,1)} %param.10, s32[8]{0:T(128)} %param.15), kind=kOutput, calls=%fused_computation.161 | convolution fusion | flops 8400894 | bytes 1097760 | tf_op jit(solution)/shard_map/dot_general | solution.py:63
  2.9 3.0 %collective-permute-start = (bf16[8,1024]{1,0:T(8,128)(2,1)S(1)}, bf16[8,1024]{1,0:T(8,128)(2,1)S(1)}, u32[]{:S(2)}, u32[]{:S(2)}) collective-permute-start(bf16[8,1024]{1,0:T(8,128)(2,1)S(1)} %get-tuple-element.53), channel_id=1, source_target_pairs={{0,2},{1,3},{2,0},{3,1},{4,6},{5,7},{6,4},{7,5},{8,10},{9,11},{10,... | collective-permute-start | bytes 49160 | tf_op jit(solution)/shard_map/ppermute | solution.py:53
  7.5 3.0 %convolution_convert_fusion = bf16[512,1024]{1,0:T(8,128)(2,1)} fusion(bf16[512,1024]{1,0:T(8,128)(2,1)} %param.10, s32[512]{0:T(512)S(1)} %broadcast_select_fusion), kind=kOutput, calls=%fused_computation.28 | convolution fusion | flops 537657344 | bytes 2099200 | tf_op jit(solution)/shard_map/dot_general | solution.py:64
  10.4 5.0 %all-to-all-start = ((bf16[32,16,1024]{2,1,0:T(8,128)(2,1)}), bf16[32,16,1024]{2,1,0:T(8,128)(2,1)}, u32[]{:S(2)}, u32[]{:S(2)}) async-start(bf16[32,16,1024]{2,1,0:T(8,128)(2,1)} %bitcast.66), calls=%async_computation | async-start | bytes 2097152 | tf_op jit(solution)/shard_map/all_to_all | solution.py:65
  15.6 5.8 %add_convert_fusion = bf16[512,1280]{1,0:T(8,128)(2,1)S(1)} fusion(s32[512]{0:T(512)S(1)} %bitcast.68, s32[512]{0:T(512)S(1)} %bitcast.69, s32[512]{0:T(512)S(1)} %bitcast.70, s32[512]{0:T(512)S(1)} %bitcast.71, s32[512]{0:T(512)S(1)} %bitcast.72, s32[512]{0:T(512)S(1)} %bitcast.73, s32[512]{0:T(512)S(1)} %bitcast.74, s32[512]{0:T(512)S(1)} %bitcast.75, ...), kind=kLoop, calls=%fused_computation | loop fusion | flops 31457280 | bytes 1343488 | tf_op jit(solution)/shard_map/convert_element_type | solution.py:83
  21.4 2.7 %collective-permute-start.1 = (bf16[16,1024]{1,0:T(8,128)(2,1)S(1)}, bf16[16,1024]{1,0:T(8,128)(2,1)S(1)}, u32[]{:S(2)}, u32[]{:S(2)}) collective-permute-start(bf16[16,1024]{1,0:T(8,128)(2,1)S(1)} %pad_maximum_fusion.6), channel_id=1, source_target_pairs={{0,4},{1,5},{2,6},{3,7},{4,0},{5,1},{6,2},{7,3},{8,12},{9,13},{10,... | collective-permute-start | bytes 98312 | tf_op jit(solution)/shard_map/ppermute | solution.py:53
  24.1 4.2 %fusion.59 = f32[512,1024]{1,0:T(8,128)} fusion(bf16[512,1024]{1,0:T(8,128)(2,1)S(1)} %copy-done.2, bf16[1024,1024]{1,0:T(8,128)(2,1)} %param.16), kind=kOutput, calls=%fused_computation.188 | convolution fusion | flops 1073741824 | bytes 5242880 | tf_op jit(solution)/shard_map/dot_general | solution.py:87
  28.2 14.7 %collective-permute-done.1 = bf16[16,1024]{1,0:T(8,128)(2,1)S(1)} collective-permute-done((bf16[16,1024]{1,0:T(8,128)(2,1)S(1)}, bf16[16,1024]{1,0:T(8,128)(2,1)S(1)}, u32[]{:S(2)}, u32[]{:S(2)}) %collective-permute-start.1) | collective-permute-done | bytes 32800 | tf_op jit(solution)/shard_map/ppermute | solution.py:53
  45.0 2.2 %collective-permute-done.2 = bf16[32,1024]{1,0:T(8,128)(2,1)S(1)} collective-permute-done((bf16[32,1024]{1,0:T(8,128)(2,1)S(1)}, bf16[32,1024]{1,0:T(8,128)(2,1)S(1)}, u32[]{:S(2)}, u32[]{:S(2)}) %collective-permute-start.2) | collective-permute-done | bytes 65568 | tf_op jit(solution)/shard_map/ppermute | solution.py:53
  50.0 2.2 %collective-permute-done.3 = bf16[64,1024]{1,0:T(8,128)(2,1)S(1)} collective-permute-done((bf16[64,1024]{1,0:T(8,128)(2,1)S(1)}, bf16[64,1024]{1,0:T(8,128)(2,1)S(1)}, u32[]{:S(2)}, u32[]{:S(2)}) %collective-permute-start.3) | collective-permute-done | bytes 131104 | tf_op jit(solution)/shard_map/ppermute | solution.py:53
  55.7 2.2 %fusion.5 = f32[512,1024]{1,0:T(8,128)S(1)} fusion(bf16[512,1024]{1,0:T(8,128)(2,1)} %bitcast.19, bf16[512,1280]{1,0:T(8,128)(2,1)} %copy-done.3), kind=kOutput, calls=%fused_computation.51 | convolution fusion | flops 536870912 | bytes 3670016 | tf_op jit(solution)/shard_map/dot_general | solution.py:88
  58.0 2.7 %multiply_convert_fusion.3 = bf16[512,1024]{1,0:T(8,128)(2,1)} fusion(f32[512,1024]{1,0:T(8,128)S(1)} %copy-done.6, f32[512,1024]{1,0:T(8,128)S(1)} %fusion.5, bf16[256,1024]{1,0:T(8,128)(2,1)} %constant_dynamic-update-slice_fusion.5, f32[512]{0:T(512)S(1)} %convert_divide_fusion, bf16[512,1280]{1,0:T(8,128)(2,1)} %copy-done.3), kind=kOutput, calls=%fused_computation.24 | convolution fusion | flops 270532608 | bytes 6031360 | tf_op jit(solution)/shard_map/dot_general | solution.py:89
  60.7 4.2 %multiply_convert_fusion.1 = (bf16[512,1024]{1,0:T(8,128)(2,1)S(1)}, bf16[512,1024]{1,0:T(8,128)(2,1)}) fusion(bf16[512,1024]{1,0:T(8,128)(2,1)S(1)} %copy-done.26, bf16[512,1024]{1,0:T(8,128)(2,1)} %multiply_convert_fusion.3, bf16[1024,1024]{1,0:T(8,128)(2,1)S(1)} %copy-done, f32[512,1024]{1,0:T(8,128)S(1)} %copy-done.28, f32[1024]{0:T(1024)S(1)} %copy-done.27), kind=kOutput, calls=%fused_computation.21 | convolution fusion | flops 1081081856 | bytes 8392704 | tf_op jit(solution)/shard_map/dot_general | solution.py:92
  73.3 2.3 %collective-permute-done.6 = bf16[64,1024]{1,0:T(8,128)(2,1)S(1)} collective-permute-done((bf16[64,1024]{1,0:T(8,128)(2,1)S(1)}, bf16[64,1024]{1,0:T(8,128)(2,1)S(1)}, u32[]{:S(2)}, u32[]{:S(2)}) %collective-permute-start.6) | collective-permute-done | bytes 131104 | tf_op jit(solution)/shard_map/ppermute | solution.py:53
  88.5 6.7 %collective-permute-done.10 = bf16[512,512]{0,1:T(8,128)(2,1)} collective-permute-done((bf16[512,512]{0,1:T(8,128)(2,1)S(1)}, bf16[512,512]{0,1:T(8,128)(2,1)}, u32[]{:S(2)}, u32[]{:S(2)}) %collective-permute-start.10) | collective-permute-done | bytes 524320 | tf_op jit(solution)/shard_map/ppermute | solution.py:53
  101.1 2.7 %collective-permute-done.11 = bf16[256,512]{0,1:T(8,128)(2,1)S(1)} collective-permute-done((bf16[256,512]{0,1:T(8,128)(2,1)S(1)}, bf16[256,512]{0,1:T(8,128)(2,1)S(1)}, u32[]{:S(2)}, u32[]{:S(2)}) %collective-permute-start.11) | collective-permute-done | bytes 262176 | tf_op jit(solution)/shard_map/ppermute | solution.py:53
  104.9 2.2 %collective-permute-done.14 = bf16[256,512]{0,1:T(8,128)(2,1)S(1)} collective-permute-done((bf16[256,512]{0,1:T(8,128)(2,1)S(1)}, bf16[256,512]{0,1:T(8,128)(2,1)S(1)}, u32[]{:S(2)}, u32[]{:S(2)}) %collective-permute-start.14) | collective-permute-done | bytes 262176 | tf_op jit(solution)/shard_map/ppermute | solution.py:53
  111.7 2.6 %collective-permute-start.17 = (bf16[144,512]{0,1:T(8,128)(2,1)}, bf16[144,512]{0,1:T(8,128)(2,1)}, u32[]{:S(2)}, u32[]{:S(2)}) collective-permute-start(bf16[144,512]{0,1:T(8,128)(2,1)} %pad_maximum_fusion.2), channel_id=1, source_target_pairs={{0,6},{1,7},{2,4},{3,5},{4,2},{5,3},{6,0},{7,1},{8,14},{9,15},{10,... | collective-permute-start | bytes 442376 | tf_op jit(solution)/shard_map/ppermute | solution.py:53
  116.2 3.5 %all-to-all-start.1 = ((bf16[32,16,1024]{2,1,0:T(8,128)(2,1)}), bf16[32,16,1024]{2,1,0:T(8,128)(2,1)}, u32[]{:S(2)}, u32[]{:S(2)}) async-start(bf16[32,16,1024]{2,1,0:T(8,128)(2,1)} %bitcast.65), calls=%async_computation.1 | async-start | bytes 2097152 | tf_op jit(solution)/shard_map/all_to_all | solution.py:98
  119.8 13.2 %collective-permute-done.16 = bf16[144,512]{0,1:T(8,128)(2,1)S(1)} collective-permute-done((bf16[144,512]{0,1:T(8,128)(2,1)}, bf16[144,512]{0,1:T(8,128)(2,1)S(1)}, u32[]{:S(2)}, u32[]{:S(2)}) %collective-permute-start.16) | collective-permute-done | bytes 147488 | tf_op jit(solution)/shard_map/ppermute | solution.py:53
  136.0 11.7 %collective-permute-start.18 = (bf16[2,64,512]{1,2,0:T(8,128)(2,1)}, bf16[2,64,512]{1,2,0:T(8,128)(2,1)}, u32[]{:S(2)}, u32[]{:S(2)}) collective-permute-start(bf16[2,64,512]{1,2,0:T(8,128)(2,1)} %pad_maximum_fusion.3), channel_id=1, source_target_pairs={{0,2},{1,3},{2,0},{3,1},{4,6},{5,7},{6,4},{7,5},{8,10},{9,11},{10,... | collective-permute-start | bytes 393224 | tf_op jit(solution)/shard_map/ppermute | solution.py:53
  147.7 2.4 %collective-permute-start.20 = (bf16[2,64,512]{1,2,0:T(8,128)(2,1)}, bf16[2,64,512]{1,2,0:T(8,128)(2,1)}, u32[]{:S(2)}, u32[]{:S(2)}) collective-permute-start(bf16[2,64,512]{1,2,0:T(8,128)(2,1)} %pad_maximum_fusion.3), channel_id=1, source_target_pairs={{0,6},{1,7},{2,4},{3,5},{4,2},{5,3},{6,0},{7,1},{8,14},{9,15},{10,... | collective-permute-start | bytes 393224 | tf_op jit(solution)/shard_map/ppermute | solution.py:53
  151.5 4.9 %collective-permute-done.18 = bf16[2,64,512]{1,2,0:T(8,128)(2,1)} collective-permute-done((bf16[2,64,512]{1,2,0:T(8,128)(2,1)}, bf16[2,64,512]{1,2,0:T(8,128)(2,1)}, u32[]{:S(2)}, u32[]{:S(2)}) %collective-permute-start.18) | collective-permute-done | bytes 131104 | tf_op jit(solution)/shard_map/ppermute | solution.py:53
  157.4 15.4 %collective-permute-done.19 = bf16[2,64,512]{1,2,0:T(8,128)(2,1)} collective-permute-done((bf16[2,64,512]{1,2,0:T(8,128)(2,1)}, bf16[2,64,512]{1,2,0:T(8,128)(2,1)}, u32[]{:S(2)}, u32[]{:S(2)}) %collective-permute-start.19) | collective-permute-done | bytes 131104 | tf_op jit(solution)/shard_map/ppermute | solution.py:53
  179.4 3.1 %collective-permute-done.24 = bf16[256,512]{1,0:T(8,128)(2,1)} collective-permute-done((bf16[256,512]{1,0:T(8,128)(2,1)S(1)}, bf16[256,512]{1,0:T(8,128)(2,1)}, u32[]{:S(2)}, u32[]{:S(2)}) %collective-permute-start.24) | collective-permute-done | bytes 262176 | tf_op jit(solution)/shard_map/ppermute | solution.py:53
  185.1 2.9 %collective-permute-done.21 = bf16[256,512]{1,0:T(8,128)(2,1)S(1)} collective-permute-done((bf16[256,512]{1,0:T(8,128)(2,1)}, bf16[256,512]{1,0:T(8,128)(2,1)S(1)}, u32[]{:S(2)}, u32[]{:S(2)}) %collective-permute-start.21) | collective-permute-done | bytes 262176 | tf_op jit(solution)/shard_map/ppermute | solution.py:53
  193.0 2.6 %fusion.60 = f32[512,1024]{1,0:T(8,128)} fusion(bf16[512,1024]{1,0:T(8,128)(2,1)S(1)} %copy-done.16, bf16[1024,1024]{1,0:T(8,128)(2,1)S(1)} %copy-done.25), kind=kOutput, calls=%fused_computation.189 | convolution fusion | flops 1073741824 | bytes 5242880 | tf_op jit(solution)/shard_map/dot_general | solution.py:21
  199.5 2.8 %maximum_select_fusion.2 = bf16[1024,512]{1,0:T(8,128)(2,1)} fusion(bf16[512,512]{1,0:T(8,128)(2,1)} %collective-permute-done.22, bf16[512,512]{1,0:T(8,128)(2,1)} %maximum_select_fusion.4, pred[]{:T(512)S(6)} %eq.351), kind=kLoop, calls=%fused_computation.31 | loop fusion | flops 4718592 | bytes 2097153 | tf_op jit(solution)/shard_map/jit(_where)/select_n | solution.py:168
  203.2 2.0 fusion
  205.3 3.1 %add_convert_fusion.1 = bf16[512,1024]{1,0:T(8,128)(2,1)} fusion(f32[512,1024]{1,0:T(8,128)S(1)} %fusion, f32[512,1024]{1,0:T(8,128)} %fusion.60, f32[512,1024]{1,0:T(8,128)S(1)} %copy-done.5, bf16[8,1024]{1,0:T(8,128)(2,1)S(1)} %get-tuple-element.4, bf16[8,1024]{1,0:T(8,128)(2,1)S(1)} %get-tuple-element.5, pred[8,512]{1,0:T(8,128)(4,1)S(1)} %iota_compare_fusion.20), kind=kOutput, calls=%fused_computation.19 | convolution fusion | flops 18948096 | bytes 7376896 | tf_op jit(solution)/shard_map/dot_general | solution.py:17
  208.4 3.7 %maximum_select_fusion.1 = bf16[1024,1024]{1,0:T(8,128)(2,1)} fusion(bf16[1024,512]{1,0:T(8,128)(2,1)} %collective-permute-done.26, bf16[1024,512]{1,0:T(8,128)(2,1)S(1)} %maximum_select_fusion.3, pred[]{:T(512)S(6)} %eq.350), kind=kLoop, calls=%fused_computation.18 | loop fusion | flops 9437184 | bytes 4194305 | tf_op jit(solution)/shard_map/jit(_where)/select_n | solution.py:178
  212.1 4.4 %maximum_select_fusion = bf16[1024,1024]{1,0:T(8,128)(2,1)} fusion(bf16[1024,512]{1,0:T(8,128)(2,1)} %collective-permute-done.23, bf16[1024,512]{1,0:T(8,128)(2,1)} %maximum_select_fusion.2, pred[]{:T(512)S(6)} %eq.350), kind=kLoop, calls=%fused_computation.17 | loop fusion | flops 9437184 | bytes 4194305 | tf_op jit(solution)/shard_map/jit(_where)/select_n | solution.py:178
  (186 shorter events, 68.7 us)
Async XLA Ops:
  0.6 60.1 %copy-start = (bf16[1024,1024]{1,0:T(8,128)(2,1)S(1)}, bf16[1024,1024]{1,0:T(8,128)(2,1)}, u32[]{:S(2)}) copy-start(bf16[1024,1024]{1,0:T(8,128)(2,1)} %param.17) | copy-start | bytes 6291460
  2.9 18.5 %collective-permute-start = (bf16[8,1024]{1,0:T(8,128)(2,1)S(1)}, bf16[8,1024]{1,0:T(8,128)(2,1)S(1)}, u32[]{:S(2)}, u32[]{:S(2)}) collective-permute-start(bf16[8,1024]{1,0:T(8,128)(2,1)S(1)} %get-tuple-element.53), channel_id=1, source_target_pairs={{0,2},{1,3},{2,0},{3,1},{4,6},{5,7},{6,4},{7,5},{8,10},{9,11},{10,... | collective-permute-start | bytes 49160 | tf_op jit(solution)/shard_map/ppermute | solution.py:53
  10.4 45.3 %all-to-all-start = ((bf16[32,16,1024]{2,1,0:T(8,128)(2,1)}), bf16[32,16,1024]{2,1,0:T(8,128)(2,1)}, u32[]{:S(2)}, u32[]{:S(2)}) async-start(bf16[32,16,1024]{2,1,0:T(8,128)(2,1)} %bitcast.66), calls=%async_computation | async-start | bytes 2097152 | tf_op jit(solution)/shard_map/all_to_all | solution.py:65
  21.4 31.5 %copy-start.3 = (bf16[512,1280]{1,0:T(8,128)(2,1)}, bf16[512,1280]{1,0:T(8,128)(2,1)S(1)}, u32[]{:S(2)}) copy-start(bf16[512,1280]{1,0:T(8,128)(2,1)S(1)} %add_convert_fusion) | copy-start | bytes 3932164
  21.4 21.5 %collective-permute-start.1 = (bf16[16,1024]{1,0:T(8,128)(2,1)S(1)}, bf16[16,1024]{1,0:T(8,128)(2,1)S(1)}, u32[]{:S(2)}, u32[]{:S(2)}) collective-permute-start(bf16[16,1024]{1,0:T(8,128)(2,1)S(1)} %pad_maximum_fusion.6), channel_id=1, source_target_pairs={{0,4},{1,5},{2,6},{3,7},{4,0},{5,1},{6,2},{7,3},{8,12},{9,13},{10,... | collective-permute-start | bytes 98312 | tf_op jit(solution)/shard_map/ppermute | solution.py:53
  42.9 4.3 %collective-permute-start.2 = (bf16[32,1024]{1,0:T(8,128)(2,1)S(1)}, bf16[32,1024]{1,0:T(8,128)(2,1)S(1)}, u32[]{:S(2)}, u32[]{:S(2)}) collective-permute-start(bf16[32,1024]{1,0:T(8,128)(2,1)S(1)} %pad_maximum_fusion.5), channel_id=1, source_target_pairs={{0,1},{1,0},{2,3},{3,2},{4,5},{5,4},{6,7},{7,6},{8,9},{9,8},{10,11... | collective-permute-start | bytes 196616 | tf_op jit(solution)/shard_map/ppermute | solution.py:53
  47.2 5.0 %collective-permute-start.3 = (bf16[64,1024]{1,0:T(8,128)(2,1)S(1)}, bf16[64,1024]{1,0:T(8,128)(2,1)S(1)}, u32[]{:S(2)}, u32[]{:S(2)}) collective-permute-start(bf16[64,1024]{1,0:T(8,128)(2,1)S(1)} %pad_maximum_fusion.4), channel_id=1, source_target_pairs={{0,16},{1,17},{2,18},{3,19},{4,20},{5,21},{6,22},{7,23},{8,24},{9,... | collective-permute-start | bytes 393224 | tf_op jit(solution)/shard_map/ppermute | solution.py:53
  52.9 2.0 collective-permute-start.4
  67.9 1.7 collective-permute-start.5
  68.5 12.1 %collective-permute-start.9 = (bf16[512,1024]{1,0:T(8,128)(2,1)S(1)}, bf16[512,1024]{1,0:T(8,128)(2,1)}, u32[]{:S(2)}, u32[]{:S(2)}) collective-permute-start(bf16[512,1024]{1,0:T(8,128)(2,1)S(1)} %copy-done.2), channel_id=1, source_target_pairs={{0,8},{1,9},{2,10},{3,11},{4,12},{5,13},{6,14},{7,15},{8,0},{9,1},... | collective-permute-start | bytes 3145736 | tf_op jit(solution)/shard_map/ppermute | solution.py:53
  68.6 15.7 %collective-permute-start.12 = (bf16[512,1024]{1,0:T(8,128)(2,1)}, bf16[512,1024]{1,0:T(8,128)(2,1)S(1)}, u32[]{:S(2)}, u32[]{:S(2)}) collective-permute-start(bf16[512,1024]{1,0:T(8,128)(2,1)} %multiply_convert_fusion.3), channel_id=1, source_target_pairs={{0,8},{1,9},{2,10},{3,11},{4,12},{5,13},{6,14},{7,15},{8,0},{9,1},... | collective-permute-start | bytes 3145736 | tf_op jit(solution)/shard_map/ppermute | solution.py:53
  69.7 5.8 %collective-permute-start.6 = (bf16[64,1024]{1,0:T(8,128)(2,1)S(1)}, bf16[64,1024]{1,0:T(8,128)(2,1)S(1)}, u32[]{:S(2)}, u32[]{:S(2)}) collective-permute-start(bf16[64,1024]{1,0:T(8,128)(2,1)S(1)} %slice.279), channel_id=1, source_target_pairs={{0,16},{1,17},{2,18},{3,19},{4,20},{5,21},{6,22},{7,23},{8,24},{9,... | collective-permute-start | bytes 393224 | tf_op jit(solution)/shard_map/ppermute | solution.py:53
  73.1 7.5 %collective-permute-start.8 = (bf16[512,512]{1,0:T(8,128)(2,1)S(1)}, bf16[512,512]{1,0:T(8,128)(2,1)S(1)}, u32[]{:S(2)}, u32[]{:S(2)}) collective-permute-start(bf16[512,512]{1,0:T(8,128)(2,1)S(1)} %constant_dynamic-slice_fusion), channel_id=1, source_target_pairs={{0,8},{1,9},{2,10},{3,11},{4,12},{5,13},{6,14},{7,15},{8,0},{9,1},... | collective-permute-start | bytes 1572872 | tf_op jit(solution)/shard_map/ppermute | solution.py:53
  75.6 4.3 %collective-permute-start.7 = (bf16[32,1024]{1,0:T(8,128)(2,1)S(1)}, bf16[32,1024]{1,0:T(8,128)(2,1)S(1)}, u32[]{:S(2)}, u32[]{:S(2)}) collective-permute-start(bf16[32,1024]{1,0:T(8,128)(2,1)S(1)} %slice.280), channel_id=1, source_target_pairs={{0,1},{1,0},{2,3},{3,2},{4,5},{5,4},{6,7},{7,6},{8,9},{9,8},{10,11... | collective-permute-start | bytes 196616 | tf_op jit(solution)/shard_map/ppermute | solution.py:53
  82.7 12.5 %collective-permute-start.10 = (bf16[512,512]{0,1:T(8,128)(2,1)S(1)}, bf16[512,512]{0,1:T(8,128)(2,1)}, u32[]{:S(2)}, u32[]{:S(2)}) collective-permute-start(bf16[512,512]{0,1:T(8,128)(2,1)S(1)} %fusion.1), channel_id=1, source_target_pairs={{0,16},{1,17},{2,18},{3,19},{4,20},{5,21},{6,22},{7,23},{8,24},{9,... | collective-permute-start | bytes 1572872 | tf_op jit(solution)/shard_map/ppermute | solution.py:53
  85.9 13.4 %collective-permute-start.13 = (bf16[512,512]{0,1:T(8,128)(2,1)}, bf16[512,512]{0,1:T(8,128)(2,1)}, u32[]{:S(2)}, u32[]{:S(2)}) collective-permute-start(bf16[512,512]{0,1:T(8,128)(2,1)} %dynamic-slice_convert_fusion), channel_id=1, source_target_pairs={{0,1},{1,0},{2,3},{3,2},{4,5},{5,4},{6,7},{7,6},{8,9},{9,8},{10,11... | collective-permute-start | bytes 1572872 | tf_op jit(solution)/shard_map/ppermute | solution.py:53
  96.8 7.0 %collective-permute-start.11 = (bf16[256,512]{0,1:T(8,128)(2,1)S(1)}, bf16[256,512]{0,1:T(8,128)(2,1)S(1)}, u32[]{:S(2)}, u32[]{:S(2)}) collective-permute-start(bf16[256,512]{0,1:T(8,128)(2,1)S(1)} %dynamic-slice_convert_fusion.3), channel_id=1, source_target_pairs={{0,1},{1,0},{2,3},{3,2},{4,5},{5,4},{6,7},{7,6},{8,9},{9,8},{10,11... | collective-permute-start | bytes 786440 | tf_op jit(solution)/shard_map/ppermute | solution.py:53
  100.6 6.4 %collective-permute-start.14 = (bf16[256,512]{0,1:T(8,128)(2,1)S(1)}, bf16[256,512]{0,1:T(8,128)(2,1)S(1)}, u32[]{:S(2)}, u32[]{:S(2)}) collective-permute-start(bf16[256,512]{0,1:T(8,128)(2,1)S(1)} %dynamic-slice_convert_fusion.2), channel_id=1, source_target_pairs={{0,16},{1,17},{2,18},{3,19},{4,20},{5,21},{6,22},{7,23},{8,24},{9,... | collective-permute-start | bytes 786440 | tf_op jit(solution)/shard_map/ppermute | solution.py:53
  108.2 11.5 %collective-permute-start.15 = (bf16[144,512]{0,1:T(8,128)(2,1)}, bf16[144,512]{0,1:T(8,128)(2,1)S(1)}, u32[]{:S(2)}, u32[]{:S(2)}) collective-permute-start(bf16[144,512]{0,1:T(8,128)(2,1)} %pad_maximum_fusion), channel_id=1, source_target_pairs={{0,2},{1,3},{2,0},{3,1},{4,6},{5,7},{6,4},{7,5},{8,10},{9,11},{10,... | collective-permute-start | bytes 442376 | tf_op jit(solution)/shard_map/ppermute | solution.py:53
  109.1 23.9 %collective-permute-start.16 = (bf16[144,512]{0,1:T(8,128)(2,1)}, bf16[144,512]{0,1:T(8,128)(2,1)S(1)}, u32[]{:S(2)}, u32[]{:S(2)}) collective-permute-start(bf16[144,512]{0,1:T(8,128)(2,1)} %pad_maximum_fusion.1), channel_id=1, source_target_pairs={{0,4},{1,5},{2,6},{3,7},{4,0},{5,1},{6,2},{7,3},{8,12},{9,13},{10,... | collective-permute-start | bytes 442376 | tf_op jit(solution)/shard_map/ppermute | solution.py:53
  111.7 21.3 %collective-permute-start.17 = (bf16[144,512]{0,1:T(8,128)(2,1)}, bf16[144,512]{0,1:T(8,128)(2,1)}, u32[]{:S(2)}, u32[]{:S(2)}) collective-permute-start(bf16[144,512]{0,1:T(8,128)(2,1)} %pad_maximum_fusion.2), channel_id=1, source_target_pairs={{0,6},{1,7},{2,4},{3,5},{4,2},{5,3},{6,0},{7,1},{8,14},{9,15},{10,... | collective-permute-start | bytes 442376 | tf_op jit(solution)/shard_map/ppermute | solution.py:53
  116.2 87.0 %all-to-all-start.1 = ((bf16[32,16,1024]{2,1,0:T(8,128)(2,1)}), bf16[32,16,1024]{2,1,0:T(8,128)(2,1)}, u32[]{:S(2)}, u32[]{:S(2)}) async-start(bf16[32,16,1024]{2,1,0:T(8,128)(2,1)} %bitcast.65), calls=%async_computation.1 | async-start | bytes 2097152 | tf_op jit(solution)/shard_map/all_to_all | solution.py:98
  136.0 20.5 %collective-permute-start.18 = (bf16[2,64,512]{1,2,0:T(8,128)(2,1)}, bf16[2,64,512]{1,2,0:T(8,128)(2,1)}, u32[]{:S(2)}, u32[]{:S(2)}) collective-permute-start(bf16[2,64,512]{1,2,0:T(8,128)(2,1)} %pad_maximum_fusion.3), channel_id=1, source_target_pairs={{0,2},{1,3},{2,0},{3,1},{4,6},{5,7},{6,4},{7,5},{8,10},{9,11},{10,... | collective-permute-start | bytes 393224 | tf_op jit(solution)/shard_map/ppermute | solution.py:53
  147.6 25.2 %collective-permute-start.19 = (bf16[2,64,512]{1,2,0:T(8,128)(2,1)}, bf16[2,64,512]{1,2,0:T(8,128)(2,1)}, u32[]{:S(2)}, u32[]{:S(2)}) collective-permute-start(bf16[2,64,512]{1,2,0:T(8,128)(2,1)} %pad_maximum_fusion.3), channel_id=1, source_target_pairs={{0,4},{1,5},{2,6},{3,7},{4,0},{5,1},{6,2},{7,3},{8,12},{9,13},{10,... | collective-permute-start | bytes 393224 | tf_op jit(solution)/shard_map/ppermute | solution.py:53
  147.7 27.2 %collective-permute-start.20 = (bf16[2,64,512]{1,2,0:T(8,128)(2,1)}, bf16[2,64,512]{1,2,0:T(8,128)(2,1)}, u32[]{:S(2)}, u32[]{:S(2)}) collective-permute-start(bf16[2,64,512]{1,2,0:T(8,128)(2,1)} %pad_maximum_fusion.3), channel_id=1, source_target_pairs={{0,6},{1,7},{2,4},{3,5},{4,2},{5,3},{6,0},{7,1},{8,14},{9,15},{10,... | collective-permute-start | bytes 393224 | tf_op jit(solution)/shard_map/ppermute | solution.py:53
  151.4 27.9 %copy-start.24 = (s32[8]{0:T(128)S(1)}, s32[8]{0:T(128)}, u32[]{:S(2)}) copy-start(s32[8]{0:T(128)} %param.15) | copy-start | bytes 100
  176.0 6.5 %collective-permute-start.24 = (bf16[256,512]{1,0:T(8,128)(2,1)S(1)}, bf16[256,512]{1,0:T(8,128)(2,1)}, u32[]{:S(2)}, u32[]{:S(2)}) collective-permute-start(bf16[256,512]{1,0:T(8,128)(2,1)S(1)} %constant_dynamic-update-slice_fusion.11), channel_id=1, source_target_pairs={{0,16},{1,17},{2,18},{3,19},{4,20},{5,21},{6,22},{7,23},{8,24},{9,... | collective-permute-start | bytes 786440 | tf_op jit(solution)/shard_map/ppermute | solution.py:53
  178.6 9.5 %collective-permute-start.21 = (bf16[256,512]{1,0:T(8,128)(2,1)}, bf16[256,512]{1,0:T(8,128)(2,1)S(1)}, u32[]{:S(2)}, u32[]{:S(2)}) collective-permute-start(bf16[256,512]{1,0:T(8,128)(2,1)} %constant_dynamic-update-slice_fusion.15), channel_id=1, source_target_pairs={{0,1},{1,0},{2,3},{3,2},{4,5},{5,4},{6,7},{7,6},{8,9},{9,8},{10,11... | collective-permute-start | bytes 786440 | tf_op jit(solution)/shard_map/ppermute | solution.py:53
  183.7 13.3 %collective-permute-start.25 = (bf16[512,512]{1,0:T(8,128)(2,1)S(1)}, bf16[512,512]{1,0:T(8,128)(2,1)}, u32[]{:S(2)}, u32[]{:S(2)}) collective-permute-start(bf16[512,512]{1,0:T(8,128)(2,1)S(1)} %maximum_select_fusion.5), channel_id=1, source_target_pairs={{0,1},{1,0},{2,3},{3,2},{4,5},{5,4},{6,7},{7,6},{8,9},{9,8},{10,11... | collective-permute-start | bytes 1572872 | tf_op jit(solution)/shard_map/ppermute | solution.py:53
  190.0 9.5 %collective-permute-start.22 = (bf16[512,512]{1,0:T(8,128)(2,1)}, bf16[512,512]{1,0:T(8,128)(2,1)}, u32[]{:S(2)}, u32[]{:S(2)}) collective-permute-start(bf16[512,512]{1,0:T(8,128)(2,1)} %maximum_select_fusion.4), channel_id=1, source_target_pairs={{0,16},{1,17},{2,18},{3,19},{4,20},{5,21},{6,22},{7,23},{8,24},{9,... | collective-permute-start | bytes 1572872 | tf_op jit(solution)/shard_map/ppermute | solution.py:53
  198.6 9.8 %collective-permute-start.26 = (bf16[1024,512]{1,0:T(8,128)(2,1)S(1)}, bf16[1024,512]{1,0:T(8,128)(2,1)}, u32[]{:S(2)}, u32[]{:S(2)}) collective-permute-start(bf16[1024,512]{1,0:T(8,128)(2,1)S(1)} %maximum_select_fusion.3), channel_id=1, source_target_pairs={{0,8},{1,9},{2,10},{3,11},{4,12},{5,13},{6,14},{7,15},{8,0},{9,1},... | collective-permute-start | bytes 3145736 | tf_op jit(solution)/shard_map/ppermute | solution.py:53
  202.3 9.8 %collective-permute-start.23 = (bf16[1024,512]{1,0:T(8,128)(2,1)}, bf16[1024,512]{1,0:T(8,128)(2,1)}, u32[]{:S(2)}, u32[]{:S(2)}) collective-permute-start(bf16[1024,512]{1,0:T(8,128)(2,1)} %maximum_select_fusion.2), channel_id=1, source_target_pairs={{0,8},{1,9},{2,10},{3,11},{4,12},{5,13},{6,14},{7,15},{8,0},{9,1},... | collective-permute-start | bytes 3145736 | tf_op jit(solution)/shard_map/ppermute | solution.py:53
  (26 other events, 145.8 us)

commit v2 on v0

v2 whole, which is shorter than its diff:
```python
import functools

import jax
import jax.numpy as jnp
from jax import lax
from jax.experimental import pallas as pl
from jax.experimental.pallas import tpu as pltpu
from jax.sharding import PartitionSpec as P

AXES = ("row", "col")
BF16 = jnp.bfloat16
F32 = jnp.float32
CHUNK = 256
HBM = pl.BlockSpec(memory_space=pl.ANY)
VMEM_LIMIT = 56 << 20
SMEM = pl.BlockSpec(memory_space=pltpu.SMEM)


def mul(left, right):
    return jnp.dot(left, right, preferred_element_type=F32)


def mul_t(left, right):
    return lax.dot_general(left, right, (((1,), (1,)), ((), ())), preferred_element_type=F32)


def t_mul(left, right):
    return lax.dot_general(left, right, (((0,), (0,)), ((), ())), preferred_element_type=F32)


def run(body, scalars, ins, outs, flops=0, scratch=()):
    n_in, n_out = len(ins), len(outs)
    outs = [jax.ShapeDtypeStruct(shape, dtype) for shape, dtype in outs]

    def kernel(*refs):
        scalar_ref, refs = refs[0], refs[1:]
        in_hbm, out_hbm = refs[:n_in], refs[n_in : n_in + n_out]
        refs = refs[n_in + n_out :]
        in_buf, out_buf = refs[:n_in], refs[n_in : n_in + n_out]
        extra, (in_sem, out_sem) = refs[n_in + n_out : -2], refs[-2:]
        loads = [pltpu.make_async_copy(in_hbm[i], in_buf[i], in_sem.at[i]) for i in range(n_in)]
        stores = [pltpu.make_async_copy(out_buf[i], out_hbm[i], out_sem.at[i]) for i in range(n_out)]
        for load in loads:
            load.start()

        def need(*which):
            for i in which:
                loads[i].wait()

        def emit(*which):
            for i in which:
                stores[i].start()

        body(scalar_ref, in_buf, out_buf, need, emit, *extra)
        for store in stores:
            store.wait()

    held = sum(a.size * a.dtype.itemsize for a in [*ins, *outs])
    return pl.pallas_call(
        kernel,
        out_shape=outs,
        in_specs=[SMEM] + [HBM] * n_in,
        out_specs=[HBM] * n_out,
        scratch_shapes=[pltpu.VMEM(a.shape, a.dtype) for a in [*ins, *outs]]
        + list(scratch)
        + [pltpu.SemaphoreType.DMA((n_in,)), pltpu.SemaphoreType.DMA((n_out,))],
        compiler_params=pltpu.CompilerParams(vmem_limit_bytes=VMEM_LIMIT),
        cost_estimate=pl.CostEstimate(flops=flops, bytes_accessed=held, transcendentals=0),
    )(scalars, *ins)


def one_hot(ids, n_local):
    rows = lax.broadcasted_iota(jnp.int32, (n_local, ids.shape[1]), 0)
    return (rows == ids).astype(F32).astype(BF16)


def pack_body(scalars, ins, outs, need, emit):
    features, send_rows, send_count, hub_rows = ins
    outgoing, own_hubs, chosen = outs
    n_local = features.shape[0]
    n_slots, n_dev = send_rows.shape[1], send_count.shape[1]
    capacity = n_slots // n_dev
    need(1, 2, 3)
    peer = lax.broadcasted_iota(jnp.int32, (n_dev, n_slots), 0)
    lane = lax.broadcasted_iota(jnp.int32, (n_dev, n_slots), 1)
    spread = (lane // capacity == peer).astype(F32)
    live = mul(send_count[...].astype(F32), spread)
    slot = lax.broadcasted_iota(jnp.int32, (1, n_slots), 1) % capacity
    ids = jnp.where(slot.astype(F32) < live, send_rows[...], -1)
    chosen[...] = ids
    emit(2)
    pick = one_hot(ids, n_local)
    pick_hub = one_hot(hub_rows[...], n_local)
    need(0)
    own_hubs[...] = t_mul(pick_hub, features[...]).astype(BF16)
    emit(1)
    outgoing[...] = t_mul(pick, features[...]).astype(BF16)
    emit(0)


def seed_body(side, ins, outs, need, emit, d_pre_all, aggregate):
    counts, arrived, hubs, summed, inv_deg, w_neigh, own_pre, cotangent, counts_t = ins
    hidden, d_pre, d_agg, d_pre_other, aggregate_t, d_arrived, hub_keep, hub_send = outs
    n_local, width = cotangent.shape
    n_slots = arrived.shape[0]
    n_hubs = hubs.shape[0]
    half = width // 2
    need(0, 1, 2, 3, 4)
    inv = inv_deg[...]
    for c in range(0, width, CHUNK):
        cols = slice(c, c + CHUNK)
        total = summed[:, cols] + mul(counts[:, :n_slots], arrived[:, cols])
        total = total + mul(counts[:, n_slots:], hubs[:, cols])
        mean = total * inv
        aggregate[:, cols] = mean.astype(BF16)
        aggregate_t[cols, :] = mean.T.astype(BF16)
    emit(4)
    need(5, 6, 7)
    for c in range(0, width, CHUNK):
        cols = slice(c, c + CHUNK)
        pre = own_pre[:, cols] + mul(aggregate[...], w_neigh[:, cols])
        sig = 0.5 + 0.5 * jnp.tanh(0.5 * pre)
        hidden[:, cols] = (pre * sig).astype(BF16)
        grad = cotangent[:, cols].astype(F32) * (sig * (1.0 + pre * (1.0 - sig)))
        grad = grad.astype(BF16)
        d_pre_all[:, cols] = grad
        part = slice(c % half, c % half + CHUNK)

        @pl.when(side[0] == c // half)
        def _():
            d_pre[:, part] = grad

        @pl.when(side[0] != c // half)
        def _():
            d_pre_other[:, part] = grad

    emit(3, 1, 0)
    need(8)
    for c in range(0, width, CHUNK):
        cols = slice(c, c + CHUNK)
        grad = (mul_t(d_pre_all[...], w_neigh[cols, :]) * inv).astype(BF16)
        d_agg[:, cols] = grad
        d_arrived[:, cols] = mul(counts_t[:n_slots, :], grad).astype(BF16)
        d_hubs = mul(counts_t[n_slots:, :], grad)
        part = slice(c % half, c % half + CHUNK)
        hub_keep[c // half, :, part] = d_hubs[: n_hubs // 2]
        hub_send[c // half, :, part] = d_hubs[n_hubs // 2 :].astype(BF16)
    emit(5, 7, 6, 2)


def hub_rows_of(total, k, rows):
    return jnp.concatenate([total[0, k * rows : (k + 1) * rows], total[1, k * rows : (k + 1) * rows]], 0)


def weight_body(n_part, with_hubs, mine, ins, outs, need, emit):
    own, peer, d_own, d_peer = ins[:4]
    rows, half = outs[0].shape
    need(*range(len(ins)))
    for k in [*range(1, n_part), 0]:
        at = pl.multiple_of((mine[0] ^ k) * rows, rows)
        for r in range(0, rows, min(rows, CHUNK)):
            block = pl.ds(at + r, min(rows, CHUNK))
            total = mul(own[block, :], d_own[...]) + mul(peer[block, :], d_peer[...])
            outs[k][r : r + min(rows, CHUNK), :] = total.astype(outs[k].dtype)
        if k > 0 and with_hubs:
            hubs = ins[4][...] + ins[5][...].astype(F32)
            size = hubs.shape[1] // n_part
            outs[k][rows:, :] = hub_rows_of(hubs, k, size).astype(BF16)
        if k > 0:
            emit(k)
    if with_hubs:
        size = ins[4].shape[1] // n_part
        outs[n_part][...] = ins[4][:, :size] + ins[5][:, :size].astype(F32)
        emit(n_part)
    emit(0)


def fold_body(n_part, n_got, mine, ins, outs, need, emit, total):
    self_keep, neigh_keep, hubs = ins[:3]
    self_got, neigh_got = ins[3 : 3 + n_got], ins[3 + n_got :]
    size = self_keep.shape[0]
    rows = size // n_part
    n_hub = hubs.shape[1]
    need(*range(len(ins)))
    together = len(neigh_got) == 0
    self_value, neigh_value = self_keep[...], neigh_keep[...]
    first, second = hubs[0], hubs[1]
    for i in range(n_got):
        self_value = self_value + self_got[i][:size, :].astype(F32)
        if together:
            neigh_value = neigh_value + self_got[i][size : 2 * size, :].astype(F32)
            tail = self_got[i][2 * size :, :].astype(F32)
        else:
            neigh_value = neigh_value + neigh_got[i][...].astype(F32)
            tail = self_got[i][size:, :].astype(F32)
        first = first + tail[:n_hub]
        second = second + tail[n_hub:]
    if n_part == 1:
        outs[0][:size, :] = self_value.astype(BF16)
        outs[0][size:, :] = neigh_value.astype(BF16)
        outs[1][0] = first
        outs[1][1] = second
        emit(0, 1)
        return
    n_hub = n_hub // n_part
    total[0] = self_value
    total[1] = neigh_value
    for k in [*range(1, n_part), 0]:
        at = pl.ds(pl.multiple_of((mine[0] ^ k) * rows, rows), rows)
        span = slice(k * n_hub, (k + 1) * n_hub)
        if k > 0:
            outs[k + 2][:rows, :] = total[0, at, :].astype(BF16)
            outs[k + 2][rows : 2 * rows, :] = total[1, at, :].astype(BF16)
            outs[k + 2][2 * rows :, :] = jnp.concatenate([first[span], second[span]], 0).astype(BF16)
            emit(k + 2)
    at = pl.ds(pl.multiple_of(mine[0] * rows, rows), rows)
    outs[0][...] = total[0, at, :]
    outs[1][...] = total[1, at, :]
    outs[2][0] = first[:n_hub]
    outs[2][1] = second[:n_hub]
    emit(0, 1, 2)


def node_body(side, ins, outs, need, emit):
    w_self, d_pre, d_other, counts_t, d_agg, chosen, returned, hub_rows, hub_back = ins
    (grad_x,) = outs
    n_local = d_pre.shape[0]
    width = w_self.shape[0]
    half = width // 2
    need(*range(len(ins)))
    picked = one_hot(chosen[...], n_local)
    hub_picked = one_hot(hub_rows[...], n_local)
    mine = pl.ds(pl.multiple_of(side[0] * half, half), half)
    theirs = pl.ds(pl.multiple_of((1 - side[0]) * half, half), half)
    for c in range(0, width, CHUNK):
        cols = slice(c, c + CHUNK)
        part = slice(c % half, c % half + CHUNK)
        back = hub_back[c // half, :, part]
        high = back.astype(BF16)
        low = (back - high.astype(F32)).astype(BF16)
        total = mul_t(d_pre[...], w_self[cols, mine]) + mul_t(d_other[...], w_self[cols, theirs])
        total = total + mul(counts_t[...], d_agg[:, cols])
        total = total + mul(picked, returned[:, cols])
        total = total + mul(hub_picked, high) + mul(hub_picked, low)
        grad_x[:, cols] = total.astype(BF16)
    emit(0)


def place_body(n_xy, n_z, where, ins, outs, need, emit):
    size, half = ins[0].shape
    size = size // 2
    rows = size // n_z
    for i in range(2 * n_xy):
        core, k = divmod(i, n_xy)
        need(i)
        cols = pl.ds(pl.multiple_of((where[0] ^ core) * half, half), half)
        for grad in range(2):
            for j in range(n_z):
                at = (where[1] ^ k) * size + (where[2] ^ j) * rows
                piece = ins[i][(2 * j + grad) * rows : (2 * j + grad + 1) * rows, :]
                outs[grad][pl.ds(pl.multiple_of(at, rows), rows), cols] = piece
    emit(0, 1)


def on_device(
    features,
    neighbours,
    degrees,
    send_rows,
    send_count,
    hub_rows,
    w_self,
    w_neigh,
    bias_term,
    cotangent,
):
    n_row = lax.axis_size("row")
    n_col = lax.axis_size("col")
    n_dev = n_row * n_col
    me = lax.axis_index("row") * n_col + lax.axis_index("col")
    n_local, width = features.shape
    fanout = neighbours.shape[1]
    n_slots = send_rows.shape[1]
    capacity = n_slots // n_dev
    n_hub = hub_rows.shape[0]
    n_hubs = n_dev * n_hub
    half = width // 2
    hub_base = n_local + n_slots
    wide = (n_local, width)

    core = n_col
    xy_bits = [1] + [n_col << i for i in range(1, n_row.bit_length() - 1)]
    z_bits = [1 << i for i in range(1, n_col.bit_length() - 1)]
    hub_bits = z_bits + xy_bits + [core]
    n_xy, n_z = 1 << len(xy_bits), 1 << len(z_bits)

    def spread(bits, k):
        return sum(mask for i, mask in enumerate(bits) if k >> i & 1)

    def bit(mask):
        return (me & mask) // mask

    def place_of(bits):
        return sum(bit(mask) << i for i, mask in enumerate(bits))

    def swap(value, mask):
        return lax.ppermute(value, AXES, [(i, i ^ mask) for i in range(n_dev)])

    side, xy_me, z_me = bit(core), place_of(xy_bits), place_of(z_bits)

    hub_row = hub_rows.reshape(1, n_hub)
    outgoing, own_hubs, chosen = run(
        pack_body,
        side[None],
        [features, send_rows, send_count, hub_row],
        [((n_slots, width), BF16), ((n_hub, width), BF16), ((1, n_slots), jnp.int32)],
        flops=2 * n_slots * n_local * width,
    )
    arrived = lax.all_to_all(
        outgoing.reshape(n_dev, capacity, width), AXES, split_axis=0, concat_axis=0, tiled=True
    ).reshape(n_slots, width)

    hubs = jnp.concatenate([own_hubs] + [swap(own_hubs, spread(z_bits, k)) for k in range(1, n_z)], 0)
    for mask in xy_bits + [core]:
        hubs = jnp.concatenate([hubs, swap(hubs, mask)], 0)
    feat_t = features.T
    peer_feat_t = swap(feat_t, core)

    hub_id = neighbours - hub_base
    relative = (hub_id // n_hub) ^ me
    spot = sum(((relative & mask) // mask) << i for i, mask in enumerate(hub_bits))
    where_to = jnp.where(hub_id >= 0, hub_base + spot * n_hub + hub_id % n_hub, neighbours)
    where_to = jnp.where(jnp.arange(fanout, dtype=jnp.int32)[None, :] < degrees[:, None], where_to, -1)
    to_t = where_to.T

    def count(first, last):
        ids = jnp.arange(first, last, dtype=jnp.int32)
        found = sum((where_to[:, j : j + 1] == ids[None, :]).astype(F32) for j in range(fanout))
        found_t = sum((to_t[j : j + 1, :] == ids[:, None]).astype(F32) for j in range(fanout))
        return found.astype(BF16), found_t.astype(BF16)

    counts_own, counts_own_t = count(0, n_local)
    counts_far, counts_far_t = count(n_local, hub_base + n_hubs)
    inv_deg = 1.0 / degrees.astype(F32)[:, None]
    summed = mul(counts_own, features)
    own_pre = mul(features, w_self) + bias_term[None, :]

    hidden, d_pre, d_agg, d_other, agg_t, d_arrived, hub_keep, hub_send = run(
        seed_body,
        side[None],
        [counts_far, arrived, hubs, summed, inv_deg, w_neigh, own_pre, cotangent, counts_far_t],
        [
            (wide, BF16),
            ((n_local, half), BF16),
            (wide, BF16),
            ((n_local, half), BF16),
            ((width, n_local), BF16),
            ((n_slots, width), BF16),
            ((2, n_hubs // 2, half), F32),
            ((2, n_hubs // 2, half), BF16),
        ],
        flops=4 * n_local * width * (width + n_slots + n_hubs),
        scratch=[pltpu.VMEM(wide, BF16), pltpu.VMEM(wide, BF16)],
    )
    returned = lax.all_to_all(
        d_arrived.reshape(n_dev, capacity, width), AXES, split_axis=0, concat_axis=0, tiled=True
    ).reshape(n_slots, width)
    peer_d_pre = swap(d_other, core)
    hub_got = swap(hub_send, core)
    peer_agg_t = swap(agg_t, core)

    xy_rows, z_rows = width // n_xy, width // n_xy // n_z
    hub_xy, hub_z = n_hubs // 2 // n_xy, n_hubs // 2 // n_xy // n_z

    def reduce_start(own, peer, with_hubs):
        extra = 2 * hub_xy if with_hubs else 0
        outs = [((xy_rows, half), F32)] + [((xy_rows + extra, half), BF16)] * (n_xy - 1)
        hub_in = [hub_keep, hub_got] if with_hubs else []
        hub_out = [((2, hub_xy, half), F32)] if with_hubs else []
        return run(
            functools.partial(weight_body, n_xy, with_hubs),
            xy_me[None],
            [own, peer, d_pre, peer_d_pre] + hub_in,
            outs + hub_out,
            flops=4 * width * half * n_local,
        )

    def across(parts, bits):
        return [swap(part, spread(bits, k + 1)) for k, part in enumerate(parts)]

    self_parts = reduce_start(feat_t, peer_feat_t, True)
    self_got = across(self_parts[1:n_xy], xy_bits)
    neigh_parts = reduce_start(agg_t, peer_agg_t, False)
    neigh_got = across(neigh_parts[1:n_xy], xy_bits)
    parts = run(
        functools.partial(fold_body, n_z, n_xy - 1),
        z_me[None],
        [self_parts[0], neigh_parts[0], self_parts[n_xy]] + self_got + neigh_got,
        [((z_rows, half), F32)] * 2
        + [((2, hub_z, half), F32)]
        + [((2 * z_rows + 2 * hub_z, half), BF16)] * (n_z - 1),
        scratch=[pltpu.VMEM((2, xy_rows, half), F32)],
    )
    own, hub_back = run(
        functools.partial(fold_body, 1, n_z - 1),
        z_me[None],
        list(parts[:3]) + across(parts[3:], z_bits),
        [((2 * z_rows, half), BF16), ((2, hub_z, half), F32)],
        scratch=[pltpu.VMEM((2, 8, half), F32)],
    )
    line = jnp.concatenate([own] + across([own] * (n_z - 1), z_bits), 0)
    line, returned = lax.optimization_barrier((line, returned))
    blocks = [line] + across([line] * (n_xy - 1), xy_bits)
    blocks = blocks + [swap(one, core) for one in blocks]
    grad_self, grad_neigh = run(
        functools.partial(place_body, n_xy, n_z),
        jnp.stack([side, xy_me, z_me]),
        blocks,
        [((width, width), BF16)] * 2,
    )
    (grad_x,) = run(
        node_body,
        side[None],
        [w_self, d_pre, d_other, counts_own_t, d_agg, chosen, returned, hub_row, hub_back],
        [(wide, BF16)],
        flops=2 * n_local * width * (width + n_local + n_slots),
    )
    return hidden, grad_x, grad_self, grad_neigh


def solution(mesh):
    split = P(AXES, None)
    in_specs = (split, split, P(AXES), split, split, P(AXES), P(), P(), P(), split)
    out_specs = (split, split, P(), P())
    return jax.shard_map(
        on_device, mesh=mesh, in_specs=in_specs, out_specs=out_specs, check_vma=False
    )
```

time: 453 us -> 191 us (0.42)
  blocking collectives: 225 us -> 0 us
  other arithmetic: 95.8 us -> 12.6 us
  waiting for transfers between devices: 0.69 us -> 69.5 us
  local copies, waits for them, and re-layouts: 73 us -> 10.3 us
  Pallas kernels: 0 us -> 41.4 us
  starting transfers between devices: 10.9 us -> 44.1 us
  matrix products: 31.9 us -> 8.31 us
  between operations: 14.2 us -> 1.19 us
    psum x1 -> x0, blocking collectives: 176 us -> none  [on_device(): grad_self, grad_neigh = lax.psum((self_part, neigh_part), ('row', 'col'))]
    scatter-add x3 -> x0, other arithmetic: 85.8 us -> none  [the longest x1 73.6 us: spread_tile(): d_table.at[target.reshape(-1)]]
    ppermute x0 -> x29, waiting for transfers between devices: none -> 69.5 us  [swap(): return lax.ppermute(value, AXES, [(i, i ^ mask) for i in range(n_dev)])]
    all_gather x2 -> x0, blocking collectives: 49.2 us -> none  [the longest x1 41.4 us: on_device(): by_column = lax.all_gather(own_hubs, 'col', axis=0, tiled=True)]
    gather x3 -> x0, local copies, waits for them, and re-layouts: 48.2 us -> none  [the longest x1 42.8 us: gather_tile(): picked = src_table[neighbours]]
    pallas_call x0 -> x8, Pallas kernels: none -> 41.4 us  [run(): pl.pallas_call(kernel, out_shape=outs, in_specs=[SMEM] + [HBM] * n_in, ou...]
    ppermute x0 -> x29, starting transfers between devices: none -> 31 us  [swap(): return lax.ppermute(value, AXES, [(i, i ^ mask) for i in range(n_dev)])]
    dot_general x7 -> x2, matrix products: 31.9 us -> 8.31 us  [mul(): return jnp.dot(left, right, preferred_element_type=F32)]
  transfers between devices with their start and end apart: 3 -> 31, of which waited for: 0 -> 16; matrix products, arithmetic and copies ran while one was open for 7% -> 14% of each run, Pallas kernels for 0% -> 18%
where the time goes in v2:
time: 191 us; the launch traced here: 187 us
  waiting for transfers between devices  69.5 us (36%)
  starting transfers between devices  44.1 us (23%)
  Pallas kernels  41.4 us (22%)
  other arithmetic  12.6 us (7%)
  local copies, waits for them, and re-layouts  10.3 us (5%)
  matrix products  8.31 us (4%)
    ppermute x29, waiting for transfers between devices, swap(): return lax.ppermute(value, AXES, [(i, i ^ mask) for i in range(n_dev)])  69.5 us
    pallas_call x8, Pallas kernels, run(): pl.pallas_call(kernel, out_shape=outs, in_specs=[SMEM] + [HBM] * n_in, ou...  41.4 us
    ppermute x29, starting transfers between devices, swap(): return lax.ppermute(value, AXES, [(i, i ^ mask) for i in range(n_dev)])  31 us
    convert_element_type x3, other arithmetic, count(): return (found.astype(BF16), found_t.astype(BF16))  10.7 us
    dot_general x2, matrix products, mul(): return jnp.dot(left, right, preferred_element_type=F32)  8.31 us
    unnamed x62, local copies, waits for them, and re-layouts  7.98 us
    all_to_all x1, starting transfers between devices, on_device(): lax.all_to_all(d_arrived.reshape(n_dev, capacity, width), AXES, split_axi...  7.05 us
    all_to_all x1, starting transfers between devices, on_device(): lax.all_to_all(outgoing.reshape(n_dev, capacity, width), AXES, split_axis...  6.06 us
  transfers between devices with their start and end apart: 31, of which 16 were waited for; matrix products, arithmetic and copies ran while one was open for 14% of the time, Pallas kernels for 18%

profile of v2, /device:TPU:0, one launch (start us, length us, event | category | flops | bytes accessed | tf_op | source)
XLA Modules:
  0.0 187.5 jit_solution(3969905222864365043)
XLA Ops:
  0.7 3.3 %shard_map.129 = (bf16[512,1024]{1,0:T(8,128)(2,1)}, bf16[8,1024]{1,0:T(8,128)(2,1)}, s32[1,512]{1,0:T(1,128)}) custom-call(s32[1]{0:T(128)} %bitcast.refs_0_, bf16[512,1024]{1,0:T(8,128)(2,1)} %refs_1_.2, s32[1,512]{1,0:T(1,128)} %refs_2_.1, s32[1,32]{1,0:T(1,128)} %refs_3_.1, s32[1,8]{1,0:T(1,128)} %bitcast.118), custom_call_target="tpu_custom_call" | custom-call | flops 536870912 | bytes 2117792 | tf_op jit(solution)/shard_map/pallas_call | solution.py:59
  4.0 3.1 %collective-permute-start = (bf16[8,1024]{1,0:T(8,128)(2,1)}, bf16[8,1024]{1,0:T(8,128)(2,1)S(1)}, u32[]{:S(2)}, u32[]{:S(2)}) collective-permute-start(bf16[8,1024]{1,0:T(8,128)(2,1)} %get-tuple-element.37), channel_id=1, source_target_pairs={{0,2},{1,3},{2,0},{3,1},{4,6},{5,7},{6,4},{7,5},{8,10},{9,11},{10,... | collective-permute-start | bytes 49160 | tf_op jit(solution)/shard_map/ppermute | solution.py:307
  7.0 2.6 %collective-permute-start.1 = (bf16[8,1024]{1,0:T(8,128)(2,1)}, bf16[8,1024]{1,0:T(8,128)(2,1)S(1)}, u32[]{:S(2)}, u32[]{:S(2)}) collective-permute-start(bf16[8,1024]{1,0:T(8,128)(2,1)} %get-tuple-element.37), channel_id=1, source_target_pairs={{0,4},{1,5},{2,6},{3,7},{4,0},{5,1},{6,2},{7,3},{8,12},{9,13},{10,... | collective-permute-start | bytes 49160 | tf_op jit(solution)/shard_map/ppermute | solution.py:307
  9.6 6.1 %all-to-all-start = ((bf16[32,16,1024]{2,1,0:T(8,128)(2,1)}), bf16[32,16,1024]{2,1,0:T(8,128)(2,1)S(1)}, u32[]{:S(2)}, u32[]{:S(2)}) async-start(bf16[32,16,1024]{2,1,0:T(8,128)(2,1)} %bitcast.51), calls=%async_computation | async-start | bytes 2097152 | tf_op jit(solution)/shard_map/all_to_all | solution.py:319
  17.0 3.4 %add_convert_fusion.refs_9_ = bf16[768,512]{1,0:T(8,128)(2,1)} fusion(s32[512]{0:T(512)S(1)} %bitcast.55, s32[512]{0:T(512)S(1)} %bitcast.57, s32[512]{0:T(512)S(1)} %bitcast.59, s32[512]{0:T(512)S(1)} %bitcast.61, s32[512]{0:T(512)S(1)} %bitcast.63, s32[512]{0:T(512)S(1)} %bitcast.65, s32[512]{0:T(512)S(1)} %bitcast.67, s32[512]{0:T(512)S(1)} %bitcast.69, ...), kind=kLoop, calls=%fused_computation | loop fusion | flops 18874368 | bytes 822272 | tf_op jit(solution)/shard_map/convert_element_type | solution.py:340
  20.4 4.1 %fusion.refs_4_ = f32[512,1024]{1,0:T(8,128)} fusion(bf16[512,1024]{1,0:T(8,128)(2,1)S(1)} %copy-done.1, s32[512]{0:T(512)S(1)} %bitcast.87, s32[512]{0:T(512)S(1)} %bitcast.89, s32[512]{0:T(512)S(1)} %bitcast.91, s32[512]{0:T(512)S(1)} %bitcast.93, s32[512]{0:T(512)S(1)} %bitcast.95, s32[512]{0:T(512)S(1)} %bitcast.97, s32[512]{0:T(512)S(1)} %bitcast.99, ...), kind=kOutput, calls=%fused_computation.37 | convolution fusion | flops 549453824 | bytes 3178496 | tf_op jit(solution)/shard_map/dot_general | solution.py:20
  24.6 4.4 %add_convert_fusion.1.refs_1_ = bf16[512,768]{1,0:T(8,128)(2,1)} fusion(s32[768]{0:T(1024)S(1)} %iota_add_fusion, s32[512]{0:T(512)S(1)} %bitcast.88, s32[512]{0:T(512)S(1)} %bitcast.90, s32[512]{0:T(512)S(1)} %bitcast.92, s32[512]{0:T(512)S(1)} %bitcast.94, s32[512]{0:T(512)S(1)} %bitcast.96, s32[512]{0:T(512)S(1)} %bitcast.98, s32[512]{0:T(512)S(1)} %bitcast.100, ...), kind=kLoop, calls=%fused_computation.1 | loop fusion | flops 18874368 | bytes 822272 | tf_op jit(solution)/shard_map/convert_element_type | solution.py:340
  37.3 3.1 %collective-permute-done.4 = bf16[64,1024]{1,0:T(8,128)(2,1)S(1)} collective-permute-done((bf16[64,1024]{1,0:T(8,128)(2,1)S(1)}, bf16[64,1024]{1,0:T(8,128)(2,1)S(1)}, u32[]{:S(2)}, u32[]{:S(2)}) %collective-permute-start.4) | collective-permute-done | bytes 131104 | tf_op jit(solution)/shard_map/ppermute | solution.py:307
  41.1 4.2 %convolution_add_fusion.refs_7_ = f32[512,1024]{1,0:T(8,128)} fusion(bf16[512,1024]{1,0:T(8,128)(2,1)S(1)} %copy-done.1, bf16[1024,1024]{1,0:T(8,128)(2,1)} %refs_1_.3, f32[1024]{0:T(1024)S(1)} %copy-done.27), kind=kOutput, calls=%fused_computation.2 | convolution fusion | flops 1074266112 | bytes 5246976 | tf_op jit(solution)/shard_map/dot_general | solution.py:20
  47.0 12.9 %shard_map.130 = (bf16[512,1024]{1,0:T(8,128)(2,1)}, bf16[512,512]{1,0:T(8,128)(2,1)}, bf16[512,1024]{1,0:T(8,128)(2,1)}, bf16[512,512]{1,0:T(8,128)(2,1)}, bf16...) custom-call(s32[1]{0:T(128)} %bitcast.refs_0_, ...), custom_call_target="tpu_custom_call" | custom-call | flops 3758096384 | bytes 16517120 | tf_op jit(solution)/shard_map/pallas_call | solution.py:59
  59.9 7.1 %all-to-all-start.1 = ((bf16[32,16,1024]{2,1,0:T(8,128)(2,1)}), bf16[32,16,1024]{2,1,0:T(8,128)(2,1)S(1)}, u32[]{:S(2)}, u32[]{:S(2)}) async-start(bf16[32,16,1024]{2,1,0:T(8,128)(2,1)} %bitcast.48), calls=%async_computation.1 | async-start | bytes 2097152 | tf_op jit(solution)/shard_map/all_to_all | solution.py:365
  67.6 3.3 %collective-permute-done.8.refs_6_ = bf16[2,128,512]{2,1,0:T(8,128)(2,1)} collective-permute-done((bf16[2,128,512]{2,1,0:T(8,128)(2,1)S(1)}, bf16[2,128,512]{2,1,0:T(8,128)(2,1)}, u32[]{:S(2)}, u32[]{:S(2)}) %collective-permute-start.8) | collective-permute-done | bytes 262176 | tf_op jit(solution)/shard_map/ppermute | solution.py:307
  70.9 4.5 %shard_map.131 = (f32[256,512]{1,0:T(8,128)}, bf16[320,512]{1,0:T(8,128)(2,1)}, bf16[320,512]{1,0:T(8,128)(2,1)}, bf16[320,512]{1,0:T(8,128)(2,1)}, f32[2,32,512]{2,1,0:T(8,128)}) custom-call(s32[1]{0:T(128)} %bitcast.39.refs_0_, bf16[1024,512]{1,0:T(8,128)(2,1)} %bitcast.50, bf16[1024,512]{1,0:T(8,128)(2,1)} %collective-permute-done.6.refs_2_, ...), custom_call_target="tpu_custom_call" | custom-call | flops 1073741824 | bytes 5570560 | tf_op jit(solution)/shard_map/pallas_call | solution.py:59
  79.0 3.9 %shard_map.132 = (f32[256,512]{1,0:T(8,128)}, bf16[256,512]{1,0:T(8,128)(2,1)}, bf16[256,512]{1,0:T(8,128)(2,1)}, bf16[256,512]{1,0:T(8,128)(2,1)}) custom-call(s32[1]{0:T(128)} %bitcast.39.refs_0_, bf16[1024,512]{1,0:T(8,128)(2,1)} %get-tuple-element.46.refs_1_, bf16[1024,512]{1,0:T(8,128)(2,1)} %collective-permute-done.9.refs_2_, ...), custom_call_target="tpu_custom_call" | custom-call | flops 1073741824 | bytes 4456448 | tf_op jit(solution)/shard_map/pallas_call | solution.py:59
  86.3 2.5 %collective-permute-done.10.refs_4_ = bf16[320,512]{1,0:T(8,128)(2,1)S(1)} collective-permute-done((bf16[320,512]{1,0:T(8,128)(2,1)}, bf16[320,512]{1,0:T(8,128)(2,1)S(1)}, u32[]{:S(2)}, u32[]{:S(2)}) %collective-permute-start.10) | collective-permute-done | bytes 327712 | tf_op jit(solution)/shard_map/ppermute | solution.py:307
  90.2 8.4 %collective-permute-done.12.refs_6_ = bf16[320,512]{1,0:T(8,128)(2,1)S(1)} collective-permute-done((bf16[320,512]{1,0:T(8,128)(2,1)}, bf16[320,512]{1,0:T(8,128)(2,1)S(1)}, u32[]{:S(2)}, u32[]{:S(2)}) %collective-permute-start.12) | collective-permute-done | bytes 327712 | tf_op jit(solution)/shard_map/ppermute | solution.py:307
  98.7 3.4 %collective-permute-done.13.refs_7_ = bf16[256,512]{1,0:T(8,128)(2,1)S(1)} collective-permute-done((bf16[256,512]{1,0:T(8,128)(2,1)}, bf16[256,512]{1,0:T(8,128)(2,1)S(1)}, u32[]{:S(2)}, u32[]{:S(2)}) %collective-permute-start.13) | collective-permute-done | bytes 262176 | tf_op jit(solution)/shard_map/ppermute | solution.py:307
  102.0 2.9 %collective-permute-done.14.refs_8_ = bf16[256,512]{1,0:T(8,128)(2,1)S(1)} collective-permute-done((bf16[256,512]{1,0:T(8,128)(2,1)}, bf16[256,512]{1,0:T(8,128)(2,1)S(1)}, u32[]{:S(2)}, u32[]{:S(2)}) %collective-permute-start.14) | collective-permute-done | bytes 262176 | tf_op jit(solution)/shard_map/ppermute | solution.py:307
  105.0 4.3 %collective-permute-done.15.refs_9_ = bf16[256,512]{1,0:T(8,128)(2,1)S(1)} collective-permute-done((bf16[256,512]{1,0:T(8,128)(2,1)}, bf16[256,512]{1,0:T(8,128)(2,1)S(1)}, u32[]{:S(2)}, u32[]{:S(2)}) %collective-permute-start.15) | collective-permute-done | bytes 262176 | tf_op jit(solution)/shard_map/ppermute | solution.py:307
  110.0 3.3 %shard_map.133 = (f32[64,512]{1,0:T(8,128)}, f32[64,512]{1,0:T(8,128)}, f32[2,8,512]{2,1,0:T(8,128)}, bf16[144,512]{1,0:T(8,128)(2,1)}, bf16[144,512]{1,0:T(8,128)(2,1)}, /*index=5*/bf16[144,512]{1,0:T(8,128)(2,1)}) custom-call(s32[1]{0:T(128)} %bitcast.38.refs_0_, f32[256,512]{1,0:T(8,128)} %get-tuple-element.45.refs_1_, ...), custom_call_target="tpu_custom_call" | custom-call | bytes 3686400 | tf_op jit(solution)/shard_map/pallas_call | solution.py:59
  113.3 3.1 %collective-permute-start.16 = (bf16[144,512]{1,0:T(8,128)(2,1)}, bf16[144,512]{1,0:T(8,128)(2,1)S(1)}, u32[]{:S(2)}, u32[]{:S(2)}) collective-permute-start(bf16[144,512]{1,0:T(8,128)(2,1)} %get-tuple-element.58), channel_id=1, source_target_pairs={{0,2},{1,3},{2,0},{3,1},{4,6},{5,7},{6,4},{7,5},{8,10},{9,11},{10,... | collective-permute-start | bytes 442376 | tf_op jit(solution)/shard_map/ppermute | solution.py:307
  118.8 3.2 %collective-permute-done.16.refs_4_ = bf16[144,512]{1,0:T(8,128)(2,1)S(1)} collective-permute-done((bf16[144,512]{1,0:T(8,128)(2,1)}, bf16[144,512]{1,0:T(8,128)(2,1)S(1)}, u32[]{:S(2)}, u32[]{:S(2)}) %collective-permute-start.16) | collective-permute-done | bytes 147488 | tf_op jit(solution)/shard_map/ppermute | solution.py:307
  122.0 8.3 %collective-permute-done.17.refs_5_ = bf16[144,512]{1,0:T(8,128)(2,1)S(1)} collective-permute-done((bf16[144,512]{1,0:T(8,128)(2,1)}, bf16[144,512]{1,0:T(8,128)(2,1)S(1)}, u32[]{:S(2)}, u32[]{:S(2)}) %collective-permute-start.17) | collective-permute-done | bytes 147488 | tf_op jit(solution)/shard_map/ppermute | solution.py:307
  131.0 2.0 %shard_map.134 = (bf16[128,512]{1,0:T(8,128)(2,1)}, f32[2,8,512]{2,1,0:T(8,128)}) custom-call(s32[1]{0:T(128)} %bitcast.38.refs_0_, f32[64,512]{1,0:T(8,128)} %get-tuple-element.55.refs_1_, f32[64,512]{1,0:T(8,128)} %get-tuple-element.56.refs_2_, f32[2,8,512]{2,1,0:T(8,128)} %get-tuple-element.57.refs_3_, bf16[144,512]{1,0:T(8,128)(2,1)} %copy-done.18, ...), custom_call_target="tpu_custom_call" | custom-call | bytes 901120 | tf_op jit(solution)/shard_map/pallas_call | solution.py:59
  133.0 2.5 %collective-permute-start.19 = (bf16[128,512]{1,0:T(8,128)(2,1)}, bf16[128,512]{1,0:T(8,128)(2,1)S(1)}, u32[]{:S(2)}, u32[]{:S(2)}) collective-permute-start(bf16[128,512]{1,0:T(8,128)(2,1)} %get-tuple-element.61), channel_id=1, source_target_pairs={{0,2},{1,3},{2,0},{3,1},{4,6},{5,7},{6,4},{7,5},{8,10},{9,11},{10,... | collective-permute-start | bytes 393224 | tf_op jit(solution)/shard_map/ppermute | solution.py:307
  139.7 7.5 %collective-permute-done.20 = bf16[128,512]{1,0:T(8,128)(2,1)S(1)} collective-permute-done((bf16[128,512]{1,0:T(8,128)(2,1)}, bf16[128,512]{1,0:T(8,128)(2,1)S(1)}, u32[]{:S(2)}, u32[]{:S(2)}) %collective-permute-start.20) | collective-permute-done | bytes 131104 | tf_op jit(solution)/shard_map/ppermute | solution.py:307
  149.2 2.5 %collective-permute-start.24 = (bf16[512,512]{1,0:T(8,128)(2,1)S(1)}, bf16[512,512]{1,0:T(8,128)(2,1)S(1)}, u32[]{:S(2)}, u32[]{:S(2)}) collective-permute-start(bf16[512,512]{1,0:T(8,128)(2,1)S(1)} %pad_maximum_fusion.refs_1_), channel_id=1, source_target_pairs={{0,17},{1,16},{2,19},{3,18},{4,21},{5,20},{6,23},{7,22},{8,25},{9,... | collective-permute-start | bytes 1572872 | tf_op jit(solution)/shard_map/ppermute | solution.py:307
  151.8 10.3 %collective-permute-done.22.refs_2_ = bf16[512,512]{1,0:T(8,128)(2,1)S(1)} collective-permute-done((bf16[512,512]{1,0:T(8,128)(2,1)S(1)}, bf16[512,512]{1,0:T(8,128)(2,1)S(1)}, u32[]{:S(2)}, u32[]{:S(2)}) %collective-permute-start.22) | collective-permute-done | bytes 524320 | tf_op jit(solution)/shard_map/ppermute | solution.py:307
  163.2 6.9 %collective-permute-done.24.refs_4_ = bf16[512,512]{1,0:T(8,128)(2,1)S(1)} collective-permute-done((bf16[512,512]{1,0:T(8,128)(2,1)S(1)}, bf16[512,512]{1,0:T(8,128)(2,1)S(1)}, u32[]{:S(2)}, u32[]{:S(2)}) %collective-permute-start.24) | collective-permute-done | bytes 524320 | tf_op jit(solution)/shard_map/ppermute | solution.py:307
  170.8 2.8 %add_convert_fusion.2.refs_4_ = bf16[512,512]{1,0:T(8,128)(2,1)} fusion(s32[512]{0:T(512)S(1)} %bitcast.56, s32[512]{0:T(512)S(1)} %bitcast.58, s32[512]{0:T(512)S(1)} %bitcast.60, s32[512]{0:T(512)S(1)} %bitcast.62, s32[512]{0:T(512)S(1)} %bitcast.64, s32[512]{0:T(512)S(1)} %bitcast.66, s32[512]{0:T(512)S(1)} %bitcast.68, s32[512]{0:T(512)S(1)} %bitcast.70, ...), kind=kLoop, calls=%fused_computation.3 | loop fusion | flops 12582912 | bytes 557056 | tf_op jit(solution)/shard_map/convert_element_type | solution.py:340
  173.7 6.6 %shard_map.135 = bf16[512,1024]{1,0:T(8,128)(2,1)} custom-call(s32[1]{0:T(128)} %bitcast.refs_0_, bf16[1024,1024]{1,0:T(8,128)(2,1)} %refs_1_.3, bf16[512,512]{1,0:T(8,128)(2,1)} %get-tuple-element.39.refs_3_.refs_2_, bf16[512,512]{1,0:T(8,128)(2,1)} %get-tuple-element.40.refs_3_, bf16[512,512]{1,0:T(8,128)(2,1)} %add_convert_fusion.2.refs_4_, ...), custom_call_target="tpu_custom_call" | custom-call | flops 2147483648 | bytes 6850592 | tf_op jit(solution)/shard_map/pallas_call | solution.py:59
  182.4 4.9 %shard_map.136 = (bf16[1024,1024]{1,0:T(8,128)(2,1)}, bf16[1024,1024]{1,0:T(8,128)(2,1)}) custom-call(s32[3]{0:T(128)} %pad_add_fusion.refs_0_, bf16[512,512]{1,0:T(8,128)(2,1)} %copy-done, bf16[512,512]{1,0:T(8,128)(2,1)} %copy-done.5, bf16[512,512]{1,0:T(8,128)(2,1)} %copy-done.6, bf16[512,512]{1,0:T(8,128)(2,1)} %copy-done.7, bf16[512,512]{1,0:T(8,128)(2,1)} %copy-done.8, ...), custom_call_target="tpu_custom_call" | custom-call | bytes 8388608 | tf_op jit(solution)/shard_map/pallas_call | solution.py:59
  (117 shorter events, 34.9 us)
Async XLA Ops:
  4.0 25.6 %collective-permute-start = (bf16[8,1024]{1,0:T(8,128)(2,1)}, bf16[8,1024]{1,0:T(8,128)(2,1)S(1)}, u32[]{:S(2)}, u32[]{:S(2)}) collective-permute-start(bf16[8,1024]{1,0:T(8,128)(2,1)} %get-tuple-element.37), channel_id=1, source_target_pairs={{0,2},{1,3},{2,0},{3,1},{4,6},{5,7},{6,4},{7,5},{8,10},{9,11},{10,... | collective-permute-start | bytes 49160 | tf_op jit(solution)/shard_map/ppermute | solution.py:307
  7.0 22.5 %collective-permute-start.1 = (bf16[8,1024]{1,0:T(8,128)(2,1)}, bf16[8,1024]{1,0:T(8,128)(2,1)S(1)}, u32[]{:S(2)}, u32[]{:S(2)}) collective-permute-start(bf16[8,1024]{1,0:T(8,128)(2,1)} %get-tuple-element.37), channel_id=1, source_target_pairs={{0,4},{1,5},{2,6},{3,7},{4,0},{5,1},{6,2},{7,3},{8,12},{9,13},{10,... | collective-permute-start | bytes 49160 | tf_op jit(solution)/shard_map/ppermute | solution.py:307
  9.6 19.9 %collective-permute-start.2 = (bf16[8,1024]{1,0:T(8,128)(2,1)}, bf16[8,1024]{1,0:T(8,128)(2,1)S(1)}, u32[]{:S(2)}, u32[]{:S(2)}) collective-permute-start(bf16[8,1024]{1,0:T(8,128)(2,1)} %get-tuple-element.37), channel_id=1, source_target_pairs={{0,6},{1,7},{2,4},{3,5},{4,2},{5,3},{6,0},{7,1},{8,14},{9,15},{10,... | collective-permute-start | bytes 49160 | tf_op jit(solution)/shard_map/ppermute | solution.py:307
  9.6 36.4 %all-to-all-start = ((bf16[32,16,1024]{2,1,0:T(8,128)(2,1)}), bf16[32,16,1024]{2,1,0:T(8,128)(2,1)S(1)}, u32[]{:S(2)}, u32[]{:S(2)}) async-start(bf16[32,16,1024]{2,1,0:T(8,128)(2,1)} %bitcast.51), calls=%async_computation | async-start | bytes 2097152 | tf_op jit(solution)/shard_map/all_to_all | solution.py:319
  16.3 51.3 %collective-permute-start.6 = (bf16[1024,512]{1,0:T(8,128)(2,1)S(1)}, bf16[1024,512]{1,0:T(8,128)(2,1)}, u32[]{:S(2)}, u32[]{:S(2)}) collective-permute-start(bf16[1024,512]{1,0:T(8,128)(2,1)S(1)} %bitcast.49), channel_id=1, source_target_pairs={{0,8},{1,9},{2,10},{3,11},{4,12},{5,13},{6,14},{7,15},{8,0},{9,1},... | collective-permute-start | bytes 3145736 | tf_op jit(solution)/shard_map/ppermute | solution.py:307
  29.6 4.4 %collective-permute-start.3 = (bf16[32,1024]{1,0:T(8,128)(2,1)S(1)}, bf16[32,1024]{1,0:T(8,128)(2,1)S(1)}, u32[]{:S(2)}, u32[]{:S(2)}) collective-permute-start(bf16[32,1024]{1,0:T(8,128)(2,1)S(1)} %pad_maximum_fusion.1), channel_id=1, source_target_pairs={{0,1},{1,0},{2,3},{3,2},{4,5},{5,4},{6,7},{7,6},{8,9},{9,8},{10,11... | collective-permute-start | bytes 196616 | tf_op jit(solution)/shard_map/ppermute | solution.py:307
  34.7 5.7 %collective-permute-start.4 = (bf16[64,1024]{1,0:T(8,128)(2,1)S(1)}, bf16[64,1024]{1,0:T(8,128)(2,1)S(1)}, u32[]{:S(2)}, u32[]{:S(2)}) collective-permute-start(bf16[64,1024]{1,0:T(8,128)(2,1)S(1)} %get-tuple-element.72), channel_id=1, source_target_pairs={{0,16},{1,17},{2,18},{3,19},{4,20},{5,21},{6,22},{7,23},{8,24},{9,... | collective-permute-start | bytes 393224 | tf_op jit(solution)/shard_map/ppermute | solution.py:307
  41.1 4.2 %collective-permute-start.5 = (bf16[128,1024]{1,0:T(8,128)(2,1)}, bf16[128,1024]{1,0:T(8,128)(2,1)S(1)}, u32[]{:S(2)}, u32[]{:S(2)}) collective-permute-start(bf16[128,1024]{1,0:T(8,128)(2,1)} %get-tuple-element.68), channel_id=1, source_target_pairs={{0,8},{1,9},{2,10},{3,11},{4,12},{5,13},{6,14},{7,15},{8,0},{9,1},... | collective-permute-start | bytes 786440 | tf_op jit(solution)/shard_map/ppermute | solution.py:307
  59.9 88.3 %all-to-all-start.1 = ((bf16[32,16,1024]{2,1,0:T(8,128)(2,1)}), bf16[32,16,1024]{2,1,0:T(8,128)(2,1)S(1)}, u32[]{:S(2)}, u32[]{:S(2)}) async-start(bf16[32,16,1024]{2,1,0:T(8,128)(2,1)} %bitcast.48), calls=%async_computation.1 | async-start | bytes 2097152 | tf_op jit(solution)/shard_map/all_to_all | solution.py:365
  67.0 12.1 %collective-permute-start.9 = (bf16[1024,512]{1,0:T(8,128)(2,1)S(1)}, bf16[1024,512]{1,0:T(8,128)(2,1)}, u32[]{:S(2)}, u32[]{:S(2)}) collective-permute-start(bf16[1024,512]{1,0:T(8,128)(2,1)S(1)} %copy-done.25), channel_id=1, source_target_pairs={{0,8},{1,9},{2,10},{3,11},{4,12},{5,13},{6,14},{7,15},{8,0},{9,1},... | collective-permute-start | bytes 3145736 | tf_op jit(solution)/shard_map/ppermute | solution.py:307
  67.1 3.8 %collective-permute-start.7 = (bf16[512,512]{1,0:T(8,128)(2,1)}, bf16[512,512]{1,0:T(8,128)(2,1)}, u32[]{:S(2)}, u32[]{:S(2)}) collective-permute-start(bf16[512,512]{1,0:T(8,128)(2,1)} %get-tuple-element.40.refs_3_), channel_id=1, source_target_pairs={{0,8},{1,9},{2,10},{3,11},{4,12},{5,13},{6,14},{7,15},{8,0},{9,1},... | collective-permute-start | bytes 1572872 | tf_op jit(solution)/shard_map/ppermute | solution.py:307
  67.5 3.4 %collective-permute-start.8 = (bf16[2,128,512]{2,1,0:T(8,128)(2,1)S(1)}, bf16[2,128,512]{2,1,0:T(8,128)(2,1)}, u32[]{:S(2)}, u32[]{:S(2)}) collective-permute-start(bf16[2,128,512]{2,1,0:T(8,128)(2,1)S(1)} %copy-done.26), channel_id=1, source_target_pairs={{0,8},{1,9},{2,10},{3,11},{4,12},{5,13},{6,14},{7,15},{8,0},{9,1},... | collective-permute-start | bytes 786440 | tf_op jit(solution)/shard_map/ppermute | solution.py:307
  75.5 13.3 %collective-permute-start.10 = (bf16[320,512]{1,0:T(8,128)(2,1)}, bf16[320,512]{1,0:T(8,128)(2,1)S(1)}, u32[]{:S(2)}, u32[]{:S(2)}) collective-permute-start(bf16[320,512]{1,0:T(8,128)(2,1)} %get-tuple-element.49), channel_id=1, source_target_pairs={{0,1},{1,0},{2,3},{3,2},{4,5},{5,4},{6,7},{7,6},{8,9},{9,8},{10,11... | collective-permute-start | bytes 983048 | tf_op jit(solution)/shard_map/ppermute | solution.py:307
  77.3 12.9 %collective-permute-start.11 = (bf16[320,512]{1,0:T(8,128)(2,1)}, bf16[320,512]{1,0:T(8,128)(2,1)S(1)}, u32[]{:S(2)}, u32[]{:S(2)}) collective-permute-start(bf16[320,512]{1,0:T(8,128)(2,1)} %get-tuple-element.50), channel_id=1, source_target_pairs={{0,16},{1,17},{2,18},{3,19},{4,20},{5,21},{6,22},{7,23},{8,24},{9,... | collective-permute-start | bytes 983048 | tf_op jit(solution)/shard_map/ppermute | solution.py:307
  78.8 19.9 %collective-permute-start.12 = (bf16[320,512]{1,0:T(8,128)(2,1)}, bf16[320,512]{1,0:T(8,128)(2,1)S(1)}, u32[]{:S(2)}, u32[]{:S(2)}) collective-permute-start(bf16[320,512]{1,0:T(8,128)(2,1)} %get-tuple-element.51), channel_id=1, source_target_pairs={{0,17},{1,16},{2,19},{3,18},{4,21},{5,20},{6,23},{7,22},{8,25},{9,... | collective-permute-start | bytes 983048 | tf_op jit(solution)/shard_map/ppermute | solution.py:307
  83.0 19.1 %collective-permute-start.13 = (bf16[256,512]{1,0:T(8,128)(2,1)}, bf16[256,512]{1,0:T(8,128)(2,1)S(1)}, u32[]{:S(2)}, u32[]{:S(2)}) collective-permute-start(bf16[256,512]{1,0:T(8,128)(2,1)} %get-tuple-element.52), channel_id=1, source_target_pairs={{0,1},{1,0},{2,3},{3,2},{4,5},{5,4},{6,7},{7,6},{8,9},{9,8},{10,11... | collective-permute-start | bytes 786440 | tf_op jit(solution)/shard_map/ppermute | solution.py:307
  84.8 20.1 %collective-permute-start.14 = (bf16[256,512]{1,0:T(8,128)(2,1)}, bf16[256,512]{1,0:T(8,128)(2,1)S(1)}, u32[]{:S(2)}, u32[]{:S(2)}) collective-permute-start(bf16[256,512]{1,0:T(8,128)(2,1)} %get-tuple-element.53), channel_id=1, source_target_pairs={{0,16},{1,17},{2,18},{3,19},{4,20},{5,21},{6,22},{7,23},{8,24},{9,... | collective-permute-start | bytes 786440 | tf_op jit(solution)/shard_map/ppermute | solution.py:307
  88.8 20.5 %collective-permute-start.15 = (bf16[256,512]{1,0:T(8,128)(2,1)}, bf16[256,512]{1,0:T(8,128)(2,1)S(1)}, u32[]{:S(2)}, u32[]{:S(2)}) collective-permute-start(bf16[256,512]{1,0:T(8,128)(2,1)} %get-tuple-element.54), channel_id=1, source_target_pairs={{0,17},{1,16},{2,19},{3,18},{4,21},{5,20},{6,23},{7,22},{8,25},{9,... | collective-permute-start | bytes 786440 | tf_op jit(solution)/shard_map/ppermute | solution.py:307
  113.3 8.7 %collective-permute-start.16 = (bf16[144,512]{1,0:T(8,128)(2,1)}, bf16[144,512]{1,0:T(8,128)(2,1)S(1)}, u32[]{:S(2)}, u32[]{:S(2)}) collective-permute-start(bf16[144,512]{1,0:T(8,128)(2,1)} %get-tuple-element.58), channel_id=1, source_target_pairs={{0,2},{1,3},{2,0},{3,1},{4,6},{5,7},{6,4},{7,5},{8,10},{9,11},{10,... | collective-permute-start | bytes 442376 | tf_op jit(solution)/shard_map/ppermute | solution.py:307
  116.4 13.9 %collective-permute-start.17 = (bf16[144,512]{1,0:T(8,128)(2,1)}, bf16[144,512]{1,0:T(8,128)(2,1)S(1)}, u32[]{:S(2)}, u32[]{:S(2)}) collective-permute-start(bf16[144,512]{1,0:T(8,128)(2,1)} %get-tuple-element.59), channel_id=1, source_target_pairs={{0,4},{1,5},{2,6},{3,7},{4,0},{5,1},{6,2},{7,3},{8,12},{9,13},{10,... | collective-permute-start | bytes 442376 | tf_op jit(solution)/shard_map/ppermute | solution.py:307
  117.6 12.7 %collective-permute-start.18 = (bf16[144,512]{1,0:T(8,128)(2,1)}, bf16[144,512]{1,0:T(8,128)(2,1)S(1)}, u32[]{:S(2)}, u32[]{:S(2)}) collective-permute-start(bf16[144,512]{1,0:T(8,128)(2,1)} %get-tuple-element.60), channel_id=1, source_target_pairs={{0,6},{1,7},{2,4},{3,5},{4,2},{5,3},{6,0},{7,1},{8,14},{9,15},{10,... | collective-permute-start | bytes 442376 | tf_op jit(solution)/shard_map/ppermute | solution.py:307
  133.0 6.7 %collective-permute-start.19 = (bf16[128,512]{1,0:T(8,128)(2,1)}, bf16[128,512]{1,0:T(8,128)(2,1)S(1)}, u32[]{:S(2)}, u32[]{:S(2)}) collective-permute-start(bf16[128,512]{1,0:T(8,128)(2,1)} %get-tuple-element.61), channel_id=1, source_target_pairs={{0,2},{1,3},{2,0},{3,1},{4,6},{5,7},{6,4},{7,5},{8,10},{9,11},{10,... | collective-permute-start | bytes 393224 | tf_op jit(solution)/shard_map/ppermute | solution.py:307
  135.5 11.8 %collective-permute-start.20 = (bf16[128,512]{1,0:T(8,128)(2,1)}, bf16[128,512]{1,0:T(8,128)(2,1)S(1)}, u32[]{:S(2)}, u32[]{:S(2)}) collective-permute-start(bf16[128,512]{1,0:T(8,128)(2,1)} %get-tuple-element.61), channel_id=1, source_target_pairs={{0,4},{1,5},{2,6},{3,7},{4,0},{5,1},{6,2},{7,3},{8,12},{9,13},{10,... | collective-permute-start | bytes 393224 | tf_op jit(solution)/shard_map/ppermute | solution.py:307
  136.0 11.2 %collective-permute-start.21 = (bf16[128,512]{1,0:T(8,128)(2,1)}, bf16[128,512]{1,0:T(8,128)(2,1)S(1)}, u32[]{:S(2)}, u32[]{:S(2)}) collective-permute-start(bf16[128,512]{1,0:T(8,128)(2,1)} %get-tuple-element.61), channel_id=1, source_target_pairs={{0,6},{1,7},{2,4},{3,5},{4,2},{5,3},{6,0},{7,1},{8,14},{9,15},{10,... | collective-permute-start | bytes 393224 | tf_op jit(solution)/shard_map/ppermute | solution.py:307
  148.2 32.1 %copy-start = (bf16[512,512]{1,0:T(8,128)(2,1)}, bf16[512,512]{1,0:T(8,128)(2,1)S(1)}, u32[]{:S(2)}) copy-start(bf16[512,512]{1,0:T(8,128)(2,1)S(1)} %pad_maximum_fusion.refs_1_) | copy-start | bytes 1572868
  148.2 13.9 %collective-permute-start.22 = (bf16[512,512]{1,0:T(8,128)(2,1)S(1)}, bf16[512,512]{1,0:T(8,128)(2,1)S(1)}, u32[]{:S(2)}, u32[]{:S(2)}) collective-permute-start(bf16[512,512]{1,0:T(8,128)(2,1)S(1)} %pad_maximum_fusion.refs_1_), channel_id=1, source_target_pairs={{0,1},{1,0},{2,3},{3,2},{4,5},{5,4},{6,7},{7,6},{8,9},{9,8},{10,11... | collective-permute-start | bytes 1572872 | tf_op jit(solution)/shard_map/ppermute | solution.py:307
  148.3 14.9 %collective-permute-start.23 = (bf16[512,512]{1,0:T(8,128)(2,1)S(1)}, bf16[512,512]{1,0:T(8,128)(2,1)S(1)}, u32[]{:S(2)}, u32[]{:S(2)}) collective-permute-start(bf16[512,512]{1,0:T(8,128)(2,1)S(1)} %pad_maximum_fusion.refs_1_), channel_id=1, source_target_pairs={{0,16},{1,17},{2,18},{3,19},{4,20},{5,21},{6,22},{7,23},{8,24},{9,... | collective-permute-start | bytes 1572872 | tf_op jit(solution)/shard_map/ppermute | solution.py:307
  149.2 20.9 %collective-permute-start.24 = (bf16[512,512]{1,0:T(8,128)(2,1)S(1)}, bf16[512,512]{1,0:T(8,128)(2,1)S(1)}, u32[]{:S(2)}, u32[]{:S(2)}) collective-permute-start(bf16[512,512]{1,0:T(8,128)(2,1)S(1)} %pad_maximum_fusion.refs_1_), channel_id=1, source_target_pairs={{0,17},{1,16},{2,19},{3,18},{4,21},{5,20},{6,23},{7,22},{8,25},{9,... | collective-permute-start | bytes 1572872 | tf_op jit(solution)/shard_map/ppermute | solution.py:307
  151.8 28.6 %collective-permute-start.25 = (bf16[512,512]{1,0:T(8,128)(2,1)S(1)}, bf16[512,512]{1,0:T(8,128)(2,1)S(1)}, u32[]{:S(2)}, u32[]{:S(2)}) collective-permute-start(bf16[512,512]{1,0:T(8,128)(2,1)S(1)} %pad_maximum_fusion.refs_1_), channel_id=1, source_target_pairs={{0,8},{1,9},{2,10},{3,11},{4,12},{5,13},{6,14},{7,15},{8,0},{9,1},... | collective-permute-start | bytes 1572872 | tf_op jit(solution)/shard_map/ppermute | solution.py:307
  162.1 18.3 %collective-permute-start.26 = (bf16[512,512]{1,0:T(8,128)(2,1)S(1)}, bf16[512,512]{1,0:T(8,128)(2,1)S(1)}, u32[]{:S(2)}, u32[]{:S(2)}) collective-permute-start(bf16[512,512]{1,0:T(8,128)(2,1)S(1)} %collective-permute-done.22.refs_2_), channel_id=1, source_target_pairs={{0,8},{1,9},{2,10},{3,11},{4,12},{5,13},{6,14},{7,15},{8,0},{9,1},... | collective-permute-start | bytes 1572872 | tf_op jit(solution)/shard_map/ppermute | solution.py:307
  163.2 17.2 %collective-permute-start.27 = (bf16[512,512]{1,0:T(8,128)(2,1)S(1)}, bf16[512,512]{1,0:T(8,128)(2,1)S(1)}, u32[]{:S(2)}, u32[]{:S(2)}) collective-permute-start(bf16[512,512]{1,0:T(8,128)(2,1)S(1)} %collective-permute-done.23.refs_3_), channel_id=1, source_target_pairs={{0,8},{1,9},{2,10},{3,11},{4,12},{5,13},{6,14},{7,15},{8,0},{9,1},... | collective-permute-start | bytes 1572872 | tf_op jit(solution)/shard_map/ppermute | solution.py:307
  170.1 10.3 %collective-permute-start.28 = (bf16[512,512]{1,0:T(8,128)(2,1)S(1)}, bf16[512,512]{1,0:T(8,128)(2,1)S(1)}, u32[]{:S(2)}, u32[]{:S(2)}) collective-permute-start(bf16[512,512]{1,0:T(8,128)(2,1)S(1)} %collective-permute-done.24.refs_4_), channel_id=1, source_target_pairs={{0,8},{1,9},{2,10},{3,11},{4,12},{5,13},{6,14},{7,15},{8,0},{9,1},... | collective-permute-start | bytes 1572872 | tf_op jit(solution)/shard_map/ppermute | solution.py:307
  (27 other events, 214.7 us)

commit v3 on v2

--- a/solution.py
+++ b/solution.py
@@ -10,9 +10,10 @@
 AXES = ("row", "col")
 BF16 = jnp.bfloat16
 F32 = jnp.float32
-CHUNK = 256
+CHUNK = 512
 HBM = pl.BlockSpec(memory_space=pl.ANY)
 VMEM_LIMIT = 56 << 20
+VMEM = pl.BlockSpec(memory_space=pltpu.VMEM)
 SMEM = pl.BlockSpec(memory_space=pltpu.SMEM)
 
 
@@ -28,7 +29,7 @@
     return lax.dot_general(left, right, (((0,), (0,)), ((), ())), preferred_element_type=F32)
 
 
-def run(body, scalars, ins, outs, flops=0, scratch=()):
+def run(body, scalars, ins, outs, flops=0, scratch=(), limit=0):
     n_in, n_out = len(ins), len(outs)
     outs = [jax.ShapeDtypeStruct(shape, dtype) for shape, dtype in outs]
 
@@ -64,7 +65,26 @@
         scratch_shapes=[pltpu.VMEM(a.shape, a.dtype) for a in [*ins, *outs]]
         + list(scratch)
         + [pltpu.SemaphoreType.DMA((n_in,)), pltpu.SemaphoreType.DMA((n_out,))],
-        compiler_params=pltpu.CompilerParams(vmem_limit_bytes=VMEM_LIMIT),
+        compiler_params=pltpu.CompilerParams(vmem_limit_bytes=limit or held + (8 << 20)),
+        cost_estimate=pl.CostEstimate(flops=flops, bytes_accessed=held, transcendentals=0),
+    )(scalars, *ins)
+
+
+def run_inside(body, scalars, ins, outs, flops=0, scratch=()):
+    n_in, n_out = len(ins), len(outs)
+    outs = [jax.ShapeDtypeStruct(shape, dtype) for shape, dtype in outs]
+
+    def kernel(*refs):
+        body(refs[0], refs[1 : 1 + n_in], refs[1 + n_in : 1 + n_in + n_out], *refs[1 + n_in + n_out :])
+
+    held = sum(a.size * a.dtype.itemsize for a in [*ins, *outs])
+    return pl.pallas_call(
+        kernel,
+        out_shape=outs,
+        in_specs=[SMEM] + [VMEM] * n_in,
+        out_specs=[VMEM] * n_out,
+        scratch_shapes=list(scratch),
+        compiler_params=pltpu.CompilerParams(vmem_limit_bytes=held + (8 << 20)),
         cost_estimate=pl.CostEstimate(flops=flops, bytes_accessed=held, transcendentals=0),
     )(scalars, *ins)
 
@@ -152,73 +172,70 @@
     return jnp.concatenate([total[0, k * rows : (k + 1) * rows], total[1, k * rows : (k + 1) * rows]], 0)
 
 
-def weight_body(n_part, with_hubs, mine, ins, outs, need, emit):
+def weight_body(n_part, with_hubs, mine, ins, outs, total):
     own, peer, d_own, d_peer = ins[:4]
     rows, half = outs[0].shape
-    need(*range(len(ins)))
-    for k in [*range(1, n_part), 0]:
-        at = pl.multiple_of((mine[0] ^ k) * rows, rows)
-        for r in range(0, rows, min(rows, CHUNK)):
-            block = pl.ds(at + r, min(rows, CHUNK))
-            total = mul(own[block, :], d_own[...]) + mul(peer[block, :], d_peer[...])
-            outs[k][r : r + min(rows, CHUNK), :] = total.astype(outs[k].dtype)
+    total[...] = mul(own[...], d_own[...]) + mul(peer[...], d_peer[...])
+    if with_hubs:
+        hubs = ins[4][...] + ins[5][...].astype(F32)
+        size = hubs.shape[1] // n_part
+        outs[n_part][...] = hubs[:, :size]
+    for k in range(n_part):
+        at = pl.ds(pl.multiple_of((mine[0] ^ k) * rows, rows), rows)
+        outs[k][:rows, :] = total[at, :].astype(outs[k].dtype)
         if k > 0 and with_hubs:
-            hubs = ins[4][...] + ins[5][...].astype(F32)
-            size = hubs.shape[1] // n_part
             outs[k][rows:, :] = hub_rows_of(hubs, k, size).astype(BF16)
-        if k > 0:
-            emit(k)
-    if with_hubs:
-        size = ins[4].shape[1] // n_part
-        outs[n_part][...] = ins[4][:, :size] + ins[5][:, :size].astype(F32)
-        emit(n_part)
-    emit(0)
-
-
-def fold_body(n_part, n_got, mine, ins, outs, need, emit, total):
-    self_keep, neigh_keep, hubs = ins[:3]
-    self_got, neigh_got = ins[3 : 3 + n_got], ins[3 + n_got :]
-    size = self_keep.shape[0]
-    rows = size // n_part
-    n_hub = hubs.shape[1]
-    need(*range(len(ins)))
-    together = len(neigh_got) == 0
-    self_value, neigh_value = self_keep[...], neigh_keep[...]
+
+
+def add_up(keep, hubs, got):
+    size = keep.shape[0]
+    value = keep[...]
+    for one in got:
+        value = value + one[:size, :].astype(F32)
+    if hubs is None:
+        return value, None, None
     first, second = hubs[0], hubs[1]
-    for i in range(n_got):
-        self_value = self_value + self_got[i][:size, :].astype(F32)
-        if together:
-            neigh_value = neigh_value + self_got[i][size : 2 * size, :].astype(F32)
-            tail = self_got[i][2 * size :, :].astype(F32)
-        else:
-            neigh_value = neigh_value + neigh_got[i][...].astype(F32)
-            tail = self_got[i][size:, :].astype(F32)
+    n_hub = first.shape[0]
+    for one in got:
+        tail = one[size:, :].astype(F32)
         first = first + tail[:n_hub]
         second = second + tail[n_hub:]
-    if n_part == 1:
-        outs[0][:size, :] = self_value.astype(BF16)
-        outs[0][size:, :] = neigh_value.astype(BF16)
-        outs[1][0] = first
-        outs[1][1] = second
-        emit(0, 1)
-        return
-    n_hub = n_hub // n_part
-    total[0] = self_value
-    total[1] = neigh_value
-    for k in [*range(1, n_part), 0]:
+    return value, first, second
+
+
+def fold_body(n_part, with_hubs, mine, ins, outs, total):
+    hubs = ins[1] if with_hubs else None
+    rows = outs[0].shape[0]
+    value, first, second = add_up(ins[0], hubs, ins[1 + int(with_hubs) :])
+    total[...] = value
+    if with_hubs:
+        n_hub = first.shape[0] // n_part
+        outs[n_part][0] = first[:n_hub]
+        outs[n_part][1] = second[:n_hub]
+    for k in range(n_part):
         at = pl.ds(pl.multiple_of((mine[0] ^ k) * rows, rows), rows)
-        span = slice(k * n_hub, (k + 1) * n_hub)
-        if k > 0:
-            outs[k + 2][:rows, :] = total[0, at, :].astype(BF16)
-            outs[k + 2][rows : 2 * rows, :] = total[1, at, :].astype(BF16)
-            outs[k + 2][2 * rows :, :] = jnp.concatenate([first[span], second[span]], 0).astype(BF16)
-            emit(k + 2)
-    at = pl.ds(pl.multiple_of(mine[0] * rows, rows), rows)
-    outs[0][...] = total[0, at, :]
-    outs[1][...] = total[1, at, :]
-    outs[2][0] = first[:n_hub]
-    outs[2][1] = second[:n_hub]
-    emit(0, 1, 2)
+        outs[k][:rows, :] = total[at, :].astype(outs[k].dtype)
+        if k > 0 and with_hubs:
+            span = slice(k * n_hub, (k + 1) * n_hub)
+            outs[k][rows:, :] = jnp.concatenate([first[span], second[span]], 0).astype(BF16)
+
+
+def last_body(n_got, scalars, ins, outs):
+    own, hub_back = outs
+    rows = ins[0].shape[0]
+    value, _, _ = add_up(ins[0], None, ins[3 : 3 + n_got])
+    own[:rows, :] = value.astype(BF16)
+    value, first, second = add_up(ins[1], ins[2], ins[3 + n_got :])
+    own[rows:, :] = value.astype(BF16)
+    hub_back[0] = first
+    hub_back[1] = second
+
+
+def join_body(scalars, ins, outs):
+    at = 0
+    for one in ins:
+        outs[0][at : at + one.shape[0], :] = one[...]
+        at += one.shape[0]
 
 
 def node_body(side, ins, outs, need, emit):
@@ -246,20 +263,19 @@
     emit(0)
 
 
-def place_body(n_xy, n_z, where, ins, outs, need, emit):
-    size, half = ins[0].shape
-    size = size // 2
-    rows = size // n_z
-    for i in range(2 * n_xy):
-        core, k = divmod(i, n_xy)
-        need(i)
+def place_body(n_xy, n_z, n_share, where, ins, outs):
+    half = ins[0].shape[1]
+    n_piece = n_z // n_share
+    rows = ins[0].shape[0] // n_piece // 2
+    for i, block in enumerate(ins):
+        core, share, k = i // (n_share * n_xy), i // n_xy % n_share, i % n_xy
         cols = pl.ds(pl.multiple_of((where[0] ^ core) * half, half), half)
-        for grad in range(2):
-            for j in range(n_z):
-                at = (where[1] ^ k) * size + (where[2] ^ j) * rows
-                piece = ins[i][(2 * j + grad) * rows : (2 * j + grad + 1) * rows, :]
-                outs[grad][pl.ds(pl.multiple_of(at, rows), rows), cols] = piece
-    emit(0, 1)
+        for j in range(n_piece):
+            z = where[2] ^ (share * n_piece + j)
+            at = pl.ds(pl.multiple_of(((where[1] ^ k) * n_z + z) * rows, rows), rows)
+            for grad in range(2):
+                first = (2 * j + grad) * rows
+                outs[grad][at, cols] = block[first : first + rows, :]
 
 
 def on_device(
@@ -315,6 +331,7 @@
         [features, send_rows, send_count, hub_row],
         [((n_slots, width), BF16), ((n_hub, width), BF16), ((1, n_slots), jnp.int32)],
         flops=2 * n_slots * n_local * width,
+        limit=VMEM_LIMIT,
     )
     arrived = lax.all_to_all(
         outgoing.reshape(n_dev, capacity, width), AXES, split_axis=0, concat_axis=0, tiled=True
@@ -361,6 +378,7 @@
         ],
         flops=4 * n_local * width * (width + n_slots + n_hubs),
         scratch=[pltpu.VMEM(wide, BF16), pltpu.VMEM(wide, BF16)],
+        limit=VMEM_LIMIT,
     )
     returned = lax.all_to_all(
         d_arrived.reshape(n_dev, capacity, width), AXES, split_axis=0, concat_axis=0, tiled=True
@@ -372,52 +390,68 @@
     xy_rows, z_rows = width // n_xy, width // n_xy // n_z
     hub_xy, hub_z = n_hubs // 2 // n_xy, n_hubs // 2 // n_xy // n_z
 
-    def reduce_start(own, peer, with_hubs):
-        extra = 2 * hub_xy if with_hubs else 0
-        outs = [((xy_rows, half), F32)] + [((xy_rows + extra, half), BF16)] * (n_xy - 1)
-        hub_in = [hub_keep, hub_got] if with_hubs else []
-        hub_out = [((2, hub_xy, half), F32)] if with_hubs else []
-        return run(
-            functools.partial(weight_body, n_xy, with_hubs),
+    def across(parts, bits, first=1):
+        return [swap(part, spread(bits, first + k)) for k, part in enumerate(parts)]
+
+    def in_order(values, earlier):
+        return list(lax.optimization_barrier((*values, *earlier))[: len(values)])
+
+    def start_sum(own, peer, hub_in):
+        extra = 2 * hub_xy if hub_in else 0
+        return run_inside(
+            functools.partial(weight_body, n_xy, bool(hub_in)),
             xy_me[None],
             [own, peer, d_pre, peer_d_pre] + hub_in,
-            outs + hub_out,
+            [((xy_rows, half), F32)]
+            + [((xy_rows + extra, half), BF16)] * (n_xy - 1)
+            + ([((2, hub_xy, half), F32)] if hub_in else []),
             flops=4 * width * half * n_local,
+            scratch=[pltpu.VMEM((width, half), F32)],
         )
 
-    def across(parts, bits):
-        return [swap(part, spread(bits, k + 1)) for k, part in enumerate(parts)]
-
-    self_parts = reduce_start(feat_t, peer_feat_t, True)
-    self_got = across(self_parts[1:n_xy], xy_bits)
-    neigh_parts = reduce_start(agg_t, peer_agg_t, False)
-    neigh_got = across(neigh_parts[1:n_xy], xy_bits)
-    parts = run(
-        functools.partial(fold_body, n_z, n_xy - 1),
+    def fold(keep, hub_in, got):
+        extra = 2 * hub_z if hub_in else 0
+        return run_inside(
+            functools.partial(fold_body, n_z, bool(hub_in)),
+            z_me[None],
+            [keep] + hub_in + got,
+            [((z_rows, half), F32)]
+            + [((z_rows + extra, half), BF16)] * (n_z - 1)
+            + ([((2, hub_z, half), F32)] if hub_in else []),
+            scratch=[pltpu.VMEM((xy_rows, half), F32)],
+        )
+
+    self_xy = start_sum(feat_t, peer_feat_t, [])
+    self_got = across(self_xy[1:], xy_bits)
+    agg_pair = in_order([agg_t, peer_agg_t], self_xy)
+    neigh_xy = start_sum(*agg_pair, [hub_keep, hub_got])
+    neigh_got = across(neigh_xy[1:n_xy], xy_bits)
+    self_z = fold(self_xy[0], [], self_got)
+    self_got = across(self_z[1:], z_bits)
+    neigh_got = in_order(neigh_got, self_got)
+    neigh_z = fold(neigh_xy[0], [neigh_xy[n_xy]], neigh_got)
+    neigh_got = across(neigh_z[1:n_z], z_bits)
+    own, hub_back = run_inside(
+        functools.partial(last_body, n_z - 1),
         z_me[None],
-        [self_parts[0], neigh_parts[0], self_parts[n_xy]] + self_got + neigh_got,
-        [((z_rows, half), F32)] * 2
-        + [((2, hub_z, half), F32)]
-        + [((2 * z_rows + 2 * hub_z, half), BF16)] * (n_z - 1),
-        scratch=[pltpu.VMEM((2, xy_rows, half), F32)],
-    )
-    own, hub_back = run(
-        functools.partial(fold_body, 1, n_z - 1),
-        z_me[None],
-        list(parts[:3]) + across(parts[3:], z_bits),
+        [self_z[0], neigh_z[0], neigh_z[n_z]] + self_got + neigh_got,
         [((2 * z_rows, half), BF16), ((2, hub_z, half), F32)],
-        scratch=[pltpu.VMEM((2, 8, half), F32)],
-    )
-    line = jnp.concatenate([own] + across([own] * (n_z - 1), z_bits), 0)
-    line, returned = lax.optimization_barrier((line, returned))
-    blocks = [line] + across([line] * (n_xy - 1), xy_bits)
-    blocks = blocks + [swap(one, core) for one in blocks]
-    grad_self, grad_neigh = run(
-        functools.partial(place_body, n_xy, n_z),
-        jnp.stack([side, xy_me, z_me]),
-        blocks,
-        [((width, width), BF16)] * 2,
-    )
+    )
+
+    line = [own] + across([own] * (n_z - 1), z_bits)
+    n_share = 2
+    n_piece = n_z // n_share
+    got = []
+    for share in range(n_share):
+        (piece,) = run_inside(
+            join_body,
+            z_me[None],
+            line[share * n_piece : (share + 1) * n_piece],
+            [((n_piece * 2 * z_rows, half), BF16)],
+        )
+        if share > 0:
+            (piece,) = in_order([piece], got[-1])
+        got.append([piece] + across([piece] * (n_xy - 1), xy_bits))
     (grad_x,) = run(
         node_body,
         side[None],
@@ -425,6 +459,14 @@
         [(wide, BF16)],
         flops=2 * n_local * width * (width + n_local + n_slots),
     )
+    got[-1] = in_order(got[-1], [grad_x])
+    blocks = [one for share in got for one in share]
+    grad_self, grad_neigh = run_inside(
+        functools.partial(place_body, n_xy, n_z, n_share),
+        jnp.stack([side, xy_me, z_me]),
+        blocks + [swap(one, core) for one in blocks],
+        [((width, width), BF16)] * 2,
+    )
     return hidden, grad_x, grad_self, grad_neigh
 
 

time: 191 us -> 165 us (0.86)
  waiting for transfers between devices: 69.5 us -> 44 us
  Pallas kernels: 41.4 us -> 29.5 us
  starting transfers between devices: 44.1 us -> 55.3 us
  local copies, waits for them, and re-layouts: 10.3 us -> 14.3 us
  other arithmetic: 12.6 us -> 10.3 us
    ppermute x29 -> x39, waiting for transfers between devices: 69.5 us -> 44 us  [swap(): return lax.ppermute(value, AXES, [(i, i ^ mask) for i in range(n_dev)])]
    pallas_call x8 -> x3, Pallas kernels: 41.4 us -> 17.5 us  [run(): pl.pallas_call(kernel, out_shape=outs, in_specs=[SMEM] + [HBM] * n_in, ou...]
    pallas_call x0 -> x8, Pallas kernels: none -> 12 us  [run_inside(): pl.pallas_call(kernel, out_shape=outs, in_specs=[SMEM] + [VMEM] * n_in, o...]
    ppermute x29 -> x39, starting transfers between devices: 31 us -> 42.5 us  [swap(): return lax.ppermute(value, AXES, [(i, i ^ mask) for i in range(n_dev)])]
    unnamed x62 -> x88, local copies, waits for them, and re-layouts: 7.98 us -> 11.9 us
  transfers between devices with their start and end apart: 31 -> 41, of which waited for: 16 -> 19; matrix products, arithmetic and copies ran while one was open for 14% -> 15% of each run, Pallas kernels for 18% -> 14%
where the time goes in v3:
time: 165 us; the launch traced here: 163 us
  starting transfers between devices  55.3 us (34%)
  waiting for transfers between devices  44 us (27%)
  Pallas kernels  29.5 us (18%)
  local copies, waits for them, and re-layouts  14.3 us (9%)
  other arithmetic  10.3 us (6%)
  matrix products  8.35 us (5%)
    ppermute x39, waiting for transfers between devices, swap(): return lax.ppermute(value, AXES, [(i, i ^ mask) for i in range(n_dev)])  44 us
    ppermute x39, starting transfers between devices, swap(): return lax.ppermute(value, AXES, [(i, i ^ mask) for i in range(n_dev)])  42.5 us
    pallas_call x3, Pallas kernels, run(): pl.pallas_call(kernel, out_shape=outs, in_specs=[SMEM] + [HBM] * n_in, ou...  17.5 us
    pallas_call x8, Pallas kernels, run_inside(): pl.pallas_call(kernel, out_shape=outs, in_specs=[SMEM] + [VMEM] * n_in, o...  12 us
    unnamed x88, local copies, waits for them, and re-layouts  11.9 us
    convert_element_type x3, other arithmetic, count(): return (found.astype(BF16), found_t.astype(BF16))  9.9 us
    dot_general x2, matrix products, mul(): return jnp.dot(left, right, preferred_element_type=F32)  8.35 us
    all_to_all x1, starting transfers between devices, on_device(): lax.all_to_all(d_arrived.reshape(n_dev, capacity, width), AXES, split_axi...  6.63 us
  transfers between devices with their start and end apart: 41, of which 19 were waited for; matrix products, arithmetic and copies ran while one was open for 15% of the time, Pallas kernels for 14%

profile of v3, /device:TPU:0, one launch (start us, length us, event | category | flops | bytes accessed | tf_op | source)
XLA Modules:
  0.0 163.1 jit_solution(14504990422163795251)
XLA Ops:
  0.7 3.3 %shard_map.129 = (bf16[512,1024]{1,0:T(8,128)(2,1)}, bf16[8,1024]{1,0:T(8,128)(2,1)}, s32[1,512]{1,0:T(1,128)}) custom-call(s32[1]{0:T(128)} %bitcast.refs_0_, bf16[512,1024]{1,0:T(8,128)(2,1)} %refs_1_.2, s32[1,512]{1,0:T(1,128)} %refs_2_.1, s32[1,32]{1,0:T(1,128)} %refs_3_.1, s32[1,8]{1,0:T(1,128)} %bitcast.50), custom_call_target="tpu_custom_call" | custom-call | flops 536870912 | bytes 2117792 | tf_op jit(solution)/shard_map/pallas_call | solution.py:60
  4.0 3.1 %collective-permute-start = (bf16[8,1024]{1,0:T(8,128)(2,1)}, bf16[8,1024]{1,0:T(8,128)(2,1)S(1)}, u32[]{:S(2)}, u32[]{:S(2)}) collective-permute-start(bf16[8,1024]{1,0:T(8,128)(2,1)} %get-tuple-element.48), channel_id=1, source_target_pairs={{0,2},{1,3},{2,0},{3,1},{4,6},{5,7},{6,4},{7,5},{8,10},{9,11},{10,... | collective-permute-start | bytes 49160 | tf_op jit(solution)/shard_map/ppermute | solution.py:323
  7.0 2.6 %collective-permute-start.1 = (bf16[8,1024]{1,0:T(8,128)(2,1)}, bf16[8,1024]{1,0:T(8,128)(2,1)S(1)}, u32[]{:S(2)}, u32[]{:S(2)}) collective-permute-start(bf16[8,1024]{1,0:T(8,128)(2,1)} %get-tuple-element.48), channel_id=1, source_target_pairs={{0,4},{1,5},{2,6},{3,7},{4,0},{5,1},{6,2},{7,3},{8,12},{9,13},{10,... | collective-permute-start | bytes 49160 | tf_op jit(solution)/shard_map/ppermute | solution.py:323
  9.6 6.2 %all-to-all-start = ((bf16[32,16,1024]{2,1,0:T(8,128)(2,1)}), bf16[32,16,1024]{2,1,0:T(8,128)(2,1)}, u32[]{:S(2)}, u32[]{:S(2)}) async-start(bf16[32,16,1024]{2,1,0:T(8,128)(2,1)} %bitcast.53), calls=%async_computation | async-start | bytes 2097152 | tf_op jit(solution)/shard_map/all_to_all | solution.py:336
  17.1 3.4 %add_convert_fusion.refs_9_ = bf16[768,512]{1,0:T(8,128)(2,1)} fusion(s32[512]{0:T(512)S(1)} %bitcast.56, s32[512]{0:T(512)S(1)} %bitcast.58, s32[512]{0:T(512)S(1)} %bitcast.60, s32[512]{0:T(512)S(1)} %bitcast.62, s32[512]{0:T(512)S(1)} %bitcast.64, s32[512]{0:T(512)S(1)} %bitcast.66, s32[512]{0:T(512)S(1)} %bitcast.68, s32[512]{0:T(512)S(1)} %bitcast.70, ...), kind=kLoop, calls=%fused_computation | loop fusion | flops 18874368 | bytes 822272 | tf_op jit(solution)/shard_map/convert_element_type | solution.py:357
  20.6 4.2 %fusion.refs_4_ = f32[512,1024]{1,0:T(8,128)} fusion(bf16[512,1024]{1,0:T(8,128)(2,1)S(1)} %copy-done.12, s32[512]{0:T(512)S(1)} %bitcast.88, s32[512]{0:T(512)S(1)} %bitcast.90, s32[512]{0:T(512)S(1)} %bitcast.92, s32[512]{0:T(512)S(1)} %bitcast.94, s32[512]{0:T(512)S(1)} %bitcast.96, s32[512]{0:T(512)S(1)} %bitcast.98, s32[512]{0:T(512)S(1)} %bitcast.100, ...), kind=kOutput, calls=%fused_computation.37 | convolution fusion | flops 549453824 | bytes 3178496 | tf_op jit(solution)/shard_map/dot_general | solution.py:21
  24.9 4.4 %add_convert_fusion.1.refs_1_ = bf16[512,768]{1,0:T(8,128)(2,1)} fusion(s32[768]{0:T(1024)S(1)} %iota_add_fusion, s32[512]{0:T(512)S(1)} %bitcast.89, s32[512]{0:T(512)S(1)} %bitcast.91, s32[512]{0:T(512)S(1)} %bitcast.93, s32[512]{0:T(512)S(1)} %bitcast.95, s32[512]{0:T(512)S(1)} %bitcast.97, s32[512]{0:T(512)S(1)} %bitcast.99, s32[512]{0:T(512)S(1)} %bitcast.101, ...), kind=kLoop, calls=%fused_computation.1 | loop fusion | flops 18874368 | bytes 822272 | tf_op jit(solution)/shard_map/convert_element_type | solution.py:357
  29.9 1.7 %collective-permute-start.3 = (bf16[32,1024]{1,0:T(8,128)(2,1)S(1)}, bf16[32,1024]{1,0:T(8,128)(2,1)S(1)}, u32[]{:S(2)}, u32[]{:S(2)}) collective-permute-start(bf16[32,1024]{1,0:T(8,128)(2,1)S(1)} %pad_maximum_fusion), channel_id=1, source_target_pairs={{0,1},{1,0},{2,3},{3,2},{4,5},{5,4},{6,7},{7,6},{8,9},{9,8},{10,11... | collective-permute-start | bytes 196616 | tf_op jit(solution)/shard_map/ppermute | solution.py:323
  35.1 1.7 %collective-permute-start.4 = (bf16[64,1024]{1,0:T(8,128)(2,1)S(1)}, bf16[64,1024]{1,0:T(8,128)(2,1)S(1)}, u32[]{:S(2)}, u32[]{:S(2)}) collective-permute-start(bf16[64,1024]{1,0:T(8,128)(2,1)S(1)} %get-tuple-element.94), channel_id=1, source_target_pairs={{0,16},{1,17},{2,18},{3,19},{4,20},{5,21},{6,22},{7,23},{8,24},{9,... | collective-permute-start | bytes 393224 | tf_op jit(solution)/shard_map/ppermute | solution.py:323
  37.7 3.1 %collective-permute-done.4 = bf16[64,1024]{1,0:T(8,128)(2,1)S(1)} collective-permute-done((bf16[64,1024]{1,0:T(8,128)(2,1)S(1)}, bf16[64,1024]{1,0:T(8,128)(2,1)S(1)}, u32[]{:S(2)}, u32[]{:S(2)}) %collective-permute-start.4) | collective-permute-done | bytes 131104 | tf_op jit(solution)/shard_map/ppermute | solution.py:323
  41.5 4.2 %convolution_add_fusion.refs_7_ = f32[512,1024]{1,0:T(8,128)} fusion(bf16[512,1024]{1,0:T(8,128)(2,1)S(1)} %copy-done.12, bf16[1024,1024]{1,0:T(8,128)(2,1)} %refs_1_.3, f32[1024]{0:T(1024)S(1)} %copy-done.40), kind=kOutput, calls=%fused_computation.2 | convolution fusion | flops 1074266112 | bytes 5246976 | tf_op jit(solution)/shard_map/dot_general | solution.py:21
  46.4 9.8 %shard_map.130 = (bf16[512,1024]{1,0:T(8,128)(2,1)}, bf16[512,512]{1,0:T(8,128)(2,1)}, bf16[512,1024]{1,0:T(8,128)(2,1)}, bf16[512,512]{1,0:T(8,128)(2,1)}, bf16...) custom-call(s32[1]{0:T(128)} %bitcast.refs_0_, ...), custom_call_target="tpu_custom_call" | custom-call | flops 3758096384 | bytes 16517120 | tf_op jit(solution)/shard_map/pallas_call | solution.py:60
  56.9 6.6 %all-to-all-start.1 = ((bf16[32,16,1024]{2,1,0:T(8,128)(2,1)}), bf16[32,16,1024]{2,1,0:T(8,128)(2,1)S(1)}, u32[]{:S(2)}, u32[]{:S(2)}) async-start(bf16[32,16,1024]{2,1,0:T(8,128)(2,1)} %bitcast.52), calls=%async_computation.1 | async-start | bytes 2097152 | tf_op jit(solution)/shard_map/all_to_all | solution.py:383
  66.9 3.4 %shard_map.131 = (f32[256,512]{1,0:T(8,128)S(1)}, bf16[256,512]{1,0:T(8,128)(2,1)}, bf16[256,512]{1,0:T(8,128)(2,1)}, bf16[256,512]{1,0:T(8,128)(2,1)S(1)}) custom-call(s32[1]{0:T(128)} %bitcast.41.refs_0_, bf16[1024,512]{1,0:T(8,128)(2,1)S(1)} %bitcast.49, bf16[1024,512]{1,0:T(8,128)(2,1)S(1)} %copy-done.2, bf16[512,512]{1,0:T(8,128)(2,1)S(1)} %copy-done.6, ...), custom_call_target="tpu_custom_call" | custom-call | flops 1073741824 | bytes 4456448 | tf_op jit(solution)/shard_map/pallas_call | solution.py:81
  70.3 2.6 %collective-permute-start.10 = (bf16[256,512]{1,0:T(8,128)(2,1)S(1)}, bf16[256,512]{1,0:T(8,128)(2,1)S(1)}, u32[]{:S(2)}, u32[]{:S(2)}) collective-permute-start(bf16[256,512]{1,0:T(8,128)(2,1)S(1)} %get-tuple-element.58), channel_id=1, source_target_pairs={{0,17},{1,16},{2,19},{3,18},{4,21},{5,20},{6,23},{7,22},{8,25},{9,... | collective-permute-start | bytes 786440 | tf_op jit(solution)/shard_map/ppermute | solution.py:323
  73.8 3.6 %shard_map.133 = (f32[256,512]{1,0:T(8,128)S(1)}, bf16[320,512]{1,0:T(8,128)(2,1)}, bf16[320,512]{1,0:T(8,128)(2,1)}, bf16[320,512]{1,0:T(8,128)(2,1)}, f32[2,32,512]{2,1,0:T(8,128)S(1)}) custom-call(s32[1]{0:T(128)} %bitcast.41.refs_0_, bf16[1024,512]{1,0:T(8,128)(2,1)S(1)} %copy-done.3, bf16[1024,512]{1,0:T(8,128)(2,1)} %collective-permute-done.11.refs_2_, ...), custom_call_target="tpu_custom_call" | custom-call | flops 1073741824 | bytes 5570560 | tf_op jit(solution)/shard_map/pallas_call | solution.py:81
  80.6 5.0 %collective-permute-done.10.refs_4_ = bf16[256,512]{1,0:T(8,128)(2,1)S(1)} collective-permute-done((bf16[256,512]{1,0:T(8,128)(2,1)S(1)}, bf16[256,512]{1,0:T(8,128)(2,1)S(1)}, u32[]{:S(2)}, u32[]{:S(2)}) %collective-permute-start.10) | collective-permute-done | bytes 262176 | tf_op jit(solution)/shard_map/ppermute | solution.py:323
  85.5 4.1 %collective-permute-done.8.refs_2_ = bf16[256,512]{1,0:T(8,128)(2,1)} collective-permute-done((bf16[256,512]{1,0:T(8,128)(2,1)}, bf16[256,512]{1,0:T(8,128)(2,1)}, u32[]{:S(2)}, u32[]{:S(2)}) %collective-permute-start.8) | collective-permute-done | bytes 262176 | tf_op jit(solution)/shard_map/ppermute | solution.py:323
  92.3 2.6 %collective-permute-start.16 = (bf16[64,512]{1,0:T(8,128)(2,1)S(1)}, bf16[64,512]{1,0:T(8,128)(2,1)S(1)}, u32[]{:S(2)}, u32[]{:S(2)}) collective-permute-start(bf16[64,512]{1,0:T(8,128)(2,1)S(1)} %get-tuple-element.70), channel_id=1, source_target_pairs={{0,2},{1,3},{2,0},{3,1},{4,6},{5,7},{6,4},{7,5},{8,10},{9,11},{10,... | collective-permute-start | bytes 196616 | tf_op jit(solution)/shard_map/ppermute | solution.py:323
  97.2 2.6 %collective-permute-start.18 = (bf16[64,512]{1,0:T(8,128)(2,1)S(1)}, bf16[64,512]{1,0:T(8,128)(2,1)S(1)}, u32[]{:S(2)}, u32[]{:S(2)}) collective-permute-start(bf16[64,512]{1,0:T(8,128)(2,1)S(1)} %get-tuple-element.72), channel_id=1, source_target_pairs={{0,6},{1,7},{2,4},{3,5},{4,2},{5,3},{6,0},{7,1},{8,14},{9,15},{10,... | collective-permute-start | bytes 196616 | tf_op jit(solution)/shard_map/ppermute | solution.py:323
  101.5 1.8 %collective-permute-done.18.refs_6_ = bf16[64,512]{1,0:T(8,128)(2,1)S(1)} collective-permute-done((bf16[64,512]{1,0:T(8,128)(2,1)S(1)}, bf16[64,512]{1,0:T(8,128)(2,1)S(1)}, u32[]{:S(2)}, u32[]{:S(2)}) %collective-permute-start.18) | collective-permute-done | bytes 65568 | tf_op jit(solution)/shard_map/ppermute | solution.py:323
  103.4 2.9 %collective-permute-done.15.refs_5_ = bf16[320,512]{1,0:T(8,128)(2,1)S(1)} collective-permute-done((bf16[320,512]{1,0:T(8,128)(2,1)}, bf16[320,512]{1,0:T(8,128)(2,1)S(1)}, u32[]{:S(2)}, u32[]{:S(2)}) %collective-permute-start.15) | collective-permute-done | bytes 327712 | tf_op jit(solution)/shard_map/ppermute | solution.py:323
  107.5 2.6 %collective-permute-start.20 = (bf16[80,512]{1,0:T(8,128)(2,1)S(1)}, bf16[80,512]{1,0:T(8,128)(2,1)S(1)}, u32[]{:S(2)}, u32[]{:S(2)}) collective-permute-start(bf16[80,512]{1,0:T(8,128)(2,1)S(1)} %get-tuple-element.79), channel_id=1, source_target_pairs={{0,4},{1,5},{2,6},{3,7},{4,0},{5,1},{6,2},{7,3},{8,12},{9,13},{10,... | collective-permute-start | bytes 245768 | tf_op jit(solution)/shard_map/ppermute | solution.py:323
  112.9 4.3 %collective-permute-done.21.refs_9_ = bf16[80,512]{1,0:T(8,128)(2,1)S(1)} collective-permute-done((bf16[80,512]{1,0:T(8,128)(2,1)S(1)}, bf16[80,512]{1,0:T(8,128)(2,1)S(1)}, u32[]{:S(2)}, u32[]{:S(2)}) %collective-permute-start.21) | collective-permute-done | bytes 81952 | tf_op jit(solution)/shard_map/ppermute | solution.py:323
  118.9 3.4 %collective-permute-done.22.refs_2_ = bf16[128,512]{1,0:T(8,128)(2,1)S(1)} collective-permute-done((bf16[128,512]{1,0:T(8,128)(2,1)S(1)}, bf16[128,512]{1,0:T(8,128)(2,1)S(1)}, u32[]{:S(2)}, u32[]{:S(2)}) %collective-permute-start.22) | collective-permute-done | bytes 131104 | tf_op jit(solution)/shard_map/ppermute | solution.py:323
  125.9 3.6 %collective-permute-start.26 = (bf16[128,512]{1,0:T(8,128)(2,1)S(1)}, bf16[128,512]{1,0:T(8,128)(2,1)S(1)}, u32[]{:S(2)}, u32[]{:S(2)}) collective-permute-start(bf16[128,512]{1,0:T(8,128)(2,1)S(1)} %get-tuple-element.82.refs_1_), channel_id=1, source_target_pairs={{0,4},{1,5},{2,6},{3,7},{4,0},{5,1},{6,2},{7,3},{8,12},{9,13},{10,... | collective-permute-start | bytes 393224 | tf_op jit(solution)/shard_map/ppermute | solution.py:323
  129.9 8.2 %collective-permute-done.26.refs_1_ = bf16[128,512]{1,0:T(8,128)(2,1)S(1)} collective-permute-done((bf16[128,512]{1,0:T(8,128)(2,1)S(1)}, bf16[128,512]{1,0:T(8,128)(2,1)S(1)}, u32[]{:S(2)}, u32[]{:S(2)}) %collective-permute-start.26) | collective-permute-done | bytes 131104 | tf_op jit(solution)/shard_map/ppermute | solution.py:323
  139.7 2.0 %collective-permute-start.30 = (bf16[256,512]{1,0:T(8,128)(2,1)S(1)}, bf16[256,512]{1,0:T(8,128)(2,1)}, u32[]{:S(2)}, u32[]{:S(2)}) collective-permute-start(bf16[256,512]{1,0:T(8,128)(2,1)S(1)} %shard_map.138.refs_5_), channel_id=1, source_target_pairs={{0,17},{1,16},{2,19},{3,18},{4,21},{5,20},{6,23},{7,22},{8,25},{9,... | collective-permute-start | bytes 786440 | tf_op jit(solution)/shard_map/ppermute | solution.py:323
  141.7 2.9 %collective-permute-done.28.refs_6_ = bf16[256,512]{1,0:T(8,128)(2,1)S(1)} collective-permute-done((bf16[256,512]{1,0:T(8,128)(2,1)S(1)}, bf16[256,512]{1,0:T(8,128)(2,1)S(1)}, u32[]{:S(2)}, u32[]{:S(2)}) %collective-permute-start.28) | collective-permute-done | bytes 262176 | tf_op jit(solution)/shard_map/ppermute | solution.py:323
  144.7 2.1 %add_convert_fusion.2.refs_4_ = bf16[512,512]{1,0:T(8,128)(2,1)S(1)} fusion(s32[512]{0:T(512)S(1)} %bitcast.57, s32[512]{0:T(512)S(1)} %bitcast.59, s32[512]{0:T(512)S(1)} %bitcast.61, s32[512]{0:T(512)S(1)} %bitcast.63, s32[512]{0:T(512)S(1)} %bitcast.65, s32[512]{0:T(512)S(1)} %bitcast.67, s32[512]{0:T(512)S(1)} %bitcast.69, s32[512]{0:T(512)S(1)} %bitcast.71, ...), kind=kLoop, calls=%fused_computation.3 | loop fusion | flops 12582912 | bytes 557056 | tf_op jit(solution)/shard_map/convert_element_type | solution.py:357
  151.7 4.4 %shard_map.136 = bf16[512,1024]{1,0:T(8,128)(2,1)} custom-call(s32[1]{0:T(128)} %bitcast.refs_0_, bf16[1024,1024]{1,0:T(8,128)(2,1)S(1)} %copy-done, bf16[512,512]{1,0:T(8,128)(2,1)S(1)} %copy-done.8, bf16[512,512]{1,0:T(8,128)(2,1)S(1)} %copy-done.4, bf16[512,512]{1,0:T(8,128)(2,1)S(1)} %add_convert_fusion.2.refs_4_, bf16[512,1024]{1,0:T(8,128)(2,1)S(1)} %copy-done.10, ...), custom_call_target="tpu_custom_call" | custom-call | flops 2147483648 | bytes 6850592 | tf_op jit(solution)/shard_map/pallas_call | solution.py:60
  159.5 3.5 %shard_map.139 = (bf16[1024,1024]{1,0:T(8,128)(2,1)}, bf16[1024,1024]{1,0:T(8,128)(2,1)}) custom-call(s32[3]{0:T(128)S(1)} %pad_add_fusion.refs_0_, bf16[256,512]{1,0:T(8,128)(2,1)S(1)} %shard_map.137.refs_1_, bf16[256,512]{1,0:T(8,128)(2,1)S(1)} %collective-permute-done.23.refs_2_, bf16[256,512]{1,0:T(8,128)(2,1)S(1)} %collective-permute-done.24.refs_3_, ...), custom_call_target="tpu_custom_call" | custom-call | bytes 8388608 | tf_op jit(solution)/shard_map/pallas_call | solution.py:81
  (165 shorter events, 42.0 us)
Async XLA Ops:
  4.0 26.0 %collective-permute-start = (bf16[8,1024]{1,0:T(8,128)(2,1)}, bf16[8,1024]{1,0:T(8,128)(2,1)S(1)}, u32[]{:S(2)}, u32[]{:S(2)}) collective-permute-start(bf16[8,1024]{1,0:T(8,128)(2,1)} %get-tuple-element.48), channel_id=1, source_target_pairs={{0,2},{1,3},{2,0},{3,1},{4,6},{5,7},{6,4},{7,5},{8,10},{9,11},{10,... | collective-permute-start | bytes 49160 | tf_op jit(solution)/shard_map/ppermute | solution.py:323
  7.0 22.9 %collective-permute-start.1 = (bf16[8,1024]{1,0:T(8,128)(2,1)}, bf16[8,1024]{1,0:T(8,128)(2,1)S(1)}, u32[]{:S(2)}, u32[]{:S(2)}) collective-permute-start(bf16[8,1024]{1,0:T(8,128)(2,1)} %get-tuple-element.48), channel_id=1, source_target_pairs={{0,4},{1,5},{2,6},{3,7},{4,0},{5,1},{6,2},{7,3},{8,12},{9,13},{10,... | collective-permute-start | bytes 49160 | tf_op jit(solution)/shard_map/ppermute | solution.py:323
  9.6 20.3 %collective-permute-start.2 = (bf16[8,1024]{1,0:T(8,128)(2,1)}, bf16[8,1024]{1,0:T(8,128)(2,1)S(1)}, u32[]{:S(2)}, u32[]{:S(2)}) collective-permute-start(bf16[8,1024]{1,0:T(8,128)(2,1)} %get-tuple-element.48), channel_id=1, source_target_pairs={{0,6},{1,7},{2,4},{3,5},{4,2},{5,3},{6,0},{7,1},{8,14},{9,15},{10,... | collective-permute-start | bytes 49160 | tf_op jit(solution)/shard_map/ppermute | solution.py:323
  9.6 36.8 %all-to-all-start = ((bf16[32,16,1024]{2,1,0:T(8,128)(2,1)}), bf16[32,16,1024]{2,1,0:T(8,128)(2,1)}, u32[]{:S(2)}, u32[]{:S(2)}) async-start(bf16[32,16,1024]{2,1,0:T(8,128)(2,1)} %bitcast.53), calls=%async_computation | async-start | bytes 2097152 | tf_op jit(solution)/shard_map/all_to_all | solution.py:336
  16.4 47.3 %collective-permute-start.6 = (bf16[1024,512]{1,0:T(8,128)(2,1)S(1)}, bf16[1024,512]{1,0:T(8,128)(2,1)S(1)}, u32[]{:S(2)}, u32[]{:S(2)}) collective-permute-start(bf16[1024,512]{1,0:T(8,128)(2,1)S(1)} %bitcast.48), channel_id=1, source_target_pairs={{0,8},{1,9},{2,10},{3,11},{4,12},{5,13},{6,14},{7,15},{8,0},{9,1},... | collective-permute-start | bytes 3145736 | tf_op jit(solution)/shard_map/ppermute | solution.py:323
  35.1 5.7 %collective-permute-start.4 = (bf16[64,1024]{1,0:T(8,128)(2,1)S(1)}, bf16[64,1024]{1,0:T(8,128)(2,1)S(1)}, u32[]{:S(2)}, u32[]{:S(2)}) collective-permute-start(bf16[64,1024]{1,0:T(8,128)(2,1)S(1)} %get-tuple-element.94), channel_id=1, source_target_pairs={{0,16},{1,17},{2,18},{3,19},{4,20},{5,21},{6,22},{7,23},{8,24},{9,... | collective-permute-start | bytes 393224 | tf_op jit(solution)/shard_map/ppermute | solution.py:323
  56.2 17.5 %collective-permute-start.11 = (bf16[1024,512]{1,0:T(8,128)(2,1)}, bf16[1024,512]{1,0:T(8,128)(2,1)}, u32[]{:S(2)}, u32[]{:S(2)}) collective-permute-start(bf16[1024,512]{1,0:T(8,128)(2,1)} %get-tuple-element.61.refs_1_), channel_id=1, source_target_pairs={{0,8},{1,9},{2,10},{3,11},{4,12},{5,13},{6,14},{7,15},{8,0},{9,1},... | collective-permute-start | bytes 3145736 | tf_op jit(solution)/shard_map/ppermute | solution.py:323
  56.8 7.9 %collective-permute-start.7 = (bf16[512,512]{1,0:T(8,128)(2,1)}, bf16[512,512]{1,0:T(8,128)(2,1)}, u32[]{:S(2)}, u32[]{:S(2)}) collective-permute-start(bf16[512,512]{1,0:T(8,128)(2,1)} %get-tuple-element.51.refs_3_), channel_id=1, source_target_pairs={{0,8},{1,9},{2,10},{3,11},{4,12},{5,13},{6,14},{7,15},{8,0},{9,1},... | collective-permute-start | bytes 1572872 | tf_op jit(solution)/shard_map/ppermute | solution.py:323
  56.9 89.9 %all-to-all-start.1 = ((bf16[32,16,1024]{2,1,0:T(8,128)(2,1)}), bf16[32,16,1024]{2,1,0:T(8,128)(2,1)S(1)}, u32[]{:S(2)}, u32[]{:S(2)}) async-start(bf16[32,16,1024]{2,1,0:T(8,128)(2,1)} %bitcast.52), calls=%async_computation.1 | async-start | bytes 2097152 | tf_op jit(solution)/shard_map/all_to_all | solution.py:383
  63.5 10.2 %collective-permute-start.12 = (bf16[2,128,512]{2,1,0:T(8,128)(2,1)}, bf16[2,128,512]{2,1,0:T(8,128)(2,1)S(1)}, u32[]{:S(2)}, u32[]{:S(2)}) collective-permute-start(bf16[2,128,512]{2,1,0:T(8,128)(2,1)} %get-tuple-element.64), channel_id=1, source_target_pairs={{0,8},{1,9},{2,10},{3,11},{4,12},{5,13},{6,14},{7,15},{8,0},{9,1},... | collective-permute-start | bytes 786440 | tf_op jit(solution)/shard_map/ppermute | solution.py:323
  70.3 15.2 %collective-permute-start.10 = (bf16[256,512]{1,0:T(8,128)(2,1)S(1)}, bf16[256,512]{1,0:T(8,128)(2,1)S(1)}, u32[]{:S(2)}, u32[]{:S(2)}) collective-permute-start(bf16[256,512]{1,0:T(8,128)(2,1)S(1)} %get-tuple-element.58), channel_id=1, source_target_pairs={{0,17},{1,16},{2,19},{3,18},{4,21},{5,20},{6,23},{7,22},{8,25},{9,... | collective-permute-start | bytes 786440 | tf_op jit(solution)/shard_map/ppermute | solution.py:323
  72.9 16.8 %collective-permute-start.8 = (bf16[256,512]{1,0:T(8,128)(2,1)}, bf16[256,512]{1,0:T(8,128)(2,1)}, u32[]{:S(2)}, u32[]{:S(2)}) collective-permute-start(bf16[256,512]{1,0:T(8,128)(2,1)} %get-tuple-element.56), channel_id=1, source_target_pairs={{0,1},{1,0},{2,3},{3,2},{4,5},{5,4},{6,7},{7,6},{8,9},{9,8},{10,11... | collective-permute-start | bytes 786440 | tf_op jit(solution)/shard_map/ppermute | solution.py:323
  73.4 17.6 %collective-permute-start.9 = (bf16[256,512]{1,0:T(8,128)(2,1)}, bf16[256,512]{1,0:T(8,128)(2,1)}, u32[]{:S(2)}, u32[]{:S(2)}) collective-permute-start(bf16[256,512]{1,0:T(8,128)(2,1)} %get-tuple-element.57), channel_id=1, source_target_pairs={{0,16},{1,17},{2,18},{3,19},{4,20},{5,21},{6,22},{7,23},{8,24},{9,... | collective-permute-start | bytes 786440 | tf_op jit(solution)/shard_map/ppermute | solution.py:323
  77.4 25.9 %collective-permute-start.13 = (bf16[320,512]{1,0:T(8,128)(2,1)}, bf16[320,512]{1,0:T(8,128)(2,1)S(1)}, u32[]{:S(2)}, u32[]{:S(2)}) collective-permute-start(bf16[320,512]{1,0:T(8,128)(2,1)} %get-tuple-element.67), channel_id=1, source_target_pairs={{0,1},{1,0},{2,3},{3,2},{4,5},{5,4},{6,7},{7,6},{8,9},{9,8},{10,11... | collective-permute-start | bytes 983048 | tf_op jit(solution)/shard_map/ppermute | solution.py:323
  79.1 24.3 %collective-permute-start.14 = (bf16[320,512]{1,0:T(8,128)(2,1)}, bf16[320,512]{1,0:T(8,128)(2,1)S(1)}, u32[]{:S(2)}, u32[]{:S(2)}) collective-permute-start(bf16[320,512]{1,0:T(8,128)(2,1)} %get-tuple-element.68), channel_id=1, source_target_pairs={{0,16},{1,17},{2,18},{3,19},{4,20},{5,21},{6,22},{7,23},{8,24},{9,... | collective-permute-start | bytes 983048 | tf_op jit(solution)/shard_map/ppermute | solution.py:323
  85.5 20.7 %collective-permute-start.15 = (bf16[320,512]{1,0:T(8,128)(2,1)}, bf16[320,512]{1,0:T(8,128)(2,1)S(1)}, u32[]{:S(2)}, u32[]{:S(2)}) collective-permute-start(bf16[320,512]{1,0:T(8,128)(2,1)} %get-tuple-element.69), channel_id=1, source_target_pairs={{0,17},{1,16},{2,19},{3,18},{4,21},{5,20},{6,23},{7,22},{8,25},{9,... | collective-permute-start | bytes 983048 | tf_op jit(solution)/shard_map/ppermute | solution.py:323
  94.8 6.7 %collective-permute-start.17 = (bf16[64,512]{1,0:T(8,128)(2,1)S(1)}, bf16[64,512]{1,0:T(8,128)(2,1)S(1)}, u32[]{:S(2)}, u32[]{:S(2)}) collective-permute-start(bf16[64,512]{1,0:T(8,128)(2,1)S(1)} %get-tuple-element.71), channel_id=1, source_target_pairs={{0,4},{1,5},{2,6},{3,7},{4,0},{5,1},{6,2},{7,3},{8,12},{9,13},{10,... | collective-permute-start | bytes 196616 | tf_op jit(solution)/shard_map/ppermute | solution.py:323
  97.2 6.1 %collective-permute-start.18 = (bf16[64,512]{1,0:T(8,128)(2,1)S(1)}, bf16[64,512]{1,0:T(8,128)(2,1)S(1)}, u32[]{:S(2)}, u32[]{:S(2)}) collective-permute-start(bf16[64,512]{1,0:T(8,128)(2,1)S(1)} %get-tuple-element.72), channel_id=1, source_target_pairs={{0,6},{1,7},{2,4},{3,5},{4,2},{5,3},{6,0},{7,1},{8,14},{9,15},{10,... | collective-permute-start | bytes 196616 | tf_op jit(solution)/shard_map/ppermute | solution.py:323
  106.6 5.5 %collective-permute-start.19 = (bf16[80,512]{1,0:T(8,128)(2,1)S(1)}, bf16[80,512]{1,0:T(8,128)(2,1)S(1)}, u32[]{:S(2)}, u32[]{:S(2)}) collective-permute-start(bf16[80,512]{1,0:T(8,128)(2,1)S(1)} %get-tuple-element.78), channel_id=1, source_target_pairs={{0,2},{1,3},{2,0},{3,1},{4,6},{5,7},{6,4},{7,5},{8,10},{9,11},{10,... | collective-permute-start | bytes 245768 | tf_op jit(solution)/shard_map/ppermute | solution.py:323
  107.5 5.4 %collective-permute-start.20 = (bf16[80,512]{1,0:T(8,128)(2,1)S(1)}, bf16[80,512]{1,0:T(8,128)(2,1)S(1)}, u32[]{:S(2)}, u32[]{:S(2)}) collective-permute-start(bf16[80,512]{1,0:T(8,128)(2,1)S(1)} %get-tuple-element.79), channel_id=1, source_target_pairs={{0,4},{1,5},{2,6},{3,7},{4,0},{5,1},{6,2},{7,3},{8,12},{9,13},{10,... | collective-permute-start | bytes 245768 | tf_op jit(solution)/shard_map/ppermute | solution.py:323
  110.1 7.1 %collective-permute-start.21 = (bf16[80,512]{1,0:T(8,128)(2,1)S(1)}, bf16[80,512]{1,0:T(8,128)(2,1)S(1)}, u32[]{:S(2)}, u32[]{:S(2)}) collective-permute-start(bf16[80,512]{1,0:T(8,128)(2,1)S(1)} %get-tuple-element.80), channel_id=1, source_target_pairs={{0,6},{1,7},{2,4},{3,5},{4,2},{5,3},{6,0},{7,1},{8,14},{9,15},{10,... | collective-permute-start | bytes 245768 | tf_op jit(solution)/shard_map/ppermute | solution.py:323
  122.3 15.8 %collective-permute-start.23 = (bf16[256,512]{1,0:T(8,128)(2,1)S(1)}, bf16[256,512]{1,0:T(8,128)(2,1)S(1)}, u32[]{:S(2)}, u32[]{:S(2)}) collective-permute-start(bf16[256,512]{1,0:T(8,128)(2,1)S(1)} %shard_map.137.refs_1_), channel_id=1, source_target_pairs={{0,1},{1,0},{2,3},{3,2},{4,5},{5,4},{6,7},{7,6},{8,9},{9,8},{10,11... | collective-permute-start | bytes 786440 | tf_op jit(solution)/shard_map/ppermute | solution.py:323
  123.5 14.6 %collective-permute-start.24 = (bf16[256,512]{1,0:T(8,128)(2,1)S(1)}, bf16[256,512]{1,0:T(8,128)(2,1)S(1)}, u32[]{:S(2)}, u32[]{:S(2)}) collective-permute-start(bf16[256,512]{1,0:T(8,128)(2,1)S(1)} %shard_map.137.refs_1_), channel_id=1, source_target_pairs={{0,16},{1,17},{2,18},{3,19},{4,20},{5,21},{6,22},{7,23},{8,24},{9,... | collective-permute-start | bytes 786440 | tf_op jit(solution)/shard_map/ppermute | solution.py:323
  124.7 13.4 %collective-permute-start.25 = (bf16[256,512]{1,0:T(8,128)(2,1)S(1)}, bf16[256,512]{1,0:T(8,128)(2,1)S(1)}, u32[]{:S(2)}, u32[]{:S(2)}) collective-permute-start(bf16[256,512]{1,0:T(8,128)(2,1)S(1)} %shard_map.137.refs_1_), channel_id=1, source_target_pairs={{0,17},{1,16},{2,19},{3,18},{4,21},{5,20},{6,23},{7,22},{8,25},{9,... | collective-permute-start | bytes 786440 | tf_op jit(solution)/shard_map/ppermute | solution.py:323
  125.9 12.2 %collective-permute-start.26 = (bf16[128,512]{1,0:T(8,128)(2,1)S(1)}, bf16[128,512]{1,0:T(8,128)(2,1)S(1)}, u32[]{:S(2)}, u32[]{:S(2)}) collective-permute-start(bf16[128,512]{1,0:T(8,128)(2,1)S(1)} %get-tuple-element.82.refs_1_), channel_id=1, source_target_pairs={{0,4},{1,5},{2,6},{3,7},{4,0},{5,1},{6,2},{7,3},{8,12},{9,13},{10,... | collective-permute-start | bytes 393224 | tf_op jit(solution)/shard_map/ppermute | solution.py:323
  129.5 8.6 %collective-permute-start.27 = (bf16[128,512]{1,0:T(8,128)(2,1)S(1)}, bf16[128,512]{1,0:T(8,128)(2,1)S(1)}, u32[]{:S(2)}, u32[]{:S(2)}) collective-permute-start(bf16[128,512]{1,0:T(8,128)(2,1)S(1)} %get-tuple-element.82.refs_1_), channel_id=1, source_target_pairs={{0,6},{1,7},{2,4},{3,5},{4,2},{5,3},{6,0},{7,1},{8,14},{9,15},{10,... | collective-permute-start | bytes 393224 | tf_op jit(solution)/shard_map/ppermute | solution.py:323
  138.1 6.4 %collective-permute-start.28 = (bf16[256,512]{1,0:T(8,128)(2,1)S(1)}, bf16[256,512]{1,0:T(8,128)(2,1)S(1)}, u32[]{:S(2)}, u32[]{:S(2)}) collective-permute-start(bf16[256,512]{1,0:T(8,128)(2,1)S(1)} %shard_map.138.refs_5_), channel_id=1, source_target_pairs={{0,1},{1,0},{2,3},{3,2},{4,5},{5,4},{6,7},{7,6},{8,9},{9,8},{10,11... | collective-permute-start | bytes 786440 | tf_op jit(solution)/shard_map/ppermute | solution.py:323
  138.7 18.1 %collective-permute-start.31 = (bf16[256,512]{1,0:T(8,128)(2,1)S(1)}, bf16[256,512]{1,0:T(8,128)(2,1)S(1)}, u32[]{:S(2)}, u32[]{:S(2)}) collective-permute-start(bf16[256,512]{1,0:T(8,128)(2,1)S(1)} %shard_map.137.refs_1_), channel_id=1, source_target_pairs={{0,8},{1,9},{2,10},{3,11},{4,12},{5,13},{6,14},{7,15},{8,0},{9,1},... | collective-permute-start | bytes 786440 | tf_op jit(solution)/shard_map/ppermute | solution.py:323
  138.7 17.4 %collective-permute-start.29 = (bf16[256,512]{1,0:T(8,128)(2,1)S(1)}, bf16[256,512]{1,0:T(8,128)(2,1)}, u32[]{:S(2)}, u32[]{:S(2)}) collective-permute-start(bf16[256,512]{1,0:T(8,128)(2,1)S(1)} %shard_map.138.refs_5_), channel_id=1, source_target_pairs={{0,16},{1,17},{2,18},{3,19},{4,20},{5,21},{6,22},{7,23},{8,24},{9,... | collective-permute-start | bytes 786440 | tf_op jit(solution)/shard_map/ppermute | solution.py:323
  139.7 16.9 %collective-permute-start.30 = (bf16[256,512]{1,0:T(8,128)(2,1)S(1)}, bf16[256,512]{1,0:T(8,128)(2,1)}, u32[]{:S(2)}, u32[]{:S(2)}) collective-permute-start(bf16[256,512]{1,0:T(8,128)(2,1)S(1)} %shard_map.138.refs_5_), channel_id=1, source_target_pairs={{0,17},{1,16},{2,19},{3,18},{4,21},{5,20},{6,23},{7,22},{8,25},{9,... | collective-permute-start | bytes 786440 | tf_op jit(solution)/shard_map/ppermute | solution.py:323
  141.7 15.5 %collective-permute-start.32 = (bf16[256,512]{1,0:T(8,128)(2,1)S(1)}, bf16[256,512]{1,0:T(8,128)(2,1)}, u32[]{:S(2)}, u32[]{:S(2)}) collective-permute-start(bf16[256,512]{1,0:T(8,128)(2,1)S(1)} %collective-permute-done.23.refs_2_), channel_id=1, source_target_pairs={{0,8},{1,9},{2,10},{3,11},{4,12},{5,13},{6,14},{7,15},{8,0},{9,1},... | collective-permute-start | bytes 786440 | tf_op jit(solution)/shard_map/ppermute | solution.py:323
  144.6 12.7 %collective-permute-start.33 = (bf16[256,512]{1,0:T(8,128)(2,1)S(1)}, bf16[256,512]{1,0:T(8,128)(2,1)}, u32[]{:S(2)}, u32[]{:S(2)}) collective-permute-start(bf16[256,512]{1,0:T(8,128)(2,1)S(1)} %collective-permute-done.24.refs_3_), channel_id=1, source_target_pairs={{0,8},{1,9},{2,10},{3,11},{4,12},{5,13},{6,14},{7,15},{8,0},{9,1},... | collective-permute-start | bytes 786440 | tf_op jit(solution)/shard_map/ppermute | solution.py:323
  (50 other events, 715.6 us)

commit v4 on v3

--- a/solution.py
+++ b/solution.py
@@ -66,7 +66,7 @@
         + list(scratch)
         + [pltpu.SemaphoreType.DMA((n_in,)), pltpu.SemaphoreType.DMA((n_out,))],
         compiler_params=pltpu.CompilerParams(vmem_limit_bytes=limit or held + (8 << 20)),
-        cost_estimate=pl.CostEstimate(flops=flops, bytes_accessed=held, transcendentals=0),
+        cost_estimate=pl.CostEstimate(flops=0, bytes_accessed=0, transcendentals=0),
     )(scalars, *ins)
 
 
@@ -85,7 +85,7 @@
         out_specs=[VMEM] * n_out,
         scratch_shapes=list(scratch),
         compiler_params=pltpu.CompilerParams(vmem_limit_bytes=held + (8 << 20)),
-        cost_estimate=pl.CostEstimate(flops=flops, bytes_accessed=held, transcendentals=0),
+        cost_estimate=pl.CostEstimate(flops=0, bytes_accessed=0, transcendentals=0),
     )(scalars, *ins)
 
 
@@ -220,15 +220,13 @@
             outs[k][rows:, :] = jnp.concatenate([first[span], second[span]], 0).astype(BF16)
 
 
-def last_body(n_got, scalars, ins, outs):
-    own, hub_back = outs
-    rows = ins[0].shape[0]
-    value, _, _ = add_up(ins[0], None, ins[3 : 3 + n_got])
-    own[:rows, :] = value.astype(BF16)
-    value, first, second = add_up(ins[1], ins[2], ins[3 + n_got :])
-    own[rows:, :] = value.astype(BF16)
-    hub_back[0] = first
-    hub_back[1] = second
+def last_body(with_hubs, scalars, ins, outs):
+    hubs = ins[1] if with_hubs else None
+    value, first, second = add_up(ins[0], hubs, ins[1 + int(with_hubs) :])
+    outs[0][...] = value.astype(BF16)
+    if with_hubs:
+        outs[1][0] = first
+        outs[1][1] = second
 
 
 def join_body(scalars, ins, outs):
@@ -263,19 +261,15 @@
     emit(0)
 
 
-def place_body(n_xy, n_z, n_share, where, ins, outs):
+def place_body(n_xy, n_z, where, ins, outs):
     half = ins[0].shape[1]
-    n_piece = n_z // n_share
-    rows = ins[0].shape[0] // n_piece // 2
+    rows = ins[0].shape[0] // n_z
     for i, block in enumerate(ins):
-        core, share, k = i // (n_share * n_xy), i // n_xy % n_share, i % n_xy
+        core, k = divmod(i, n_xy)
         cols = pl.ds(pl.multiple_of((where[0] ^ core) * half, half), half)
-        for j in range(n_piece):
-            z = where[2] ^ (share * n_piece + j)
-            at = pl.ds(pl.multiple_of(((where[1] ^ k) * n_z + z) * rows, rows), rows)
-            for grad in range(2):
-                first = (2 * j + grad) * rows
-                outs[grad][at, cols] = block[first : first + rows, :]
+        for j in range(n_z):
+            at = pl.ds(pl.multiple_of(((where[1] ^ k) * n_z + (where[2] ^ j)) * rows, rows), rows)
+            outs[0][at, cols] = block[j * rows : (j + 1) * rows, :]
 
 
 def on_device(
@@ -426,32 +420,41 @@
     agg_pair = in_order([agg_t, peer_agg_t], self_xy)
     neigh_xy = start_sum(*agg_pair, [hub_keep, hub_got])
     neigh_got = across(neigh_xy[1:n_xy], xy_bits)
+    self_got = in_order(self_got, neigh_xy)
     self_z = fold(self_xy[0], [], self_got)
     self_got = across(self_z[1:], z_bits)
     neigh_got = in_order(neigh_got, self_got)
     neigh_z = fold(neigh_xy[0], [neigh_xy[n_xy]], neigh_got)
     neigh_got = across(neigh_z[1:n_z], z_bits)
-    own, hub_back = run_inside(
-        functools.partial(last_body, n_z - 1),
-        z_me[None],
-        [self_z[0], neigh_z[0], neigh_z[n_z]] + self_got + neigh_got,
-        [((2 * z_rows, half), BF16), ((2, hub_z, half), F32)],
-    )
-
-    line = [own] + across([own] * (n_z - 1), z_bits)
-    n_share = 2
-    n_piece = n_z // n_share
-    got = []
-    for share in range(n_share):
-        (piece,) = run_inside(
-            join_body,
+
+    def finish(keep, hub_in, got):
+        return run_inside(
+            functools.partial(last_body, bool(hub_in)),
             z_me[None],
-            line[share * n_piece : (share + 1) * n_piece],
-            [((n_piece * 2 * z_rows, half), BF16)],
+            [keep] + hub_in + got,
+            [((z_rows, half), BF16)] + ([((2, hub_z, half), F32)] if hub_in else []),
         )
-        if share > 0:
-            (piece,) = in_order([piece], got[-1])
-        got.append([piece] + across([piece] * (n_xy - 1), xy_bits))
+
+    def gather_line(own):
+        pieces = [own] + across([own] * (n_z - 1), z_bits)
+        return run_inside(join_body, z_me[None], pieces, [((xy_rows, half), BF16)])[0]
+
+    def place(blocks):
+        return run_inside(
+            functools.partial(place_body, n_xy, n_z),
+            jnp.stack([side, xy_me, z_me]),
+            blocks + [swap(one, core) for one in blocks],
+            [((width, width), BF16)],
+        )[0]
+
+    (self_own,) = finish(self_z[0], [], self_got)
+    neigh_own, hub_back = finish(neigh_z[0], [neigh_z[n_z]], neigh_got)
+    self_line = gather_line(self_own)
+    self_blocks = [self_line] + across([self_line] * (n_xy - 1), xy_bits)
+    neigh_line = gather_line(neigh_own)
+    (neigh_line,) = in_order([neigh_line], self_blocks)
+    neigh_blocks = [neigh_line] + across([neigh_line] * (n_xy - 1), xy_bits)
+    grad_self = place(self_blocks)
     (grad_x,) = run(
         node_body,
         side[None],
@@ -459,14 +462,7 @@
         [(wide, BF16)],
         flops=2 * n_local * width * (width + n_local + n_slots),
     )
-    got[-1] = in_order(got[-1], [grad_x])
-    blocks = [one for share in got for one in share]
-    grad_self, grad_neigh = run_inside(
-        functools.partial(place_body, n_xy, n_z, n_share),
-        jnp.stack([side, xy_me, z_me]),
-        blocks + [swap(one, core) for one in blocks],
-        [((width, width), BF16)] * 2,
-    )
+    grad_neigh = place(in_order(neigh_blocks, [grad_x, grad_self]))
     return hidden, grad_x, grad_self, grad_neigh
 
 

time: 165 us -> 154 us (0.933)
  local copies, waits for them, and re-layouts: 14.3 us -> 7.47 us
    unnamed x88 -> x42, local copies, waits for them, and re-layouts: 11.9 us -> 6.51 us
    all_to_all x1, starting transfers between devices: 6.63 us -> 4.7 us  [on_device(): lax.all_to_all(d_arrived.reshape(n_dev, capacity, width), AXES, split_axi...]
    ppermute x39 -> x42, waiting for transfers between devices: 44 us -> 42.1 us  [swap(): return lax.ppermute(value, AXES, [(i, i ^ mask) for i in range(n_dev)])]
    ppermute x39 -> x42, starting transfers between devices: 42.5 us -> 43.5 us  [swap(): return lax.ppermute(value, AXES, [(i, i ^ mask) for i in range(n_dev)])]
    pallas_call x8 -> x10, Pallas kernels: 12 us -> 12.2 us  [run_inside(): pl.pallas_call(kernel, out_shape=outs, in_specs=[SMEM] + [VMEM] * n_in, o...]
  transfers between devices with their start and end apart: 41 -> 44, of which waited for: 19 -> 18; matrix products, arithmetic and copies ran while one was open for 15% -> 12% of each run, Pallas kernels for 14% -> 16%
where the time goes in v4:
time: 154 us; the launch traced here: 153 us
  starting transfers between devices  54.4 us (35%)
  waiting for transfers between devices  43.5 us (28%)
  Pallas kernels  29.6 us (19%)
  other arithmetic  10.3 us (7%)
  local copies, waits for them, and re-layouts  7.47 us (5%)
  matrix products  6.73 us (4%)
    ppermute x42, starting transfers between devices, swap(): return lax.ppermute(value, AXES, [(i, i ^ mask) for i in range(n_dev)])  43.5 us
    ppermute x42, waiting for transfers between devices, swap(): return lax.ppermute(value, AXES, [(i, i ^ mask) for i in range(n_dev)])  42.1 us
    pallas_call x3, Pallas kernels, run(): pl.pallas_call(kernel, out_shape=outs, in_specs=[SMEM] + [HBM] * n_in, ou...  17.5 us
    pallas_call x10, Pallas kernels, run_inside(): pl.pallas_call(kernel, out_shape=outs, in_specs=[SMEM] + [VMEM] * n_in, o...  12.2 us
    convert_element_type x3, other arithmetic, count(): return (found.astype(BF16), found_t.astype(BF16))  9.92 us
    dot_general x2, matrix products, mul(): return jnp.dot(left, right, preferred_element_type=F32)  6.73 us
    unnamed x42, local copies, waits for them, and re-layouts  6.51 us
    all_to_all x1, starting transfers between devices, on_device(): lax.all_to_all(outgoing.reshape(n_dev, capacity, width), AXES, split_axis...  6.19 us
  transfers between devices with their start and end apart: 44, of which 18 were waited for; matrix products, arithmetic and copies ran while one was open for 12% of the time, Pallas kernels for 16%

profile of v4, /device:TPU:0, one launch (start us, length us, event | category | flops | bytes accessed | tf_op | source)
XLA Modules:
  0.0 153.1 jit_solution(12447676515236642710)
XLA Ops:
  0.7 3.3 %shard_map.129 = (bf16[512,1024]{1,0:T(8,128)(2,1)}, bf16[8,1024]{1,0:T(8,128)(2,1)}, s32[1,512]{1,0:T(1,128)}) custom-call(s32[1]{0:T(128)} %bitcast.refs_0_, bf16[512,1024]{1,0:T(8,128)(2,1)} %refs_1_.2, s32[1,512]{1,0:T(1,128)} %refs_2_.1, s32[1,32]{1,0:T(1,128)} %refs_3_.1, s32[1,8]{1,0:T(1,128)} %bitcast.50), custom_call_target="tpu_custom_call" | custom-call | tf_op jit(solution)/shard_map/pallas_call | solution.py:60
  4.0 3.1 %collective-permute-start = (bf16[8,1024]{1,0:T(8,128)(2,1)}, bf16[8,1024]{1,0:T(8,128)(2,1)S(1)}, u32[]{:S(2)}, u32[]{:S(2)}) collective-permute-start(bf16[8,1024]{1,0:T(8,128)(2,1)} %get-tuple-element.49), channel_id=1, source_target_pairs={{0,2},{1,3},{2,0},{3,1},{4,6},{5,7},{6,4},{7,5},{8,10},{9,11},{10,... | collective-permute-start | bytes 49160 | tf_op jit(solution)/shard_map/ppermute | solution.py:317
  7.0 2.6 %collective-permute-start.1 = (bf16[8,1024]{1,0:T(8,128)(2,1)}, bf16[8,1024]{1,0:T(8,128)(2,1)S(1)}, u32[]{:S(2)}, u32[]{:S(2)}) collective-permute-start(bf16[8,1024]{1,0:T(8,128)(2,1)} %get-tuple-element.49), channel_id=1, source_target_pairs={{0,4},{1,5},{2,6},{3,7},{4,0},{5,1},{6,2},{7,3},{8,12},{9,13},{10,... | collective-permute-start | bytes 49160 | tf_op jit(solution)/shard_map/ppermute | solution.py:317
  9.6 6.2 %all-to-all-start = ((bf16[32,16,1024]{2,1,0:T(8,128)(2,1)}), bf16[32,16,1024]{2,1,0:T(8,128)(2,1)}, u32[]{:S(2)}, u32[]{:S(2)}) async-start(bf16[32,16,1024]{2,1,0:T(8,128)(2,1)} %bitcast.53), calls=%async_computation | async-start | bytes 2097152 | tf_op jit(solution)/shard_map/all_to_all | solution.py:330
  17.0 4.5 %add_convert_fusion.1.refs_1_ = bf16[512,768]{1,0:T(8,128)(2,1)} fusion(s32[768]{0:T(1024)S(1)} %iota_add_fusion, s32[512]{0:T(512)S(1)} %bitcast.88, s32[512]{0:T(512)S(1)} %bitcast.90, s32[512]{0:T(512)S(1)} %bitcast.92, s32[512]{0:T(512)S(1)} %bitcast.94, s32[512]{0:T(512)S(1)} %bitcast.96, s32[512]{0:T(512)S(1)} %bitcast.98, s32[512]{0:T(512)S(1)} %bitcast.100, ...), kind=kLoop, calls=%fused_computation.1 | loop fusion | flops 18874368 | bytes 822272 | tf_op jit(solution)/shard_map/convert_element_type | solution.py:351
  21.5 3.4 %add_convert_fusion.refs_9_ = bf16[768,512]{1,0:T(8,128)(2,1)} fusion(s32[512]{0:T(512)S(1)} %bitcast.56, s32[512]{0:T(512)S(1)} %bitcast.58, s32[512]{0:T(512)S(1)} %bitcast.60, s32[512]{0:T(512)S(1)} %bitcast.62, s32[512]{0:T(512)S(1)} %bitcast.64, s32[512]{0:T(512)S(1)} %bitcast.66, s32[512]{0:T(512)S(1)} %bitcast.68, s32[512]{0:T(512)S(1)} %bitcast.70, ...), kind=kLoop, calls=%fused_computation | loop fusion | flops 18874368 | bytes 822272 | tf_op jit(solution)/shard_map/convert_element_type | solution.py:351
  25.0 1.7 %collective-permute-start.3 = (bf16[32,1024]{1,0:T(8,128)(2,1)S(1)}, bf16[32,1024]{1,0:T(8,128)(2,1)S(1)}, u32[]{:S(2)}, u32[]{:S(2)}) collective-permute-start(bf16[32,1024]{1,0:T(8,128)(2,1)S(1)} %pad_maximum_fusion), channel_id=1, source_target_pairs={{0,1},{1,0},{2,3},{3,2},{4,5},{5,4},{6,7},{7,6},{8,9},{9,8},{10,11... | collective-permute-start | bytes 196616 | tf_op jit(solution)/shard_map/ppermute | solution.py:317
  26.7 5.2 %collective-permute-done.3 = bf16[32,1024]{1,0:T(8,128)(2,1)S(1)} collective-permute-done((bf16[32,1024]{1,0:T(8,128)(2,1)S(1)}, bf16[32,1024]{1,0:T(8,128)(2,1)S(1)}, u32[]{:S(2)}, u32[]{:S(2)}) %collective-permute-start.3) | collective-permute-done | bytes 65568 | tf_op jit(solution)/shard_map/ppermute | solution.py:317
  32.5 4.2 %fusion.refs_4_ = f32[512,1024]{1,0:T(8,128)} fusion(bf16[512,1024]{1,0:T(8,128)(2,1)S(1)} %copy-done.11, s32[512]{0:T(512)S(1)} %bitcast.89, s32[512]{0:T(512)S(1)} %bitcast.91, s32[512]{0:T(512)S(1)} %bitcast.93, s32[512]{0:T(512)S(1)} %bitcast.95, s32[512]{0:T(512)S(1)} %bitcast.97, s32[512]{0:T(512)S(1)} %bitcast.99, s32[512]{0:T(512)S(1)} %bitcast.101, ...), kind=kOutput, calls=%fused_computation.37 | convolution fusion | flops 549453824 | bytes 3178496 | tf_op jit(solution)/shard_map/dot_general | solution.py:21
  36.7 1.7 %collective-permute-done.4 = bf16[64,1024]{1,0:T(8,128)(2,1)S(1)} collective-permute-done((bf16[64,1024]{1,0:T(8,128)(2,1)S(1)}, bf16[64,1024]{1,0:T(8,128)(2,1)S(1)}, u32[]{:S(2)}, u32[]{:S(2)}) %collective-permute-start.4) | collective-permute-done | bytes 131104 | tf_op jit(solution)/shard_map/ppermute | solution.py:317
  38.6 2.6 %convolution_add_fusion.refs_7_ = f32[512,1024]{1,0:T(8,128)} fusion(bf16[512,1024]{1,0:T(8,128)(2,1)S(1)} %copy-done.11, bf16[1024,1024]{1,0:T(8,128)(2,1)S(1)} %copy-done.1, f32[1024]{0:T(1024)S(1)} %copy-done.17), kind=kOutput, calls=%fused_computation.2 | convolution fusion | flops 1074266112 | bytes 5246976 | tf_op jit(solution)/shard_map/dot_general | solution.py:21
  43.4 9.8 %shard_map.130 = (bf16[512,1024]{1,0:T(8,128)(2,1)}, bf16[512,512]{1,0:T(8,128)(2,1)}, bf16[512,1024]{1,0:T(8,128)(2,1)}, bf16[512,512]{1,0:T(8,128)(2,1)}, bf16...) custom-call(s32[1]{0:T(128)} %bitcast.refs_0_, ...), custom_call_target="tpu_custom_call" | custom-call | tf_op jit(solution)/shard_map/pallas_call | solution.py:60
  53.3 4.7 %all-to-all-start.1 = ((bf16[32,16,1024]{2,1,0:T(8,128)(2,1)}), bf16[32,16,1024]{2,1,0:T(8,128)(2,1)S(1)}, u32[]{:S(2)}, u32[]{:S(2)}) async-start(bf16[32,16,1024]{2,1,0:T(8,128)(2,1)} %bitcast.52), calls=%async_computation.1 | async-start | bytes 2097152 | tf_op jit(solution)/shard_map/all_to_all | solution.py:377
  60.2 3.4 %shard_map.131 = (f32[256,512]{1,0:T(8,128)S(1)}, bf16[256,512]{1,0:T(8,128)(2,1)}, bf16[256,512]{1,0:T(8,128)(2,1)}, bf16[256,512]{1,0:T(8,128)(2,1)}) custom-call(s32[1]{0:T(128)} %bitcast.41.refs_0_, bf16[1024,512]{1,0:T(8,128)(2,1)S(1)} %bitcast.48, bf16[1024,512]{1,0:T(8,128)(2,1)} %collective-permute-done.7.refs_2_, bf16[512,512]{1,0:T(8,128)(2,1)S(1)} %copy-done, ...), custom_call_target="tpu_custom_call" | custom-call | tf_op jit(solution)/shard_map/pallas_call | solution.py:81
  70.2 2.7 %shard_map.132 = (f32[256,512]{1,0:T(8,128)S(1)}, bf16[320,512]{1,0:T(8,128)(2,1)S(1)}, bf16[320,512]{1,0:T(8,128)(2,1)S(1)}, bf16[320,512]{1,0:T(8,128)(2,1)S(1)}, f32[2,32,512]{2,1,0:T(8,128)S(1)}) custom-call(s32[1]{0:T(128)} %bitcast.41.refs_0_, bf16[1024,512]{1,0:T(8,128)(2,1)S(1)} %copy-done.4, bf16[1024,512]{1,0:T(8,128)(2,1)} %collective-permute-done.6.refs_2_, ...), custom_call_target="tpu_custom_call" | custom-call | tf_op jit(solution)/shard_map/pallas_call | solution.py:81
  72.9 7.2 %collective-permute-done.13.refs_2_ = bf16[256,512]{1,0:T(8,128)(2,1)S(1)} collective-permute-done((bf16[256,512]{1,0:T(8,128)(2,1)}, bf16[256,512]{1,0:T(8,128)(2,1)S(1)}, u32[]{:S(2)}, u32[]{:S(2)}) %collective-permute-start.13) | collective-permute-done | bytes 262176 | tf_op jit(solution)/shard_map/ppermute | solution.py:317
  80.1 4.8 %collective-permute-done.15.refs_4_ = bf16[256,512]{1,0:T(8,128)(2,1)} collective-permute-done((bf16[256,512]{1,0:T(8,128)(2,1)}, bf16[256,512]{1,0:T(8,128)(2,1)}, u32[]{:S(2)}, u32[]{:S(2)}) %collective-permute-start.15) | collective-permute-done | bytes 262176 | tf_op jit(solution)/shard_map/ppermute | solution.py:317
  86.1 3.8 %collective-permute-start.16 = (bf16[64,512]{1,0:T(8,128)(2,1)S(1)}, bf16[64,512]{1,0:T(8,128)(2,1)S(1)}, u32[]{:S(2)}, u32[]{:S(2)}) collective-permute-start(bf16[64,512]{1,0:T(8,128)(2,1)S(1)} %get-tuple-element.73), channel_id=1, source_target_pairs={{0,2},{1,3},{2,0},{3,1},{4,6},{5,7},{6,4},{7,5},{8,10},{9,11},{10,... | collective-permute-start | bytes 196616 | tf_op jit(solution)/shard_map/ppermute | solution.py:317
  90.5 1.9 %collective-permute-start.18 = (bf16[64,512]{1,0:T(8,128)(2,1)S(1)}, bf16[64,512]{1,0:T(8,128)(2,1)S(1)}, u32[]{:S(2)}, u32[]{:S(2)}) collective-permute-start(bf16[64,512]{1,0:T(8,128)(2,1)S(1)} %get-tuple-element.75), channel_id=1, source_target_pairs={{0,6},{1,7},{2,4},{3,5},{4,2},{5,3},{6,0},{7,1},{8,14},{9,15},{10,... | collective-permute-start | bytes 196616 | tf_op jit(solution)/shard_map/ppermute | solution.py:317
  99.6 2.3 %collective-permute-done.22.refs_2_ = bf16[64,512]{1,0:T(8,128)(2,1)S(1)} collective-permute-done((bf16[64,512]{1,0:T(8,128)(2,1)S(1)}, bf16[64,512]{1,0:T(8,128)(2,1)S(1)}, u32[]{:S(2)}, u32[]{:S(2)}) %collective-permute-start.22) | collective-permute-done | bytes 65568 | tf_op jit(solution)/shard_map/ppermute | solution.py:317
  101.9 2.0 %collective-permute-start.24 = (bf16[64,512]{1,0:T(8,128)(2,1)S(1)}, bf16[64,512]{1,0:T(8,128)(2,1)S(1)}, u32[]{:S(2)}, u32[]{:S(2)}) collective-permute-start(bf16[64,512]{1,0:T(8,128)(2,1)S(1)} %shard_map.137.refs_1_), channel_id=1, source_target_pairs={{0,6},{1,7},{2,4},{3,5},{4,2},{5,3},{6,0},{7,1},{8,14},{9,15},{10,... | collective-permute-start | bytes 196616 | tf_op jit(solution)/shard_map/ppermute | solution.py:317
  103.9 1.9 %collective-permute-done.23.refs_3_ = bf16[64,512]{1,0:T(8,128)(2,1)S(1)} collective-permute-done((bf16[64,512]{1,0:T(8,128)(2,1)S(1)}, bf16[64,512]{1,0:T(8,128)(2,1)S(1)}, u32[]{:S(2)}, u32[]{:S(2)}) %collective-permute-start.23) | collective-permute-done | bytes 65568 | tf_op jit(solution)/shard_map/ppermute | solution.py:317
  105.8 2.1 %collective-permute-done.24.refs_4_ = bf16[64,512]{1,0:T(8,128)(2,1)S(1)} collective-permute-done((bf16[64,512]{1,0:T(8,128)(2,1)S(1)}, bf16[64,512]{1,0:T(8,128)(2,1)S(1)}, u32[]{:S(2)}, u32[]{:S(2)}) %collective-permute-start.24) | collective-permute-done | bytes 65568 | tf_op jit(solution)/shard_map/ppermute | solution.py:317
  111.8 2.6 %collective-permute-start.20 = (bf16[80,512]{1,0:T(8,128)(2,1)S(1)}, bf16[80,512]{1,0:T(8,128)(2,1)S(1)}, u32[]{:S(2)}, u32[]{:S(2)}) collective-permute-start(bf16[80,512]{1,0:T(8,128)(2,1)S(1)} %get-tuple-element.82), channel_id=1, source_target_pairs={{0,4},{1,5},{2,6},{3,7},{4,0},{5,1},{6,2},{7,3},{8,12},{9,13},{10,... | collective-permute-start | bytes 245768 | tf_op jit(solution)/shard_map/ppermute | solution.py:317
  114.4 3.3 %collective-permute-done.25.refs_2_ = bf16[256,512]{1,0:T(8,128)(2,1)S(1)} collective-permute-done((bf16[256,512]{1,0:T(8,128)(2,1)S(1)}, bf16[256,512]{1,0:T(8,128)(2,1)S(1)}, u32[]{:S(2)}, u32[]{:S(2)}) %collective-permute-start.25) | collective-permute-done | bytes 262176 | tf_op jit(solution)/shard_map/ppermute | solution.py:317
  119.5 4.9 %collective-permute-done.21.refs_5_ = bf16[80,512]{1,0:T(8,128)(2,1)S(1)} collective-permute-done((bf16[80,512]{1,0:T(8,128)(2,1)S(1)}, bf16[80,512]{1,0:T(8,128)(2,1)S(1)}, u32[]{:S(2)}, u32[]{:S(2)}) %collective-permute-start.21) | collective-permute-done | bytes 81952 | tf_op jit(solution)/shard_map/ppermute | solution.py:317
  126.6 2.4 %collective-permute-start.34 = (bf16[64,512]{1,0:T(8,128)(2,1)S(1)}, bf16[64,512]{1,0:T(8,128)(2,1)S(1)}, u32[]{:S(2)}, u32[]{:S(2)}) collective-permute-start(bf16[64,512]{1,0:T(8,128)(2,1)S(1)} %get-tuple-element.86.refs_1_), channel_id=1, source_target_pairs={{0,6},{1,7},{2,4},{3,5},{4,2},{5,3},{6,0},{7,1},{8,14},{9,15},{10,... | collective-permute-start | bytes 196616 | tf_op jit(solution)/shard_map/ppermute | solution.py:317
  129.1 2.6 %collective-permute-done.33.refs_3_ = bf16[64,512]{1,0:T(8,128)(2,1)S(1)} collective-permute-done((bf16[64,512]{1,0:T(8,128)(2,1)S(1)}, bf16[64,512]{1,0:T(8,128)(2,1)S(1)}, u32[]{:S(2)}, u32[]{:S(2)}) %collective-permute-start.33) | collective-permute-done | bytes 65568 | tf_op jit(solution)/shard_map/ppermute | solution.py:317
  136.3 2.0 %add_convert_fusion.2.refs_4_ = bf16[512,512]{1,0:T(8,128)(2,1)S(1)} fusion(s32[512]{0:T(512)S(1)} %bitcast.57, s32[512]{0:T(512)S(1)} %bitcast.59, s32[512]{0:T(512)S(1)} %bitcast.61, s32[512]{0:T(512)S(1)} %bitcast.63, s32[512]{0:T(512)S(1)} %bitcast.65, s32[512]{0:T(512)S(1)} %bitcast.67, s32[512]{0:T(512)S(1)} %bitcast.69, s32[512]{0:T(512)S(1)} %bitcast.71, ...), kind=kLoop, calls=%fused_computation.3 | loop fusion | flops 12582912 | bytes 557056 | tf_op jit(solution)/shard_map/convert_element_type | solution.py:351
  138.4 2.0 %shard_map.139 = bf16[1024,1024]{1,0:T(8,128)(2,1)} custom-call(s32[3]{0:T(128)S(1)} %pad_add_fusion.refs_0_, bf16[256,512]{1,0:T(8,128)(2,1)S(1)} %shard_map.138.refs_1_, bf16[256,512]{1,0:T(8,128)(2,1)S(1)} %collective-permute-done.25.refs_2_, bf16[256,512]{1,0:T(8,128)(2,1)S(1)} %collective-permute-done.26.refs_3_, ...), custom_call_target="tpu_custom_call" | custom-call | tf_op jit(solution)/shard_map/pallas_call | solution.py:81
  143.3 4.4 %shard_map.136 = bf16[512,1024]{1,0:T(8,128)(2,1)} custom-call(s32[1]{0:T(128)} %bitcast.refs_0_, bf16[1024,1024]{1,0:T(8,128)(2,1)S(1)} %copy-done.2, bf16[512,512]{1,0:T(8,128)(2,1)S(1)} %copy-done, bf16[512,512]{1,0:T(8,128)(2,1)S(1)} %copy-done.8, bf16[512,512]{1,0:T(8,128)(2,1)S(1)} %add_convert_fusion.2.refs_4_, bf16[512,1024]{1,0:T(8,128)(2,1)S(1)} %copy-done.3, ...), custom_call_target="tpu_custom_call" | custom-call | tf_op jit(solution)/shard_map/pallas_call | solution.py:60
  150.7 2.4 %shard_map.141 = bf16[1024,1024]{1,0:T(8,128)(2,1)} custom-call(s32[3]{0:T(128)S(1)} %pad_add_fusion.refs_0_, bf16[256,512]{1,0:T(8,128)(2,1)S(1)} %shard_map.140.refs_1_, bf16[256,512]{1,0:T(8,128)(2,1)S(1)} %collective-permute-done.35.refs_2_, bf16[256,512]{1,0:T(8,128)(2,1)S(1)} %collective-permute-done.36.refs_3_, ...), custom_call_target="tpu_custom_call" | custom-call | tf_op jit(solution)/shard_map/pallas_call | solution.py:81
  (127 shorter events, 40.3 us)
Async XLA Ops:
  4.0 21.0 %collective-permute-start = (bf16[8,1024]{1,0:T(8,128)(2,1)}, bf16[8,1024]{1,0:T(8,128)(2,1)S(1)}, u32[]{:S(2)}, u32[]{:S(2)}) collective-permute-start(bf16[8,1024]{1,0:T(8,128)(2,1)} %get-tuple-element.49), channel_id=1, source_target_pairs={{0,2},{1,3},{2,0},{3,1},{4,6},{5,7},{6,4},{7,5},{8,10},{9,11},{10,... | collective-permute-start | bytes 49160 | tf_op jit(solution)/shard_map/ppermute | solution.py:317
  7.0 17.9 %collective-permute-start.1 = (bf16[8,1024]{1,0:T(8,128)(2,1)}, bf16[8,1024]{1,0:T(8,128)(2,1)S(1)}, u32[]{:S(2)}, u32[]{:S(2)}) collective-permute-start(bf16[8,1024]{1,0:T(8,128)(2,1)} %get-tuple-element.49), channel_id=1, source_target_pairs={{0,4},{1,5},{2,6},{3,7},{4,0},{5,1},{6,2},{7,3},{8,12},{9,13},{10,... | collective-permute-start | bytes 49160 | tf_op jit(solution)/shard_map/ppermute | solution.py:317
  9.6 15.3 %collective-permute-start.2 = (bf16[8,1024]{1,0:T(8,128)(2,1)}, bf16[8,1024]{1,0:T(8,128)(2,1)S(1)}, u32[]{:S(2)}, u32[]{:S(2)}) collective-permute-start(bf16[8,1024]{1,0:T(8,128)(2,1)} %get-tuple-element.49), channel_id=1, source_target_pairs={{0,6},{1,7},{2,4},{3,5},{4,2},{5,3},{6,0},{7,1},{8,14},{9,15},{10,... | collective-permute-start | bytes 49160 | tf_op jit(solution)/shard_map/ppermute | solution.py:317
  9.6 33.8 %all-to-all-start = ((bf16[32,16,1024]{2,1,0:T(8,128)(2,1)}), bf16[32,16,1024]{2,1,0:T(8,128)(2,1)}, u32[]{:S(2)}, u32[]{:S(2)}) async-start(bf16[32,16,1024]{2,1,0:T(8,128)(2,1)} %bitcast.53), calls=%async_computation | async-start | bytes 2097152 | tf_op jit(solution)/shard_map/all_to_all | solution.py:330
  16.4 42.2 %collective-permute-start.7 = (bf16[1024,512]{1,0:T(8,128)(2,1)S(1)}, bf16[1024,512]{1,0:T(8,128)(2,1)}, u32[]{:S(2)}, u32[]{:S(2)}) collective-permute-start(bf16[1024,512]{1,0:T(8,128)(2,1)S(1)} %bitcast.47), channel_id=1, source_target_pairs={{0,8},{1,9},{2,10},{3,11},{4,12},{5,13},{6,14},{7,15},{8,0},{9,1},... | collective-permute-start | bytes 3145736 | tf_op jit(solution)/shard_map/ppermute | solution.py:317
  25.0 6.9 %collective-permute-start.3 = (bf16[32,1024]{1,0:T(8,128)(2,1)S(1)}, bf16[32,1024]{1,0:T(8,128)(2,1)S(1)}, u32[]{:S(2)}, u32[]{:S(2)}) collective-permute-start(bf16[32,1024]{1,0:T(8,128)(2,1)S(1)} %pad_maximum_fusion), channel_id=1, source_target_pairs={{0,1},{1,0},{2,3},{3,2},{4,5},{5,4},{6,7},{7,6},{8,9},{9,8},{10,11... | collective-permute-start | bytes 196616 | tf_op jit(solution)/shard_map/ppermute | solution.py:317
  31.9 6.5 %collective-permute-start.4 = (bf16[64,1024]{1,0:T(8,128)(2,1)S(1)}, bf16[64,1024]{1,0:T(8,128)(2,1)S(1)}, u32[]{:S(2)}, u32[]{:S(2)}) collective-permute-start(bf16[64,1024]{1,0:T(8,128)(2,1)S(1)} %get-tuple-element.96), channel_id=1, source_target_pairs={{0,16},{1,17},{2,18},{3,19},{4,20},{5,21},{6,22},{7,23},{8,24},{9,... | collective-permute-start | bytes 393224 | tf_op jit(solution)/shard_map/ppermute | solution.py:317
  53.2 14.7 %collective-permute-start.6 = (bf16[1024,512]{1,0:T(8,128)(2,1)}, bf16[1024,512]{1,0:T(8,128)(2,1)}, u32[]{:S(2)}, u32[]{:S(2)}) collective-permute-start(bf16[1024,512]{1,0:T(8,128)(2,1)} %get-tuple-element.61.refs_1_), channel_id=1, source_target_pairs={{0,8},{1,9},{2,10},{3,11},{4,12},{5,13},{6,14},{7,15},{8,0},{9,1},... | collective-permute-start | bytes 3145736 | tf_op jit(solution)/shard_map/ppermute | solution.py:317
  53.3 87.1 %all-to-all-start.1 = ((bf16[32,16,1024]{2,1,0:T(8,128)(2,1)}), bf16[32,16,1024]{2,1,0:T(8,128)(2,1)S(1)}, u32[]{:S(2)}, u32[]{:S(2)}) async-start(bf16[32,16,1024]{2,1,0:T(8,128)(2,1)} %bitcast.52), calls=%async_computation.1 | async-start | bytes 2097152 | tf_op jit(solution)/shard_map/all_to_all | solution.py:377
  58.2 9.7 %collective-permute-start.9 = (bf16[2,128,512]{2,1,0:T(8,128)(2,1)S(1)}, bf16[2,128,512]{2,1,0:T(8,128)(2,1)}, u32[]{:S(2)}, u32[]{:S(2)}) collective-permute-start(bf16[2,128,512]{2,1,0:T(8,128)(2,1)S(1)} %copy-done.16), channel_id=1, source_target_pairs={{0,8},{1,9},{2,10},{3,11},{4,12},{5,13},{6,14},{7,15},{8,0},{9,1},... | collective-permute-start | bytes 786440 | tf_op jit(solution)/shard_map/ppermute | solution.py:317
  64.4 15.7 %collective-permute-start.13 = (bf16[256,512]{1,0:T(8,128)(2,1)}, bf16[256,512]{1,0:T(8,128)(2,1)S(1)}, u32[]{:S(2)}, u32[]{:S(2)}) collective-permute-start(bf16[256,512]{1,0:T(8,128)(2,1)} %get-tuple-element.58), channel_id=1, source_target_pairs={{0,1},{1,0},{2,3},{3,2},{4,5},{5,4},{6,7},{7,6},{8,9},{9,8},{10,11... | collective-permute-start | bytes 786440 | tf_op jit(solution)/shard_map/ppermute | solution.py:317
  66.0 14.1 %collective-permute-start.14 = (bf16[256,512]{1,0:T(8,128)(2,1)}, bf16[256,512]{1,0:T(8,128)(2,1)}, u32[]{:S(2)}, u32[]{:S(2)}) collective-permute-start(bf16[256,512]{1,0:T(8,128)(2,1)} %get-tuple-element.59), channel_id=1, source_target_pairs={{0,16},{1,17},{2,18},{3,19},{4,20},{5,21},{6,22},{7,23},{8,24},{9,... | collective-permute-start | bytes 786440 | tf_op jit(solution)/shard_map/ppermute | solution.py:317
  67.5 17.4 %collective-permute-start.15 = (bf16[256,512]{1,0:T(8,128)(2,1)}, bf16[256,512]{1,0:T(8,128)(2,1)}, u32[]{:S(2)}, u32[]{:S(2)}) collective-permute-start(bf16[256,512]{1,0:T(8,128)(2,1)} %get-tuple-element.60), channel_id=1, source_target_pairs={{0,17},{1,16},{2,19},{3,18},{4,21},{5,20},{6,23},{7,22},{8,25},{9,... | collective-permute-start | bytes 786440 | tf_op jit(solution)/shard_map/ppermute | solution.py:317
  86.1 8.0 %collective-permute-start.16 = (bf16[64,512]{1,0:T(8,128)(2,1)S(1)}, bf16[64,512]{1,0:T(8,128)(2,1)S(1)}, u32[]{:S(2)}, u32[]{:S(2)}) collective-permute-start(bf16[64,512]{1,0:T(8,128)(2,1)S(1)} %get-tuple-element.73), channel_id=1, source_target_pairs={{0,2},{1,3},{2,0},{3,1},{4,6},{5,7},{6,4},{7,5},{8,10},{9,11},{10,... | collective-permute-start | bytes 196616 | tf_op jit(solution)/shard_map/ppermute | solution.py:317
  89.9 7.5 %collective-permute-start.17 = (bf16[64,512]{1,0:T(8,128)(2,1)S(1)}, bf16[64,512]{1,0:T(8,128)(2,1)S(1)}, u32[]{:S(2)}, u32[]{:S(2)}) collective-permute-start(bf16[64,512]{1,0:T(8,128)(2,1)S(1)} %get-tuple-element.74), channel_id=1, source_target_pairs={{0,4},{1,5},{2,6},{3,7},{4,0},{5,1},{6,2},{7,3},{8,12},{9,13},{10,... | collective-permute-start | bytes 196616 | tf_op jit(solution)/shard_map/ppermute | solution.py:317
  90.5 7.0 %collective-permute-start.18 = (bf16[64,512]{1,0:T(8,128)(2,1)S(1)}, bf16[64,512]{1,0:T(8,128)(2,1)S(1)}, u32[]{:S(2)}, u32[]{:S(2)}) collective-permute-start(bf16[64,512]{1,0:T(8,128)(2,1)S(1)} %get-tuple-element.75), channel_id=1, source_target_pairs={{0,6},{1,7},{2,4},{3,5},{4,2},{5,3},{6,0},{7,1},{8,14},{9,15},{10,... | collective-permute-start | bytes 196616 | tf_op jit(solution)/shard_map/ppermute | solution.py:317
  92.3 17.4 %collective-permute-start.10 = (bf16[320,512]{1,0:T(8,128)(2,1)S(1)}, bf16[320,512]{1,0:T(8,128)(2,1)S(1)}, u32[]{:S(2)}, u32[]{:S(2)}) collective-permute-start(bf16[320,512]{1,0:T(8,128)(2,1)S(1)} %get-tuple-element.67), channel_id=1, source_target_pairs={{0,1},{1,0},{2,3},{3,2},{4,5},{5,4},{6,7},{7,6},{8,9},{9,8},{10,11... | collective-permute-start | bytes 983048 | tf_op jit(solution)/shard_map/ppermute | solution.py:317
  93.0 18.5 %collective-permute-start.11 = (bf16[320,512]{1,0:T(8,128)(2,1)S(1)}, bf16[320,512]{1,0:T(8,128)(2,1)S(1)}, u32[]{:S(2)}, u32[]{:S(2)}) collective-permute-start(bf16[320,512]{1,0:T(8,128)(2,1)S(1)} %get-tuple-element.68), channel_id=1, source_target_pairs={{0,16},{1,17},{2,18},{3,19},{4,20},{5,21},{6,22},{7,23},{8,24},{9,... | collective-permute-start | bytes 983048 | tf_op jit(solution)/shard_map/ppermute | solution.py:317
  94.1 17.4 %collective-permute-start.12 = (bf16[320,512]{1,0:T(8,128)(2,1)S(1)}, bf16[320,512]{1,0:T(8,128)(2,1)S(1)}, u32[]{:S(2)}, u32[]{:S(2)}) collective-permute-start(bf16[320,512]{1,0:T(8,128)(2,1)S(1)} %get-tuple-element.69), channel_id=1, source_target_pairs={{0,17},{1,16},{2,19},{3,18},{4,21},{5,20},{6,23},{7,22},{8,25},{9,... | collective-permute-start | bytes 983048 | tf_op jit(solution)/shard_map/ppermute | solution.py:317
  98.8 7.0 %collective-permute-start.23 = (bf16[64,512]{1,0:T(8,128)(2,1)S(1)}, bf16[64,512]{1,0:T(8,128)(2,1)S(1)}, u32[]{:S(2)}, u32[]{:S(2)}) collective-permute-start(bf16[64,512]{1,0:T(8,128)(2,1)S(1)} %shard_map.137.refs_1_), channel_id=1, source_target_pairs={{0,4},{1,5},{2,6},{3,7},{4,0},{5,1},{6,2},{7,3},{8,12},{9,13},{10,... | collective-permute-start | bytes 196616 | tf_op jit(solution)/shard_map/ppermute | solution.py:317
  107.9 9.7 %collective-permute-start.25 = (bf16[256,512]{1,0:T(8,128)(2,1)S(1)}, bf16[256,512]{1,0:T(8,128)(2,1)S(1)}, u32[]{:S(2)}, u32[]{:S(2)}) collective-permute-start(bf16[256,512]{1,0:T(8,128)(2,1)S(1)} %shard_map.138.refs_1_), channel_id=1, source_target_pairs={{0,1},{1,0},{2,3},{3,2},{4,5},{5,4},{6,7},{7,6},{8,9},{9,8},{10,11... | collective-permute-start | bytes 786440 | tf_op jit(solution)/shard_map/ppermute | solution.py:317
  108.5 16.9 %collective-permute-start.26 = (bf16[256,512]{1,0:T(8,128)(2,1)S(1)}, bf16[256,512]{1,0:T(8,128)(2,1)S(1)}, u32[]{:S(2)}, u32[]{:S(2)}) collective-permute-start(bf16[256,512]{1,0:T(8,128)(2,1)S(1)} %shard_map.138.refs_1_), channel_id=1, source_target_pairs={{0,16},{1,17},{2,18},{3,19},{4,20},{5,21},{6,22},{7,23},{8,24},{9,... | collective-permute-start | bytes 786440 | tf_op jit(solution)/shard_map/ppermute | solution.py:317
  109.8 16.8 %collective-permute-start.27 = (bf16[256,512]{1,0:T(8,128)(2,1)S(1)}, bf16[256,512]{1,0:T(8,128)(2,1)S(1)}, u32[]{:S(2)}, u32[]{:S(2)}) collective-permute-start(bf16[256,512]{1,0:T(8,128)(2,1)S(1)} %shard_map.138.refs_1_), channel_id=1, source_target_pairs={{0,17},{1,16},{2,19},{3,18},{4,21},{5,20},{6,23},{7,22},{8,25},{9,... | collective-permute-start | bytes 786440 | tf_op jit(solution)/shard_map/ppermute | solution.py:317
  111.8 6.4 %collective-permute-start.20 = (bf16[80,512]{1,0:T(8,128)(2,1)S(1)}, bf16[80,512]{1,0:T(8,128)(2,1)S(1)}, u32[]{:S(2)}, u32[]{:S(2)}) collective-permute-start(bf16[80,512]{1,0:T(8,128)(2,1)S(1)} %get-tuple-element.82), channel_id=1, source_target_pairs={{0,4},{1,5},{2,6},{3,7},{4,0},{5,1},{6,2},{7,3},{8,12},{9,13},{10,... | collective-permute-start | bytes 245768 | tf_op jit(solution)/shard_map/ppermute | solution.py:317
  117.6 16.7 %collective-permute-start.28 = (bf16[256,512]{1,0:T(8,128)(2,1)S(1)}, bf16[256,512]{1,0:T(8,128)(2,1)S(1)}, u32[]{:S(2)}, u32[]{:S(2)}) collective-permute-start(bf16[256,512]{1,0:T(8,128)(2,1)S(1)} %shard_map.138.refs_1_), channel_id=1, source_target_pairs={{0,8},{1,9},{2,10},{3,11},{4,12},{5,13},{6,14},{7,15},{8,0},{9,1},... | collective-permute-start | bytes 786440 | tf_op jit(solution)/shard_map/ppermute | solution.py:317
  117.6 17.7 %collective-permute-start.29 = (bf16[256,512]{1,0:T(8,128)(2,1)S(1)}, bf16[256,512]{1,0:T(8,128)(2,1)S(1)}, u32[]{:S(2)}, u32[]{:S(2)}) collective-permute-start(bf16[256,512]{1,0:T(8,128)(2,1)S(1)} %collective-permute-done.25.refs_2_), channel_id=1, source_target_pairs={{0,8},{1,9},{2,10},{3,11},{4,12},{5,13},{6,14},{7,15},{8,0},{9,1},... | collective-permute-start | bytes 786440 | tf_op jit(solution)/shard_map/ppermute | solution.py:317
  118.2 6.3 %collective-permute-start.21 = (bf16[80,512]{1,0:T(8,128)(2,1)S(1)}, bf16[80,512]{1,0:T(8,128)(2,1)S(1)}, u32[]{:S(2)}, u32[]{:S(2)}) collective-permute-start(bf16[80,512]{1,0:T(8,128)(2,1)S(1)} %get-tuple-element.83), channel_id=1, source_target_pairs={{0,6},{1,7},{2,4},{3,5},{4,2},{5,3},{6,0},{7,1},{8,14},{9,15},{10,... | collective-permute-start | bytes 245768 | tf_op jit(solution)/shard_map/ppermute | solution.py:317
  129.1 9.3 %collective-permute-start.30 = (bf16[256,512]{1,0:T(8,128)(2,1)S(1)}, bf16[256,512]{1,0:T(8,128)(2,1)S(1)}, u32[]{:S(2)}, u32[]{:S(2)}) collective-permute-start(bf16[256,512]{1,0:T(8,128)(2,1)S(1)} %collective-permute-done.26.refs_3_), channel_id=1, source_target_pairs={{0,8},{1,9},{2,10},{3,11},{4,12},{5,13},{6,14},{7,15},{8,0},{9,1},... | collective-permute-start | bytes 786440 | tf_op jit(solution)/shard_map/ppermute | solution.py:317
  131.7 6.7 %collective-permute-start.31 = (bf16[256,512]{1,0:T(8,128)(2,1)S(1)}, bf16[256,512]{1,0:T(8,128)(2,1)S(1)}, u32[]{:S(2)}, u32[]{:S(2)}) collective-permute-start(bf16[256,512]{1,0:T(8,128)(2,1)S(1)} %collective-permute-done.27.refs_4_), channel_id=1, source_target_pairs={{0,8},{1,9},{2,10},{3,11},{4,12},{5,13},{6,14},{7,15},{8,0},{9,1},... | collective-permute-start | bytes 786440 | tf_op jit(solution)/shard_map/ppermute | solution.py:317
  132.7 14.9 %collective-permute-start.35 = (bf16[256,512]{1,0:T(8,128)(2,1)S(1)}, bf16[256,512]{1,0:T(8,128)(2,1)S(1)}, u32[]{:S(2)}, u32[]{:S(2)}) collective-permute-start(bf16[256,512]{1,0:T(8,128)(2,1)S(1)} %shard_map.140.refs_1_), channel_id=1, source_target_pairs={{0,1},{1,0},{2,3},{3,2},{4,5},{5,4},{6,7},{7,6},{8,9},{9,8},{10,11... | collective-permute-start | bytes 786440 | tf_op jit(solution)/shard_map/ppermute | solution.py:317
  134.3 13.4 %collective-permute-start.36 = (bf16[256,512]{1,0:T(8,128)(2,1)S(1)}, bf16[256,512]{1,0:T(8,128)(2,1)S(1)}, u32[]{:S(2)}, u32[]{:S(2)}) collective-permute-start(bf16[256,512]{1,0:T(8,128)(2,1)S(1)} %shard_map.140.refs_1_), channel_id=1, source_target_pairs={{0,16},{1,17},{2,18},{3,19},{4,20},{5,21},{6,22},{7,23},{8,24},{9,... | collective-permute-start | bytes 786440 | tf_op jit(solution)/shard_map/ppermute | solution.py:317
  135.4 12.4 %collective-permute-start.37 = (bf16[256,512]{1,0:T(8,128)(2,1)S(1)}, bf16[256,512]{1,0:T(8,128)(2,1)}, u32[]{:S(2)}, u32[]{:S(2)}) collective-permute-start(bf16[256,512]{1,0:T(8,128)(2,1)S(1)} %shard_map.140.refs_1_), channel_id=1, source_target_pairs={{0,17},{1,16},{2,19},{3,18},{4,21},{5,20},{6,23},{7,22},{8,25},{9,... | collective-permute-start | bytes 786440 | tf_op jit(solution)/shard_map/ppermute | solution.py:317
  (30 other events, 126.2 us)

commit v5 on v4

--- a/solution.py
+++ b/solution.py
@@ -203,30 +203,43 @@
     return value, first, second
 
 
-def fold_body(n_part, with_hubs, mine, ins, outs, total):
+def halve_body(with_hubs, at_bit, where, ins, outs, total):
     hubs = ins[1] if with_hubs else None
-    rows = outs[0].shape[0]
     value, first, second = add_up(ins[0], hubs, ins[1 + int(with_hubs) :])
     total[...] = value
+    keep, send = outs[:2]
+    rows = keep.shape[0]
+    mine = where[at_bit]
+    keep[...] = total[pl.ds(pl.multiple_of(mine * rows, rows), rows), :]
+    send[:rows, :] = total[pl.ds(pl.multiple_of((1 - mine) * rows, rows), rows), :].astype(BF16)
     if with_hubs:
-        n_hub = first.shape[0] // n_part
-        outs[n_part][0] = first[:n_hub]
-        outs[n_part][1] = second[:n_hub]
-    for k in range(n_part):
-        at = pl.ds(pl.multiple_of((mine[0] ^ k) * rows, rows), rows)
-        outs[k][:rows, :] = total[at, :].astype(outs[k].dtype)
-        if k > 0 and with_hubs:
-            span = slice(k * n_hub, (k + 1) * n_hub)
-            outs[k][rows:, :] = jnp.concatenate([first[span], second[span]], 0).astype(BF16)
-
-
-def last_body(with_hubs, scalars, ins, outs):
+        n_hub = first.shape[0] // 2
+        outs[2][0] = first[:n_hub]
+        outs[2][1] = second[:n_hub]
+        send[rows:, :] = jnp.concatenate([first[n_hub:], second[n_hub:]], 0).astype(BF16)
+
+
+def meet_body(with_hubs, where, ins, outs):
     hubs = ins[1] if with_hubs else None
     value, first, second = add_up(ins[0], hubs, ins[1 + int(with_hubs) :])
-    outs[0][...] = value.astype(BF16)
+    rows = value.shape[0]
+    outs[0][:rows, :] = value.astype(BF16)
     if with_hubs:
-        outs[1][0] = first
-        outs[1][1] = second
+        n_hub = first.shape[0] // 2
+        outs[1][0] = first[:n_hub]
+        outs[1][1] = second[:n_hub]
+        outs[0][rows:, :] = jnp.concatenate([first[n_hub:], second[n_hub:]], 0).astype(BF16)
+
+
+def close_body(with_hubs, where, ins, outs):
+    rows = outs[0].shape[0]
+    own, got = ins[0], ins[1]
+    outs[0][...] = (own[:rows, :].astype(F32) + got[:rows, :].astype(F32)).astype(BF16)
+    if with_hubs:
+        tail = got[rows:, :].astype(F32)
+        n_hub = tail.shape[0] // 2
+        outs[1][0] = ins[2][0] + tail[:n_hub]
+        outs[1][1] = ins[2][1] + tail[n_hub:]
 
 
 def join_body(scalars, ins, outs):
@@ -301,7 +314,7 @@
     core = n_col
     xy_bits = [1] + [n_col << i for i in range(1, n_row.bit_length() - 1)]
     z_bits = [1 << i for i in range(1, n_col.bit_length() - 1)]
-    hub_bits = z_bits + xy_bits + [core]
+    hub_bits = z_bits[::-1] + xy_bits + [core]
     n_xy, n_z = 1 << len(xy_bits), 1 << len(z_bits)
 
     def spread(bits, k):
@@ -316,7 +329,8 @@
     def swap(value, mask):
         return lax.ppermute(value, AXES, [(i, i ^ mask) for i in range(n_dev)])
 
-    side, xy_me, z_me = bit(core), place_of(xy_bits), place_of(z_bits)
+    side, xy_me, z_me = bit(core), place_of(xy_bits), place_of(z_bits[-2::-1])
+    z_at = jnp.stack([bit(mask) for mask in z_bits])
 
     hub_row = hub_rows.reshape(1, n_hub)
     outgoing, own_hubs, chosen = run(
@@ -331,7 +345,7 @@
         outgoing.reshape(n_dev, capacity, width), AXES, split_axis=0, concat_axis=0, tiled=True
     ).reshape(n_slots, width)
 
-    hubs = jnp.concatenate([own_hubs] + [swap(own_hubs, spread(z_bits, k)) for k in range(1, n_z)], 0)
+    hubs = jnp.concatenate([own_hubs] + [swap(own_hubs, spread(z_bits[::-1], k)) for k in range(1, n_z)], 0)
     for mask in xy_bits + [core]:
         hubs = jnp.concatenate([hubs, swap(hubs, mask)], 0)
     feat_t = features.T
@@ -381,8 +395,8 @@
     hub_got = swap(hub_send, core)
     peer_agg_t = swap(agg_t, core)
 
-    xy_rows, z_rows = width // n_xy, width // n_xy // n_z
-    hub_xy, hub_z = n_hubs // 2 // n_xy, n_hubs // 2 // n_xy // n_z
+    xy_rows = width // n_xy
+    hub_xy = n_hubs // 2 // n_xy
 
     def across(parts, bits, first=1):
         return [swap(part, spread(bits, first + k)) for k, part in enumerate(parts)]
@@ -403,17 +417,42 @@
             scratch=[pltpu.VMEM((width, half), F32)],
         )
 
-    def fold(keep, hub_in, got):
-        extra = 2 * hub_z if hub_in else 0
+    def halve(keep, hub_in, got, at_bit):
+        rows = keep.shape[0] // 2
+        n_hub = hub_in[0].shape[1] // 2 if hub_in else 0
+        keep, send, *hub_in = run_inside(
+            functools.partial(halve_body, bool(hub_in), at_bit),
+            z_at,
+            [keep] + hub_in + got,
+            [((rows, half), F32), ((rows + 2 * n_hub, half), BF16)] + [((2, n_hub, half), F32)] * bool(hub_in),
+            scratch=[pltpu.VMEM((2 * rows, half), F32)],
+        )
+        return keep, hub_in, [swap(send, z_bits[at_bit])]
+
+    def sum_line(keep, hub_in, got):
+        for at_bit in range(len(z_bits) - 1):
+            keep, hub_in, got = halve(keep, hub_in, got, at_bit)
+        rows = keep.shape[0]
+        n_hub = hub_in[0].shape[1] // 2 if hub_in else 0
+        hub_out = [((2, n_hub, half), F32)] * bool(hub_in)
+        own, *hub_in = run_inside(
+            functools.partial(meet_body, bool(hub_in)),
+            z_at,
+            [keep] + hub_in + got,
+            [((rows + 2 * n_hub, half), BF16)] + hub_out,
+        )
         return run_inside(
-            functools.partial(fold_body, n_z, bool(hub_in)),
-            z_me[None],
-            [keep] + hub_in + got,
-            [((z_rows, half), F32)]
-            + [((z_rows + extra, half), BF16)] * (n_z - 1)
-            + ([((2, hub_z, half), F32)] if hub_in else []),
-            scratch=[pltpu.VMEM((xy_rows, half), F32)],
+            functools.partial(close_body, bool(hub_in)),
+            z_at,
+            [own, swap(own, z_bits[-1])] + hub_in,
+            [((rows, half), BF16)] + hub_out,
         )
+
+    def gather_line(own):
+        for mask in z_bits[-2::-1]:
+            pair = [own, swap(own, mask)]
+            (own,) = run_inside(join_body, z_at, pair, [((2 * own.shape[0], half), BF16)])
+        return own
 
     self_xy = start_sum(feat_t, peer_feat_t, [])
     self_got = across(self_xy[1:], xy_bits)
@@ -421,40 +460,23 @@
     neigh_xy = start_sum(*agg_pair, [hub_keep, hub_got])
     neigh_got = across(neigh_xy[1:n_xy], xy_bits)
     self_got = in_order(self_got, neigh_xy)
-    self_z = fold(self_xy[0], [], self_got)
-    self_got = across(self_z[1:], z_bits)
-    neigh_got = in_order(neigh_got, self_got)
-    neigh_z = fold(neigh_xy[0], [neigh_xy[n_xy]], neigh_got)
-    neigh_got = across(neigh_z[1:n_z], z_bits)
-
-    def finish(keep, hub_in, got):
-        return run_inside(
-            functools.partial(last_body, bool(hub_in)),
-            z_me[None],
-            [keep] + hub_in + got,
-            [((z_rows, half), BF16)] + ([((2, hub_z, half), F32)] if hub_in else []),
-        )
-
-    def gather_line(own):
-        pieces = [own] + across([own] * (n_z - 1), z_bits)
-        return run_inside(join_body, z_me[None], pieces, [((xy_rows, half), BF16)])[0]
+    (self_own,) = sum_line(self_xy[0], [], self_got)
+    neigh_own, hub_back = sum_line(neigh_xy[0], [neigh_xy[n_xy]], neigh_got)
 
     def place(blocks):
         return run_inside(
-            functools.partial(place_body, n_xy, n_z),
+            functools.partial(place_body, n_xy, n_z // 2),
             jnp.stack([side, xy_me, z_me]),
             blocks + [swap(one, core) for one in blocks],
             [((width, width), BF16)],
         )[0]
 
-    (self_own,) = finish(self_z[0], [], self_got)
-    neigh_own, hub_back = finish(neigh_z[0], [neigh_z[n_z]], neigh_got)
     self_line = gather_line(self_own)
     self_blocks = [self_line] + across([self_line] * (n_xy - 1), xy_bits)
     neigh_line = gather_line(neigh_own)
     (neigh_line,) = in_order([neigh_line], self_blocks)
     neigh_blocks = [neigh_line] + across([neigh_line] * (n_xy - 1), xy_bits)
-    grad_self = place(self_blocks)
+    grad_self = place(in_order(self_blocks, neigh_blocks[:1]))
     (grad_x,) = run(
         node_body,
         side[None],

time: 154 us -> 148 us (0.961)
  starting transfers between devices: 54.4 us -> 48.1 us
  Pallas kernels: 29.6 us -> 35.7 us
  waiting for transfers between devices: 43.5 us -> 38 us
    pallas_call x10 -> x12, Pallas kernels: 12.2 us -> 18.2 us  [run_inside(): pl.pallas_call(kernel, out_shape=outs, in_specs=[SMEM] + [VMEM] * n_in, o...]
    ppermute x42 -> x36, starting transfers between devices: 43.5 us -> 37.6 us  [swap(): return lax.ppermute(value, AXES, [(i, i ^ mask) for i in range(n_dev)])]
    ppermute x42 -> x36, waiting for transfers between devices: 42.1 us -> 36.6 us  [swap(): return lax.ppermute(value, AXES, [(i, i ^ mask) for i in range(n_dev)])]
    unnamed x42 -> x100, local copies, waits for them, and re-layouts: 6.51 us -> 6.43 us
  transfers between devices with their start and end apart: 44 -> 38, of which waited for: 18 -> 15; matrix products, arithmetic and copies ran while one was open for 12% -> 13% of each run, Pallas kernels for 16% -> 20%
where the time goes in v5:
time: 148 us
  starting transfers between devices  48.1 us (32%)
  waiting for transfers between devices  38 us (26%)
  Pallas kernels  35.7 us (24%)
  other arithmetic  10.4 us (7%)
  local copies, waits for them, and re-layouts  7.39 us (5%)
  matrix products  6.73 us (5%)
  between operations  1.5 us (1%)
    ppermute x36, starting transfers between devices, swap(): return lax.ppermute(value, AXES, [(i, i ^ mask) for i in range(n_dev)])  37.6 us
    ppermute x36, waiting for transfers between devices, swap(): return lax.ppermute(value, AXES, [(i, i ^ mask) for i in range(n_dev)])  36.6 us
    pallas_call x12, Pallas kernels, run_inside(): pl.pallas_call(kernel, out_shape=outs, in_specs=[SMEM] + [VMEM] * n_in, o...  18.2 us
    pallas_call x3, Pallas kernels, run(): pl.pallas_call(kernel, out_shape=outs, in_specs=[SMEM] + [HBM] * n_in, ou...  17.5 us
    convert_element_type x3, other arithmetic, count(): return (found.astype(BF16), found_t.astype(BF16))  9.96 us
    dot_general x2, matrix products, mul(): return jnp.dot(left, right, preferred_element_type=F32)  6.73 us
    unnamed x100, local copies, waits for them, and re-layouts  6.43 us
    all_to_all x1, starting transfers between devices, on_device(): lax.all_to_all(outgoing.reshape(n_dev, capacity, width), AXES, split_axis...  6.19 us
  transfers between devices with their start and end apart: 38, of which 15 were waited for; matrix products, arithmetic and copies ran while one was open for 13% of the time, Pallas kernels for 20%

profile of v5, /device:TPU:0, one launch (start us, length us, event | category | flops | bytes accessed | tf_op | source)
XLA Modules:
  0.0 147.8 jit_solution(16719996644308473304)
XLA Ops:
  0.7 3.3 %shard_map.129 = (bf16[512,1024]{1,0:T(8,128)(2,1)}, bf16[8,1024]{1,0:T(8,128)(2,1)}, s32[1,512]{1,0:T(1,128)}) custom-call(s32[1]{0:T(128)} %bitcast.refs_0_, bf16[512,1024]{1,0:T(8,128)(2,1)} %refs_1_.2, s32[1,512]{1,0:T(1,128)} %refs_2_.1, s32[1,32]{1,0:T(1,128)} %refs_3_.1, s32[1,8]{1,0:T(1,128)} %bitcast.52), custom_call_target="tpu_custom_call" | custom-call | tf_op jit(solution)/shard_map/pallas_call | solution.py:60
  4.0 4.1 %collective-permute-start = (bf16[8,1024]{1,0:T(8,128)(2,1)}, bf16[8,1024]{1,0:T(8,128)(2,1)S(1)}, u32[]{:S(2)}, u32[]{:S(2)}) collective-permute-start(bf16[8,1024]{1,0:T(8,128)(2,1)} %get-tuple-element.48), channel_id=1, source_target_pairs={{0,4},{1,5},{2,6},{3,7},{4,0},{5,1},{6,2},{7,3},{8,12},{9,13},{10,... | collective-permute-start | bytes 49160 | tf_op jit(solution)/shard_map/ppermute | solution.py:330
  9.6 6.2 %all-to-all-start = ((bf16[32,16,1024]{2,1,0:T(8,128)(2,1)}), bf16[32,16,1024]{2,1,0:T(8,128)(2,1)}, u32[]{:S(2)}, u32[]{:S(2)}) async-start(bf16[32,16,1024]{2,1,0:T(8,128)(2,1)} %bitcast.55), calls=%async_computation | async-start | bytes 2097152 | tf_op jit(solution)/shard_map/all_to_all | solution.py:344
  17.2 4.5 %add_convert_fusion.1.refs_1_ = bf16[512,768]{1,0:T(8,128)(2,1)} fusion(s32[768]{0:T(1024)S(1)} %iota_add_fusion, s32[512]{0:T(512)S(1)} %bitcast.90, s32[512]{0:T(512)S(1)} %bitcast.92, s32[512]{0:T(512)S(1)} %bitcast.94, s32[512]{0:T(512)S(1)} %bitcast.96, s32[512]{0:T(512)S(1)} %bitcast.98, s32[512]{0:T(512)S(1)} %bitcast.100, s32[512]{0:T(512)S(1)} %bitcast.102, ...), kind=kLoop, calls=%fused_computation.1 | loop fusion | flops 18874368 | bytes 822272 | tf_op jit(solution)/shard_map/convert_element_type | solution.py:365
  21.7 3.4 %add_convert_fusion.refs_9_ = bf16[768,512]{1,0:T(8,128)(2,1)} fusion(s32[512]{0:T(512)S(1)} %bitcast.58, s32[512]{0:T(512)S(1)} %bitcast.60, s32[512]{0:T(512)S(1)} %bitcast.62, s32[512]{0:T(512)S(1)} %bitcast.64, s32[512]{0:T(512)S(1)} %bitcast.66, s32[512]{0:T(512)S(1)} %bitcast.68, s32[512]{0:T(512)S(1)} %bitcast.70, s32[512]{0:T(512)S(1)} %bitcast.72, ...), kind=kLoop, calls=%fused_computation | loop fusion | flops 18874368 | bytes 822272 | tf_op jit(solution)/shard_map/convert_element_type | solution.py:365
  25.2 1.7 %collective-permute-start.3 = (bf16[32,1024]{1,0:T(8,128)(2,1)S(1)}, bf16[32,1024]{1,0:T(8,128)(2,1)S(1)}, u32[]{:S(2)}, u32[]{:S(2)}) collective-permute-start(bf16[32,1024]{1,0:T(8,128)(2,1)S(1)} %pad_maximum_fusion), channel_id=1, source_target_pairs={{0,1},{1,0},{2,3},{3,2},{4,5},{5,4},{6,7},{7,6},{8,9},{9,8},{10,11... | collective-permute-start | bytes 196616 | tf_op jit(solution)/shard_map/ppermute | solution.py:330
  27.0 4.9 %collective-permute-done.3 = bf16[32,1024]{1,0:T(8,128)(2,1)S(1)} collective-permute-done((bf16[32,1024]{1,0:T(8,128)(2,1)S(1)}, bf16[32,1024]{1,0:T(8,128)(2,1)S(1)}, u32[]{:S(2)}, u32[]{:S(2)}) %collective-permute-start.3) | collective-permute-done | bytes 65568 | tf_op jit(solution)/shard_map/ppermute | solution.py:330
  32.5 4.2 %fusion.refs_4_ = f32[512,1024]{1,0:T(8,128)} fusion(bf16[512,1024]{1,0:T(8,128)(2,1)S(1)} %copy-done.17, s32[512]{0:T(512)S(1)} %bitcast.91, s32[512]{0:T(512)S(1)} %bitcast.93, s32[512]{0:T(512)S(1)} %bitcast.95, s32[512]{0:T(512)S(1)} %bitcast.97, s32[512]{0:T(512)S(1)} %bitcast.99, s32[512]{0:T(512)S(1)} %bitcast.101, s32[512]{0:T(512)S(1)} %bitcast.103, ...), kind=kOutput, calls=%fused_computation.37 | convolution fusion | flops 549453824 | bytes 3178496 | tf_op jit(solution)/shard_map/dot_general | solution.py:21
  36.7 1.7 %collective-permute-done.4 = bf16[64,1024]{1,0:T(8,128)(2,1)S(1)} collective-permute-done((bf16[64,1024]{1,0:T(8,128)(2,1)S(1)}, bf16[64,1024]{1,0:T(8,128)(2,1)S(1)}, u32[]{:S(2)}, u32[]{:S(2)}) %collective-permute-start.4) | collective-permute-done | bytes 131104 | tf_op jit(solution)/shard_map/ppermute | solution.py:330
  38.6 2.6 %convolution_add_fusion.refs_7_ = f32[512,1024]{1,0:T(8,128)} fusion(bf16[512,1024]{1,0:T(8,128)(2,1)S(1)} %copy-done.17, bf16[1024,1024]{1,0:T(8,128)(2,1)S(1)} %copy-done.1, f32[1024]{0:T(1024)S(1)} %copy-done.46), kind=kOutput, calls=%fused_computation.2 | convolution fusion | flops 1074266112 | bytes 5246976 | tf_op jit(solution)/shard_map/dot_general | solution.py:21
  43.4 9.8 %shard_map.130 = (bf16[512,1024]{1,0:T(8,128)(2,1)}, bf16[512,512]{1,0:T(8,128)(2,1)}, bf16[512,1024]{1,0:T(8,128)(2,1)}, bf16[512,512]{1,0:T(8,128)(2,1)}, bf16...) custom-call(s32[1]{0:T(128)} %bitcast.refs_0_, ...), custom_call_target="tpu_custom_call" | custom-call | tf_op jit(solution)/shard_map/pallas_call | solution.py:60
  53.8 4.3 %all-to-all-start.1 = ((bf16[32,16,1024]{2,1,0:T(8,128)(2,1)}), bf16[32,16,1024]{2,1,0:T(8,128)(2,1)S(1)}, u32[]{:S(2)}, u32[]{:S(2)}) async-start(bf16[32,16,1024]{2,1,0:T(8,128)(2,1)} %bitcast.54), calls=%async_computation.1 | async-start | bytes 2097152 | tf_op jit(solution)/shard_map/all_to_all | solution.py:391
  58.3 3.5 %shard_map.131 = (f32[256,512]{1,0:T(8,128)S(1)}, bf16[256,512]{1,0:T(8,128)(2,1)S(1)}, bf16[256,512]{1,0:T(8,128)(2,1)}, bf16[256,512]{1,0:T(8,128)(2,1)}) custom-call(s32[1]{0:T(128)} %bitcast.42.refs_0_, bf16[1024,512]{1,0:T(8,128)(2,1)S(1)} %bitcast.50, bf16[1024,512]{1,0:T(8,128)(2,1)} %collective-permute-done.7.refs_2_, bf16[512,512]{1,0:T(8,128)(2,1)S(1)} %copy-done, ...), custom_call_target="tpu_custom_call" | custom-call | tf_op jit(solution)/shard_map/pallas_call | solution.py:81
  62.6 1.7 %collective-permute-start.15 = (bf16[256,512]{1,0:T(8,128)(2,1)S(1)}, bf16[256,512]{1,0:T(8,128)(2,1)S(1)}, u32[]{:S(2)}, u32[]{:S(2)}) collective-permute-start(bf16[256,512]{1,0:T(8,128)(2,1)S(1)} %get-tuple-element.57), channel_id=1, source_target_pairs={{0,1},{1,0},{2,3},{3,2},{4,5},{5,4},{6,7},{7,6},{8,9},{9,8},{10,11... | collective-permute-start | bytes 786440 | tf_op jit(solution)/shard_map/ppermute | solution.py:330
  66.2 3.6 %shard_map.132 = (f32[256,512]{1,0:T(8,128)S(1)}, bf16[320,512]{1,0:T(8,128)(2,1)}, bf16[320,512]{1,0:T(8,128)(2,1)}, bf16[320,512]{1,0:T(8,128)(2,1)}, f32[2,32,512]{2,1,0:T(8,128)S(1)}) custom-call(s32[1]{0:T(128)} %bitcast.42.refs_0_, bf16[1024,512]{1,0:T(8,128)(2,1)S(1)} %copy-done.4, bf16[1024,512]{1,0:T(8,128)(2,1)} %collective-permute-done.6.refs_2_, ...), custom_call_target="tpu_custom_call" | custom-call | tf_op jit(solution)/shard_map/pallas_call | solution.py:81
  70.4 1.7 %collective-permute-start.10 = (bf16[320,512]{1,0:T(8,128)(2,1)}, bf16[320,512]{1,0:T(8,128)(2,1)S(1)}, u32[]{:S(2)}, u32[]{:S(2)}) collective-permute-start(bf16[320,512]{1,0:T(8,128)(2,1)} %get-tuple-element.66), channel_id=1, source_target_pairs={{0,1},{1,0},{2,3},{3,2},{4,5},{5,4},{6,7},{7,6},{8,9},{9,8},{10,11... | collective-permute-start | bytes 983048 | tf_op jit(solution)/shard_map/ppermute | solution.py:330
  73.6 7.9 %collective-permute-done.15.refs_2_ = bf16[256,512]{1,0:T(8,128)(2,1)S(1)} collective-permute-done((bf16[256,512]{1,0:T(8,128)(2,1)S(1)}, bf16[256,512]{1,0:T(8,128)(2,1)S(1)}, u32[]{:S(2)}, u32[]{:S(2)}) %collective-permute-start.15) | collective-permute-done | bytes 262176 | tf_op jit(solution)/shard_map/ppermute | solution.py:330
  81.6 2.9 %collective-permute-done.17.refs_4_ = bf16[256,512]{1,0:T(8,128)(2,1)} collective-permute-done((bf16[256,512]{1,0:T(8,128)(2,1)}, bf16[256,512]{1,0:T(8,128)(2,1)}, u32[]{:S(2)}, u32[]{:S(2)}) %collective-permute-start.17) | collective-permute-done | bytes 262176 | tf_op jit(solution)/shard_map/ppermute | solution.py:330
  85.7 4.0 %collective-permute-start.18 = (bf16[128,512]{1,0:T(8,128)(2,1)S(1)}, bf16[128,512]{1,0:T(8,128)(2,1)S(1)}, u32[]{:S(2)}, u32[]{:S(2)}) collective-permute-start(bf16[128,512]{1,0:T(8,128)(2,1)S(1)} %get-tuple-element.79), channel_id=1, source_target_pairs={{0,2},{1,3},{2,0},{3,1},{4,6},{5,7},{6,4},{7,5},{8,10},{9,11},{10,... | collective-permute-start | bytes 393224 | tf_op jit(solution)/shard_map/ppermute | solution.py:330
  89.6 2.9 %collective-permute-done.18.refs_2_ = bf16[128,512]{1,0:T(8,128)(2,1)S(1)} collective-permute-done((bf16[128,512]{1,0:T(8,128)(2,1)S(1)}, bf16[128,512]{1,0:T(8,128)(2,1)S(1)}, u32[]{:S(2)}, u32[]{:S(2)}) %collective-permute-start.18) | collective-permute-done | bytes 131104 | tf_op jit(solution)/shard_map/ppermute | solution.py:330
  93.3 2.8 %collective-permute-start.19 = (bf16[128,512]{1,0:T(8,128)(2,1)S(1)}, bf16[128,512]{1,0:T(8,128)(2,1)S(1)}, u32[]{:S(2)}, u32[]{:S(2)}) collective-permute-start(bf16[128,512]{1,0:T(8,128)(2,1)S(1)} %shard_map.138.refs_1_), channel_id=1, source_target_pairs={{0,4},{1,5},{2,6},{3,7},{4,0},{5,1},{6,2},{7,3},{8,12},{9,13},{10,... | collective-permute-start | bytes 393224 | tf_op jit(solution)/shard_map/ppermute | solution.py:330
  96.1 2.5 %collective-permute-done.12.refs_5_ = bf16[320,512]{1,0:T(8,128)(2,1)} collective-permute-done((bf16[320,512]{1,0:T(8,128)(2,1)}, bf16[320,512]{1,0:T(8,128)(2,1)}, u32[]{:S(2)}, u32[]{:S(2)}) %collective-permute-start.12) | collective-permute-done | bytes 327712 | tf_op jit(solution)/shard_map/ppermute | solution.py:330
  99.8 3.2 %collective-permute-start.13 = (bf16[160,512]{1,0:T(8,128)(2,1)S(1)}, bf16[160,512]{1,0:T(8,128)(2,1)S(1)}, u32[]{:S(2)}, u32[]{:S(2)}) collective-permute-start(bf16[160,512]{1,0:T(8,128)(2,1)S(1)} %get-tuple-element.71), channel_id=1, source_target_pairs={{0,2},{1,3},{2,0},{3,1},{4,6},{5,7},{6,4},{7,5},{8,10},{9,11},{10,... | collective-permute-start | bytes 491528 | tf_op jit(solution)/shard_map/ppermute | solution.py:330
  103.6 4.4 %collective-permute-done.13.refs_3_ = bf16[160,512]{1,0:T(8,128)(2,1)S(1)} collective-permute-done((bf16[160,512]{1,0:T(8,128)(2,1)S(1)}, bf16[160,512]{1,0:T(8,128)(2,1)S(1)}, u32[]{:S(2)}, u32[]{:S(2)}) %collective-permute-start.13) | collective-permute-done | bytes 163872 | tf_op jit(solution)/shard_map/ppermute | solution.py:330
  108.6 2.5 %collective-permute-start.14 = (bf16[144,512]{1,0:T(8,128)(2,1)S(1)}, bf16[144,512]{1,0:T(8,128)(2,1)S(1)}, u32[]{:S(2)}, u32[]{:S(2)}) collective-permute-start(bf16[144,512]{1,0:T(8,128)(2,1)S(1)} %get-tuple-element.72.refs_1_), channel_id=1, source_target_pairs={{0,4},{1,5},{2,6},{3,7},{4,0},{5,1},{6,2},{7,3},{8,12},{9,13},{10,... | collective-permute-start | bytes 442376 | tf_op jit(solution)/shard_map/ppermute | solution.py:330
  111.9 1.7 %collective-permute-start.22 = (bf16[256,512]{1,0:T(8,128)(2,1)S(1)}, bf16[256,512]{1,0:T(8,128)(2,1)}, u32[]{:S(2)}, u32[]{:S(2)}) collective-permute-start(bf16[256,512]{1,0:T(8,128)(2,1)S(1)} %shard_map.140.refs_1_), channel_id=1, source_target_pairs={{0,16},{1,17},{2,18},{3,19},{4,20},{5,21},{6,22},{7,23},{8,24},{9,... | collective-permute-start | bytes 786440 | tf_op jit(solution)/shard_map/ppermute | solution.py:330
  113.5 1.7 %collective-permute-start.23 = (bf16[256,512]{1,0:T(8,128)(2,1)S(1)}, bf16[256,512]{1,0:T(8,128)(2,1)}, u32[]{:S(2)}, u32[]{:S(2)}) collective-permute-start(bf16[256,512]{1,0:T(8,128)(2,1)S(1)} %shard_map.140.refs_1_), channel_id=1, source_target_pairs={{0,17},{1,16},{2,19},{3,18},{4,21},{5,20},{6,23},{7,22},{8,25},{9,... | collective-permute-start | bytes 786440 | tf_op jit(solution)/shard_map/ppermute | solution.py:330
  117.3 4.7 %collective-permute-done.24.refs_2_ = bf16[128,512]{1,0:T(8,128)(2,1)S(1)} collective-permute-done((bf16[128,512]{1,0:T(8,128)(2,1)S(1)}, bf16[128,512]{1,0:T(8,128)(2,1)S(1)}, u32[]{:S(2)}, u32[]{:S(2)}) %collective-permute-start.24) | collective-permute-done | bytes 131104 | tf_op jit(solution)/shard_map/ppermute | solution.py:330
  130.2 2.1 %add_convert_fusion.2.refs_4_ = bf16[512,512]{1,0:T(8,128)(2,1)S(1)} fusion(s32[512]{0:T(512)S(1)} %bitcast.59, s32[512]{0:T(512)S(1)} %bitcast.61, s32[512]{0:T(512)S(1)} %bitcast.63, s32[512]{0:T(512)S(1)} %bitcast.65, s32[512]{0:T(512)S(1)} %bitcast.67, s32[512]{0:T(512)S(1)} %bitcast.69, s32[512]{0:T(512)S(1)} %bitcast.71, s32[512]{0:T(512)S(1)} %bitcast.73, ...), kind=kLoop, calls=%fused_computation.3 | loop fusion | flops 12582912 | bytes 557056 | tf_op jit(solution)/shard_map/convert_element_type | solution.py:365
  135.1 4.4 %shard_map.136 = bf16[512,1024]{1,0:T(8,128)(2,1)} custom-call(s32[1]{0:T(128)} %bitcast.refs_0_, bf16[1024,1024]{1,0:T(8,128)(2,1)S(1)} %copy-done.2, bf16[512,512]{1,0:T(8,128)(2,1)S(1)} %copy-done, bf16[512,512]{1,0:T(8,128)(2,1)S(1)} %copy-done.8, bf16[512,512]{1,0:T(8,128)(2,1)S(1)} %add_convert_fusion.2.refs_4_, bf16[512,1024]{1,0:T(8,128)(2,1)S(1)} %copy-done.3, ...), custom_call_target="tpu_custom_call" | custom-call | tf_op jit(solution)/shard_map/pallas_call | solution.py:60
  139.6 2.7 %shard_map.142 = bf16[1024,1024]{1,0:T(8,128)(2,1)} custom-call(s32[3]{0:T(128)S(1)} %pad_add_fusion.1.refs_0_, bf16[256,512]{1,0:T(8,128)(2,1)S(1)} %shard_map.140.refs_1_, bf16[256,512]{1,0:T(8,128)(2,1)S(1)} %collective-permute-done.21.refs_2_, bf16[256,512]{1,0:T(8,128)(2,1)} %collective-permute-done.22.refs_3_, ...), custom_call_target="tpu_custom_call" | custom-call | tf_op jit(solution)/shard_map/pallas_call | solution.py:81
  145.2 2.6 %shard_map.143 = bf16[1024,1024]{1,0:T(8,128)(2,1)} custom-call(s32[3]{0:T(128)S(1)} %pad_add_fusion.1.refs_0_, bf16[256,512]{1,0:T(8,128)(2,1)S(1)} %shard_map.141.refs_1_, bf16[256,512]{1,0:T(8,128)(2,1)} %collective-permute-done.29.refs_2_, bf16[256,512]{1,0:T(8,128)(2,1)} %collective-permute-done.30.refs_3_, ...), custom_call_target="tpu_custom_call" | custom-call | tf_op jit(solution)/shard_map/pallas_call | solution.py:81
  (176 shorter events, 32.2 us)
Async XLA Ops:
  4.0 21.2 %collective-permute-start = (bf16[8,1024]{1,0:T(8,128)(2,1)}, bf16[8,1024]{1,0:T(8,128)(2,1)S(1)}, u32[]{:S(2)}, u32[]{:S(2)}) collective-permute-start(bf16[8,1024]{1,0:T(8,128)(2,1)} %get-tuple-element.48), channel_id=1, source_target_pairs={{0,4},{1,5},{2,6},{3,7},{4,0},{5,1},{6,2},{7,3},{8,12},{9,13},{10,... | collective-permute-start | bytes 49160 | tf_op jit(solution)/shard_map/ppermute | solution.py:330
  8.1 17.1 %collective-permute-start.1 = (bf16[8,1024]{1,0:T(8,128)(2,1)}, bf16[8,1024]{1,0:T(8,128)(2,1)S(1)}, u32[]{:S(2)}, u32[]{:S(2)}) collective-permute-start(bf16[8,1024]{1,0:T(8,128)(2,1)} %get-tuple-element.48), channel_id=1, source_target_pairs={{0,2},{1,3},{2,0},{3,1},{4,6},{5,7},{6,4},{7,5},{8,10},{9,11},{10,... | collective-permute-start | bytes 49160 | tf_op jit(solution)/shard_map/ppermute | solution.py:330
  9.6 15.6 %collective-permute-start.2 = (bf16[8,1024]{1,0:T(8,128)(2,1)}, bf16[8,1024]{1,0:T(8,128)(2,1)S(1)}, u32[]{:S(2)}, u32[]{:S(2)}) collective-permute-start(bf16[8,1024]{1,0:T(8,128)(2,1)} %get-tuple-element.48), channel_id=1, source_target_pairs={{0,6},{1,7},{2,4},{3,5},{4,2},{5,3},{6,0},{7,1},{8,14},{9,15},{10,... | collective-permute-start | bytes 49160 | tf_op jit(solution)/shard_map/ppermute | solution.py:330
  9.6 33.8 %all-to-all-start = ((bf16[32,16,1024]{2,1,0:T(8,128)(2,1)}), bf16[32,16,1024]{2,1,0:T(8,128)(2,1)}, u32[]{:S(2)}, u32[]{:S(2)}) async-start(bf16[32,16,1024]{2,1,0:T(8,128)(2,1)} %bitcast.55), calls=%async_computation | async-start | bytes 2097152 | tf_op jit(solution)/shard_map/all_to_all | solution.py:344
  16.4 41.9 %collective-permute-start.7 = (bf16[1024,512]{1,0:T(8,128)(2,1)S(1)}, bf16[1024,512]{1,0:T(8,128)(2,1)}, u32[]{:S(2)}, u32[]{:S(2)}) collective-permute-start(bf16[1024,512]{1,0:T(8,128)(2,1)S(1)} %bitcast.49), channel_id=1, source_target_pairs={{0,8},{1,9},{2,10},{3,11},{4,12},{5,13},{6,14},{7,15},{8,0},{9,1},... | collective-permute-start | bytes 3145736 | tf_op jit(solution)/shard_map/ppermute | solution.py:330
  25.2 6.7 %collective-permute-start.3 = (bf16[32,1024]{1,0:T(8,128)(2,1)S(1)}, bf16[32,1024]{1,0:T(8,128)(2,1)S(1)}, u32[]{:S(2)}, u32[]{:S(2)}) collective-permute-start(bf16[32,1024]{1,0:T(8,128)(2,1)S(1)} %pad_maximum_fusion), channel_id=1, source_target_pairs={{0,1},{1,0},{2,3},{3,2},{4,5},{5,4},{6,7},{7,6},{8,9},{9,8},{10,11... | collective-permute-start | bytes 196616 | tf_op jit(solution)/shard_map/ppermute | solution.py:330
  31.9 6.5 %collective-permute-start.4 = (bf16[64,1024]{1,0:T(8,128)(2,1)S(1)}, bf16[64,1024]{1,0:T(8,128)(2,1)S(1)}, u32[]{:S(2)}, u32[]{:S(2)}) collective-permute-start(bf16[64,1024]{1,0:T(8,128)(2,1)S(1)} %get-tuple-element.94), channel_id=1, source_target_pairs={{0,16},{1,17},{2,18},{3,19},{4,20},{5,21},{6,22},{7,23},{8,24},{9,... | collective-permute-start | bytes 393224 | tf_op jit(solution)/shard_map/ppermute | solution.py:330
  53.2 12.9 %collective-permute-start.6 = (bf16[1024,512]{1,0:T(8,128)(2,1)}, bf16[1024,512]{1,0:T(8,128)(2,1)}, u32[]{:S(2)}, u32[]{:S(2)}) collective-permute-start(bf16[1024,512]{1,0:T(8,128)(2,1)} %get-tuple-element.60.refs_1_), channel_id=1, source_target_pairs={{0,8},{1,9},{2,10},{3,11},{4,12},{5,13},{6,14},{7,15},{8,0},{9,1},... | collective-permute-start | bytes 3145736 | tf_op jit(solution)/shard_map/ppermute | solution.py:330
  53.3 5.0 %collective-permute-start.8 = (bf16[512,512]{1,0:T(8,128)(2,1)}, bf16[512,512]{1,0:T(8,128)(2,1)S(1)}, u32[]{:S(2)}, u32[]{:S(2)}) collective-permute-start(bf16[512,512]{1,0:T(8,128)(2,1)} %get-tuple-element.51.refs_3_), channel_id=1, source_target_pairs={{0,8},{1,9},{2,10},{3,11},{4,12},{5,13},{6,14},{7,15},{8,0},{9,1},... | collective-permute-start | bytes 1572872 | tf_op jit(solution)/shard_map/ppermute | solution.py:330
  53.8 78.5 %all-to-all-start.1 = ((bf16[32,16,1024]{2,1,0:T(8,128)(2,1)}), bf16[32,16,1024]{2,1,0:T(8,128)(2,1)S(1)}, u32[]{:S(2)}, u32[]{:S(2)}) async-start(bf16[32,16,1024]{2,1,0:T(8,128)(2,1)} %bitcast.54), calls=%async_computation.1 | async-start | bytes 2097152 | tf_op jit(solution)/shard_map/all_to_all | solution.py:391
  58.2 8.0 %collective-permute-start.9 = (bf16[2,128,512]{2,1,0:T(8,128)(2,1)}, bf16[2,128,512]{2,1,0:T(8,128)(2,1)}, u32[]{:S(2)}, u32[]{:S(2)}) collective-permute-start(bf16[2,128,512]{2,1,0:T(8,128)(2,1)} %get-tuple-element.63), channel_id=1, source_target_pairs={{0,8},{1,9},{2,10},{3,11},{4,12},{5,13},{6,14},{7,15},{8,0},{9,1},... | collective-permute-start | bytes 786440 | tf_op jit(solution)/shard_map/ppermute | solution.py:330
  62.6 18.9 %collective-permute-start.15 = (bf16[256,512]{1,0:T(8,128)(2,1)S(1)}, bf16[256,512]{1,0:T(8,128)(2,1)S(1)}, u32[]{:S(2)}, u32[]{:S(2)}) collective-permute-start(bf16[256,512]{1,0:T(8,128)(2,1)S(1)} %get-tuple-element.57), channel_id=1, source_target_pairs={{0,1},{1,0},{2,3},{3,2},{4,5},{5,4},{6,7},{7,6},{8,9},{9,8},{10,11... | collective-permute-start | bytes 786440 | tf_op jit(solution)/shard_map/ppermute | solution.py:330
  64.3 17.3 %collective-permute-start.16 = (bf16[256,512]{1,0:T(8,128)(2,1)}, bf16[256,512]{1,0:T(8,128)(2,1)}, u32[]{:S(2)}, u32[]{:S(2)}) collective-permute-start(bf16[256,512]{1,0:T(8,128)(2,1)} %get-tuple-element.58), channel_id=1, source_target_pairs={{0,16},{1,17},{2,18},{3,19},{4,20},{5,21},{6,22},{7,23},{8,24},{9,... | collective-permute-start | bytes 786440 | tf_op jit(solution)/shard_map/ppermute | solution.py:330
  65.8 18.7 %collective-permute-start.17 = (bf16[256,512]{1,0:T(8,128)(2,1)}, bf16[256,512]{1,0:T(8,128)(2,1)}, u32[]{:S(2)}, u32[]{:S(2)}) collective-permute-start(bf16[256,512]{1,0:T(8,128)(2,1)} %get-tuple-element.59), channel_id=1, source_target_pairs={{0,17},{1,16},{2,19},{3,18},{4,21},{5,20},{6,23},{7,22},{8,25},{9,... | collective-permute-start | bytes 786440 | tf_op jit(solution)/shard_map/ppermute | solution.py:330
  70.4 25.7 %collective-permute-start.10 = (bf16[320,512]{1,0:T(8,128)(2,1)}, bf16[320,512]{1,0:T(8,128)(2,1)S(1)}, u32[]{:S(2)}, u32[]{:S(2)}) collective-permute-start(bf16[320,512]{1,0:T(8,128)(2,1)} %get-tuple-element.66), channel_id=1, source_target_pairs={{0,1},{1,0},{2,3},{3,2},{4,5},{5,4},{6,7},{7,6},{8,9},{9,8},{10,11... | collective-permute-start | bytes 983048 | tf_op jit(solution)/shard_map/ppermute | solution.py:330
  72.1 24.0 %collective-permute-start.11 = (bf16[320,512]{1,0:T(8,128)(2,1)}, bf16[320,512]{1,0:T(8,128)(2,1)S(1)}, u32[]{:S(2)}, u32[]{:S(2)}) collective-permute-start(bf16[320,512]{1,0:T(8,128)(2,1)} %get-tuple-element.67), channel_id=1, source_target_pairs={{0,16},{1,17},{2,18},{3,19},{4,20},{5,21},{6,22},{7,23},{8,24},{9,... | collective-permute-start | bytes 983048 | tf_op jit(solution)/shard_map/ppermute | solution.py:330
  81.5 17.1 %collective-permute-start.12 = (bf16[320,512]{1,0:T(8,128)(2,1)}, bf16[320,512]{1,0:T(8,128)(2,1)}, u32[]{:S(2)}, u32[]{:S(2)}) collective-permute-start(bf16[320,512]{1,0:T(8,128)(2,1)} %get-tuple-element.68), channel_id=1, source_target_pairs={{0,17},{1,16},{2,19},{3,18},{4,21},{5,20},{6,23},{7,22},{8,25},{9,... | collective-permute-start | bytes 983048 | tf_op jit(solution)/shard_map/ppermute | solution.py:330
  85.7 6.9 %collective-permute-start.18 = (bf16[128,512]{1,0:T(8,128)(2,1)S(1)}, bf16[128,512]{1,0:T(8,128)(2,1)S(1)}, u32[]{:S(2)}, u32[]{:S(2)}) collective-permute-start(bf16[128,512]{1,0:T(8,128)(2,1)S(1)} %get-tuple-element.79), channel_id=1, source_target_pairs={{0,2},{1,3},{2,0},{3,1},{4,6},{5,7},{6,4},{7,5},{8,10},{9,11},{10,... | collective-permute-start | bytes 393224 | tf_op jit(solution)/shard_map/ppermute | solution.py:330
  93.3 9.7 %collective-permute-start.19 = (bf16[128,512]{1,0:T(8,128)(2,1)S(1)}, bf16[128,512]{1,0:T(8,128)(2,1)S(1)}, u32[]{:S(2)}, u32[]{:S(2)}) collective-permute-start(bf16[128,512]{1,0:T(8,128)(2,1)S(1)} %shard_map.138.refs_1_), channel_id=1, source_target_pairs={{0,4},{1,5},{2,6},{3,7},{4,0},{5,1},{6,2},{7,3},{8,12},{9,13},{10,... | collective-permute-start | bytes 393224 | tf_op jit(solution)/shard_map/ppermute | solution.py:330
  99.8 8.3 %collective-permute-start.13 = (bf16[160,512]{1,0:T(8,128)(2,1)S(1)}, bf16[160,512]{1,0:T(8,128)(2,1)S(1)}, u32[]{:S(2)}, u32[]{:S(2)}) collective-permute-start(bf16[160,512]{1,0:T(8,128)(2,1)S(1)} %get-tuple-element.71), channel_id=1, source_target_pairs={{0,2},{1,3},{2,0},{3,1},{4,6},{5,7},{6,4},{7,5},{8,10},{9,11},{10,... | collective-permute-start | bytes 491528 | tf_op jit(solution)/shard_map/ppermute | solution.py:330
  103.5 7.6 %collective-permute-start.20 = (bf16[128,512]{1,0:T(8,128)(2,1)S(1)}, bf16[128,512]{1,0:T(8,128)(2,1)S(1)}, u32[]{:S(2)}, u32[]{:S(2)}) collective-permute-start(bf16[128,512]{1,0:T(8,128)(2,1)S(1)} %shard_map.139.refs_1_), channel_id=1, source_target_pairs={{0,2},{1,3},{2,0},{3,1},{4,6},{5,7},{6,4},{7,5},{8,10},{9,11},{10,... | collective-permute-start | bytes 393224 | tf_op jit(solution)/shard_map/ppermute | solution.py:330
  108.6 7.8 %collective-permute-start.14 = (bf16[144,512]{1,0:T(8,128)(2,1)S(1)}, bf16[144,512]{1,0:T(8,128)(2,1)S(1)}, u32[]{:S(2)}, u32[]{:S(2)}) collective-permute-start(bf16[144,512]{1,0:T(8,128)(2,1)S(1)} %get-tuple-element.72.refs_1_), channel_id=1, source_target_pairs={{0,4},{1,5},{2,6},{3,7},{4,0},{5,1},{6,2},{7,3},{8,12},{9,13},{10,... | collective-permute-start | bytes 442376 | tf_op jit(solution)/shard_map/ppermute | solution.py:330
  111.7 10.9 %collective-permute-start.21 = (bf16[256,512]{1,0:T(8,128)(2,1)S(1)}, bf16[256,512]{1,0:T(8,128)(2,1)S(1)}, u32[]{:S(2)}, u32[]{:S(2)}) collective-permute-start(bf16[256,512]{1,0:T(8,128)(2,1)S(1)} %shard_map.140.refs_1_), channel_id=1, source_target_pairs={{0,1},{1,0},{2,3},{3,2},{4,5},{5,4},{6,7},{7,6},{8,9},{9,8},{10,11... | collective-permute-start | bytes 786440 | tf_op jit(solution)/shard_map/ppermute | solution.py:330
  111.9 10.8 %collective-permute-start.22 = (bf16[256,512]{1,0:T(8,128)(2,1)S(1)}, bf16[256,512]{1,0:T(8,128)(2,1)}, u32[]{:S(2)}, u32[]{:S(2)}) collective-permute-start(bf16[256,512]{1,0:T(8,128)(2,1)S(1)} %shard_map.140.refs_1_), channel_id=1, source_target_pairs={{0,16},{1,17},{2,18},{3,19},{4,20},{5,21},{6,22},{7,23},{8,24},{9,... | collective-permute-start | bytes 786440 | tf_op jit(solution)/shard_map/ppermute | solution.py:330
  113.5 10.6 %collective-permute-start.23 = (bf16[256,512]{1,0:T(8,128)(2,1)S(1)}, bf16[256,512]{1,0:T(8,128)(2,1)}, u32[]{:S(2)}, u32[]{:S(2)}) collective-permute-start(bf16[256,512]{1,0:T(8,128)(2,1)S(1)} %shard_map.140.refs_1_), channel_id=1, source_target_pairs={{0,17},{1,16},{2,19},{3,18},{4,21},{5,20},{6,23},{7,22},{8,25},{9,... | collective-permute-start | bytes 786440 | tf_op jit(solution)/shard_map/ppermute | solution.py:330
  117.0 5.0 %collective-permute-start.24 = (bf16[128,512]{1,0:T(8,128)(2,1)S(1)}, bf16[128,512]{1,0:T(8,128)(2,1)S(1)}, u32[]{:S(2)}, u32[]{:S(2)}) collective-permute-start(bf16[128,512]{1,0:T(8,128)(2,1)S(1)} %get-tuple-element.80.refs_1_), channel_id=1, source_target_pairs={{0,2},{1,3},{2,0},{3,1},{4,6},{5,7},{6,4},{7,5},{8,10},{9,11},{10,... | collective-permute-start | bytes 393224 | tf_op jit(solution)/shard_map/ppermute | solution.py:330
  124.1 4.8 %collective-permute-start.26 = (bf16[256,512]{1,0:T(8,128)(2,1)S(1)}, bf16[256,512]{1,0:T(8,128)(2,1)S(1)}, u32[]{:S(2)}, u32[]{:S(2)}) collective-permute-start(bf16[256,512]{1,0:T(8,128)(2,1)S(1)} %collective-permute-done.21.refs_2_), channel_id=1, source_target_pairs={{0,8},{1,9},{2,10},{3,11},{4,12},{5,13},{6,14},{7,15},{8,0},{9,1},... | collective-permute-start | bytes 786440 | tf_op jit(solution)/shard_map/ppermute | solution.py:330
  124.7 17.6 %collective-permute-start.29 = (bf16[256,512]{1,0:T(8,128)(2,1)S(1)}, bf16[256,512]{1,0:T(8,128)(2,1)}, u32[]{:S(2)}, u32[]{:S(2)}) collective-permute-start(bf16[256,512]{1,0:T(8,128)(2,1)S(1)} %shard_map.141.refs_1_), channel_id=1, source_target_pairs={{0,1},{1,0},{2,3},{3,2},{4,5},{5,4},{6,7},{7,6},{8,9},{9,8},{10,11... | collective-permute-start | bytes 786440 | tf_op jit(solution)/shard_map/ppermute | solution.py:330
  126.3 16.0 %collective-permute-start.30 = (bf16[256,512]{1,0:T(8,128)(2,1)S(1)}, bf16[256,512]{1,0:T(8,128)(2,1)}, u32[]{:S(2)}, u32[]{:S(2)}) collective-permute-start(bf16[256,512]{1,0:T(8,128)(2,1)S(1)} %shard_map.141.refs_1_), channel_id=1, source_target_pairs={{0,16},{1,17},{2,18},{3,19},{4,20},{5,21},{6,22},{7,23},{8,24},{9,... | collective-permute-start | bytes 786440 | tf_op jit(solution)/shard_map/ppermute | solution.py:330
  126.9 15.3 %collective-permute-start.31 = (bf16[256,512]{1,0:T(8,128)(2,1)S(1)}, bf16[256,512]{1,0:T(8,128)(2,1)}, u32[]{:S(2)}, u32[]{:S(2)}) collective-permute-start(bf16[256,512]{1,0:T(8,128)(2,1)S(1)} %shard_map.141.refs_1_), channel_id=1, source_target_pairs={{0,17},{1,16},{2,19},{3,18},{4,21},{5,20},{6,23},{7,22},{8,25},{9,... | collective-permute-start | bytes 786440 | tf_op jit(solution)/shard_map/ppermute | solution.py:330
  128.9 10.6 %collective-permute-start.27 = (bf16[256,512]{1,0:T(8,128)(2,1)}, bf16[256,512]{1,0:T(8,128)(2,1)}, u32[]{:S(2)}, u32[]{:S(2)}) collective-permute-start(bf16[256,512]{1,0:T(8,128)(2,1)} %collective-permute-done.22.refs_3_), channel_id=1, source_target_pairs={{0,8},{1,9},{2,10},{3,11},{4,12},{5,13},{6,14},{7,15},{8,0},{9,1},... | collective-permute-start | bytes 786440 | tf_op jit(solution)/shard_map/ppermute | solution.py:330
  129.6 9.9 %collective-permute-start.28 = (bf16[256,512]{1,0:T(8,128)(2,1)}, bf16[256,512]{1,0:T(8,128)(2,1)}, u32[]{:S(2)}, u32[]{:S(2)}) collective-permute-start(bf16[256,512]{1,0:T(8,128)(2,1)} %collective-permute-done.23.refs_4_), channel_id=1, source_target_pairs={{0,8},{1,9},{2,10},{3,11},{4,12},{5,13},{6,14},{7,15},{8,0},{9,1},... | collective-permute-start | bytes 786440 | tf_op jit(solution)/shard_map/ppermute | solution.py:330
  (53 other events, 722.6 us)

commit v6 on v5

--- a/solution.py
+++ b/solution.py
@@ -459,7 +459,7 @@
     agg_pair = in_order([agg_t, peer_agg_t], self_xy)
     neigh_xy = start_sum(*agg_pair, [hub_keep, hub_got])
     neigh_got = across(neigh_xy[1:n_xy], xy_bits)
-    self_got = in_order(self_got, neigh_xy)
+    self_got = in_order(self_got, [*neigh_xy, counts_own_t])
     (self_own,) = sum_line(self_xy[0], [], self_got)
     neigh_own, hub_back = sum_line(neigh_xy[0], [neigh_xy[n_xy]], neigh_got)
 
@@ -483,6 +483,7 @@
         [w_self, d_pre, d_other, counts_own_t, d_agg, chosen, returned, hub_row, hub_back],
         [(wide, BF16)],
         flops=2 * n_local * width * (width + n_local + n_slots),
+        limit=VMEM_LIMIT,
     )
     grad_neigh = place(in_order(neigh_blocks, [grad_x, grad_self]))
     return hidden, grad_x, grad_self, grad_neigh

time: 148 us -> 146 us (0.986)
  local copies, waits for them, and re-layouts: 7.39 us -> 2.46 us
  waiting for transfers between devices: 38 us -> 40 us
  starting transfers between devices: 48.1 us -> 49.6 us
    unnamed x100 -> x34, local copies, waits for them, and re-layouts: 6.43 us -> 1.44 us
    pallas_call x12, Pallas kernels: 18.2 us -> 14.6 us  [run_inside(): pl.pallas_call(kernel, out_shape=outs, in_specs=[SMEM] + [VMEM] * n_in, o...]
    pallas_call x3, Pallas kernels: 17.5 us -> 19.7 us  [run(): pl.pallas_call(kernel, out_shape=outs, in_specs=[SMEM] + [HBM] * n_in, ou...]
    ppermute x36, waiting for transfers between devices: 36.6 us -> 38.7 us  [swap(): return lax.ppermute(value, AXES, [(i, i ^ mask) for i in range(n_dev)])]
  transfers between devices with their start and end apart: 38 -> 38, of which waited for: 15 -> 17; matrix products, arithmetic and copies ran while one was open for 13% -> 13% of each run, Pallas kernels for 20% -> 20%
where the time goes in v6:
time: 146 us; the launch traced here: 145 us
  starting transfers between devices  49.6 us (34%)
  waiting for transfers between devices  40 us (27%)
  Pallas kernels  34.3 us (23%)
  other arithmetic  11.1 us (8%)
  matrix products  6.72 us (5%)
  local copies, waits for them, and re-layouts  2.46 us (2%)
    ppermute x36, starting transfers between devices, swap(): return lax.ppermute(value, AXES, [(i, i ^ mask) for i in range(n_dev)])  38.9 us
    ppermute x36, waiting for transfers between devices, swap(): return lax.ppermute(value, AXES, [(i, i ^ mask) for i in range(n_dev)])  38.7 us
    pallas_call x3, Pallas kernels, run(): pl.pallas_call(kernel, out_shape=outs, in_specs=[SMEM] + [HBM] * n_in, ou...  19.7 us
    pallas_call x12, Pallas kernels, run_inside(): pl.pallas_call(kernel, out_shape=outs, in_specs=[SMEM] + [VMEM] * n_in, o...  14.6 us
    convert_element_type x3, other arithmetic, count(): return (found.astype(BF16), found_t.astype(BF16))  10.7 us
    dot_general x2, matrix products, mul(): return jnp.dot(left, right, preferred_element_type=F32)  6.72 us
    all_to_all x1, starting transfers between devices, on_device(): lax.all_to_all(outgoing.reshape(n_dev, capacity, width), AXES, split_axis...  6.2 us
    all_to_all x1, starting transfers between devices, on_device(): lax.all_to_all(d_arrived.reshape(n_dev, capacity, width), AXES, split_axi...  4.46 us
  transfers between devices with their start and end apart: 38, of which 17 were waited for; matrix products, arithmetic and copies ran while one was open for 13% of the time, Pallas kernels for 20%

profile of v6, /device:TPU:0, one launch (start us, length us, event | category | flops | bytes accessed | tf_op | source)
XLA Modules:
  0.0 145.4 jit_solution(7404832353265654780)
XLA Ops:
  0.7 3.3 %shard_map.129 = (bf16[512,1024]{1,0:T(8,128)(2,1)}, bf16[8,1024]{1,0:T(8,128)(2,1)}, s32[1,512]{1,0:T(1,128)}) custom-call(s32[1]{0:T(128)} %bitcast.refs_0_, bf16[512,1024]{1,0:T(8,128)(2,1)} %refs_1_.2, s32[1,512]{1,0:T(1,128)} %refs_2_.1, s32[1,32]{1,0:T(1,128)} %refs_3_.1, s32[1,8]{1,0:T(1,128)} %bitcast.118), custom_call_target="tpu_custom_call" | custom-call | tf_op jit(solution)/shard_map/pallas_call | solution.py:60
  4.0 4.1 %collective-permute-start = (bf16[8,1024]{1,0:T(8,128)(2,1)}, bf16[8,1024]{1,0:T(8,128)(2,1)S(1)}, u32[]{:S(2)}, u32[]{:S(2)}) collective-permute-start(bf16[8,1024]{1,0:T(8,128)(2,1)} %get-tuple-element.48), channel_id=1, source_target_pairs={{0,4},{1,5},{2,6},{3,7},{4,0},{5,1},{6,2},{7,3},{8,12},{9,13},{10,... | collective-permute-start | bytes 49160 | tf_op jit(solution)/shard_map/ppermute | solution.py:330
  9.6 6.2 %all-to-all-start = ((bf16[32,16,1024]{2,1,0:T(8,128)(2,1)}), bf16[32,16,1024]{2,1,0:T(8,128)(2,1)}, u32[]{:S(2)}, u32[]{:S(2)}) async-start(bf16[32,16,1024]{2,1,0:T(8,128)(2,1)} %bitcast.52), calls=%async_computation | async-start | bytes 2097152 | tf_op jit(solution)/shard_map/all_to_all | solution.py:344
  17.1 4.4 %add_convert_fusion.1.refs_1_ = bf16[512,768]{1,0:T(8,128)(2,1)} fusion(s32[768]{0:T(1024)S(1)} %iota_add_fusion, s32[512]{0:T(512)S(1)} %bitcast.87, s32[512]{0:T(512)S(1)} %bitcast.89, s32[512]{0:T(512)S(1)} %bitcast.91, s32[512]{0:T(512)S(1)} %bitcast.93, s32[512]{0:T(512)S(1)} %bitcast.95, s32[512]{0:T(512)S(1)} %bitcast.97, s32[512]{0:T(512)S(1)} %bitcast.99, ...), kind=kLoop, calls=%fused_computation.1 | loop fusion | flops 18874368 | bytes 822272 | tf_op jit(solution)/shard_map/convert_element_type | solution.py:365
  21.5 3.4 %add_convert_fusion.refs_9_ = bf16[768,512]{1,0:T(8,128)(2,1)} fusion(s32[512]{0:T(512)S(1)} %bitcast.55, s32[512]{0:T(512)S(1)} %bitcast.57, s32[512]{0:T(512)S(1)} %bitcast.59, s32[512]{0:T(512)S(1)} %bitcast.61, s32[512]{0:T(512)S(1)} %bitcast.63, s32[512]{0:T(512)S(1)} %bitcast.65, s32[512]{0:T(512)S(1)} %bitcast.67, s32[512]{0:T(512)S(1)} %bitcast.69, ...), kind=kLoop, calls=%fused_computation | loop fusion | flops 18874368 | bytes 822272 | tf_op jit(solution)/shard_map/convert_element_type | solution.py:365
  25.0 1.7 %collective-permute-start.3 = (bf16[32,1024]{1,0:T(8,128)(2,1)S(1)}, bf16[32,1024]{1,0:T(8,128)(2,1)S(1)}, u32[]{:S(2)}, u32[]{:S(2)}) collective-permute-start(bf16[32,1024]{1,0:T(8,128)(2,1)S(1)} %pad_maximum_fusion), channel_id=1, source_target_pairs={{0,1},{1,0},{2,3},{3,2},{4,5},{5,4},{6,7},{7,6},{8,9},{9,8},{10,11... | collective-permute-start | bytes 196616 | tf_op jit(solution)/shard_map/ppermute | solution.py:330
  26.7 5.2 %collective-permute-done.3 = bf16[32,1024]{1,0:T(8,128)(2,1)S(1)} collective-permute-done((bf16[32,1024]{1,0:T(8,128)(2,1)S(1)}, bf16[32,1024]{1,0:T(8,128)(2,1)S(1)}, u32[]{:S(2)}, u32[]{:S(2)}) %collective-permute-start.3) | collective-permute-done | bytes 65568 | tf_op jit(solution)/shard_map/ppermute | solution.py:330
  32.6 4.1 %fusion.refs_4_ = f32[512,1024]{1,0:T(8,128)} fusion(bf16[512,1024]{1,0:T(8,128)(2,1)S(1)} %copy-done.7, s32[512]{0:T(512)S(1)} %bitcast.88, s32[512]{0:T(512)S(1)} %bitcast.90, s32[512]{0:T(512)S(1)} %bitcast.92, s32[512]{0:T(512)S(1)} %bitcast.94, s32[512]{0:T(512)S(1)} %bitcast.96, s32[512]{0:T(512)S(1)} %bitcast.98, s32[512]{0:T(512)S(1)} %bitcast.100, ...), kind=kOutput, calls=%fused_computation.37 | convolution fusion | flops 549453824 | bytes 3178496 | tf_op jit(solution)/shard_map/dot_general | solution.py:21
  36.7 1.7 %collective-permute-done.4 = bf16[64,1024]{1,0:T(8,128)(2,1)S(1)} collective-permute-done((bf16[64,1024]{1,0:T(8,128)(2,1)S(1)}, bf16[64,1024]{1,0:T(8,128)(2,1)S(1)}, u32[]{:S(2)}, u32[]{:S(2)}) %collective-permute-start.4) | collective-permute-done | bytes 131104 | tf_op jit(solution)/shard_map/ppermute | solution.py:330
  38.6 2.6 %convolution_add_fusion.refs_7_ = f32[512,1024]{1,0:T(8,128)} fusion(bf16[512,1024]{1,0:T(8,128)(2,1)S(1)} %copy-done.7, bf16[1024,1024]{1,0:T(8,128)(2,1)S(1)} %copy-done.8, f32[1024]{0:T(1024)S(1)} %copy-done.13), kind=kOutput, calls=%fused_computation.2 | convolution fusion | flops 1074266112 | bytes 5246976 | tf_op jit(solution)/shard_map/dot_general | solution.py:21
  43.4 9.8 %shard_map.130 = (bf16[512,1024]{1,0:T(8,128)(2,1)}, bf16[512,512]{1,0:T(8,128)(2,1)}, bf16[512,1024]{1,0:T(8,128)(2,1)}, bf16[512,512]{1,0:T(8,128)(2,1)}, bf16...) custom-call(s32[1]{0:T(128)} %bitcast.refs_0_, ...), custom_call_target="tpu_custom_call" | custom-call | tf_op jit(solution)/shard_map/pallas_call | solution.py:60
  53.9 4.5 %all-to-all-start.1 = ((bf16[32,16,1024]{2,1,0:T(8,128)(2,1)}), bf16[32,16,1024]{2,1,0:T(8,128)(2,1)}, u32[]{:S(2)}, u32[]{:S(2)}) async-start(bf16[32,16,1024]{2,1,0:T(8,128)(2,1)} %bitcast.51), calls=%async_computation.1 | async-start | bytes 2097152 | tf_op jit(solution)/shard_map/all_to_all | solution.py:391
  58.5 2.1 %shard_map.131 = (f32[256,512]{1,0:T(8,128)S(1)}, bf16[256,512]{1,0:T(8,128)(2,1)S(1)}, bf16[256,512]{1,0:T(8,128)(2,1)}, bf16[256,512]{1,0:T(8,128)(2,1)}) custom-call(s32[1]{0:T(128)} %bitcast.42.refs_0_, bf16[1024,512]{1,0:T(8,128)(2,1)S(1)} %bitcast.50, bf16[1024,512]{1,0:T(8,128)(2,1)S(1)} %collective-permute-done.7.refs_2_, ...), custom_call_target="tpu_custom_call" | custom-call | tf_op jit(solution)/shard_map/pallas_call | solution.py:81
  64.9 3.5 %shard_map.132 = (f32[256,512]{1,0:T(8,128)S(1)}, bf16[320,512]{1,0:T(8,128)(2,1)}, bf16[320,512]{1,0:T(8,128)(2,1)}, bf16[320,512]{1,0:T(8,128)(2,1)}, f32[2,32,512]{2,1,0:T(8,128)S(1)}) custom-call(s32[1]{0:T(128)} %bitcast.42.refs_0_, bf16[1024,512]{1,0:T(8,128)(2,1)S(1)} %copy-done.1, bf16[1024,512]{1,0:T(8,128)(2,1)} %collective-permute-done.6.refs_2_, ...), custom_call_target="tpu_custom_call" | custom-call | tf_op jit(solution)/shard_map/pallas_call | solution.py:81
  68.4 1.7 %collective-permute-start.10 = (bf16[320,512]{1,0:T(8,128)(2,1)}, bf16[320,512]{1,0:T(8,128)(2,1)S(1)}, u32[]{:S(2)}, u32[]{:S(2)}) collective-permute-start(bf16[320,512]{1,0:T(8,128)(2,1)} %get-tuple-element.66), channel_id=1, source_target_pairs={{0,1},{1,0},{2,3},{3,2},{4,5},{5,4},{6,7},{7,6},{8,9},{9,8},{10,11... | collective-permute-start | bytes 983048 | tf_op jit(solution)/shard_map/ppermute | solution.py:330
  71.6 8.4 %collective-permute-done.15.refs_2_ = bf16[256,512]{1,0:T(8,128)(2,1)S(1)} collective-permute-done((bf16[256,512]{1,0:T(8,128)(2,1)S(1)}, bf16[256,512]{1,0:T(8,128)(2,1)S(1)}, u32[]{:S(2)}, u32[]{:S(2)}) %collective-permute-start.15) | collective-permute-done | bytes 262176 | tf_op jit(solution)/shard_map/ppermute | solution.py:330
  81.2 2.8 %add_convert_fusion.2.refs_4_ = bf16[512,512]{1,0:T(8,128)(2,1)} fusion(s32[512]{0:T(512)S(1)} %bitcast.56, s32[512]{0:T(512)S(1)} %bitcast.58, s32[512]{0:T(512)S(1)} %bitcast.60, s32[512]{0:T(512)S(1)} %bitcast.62, s32[512]{0:T(512)S(1)} %bitcast.64, s32[512]{0:T(512)S(1)} %bitcast.66, s32[512]{0:T(512)S(1)} %bitcast.68, s32[512]{0:T(512)S(1)} %bitcast.70, ...), kind=kLoop, calls=%fused_computation.3 | loop fusion | flops 12582912 | bytes 557056 | tf_op jit(solution)/shard_map/convert_element_type | solution.py:365
  85.0 3.3 %collective-permute-start.18 = (bf16[128,512]{1,0:T(8,128)(2,1)S(1)}, bf16[128,512]{1,0:T(8,128)(2,1)S(1)}, u32[]{:S(2)}, u32[]{:S(2)}) collective-permute-start(bf16[128,512]{1,0:T(8,128)(2,1)S(1)} %get-tuple-element.79), channel_id=1, source_target_pairs={{0,2},{1,3},{2,0},{3,1},{4,6},{5,7},{6,4},{7,5},{8,10},{9,11},{10,... | collective-permute-start | bytes 393224 | tf_op jit(solution)/shard_map/ppermute | solution.py:330
  88.2 2.9 %collective-permute-done.18.refs_2_ = bf16[128,512]{1,0:T(8,128)(2,1)S(1)} collective-permute-done((bf16[128,512]{1,0:T(8,128)(2,1)S(1)}, bf16[128,512]{1,0:T(8,128)(2,1)S(1)}, u32[]{:S(2)}, u32[]{:S(2)}) %collective-permute-start.18) | collective-permute-done | bytes 131104 | tf_op jit(solution)/shard_map/ppermute | solution.py:330
  91.8 3.4 %collective-permute-start.19 = (bf16[128,512]{1,0:T(8,128)(2,1)S(1)}, bf16[128,512]{1,0:T(8,128)(2,1)S(1)}, u32[]{:S(2)}, u32[]{:S(2)}) collective-permute-start(bf16[128,512]{1,0:T(8,128)(2,1)S(1)} %shard_map.138.refs_1_), channel_id=1, source_target_pairs={{0,4},{1,5},{2,6},{3,7},{4,0},{5,1},{6,2},{7,3},{8,12},{9,13},{10,... | collective-permute-start | bytes 393224 | tf_op jit(solution)/shard_map/ppermute | solution.py:330
  95.2 3.1 %collective-permute-done.12.refs_5_ = bf16[320,512]{1,0:T(8,128)(2,1)S(1)} collective-permute-done((bf16[320,512]{1,0:T(8,128)(2,1)}, bf16[320,512]{1,0:T(8,128)(2,1)S(1)}, u32[]{:S(2)}, u32[]{:S(2)}) %collective-permute-start.12) | collective-permute-done | bytes 327712 | tf_op jit(solution)/shard_map/ppermute | solution.py:330
  99.1 2.8 %collective-permute-start.13 = (bf16[160,512]{1,0:T(8,128)(2,1)S(1)}, bf16[160,512]{1,0:T(8,128)(2,1)S(1)}, u32[]{:S(2)}, u32[]{:S(2)}) collective-permute-start(bf16[160,512]{1,0:T(8,128)(2,1)S(1)} %get-tuple-element.71), channel_id=1, source_target_pairs={{0,2},{1,3},{2,0},{3,1},{4,6},{5,7},{6,4},{7,5},{8,10},{9,11},{10,... | collective-permute-start | bytes 491528 | tf_op jit(solution)/shard_map/ppermute | solution.py:330
  102.6 4.4 %collective-permute-done.13.refs_3_ = bf16[160,512]{1,0:T(8,128)(2,1)S(1)} collective-permute-done((bf16[160,512]{1,0:T(8,128)(2,1)S(1)}, bf16[160,512]{1,0:T(8,128)(2,1)S(1)}, u32[]{:S(2)}, u32[]{:S(2)}) %collective-permute-start.13) | collective-permute-done | bytes 163872 | tf_op jit(solution)/shard_map/ppermute | solution.py:330
  107.5 3.5 %collective-permute-start.14 = (bf16[144,512]{1,0:T(8,128)(2,1)S(1)}, bf16[144,512]{1,0:T(8,128)(2,1)S(1)}, u32[]{:S(2)}, u32[]{:S(2)}) collective-permute-start(bf16[144,512]{1,0:T(8,128)(2,1)S(1)} %get-tuple-element.72.refs_1_), channel_id=1, source_target_pairs={{0,4},{1,5},{2,6},{3,7},{4,0},{5,1},{6,2},{7,3},{8,12},{9,13},{10,... | collective-permute-start | bytes 442376 | tf_op jit(solution)/shard_map/ppermute | solution.py:330
  112.3 2.8 %collective-permute-start.23 = (bf16[256,512]{1,0:T(8,128)(2,1)S(1)}, bf16[256,512]{1,0:T(8,128)(2,1)S(1)}, u32[]{:S(2)}, u32[]{:S(2)}) collective-permute-start(bf16[256,512]{1,0:T(8,128)(2,1)S(1)} %shard_map.140.refs_1_), channel_id=1, source_target_pairs={{0,17},{1,16},{2,19},{3,18},{4,21},{5,20},{6,23},{7,22},{8,25},{9,... | collective-permute-start | bytes 786440 | tf_op jit(solution)/shard_map/ppermute | solution.py:330
  117.0 5.0 %collective-permute-done.24.refs_2_ = bf16[128,512]{1,0:T(8,128)(2,1)S(1)} collective-permute-done((bf16[128,512]{1,0:T(8,128)(2,1)S(1)}, bf16[128,512]{1,0:T(8,128)(2,1)S(1)}, u32[]{:S(2)}, u32[]{:S(2)}) %collective-permute-start.24) | collective-permute-done | bytes 131104 | tf_op jit(solution)/shard_map/ppermute | solution.py:330
  122.6 1.8 %collective-permute-done.23.refs_4_ = bf16[256,512]{1,0:T(8,128)(2,1)S(1)} collective-permute-done((bf16[256,512]{1,0:T(8,128)(2,1)S(1)}, bf16[256,512]{1,0:T(8,128)(2,1)S(1)}, u32[]{:S(2)}, u32[]{:S(2)}) %collective-permute-start.23) | collective-permute-done | bytes 262176 | tf_op jit(solution)/shard_map/ppermute | solution.py:330
  126.8 2.1 %collective-permute-start.31 = (bf16[256,512]{1,0:T(8,128)(2,1)S(1)}, bf16[256,512]{1,0:T(8,128)(2,1)S(1)}, u32[]{:S(2)}, u32[]{:S(2)}) collective-permute-start(bf16[256,512]{1,0:T(8,128)(2,1)S(1)} %shard_map.141.refs_1_), channel_id=1, source_target_pairs={{0,17},{1,16},{2,19},{3,18},{4,21},{5,20},{6,23},{7,22},{8,25},{9,... | collective-permute-start | bytes 786440 | tf_op jit(solution)/shard_map/ppermute | solution.py:330
  129.0 6.6 %shard_map.136 = bf16[512,1024]{1,0:T(8,128)(2,1)} custom-call(s32[1]{0:T(128)} %bitcast.refs_0_, bf16[1024,1024]{1,0:T(8,128)(2,1)} %refs_1_.3, bf16[512,512]{1,0:T(8,128)(2,1)} %get-tuple-element.50.refs_3_.refs_2_, bf16[512,512]{1,0:T(8,128)(2,1)} %get-tuple-element.51.refs_3_, bf16[512,512]{1,0:T(8,128)(2,1)} %add_convert_fusion.2.refs_4_, ...), custom_call_target="tpu_custom_call" | custom-call | tf_op jit(solution)/shard_map/pallas_call | solution.py:60
  135.6 2.0 %shard_map.142 = bf16[1024,1024]{1,0:T(8,128)(2,1)} custom-call(s32[3]{0:T(128)S(1)} %pad_add_fusion.1.refs_0_, bf16[256,512]{1,0:T(8,128)(2,1)S(1)} %shard_map.140.refs_1_, bf16[256,512]{1,0:T(8,128)(2,1)S(1)} %collective-permute-done.21.refs_2_, bf16[256,512]{1,0:T(8,128)(2,1)S(1)} %collective-permute-done.22.refs_3_, ...), custom_call_target="tpu_custom_call" | custom-call | tf_op jit(solution)/shard_map/pallas_call | solution.py:81
  137.6 3.0 %collective-permute-done.31.refs_4_ = bf16[256,512]{1,0:T(8,128)(2,1)S(1)} collective-permute-done((bf16[256,512]{1,0:T(8,128)(2,1)S(1)}, bf16[256,512]{1,0:T(8,128)(2,1)S(1)}, u32[]{:S(2)}, u32[]{:S(2)}) %collective-permute-start.31) | collective-permute-done | bytes 262176 | tf_op jit(solution)/shard_map/ppermute | solution.py:330
  143.3 2.0 %shard_map.143 = bf16[1024,1024]{1,0:T(8,128)(2,1)} custom-call(s32[3]{0:T(128)S(1)} %pad_add_fusion.1.refs_0_, bf16[256,512]{1,0:T(8,128)(2,1)S(1)} %shard_map.141.refs_1_, bf16[256,512]{1,0:T(8,128)(2,1)S(1)} %collective-permute-done.29.refs_2_, bf16[256,512]{1,0:T(8,128)(2,1)S(1)} %collective-permute-done.30.refs_3_, ...), custom_call_target="tpu_custom_call" | custom-call | tf_op jit(solution)/shard_map/pallas_call | solution.py:81
  (110 shorter events, 25.8 us)
Async XLA Ops:
  4.0 21.0 %collective-permute-start = (bf16[8,1024]{1,0:T(8,128)(2,1)}, bf16[8,1024]{1,0:T(8,128)(2,1)S(1)}, u32[]{:S(2)}, u32[]{:S(2)}) collective-permute-start(bf16[8,1024]{1,0:T(8,128)(2,1)} %get-tuple-element.48), channel_id=1, source_target_pairs={{0,4},{1,5},{2,6},{3,7},{4,0},{5,1},{6,2},{7,3},{8,12},{9,13},{10,... | collective-permute-start | bytes 49160 | tf_op jit(solution)/shard_map/ppermute | solution.py:330
  8.1 16.9 %collective-permute-start.1 = (bf16[8,1024]{1,0:T(8,128)(2,1)}, bf16[8,1024]{1,0:T(8,128)(2,1)S(1)}, u32[]{:S(2)}, u32[]{:S(2)}) collective-permute-start(bf16[8,1024]{1,0:T(8,128)(2,1)} %get-tuple-element.48), channel_id=1, source_target_pairs={{0,2},{1,3},{2,0},{3,1},{4,6},{5,7},{6,4},{7,5},{8,10},{9,11},{10,... | collective-permute-start | bytes 49160 | tf_op jit(solution)/shard_map/ppermute | solution.py:330
  9.6 15.3 %collective-permute-start.2 = (bf16[8,1024]{1,0:T(8,128)(2,1)}, bf16[8,1024]{1,0:T(8,128)(2,1)S(1)}, u32[]{:S(2)}, u32[]{:S(2)}) collective-permute-start(bf16[8,1024]{1,0:T(8,128)(2,1)} %get-tuple-element.48), channel_id=1, source_target_pairs={{0,6},{1,7},{2,4},{3,5},{4,2},{5,3},{6,0},{7,1},{8,14},{9,15},{10,... | collective-permute-start | bytes 49160 | tf_op jit(solution)/shard_map/ppermute | solution.py:330
  9.6 33.8 %all-to-all-start = ((bf16[32,16,1024]{2,1,0:T(8,128)(2,1)}), bf16[32,16,1024]{2,1,0:T(8,128)(2,1)}, u32[]{:S(2)}, u32[]{:S(2)}) async-start(bf16[32,16,1024]{2,1,0:T(8,128)(2,1)} %bitcast.52), calls=%async_computation | async-start | bytes 2097152 | tf_op jit(solution)/shard_map/all_to_all | solution.py:344
  16.5 42.0 %collective-permute-start.7 = (bf16[1024,512]{1,0:T(8,128)(2,1)S(1)}, bf16[1024,512]{1,0:T(8,128)(2,1)S(1)}, u32[]{:S(2)}, u32[]{:S(2)}) collective-permute-start(bf16[1024,512]{1,0:T(8,128)(2,1)S(1)} %bitcast.49), channel_id=1, source_target_pairs={{0,8},{1,9},{2,10},{3,11},{4,12},{5,13},{6,14},{7,15},{8,0},{9,1},... | collective-permute-start | bytes 3145736 | tf_op jit(solution)/shard_map/ppermute | solution.py:330
  25.0 6.9 %collective-permute-start.3 = (bf16[32,1024]{1,0:T(8,128)(2,1)S(1)}, bf16[32,1024]{1,0:T(8,128)(2,1)S(1)}, u32[]{:S(2)}, u32[]{:S(2)}) collective-permute-start(bf16[32,1024]{1,0:T(8,128)(2,1)S(1)} %pad_maximum_fusion), channel_id=1, source_target_pairs={{0,1},{1,0},{2,3},{3,2},{4,5},{5,4},{6,7},{7,6},{8,9},{9,8},{10,11... | collective-permute-start | bytes 196616 | tf_op jit(solution)/shard_map/ppermute | solution.py:330
  32.0 6.5 %collective-permute-start.4 = (bf16[64,1024]{1,0:T(8,128)(2,1)S(1)}, bf16[64,1024]{1,0:T(8,128)(2,1)S(1)}, u32[]{:S(2)}, u32[]{:S(2)}) collective-permute-start(bf16[64,1024]{1,0:T(8,128)(2,1)S(1)} %get-tuple-element.94), channel_id=1, source_target_pairs={{0,16},{1,17},{2,18},{3,19},{4,20},{5,21},{6,22},{7,23},{8,24},{9,... | collective-permute-start | bytes 393224 | tf_op jit(solution)/shard_map/ppermute | solution.py:330
  38.5 3.6 %collective-permute-start.5 = (bf16[128,1024]{1,0:T(8,128)(2,1)S(1)}, bf16[128,1024]{1,0:T(8,128)(2,1)S(1)}, u32[]{:S(2)}, u32[]{:S(2)}) collective-permute-start(bf16[128,1024]{1,0:T(8,128)(2,1)S(1)} %get-tuple-element.90), channel_id=1, source_target_pairs={{0,8},{1,9},{2,10},{3,11},{4,12},{5,13},{6,14},{7,15},{8,0},{9,1},... | collective-permute-start | bytes 786440 | tf_op jit(solution)/shard_map/ppermute | solution.py:330
  53.3 11.6 %collective-permute-start.6 = (bf16[1024,512]{1,0:T(8,128)(2,1)}, bf16[1024,512]{1,0:T(8,128)(2,1)}, u32[]{:S(2)}, u32[]{:S(2)}) collective-permute-start(bf16[1024,512]{1,0:T(8,128)(2,1)} %get-tuple-element.60.refs_1_), channel_id=1, source_target_pairs={{0,8},{1,9},{2,10},{3,11},{4,12},{5,13},{6,14},{7,15},{8,0},{9,1},... | collective-permute-start | bytes 3145736 | tf_op jit(solution)/shard_map/ppermute | solution.py:330
  53.4 5.1 %collective-permute-start.8 = (bf16[512,512]{1,0:T(8,128)(2,1)}, bf16[512,512]{1,0:T(8,128)(2,1)S(1)}, u32[]{:S(2)}, u32[]{:S(2)}) collective-permute-start(bf16[512,512]{1,0:T(8,128)(2,1)} %get-tuple-element.51.refs_3_), channel_id=1, source_target_pairs={{0,8},{1,9},{2,10},{3,11},{4,12},{5,13},{6,14},{7,15},{8,0},{9,1},... | collective-permute-start | bytes 1572872 | tf_op jit(solution)/shard_map/ppermute | solution.py:330
  53.9 75.1 %all-to-all-start.1 = ((bf16[32,16,1024]{2,1,0:T(8,128)(2,1)}), bf16[32,16,1024]{2,1,0:T(8,128)(2,1)}, u32[]{:S(2)}, u32[]{:S(2)}) async-start(bf16[32,16,1024]{2,1,0:T(8,128)(2,1)} %bitcast.51), calls=%async_computation.1 | async-start | bytes 2097152 | tf_op jit(solution)/shard_map/all_to_all | solution.py:391
  58.3 6.5 %collective-permute-start.9 = (bf16[2,128,512]{2,1,0:T(8,128)(2,1)}, bf16[2,128,512]{2,1,0:T(8,128)(2,1)S(1)}, u32[]{:S(2)}, u32[]{:S(2)}) collective-permute-start(bf16[2,128,512]{2,1,0:T(8,128)(2,1)} %get-tuple-element.63), channel_id=1, source_target_pairs={{0,8},{1,9},{2,10},{3,11},{4,12},{5,13},{6,14},{7,15},{8,0},{9,1},... | collective-permute-start | bytes 786440 | tf_op jit(solution)/shard_map/ppermute | solution.py:330
  61.4 18.6 %collective-permute-start.15 = (bf16[256,512]{1,0:T(8,128)(2,1)S(1)}, bf16[256,512]{1,0:T(8,128)(2,1)S(1)}, u32[]{:S(2)}, u32[]{:S(2)}) collective-permute-start(bf16[256,512]{1,0:T(8,128)(2,1)S(1)} %get-tuple-element.57), channel_id=1, source_target_pairs={{0,1},{1,0},{2,3},{3,2},{4,5},{5,4},{6,7},{7,6},{8,9},{9,8},{10,11... | collective-permute-start | bytes 786440 | tf_op jit(solution)/shard_map/ppermute | solution.py:330
  63.0 21.1 %collective-permute-start.16 = (bf16[256,512]{1,0:T(8,128)(2,1)}, bf16[256,512]{1,0:T(8,128)(2,1)S(1)}, u32[]{:S(2)}, u32[]{:S(2)}) collective-permute-start(bf16[256,512]{1,0:T(8,128)(2,1)} %get-tuple-element.58), channel_id=1, source_target_pairs={{0,16},{1,17},{2,18},{3,19},{4,20},{5,21},{6,22},{7,23},{8,24},{9,... | collective-permute-start | bytes 786440 | tf_op jit(solution)/shard_map/ppermute | solution.py:330
  64.5 19.7 %collective-permute-start.17 = (bf16[256,512]{1,0:T(8,128)(2,1)}, bf16[256,512]{1,0:T(8,128)(2,1)S(1)}, u32[]{:S(2)}, u32[]{:S(2)}) collective-permute-start(bf16[256,512]{1,0:T(8,128)(2,1)} %get-tuple-element.59), channel_id=1, source_target_pairs={{0,17},{1,16},{2,19},{3,18},{4,21},{5,20},{6,23},{7,22},{8,25},{9,... | collective-permute-start | bytes 786440 | tf_op jit(solution)/shard_map/ppermute | solution.py:330
  68.4 26.7 %collective-permute-start.10 = (bf16[320,512]{1,0:T(8,128)(2,1)}, bf16[320,512]{1,0:T(8,128)(2,1)S(1)}, u32[]{:S(2)}, u32[]{:S(2)}) collective-permute-start(bf16[320,512]{1,0:T(8,128)(2,1)} %get-tuple-element.66), channel_id=1, source_target_pairs={{0,1},{1,0},{2,3},{3,2},{4,5},{5,4},{6,7},{7,6},{8,9},{9,8},{10,11... | collective-permute-start | bytes 983048 | tf_op jit(solution)/shard_map/ppermute | solution.py:330
  70.1 25.1 %collective-permute-start.11 = (bf16[320,512]{1,0:T(8,128)(2,1)}, bf16[320,512]{1,0:T(8,128)(2,1)S(1)}, u32[]{:S(2)}, u32[]{:S(2)}) collective-permute-start(bf16[320,512]{1,0:T(8,128)(2,1)} %get-tuple-element.67), channel_id=1, source_target_pairs={{0,16},{1,17},{2,18},{3,19},{4,20},{5,21},{6,22},{7,23},{8,24},{9,... | collective-permute-start | bytes 983048 | tf_op jit(solution)/shard_map/ppermute | solution.py:330
  79.9 18.4 %collective-permute-start.12 = (bf16[320,512]{1,0:T(8,128)(2,1)}, bf16[320,512]{1,0:T(8,128)(2,1)S(1)}, u32[]{:S(2)}, u32[]{:S(2)}) collective-permute-start(bf16[320,512]{1,0:T(8,128)(2,1)} %get-tuple-element.68), channel_id=1, source_target_pairs={{0,17},{1,16},{2,19},{3,18},{4,21},{5,20},{6,23},{7,22},{8,25},{9,... | collective-permute-start | bytes 983048 | tf_op jit(solution)/shard_map/ppermute | solution.py:330
  85.0 6.2 %collective-permute-start.18 = (bf16[128,512]{1,0:T(8,128)(2,1)S(1)}, bf16[128,512]{1,0:T(8,128)(2,1)S(1)}, u32[]{:S(2)}, u32[]{:S(2)}) collective-permute-start(bf16[128,512]{1,0:T(8,128)(2,1)S(1)} %get-tuple-element.79), channel_id=1, source_target_pairs={{0,2},{1,3},{2,0},{3,1},{4,6},{5,7},{6,4},{7,5},{8,10},{9,11},{10,... | collective-permute-start | bytes 393224 | tf_op jit(solution)/shard_map/ppermute | solution.py:330
  91.8 10.1 %collective-permute-start.19 = (bf16[128,512]{1,0:T(8,128)(2,1)S(1)}, bf16[128,512]{1,0:T(8,128)(2,1)S(1)}, u32[]{:S(2)}, u32[]{:S(2)}) collective-permute-start(bf16[128,512]{1,0:T(8,128)(2,1)S(1)} %shard_map.138.refs_1_), channel_id=1, source_target_pairs={{0,4},{1,5},{2,6},{3,7},{4,0},{5,1},{6,2},{7,3},{8,12},{9,13},{10,... | collective-permute-start | bytes 393224 | tf_op jit(solution)/shard_map/ppermute | solution.py:330
  99.1 7.9 %collective-permute-start.13 = (bf16[160,512]{1,0:T(8,128)(2,1)S(1)}, bf16[160,512]{1,0:T(8,128)(2,1)S(1)}, u32[]{:S(2)}, u32[]{:S(2)}) collective-permute-start(bf16[160,512]{1,0:T(8,128)(2,1)S(1)} %get-tuple-element.71), channel_id=1, source_target_pairs={{0,2},{1,3},{2,0},{3,1},{4,6},{5,7},{6,4},{7,5},{8,10},{9,11},{10,... | collective-permute-start | bytes 491528 | tf_op jit(solution)/shard_map/ppermute | solution.py:330
  102.5 8.5 %collective-permute-start.20 = (bf16[128,512]{1,0:T(8,128)(2,1)S(1)}, bf16[128,512]{1,0:T(8,128)(2,1)S(1)}, u32[]{:S(2)}, u32[]{:S(2)}) collective-permute-start(bf16[128,512]{1,0:T(8,128)(2,1)S(1)} %shard_map.139.refs_1_), channel_id=1, source_target_pairs={{0,2},{1,3},{2,0},{3,1},{4,6},{5,7},{6,4},{7,5},{8,10},{9,11},{10,... | collective-permute-start | bytes 393224 | tf_op jit(solution)/shard_map/ppermute | solution.py:330
  107.5 8.8 %collective-permute-start.14 = (bf16[144,512]{1,0:T(8,128)(2,1)S(1)}, bf16[144,512]{1,0:T(8,128)(2,1)S(1)}, u32[]{:S(2)}, u32[]{:S(2)}) collective-permute-start(bf16[144,512]{1,0:T(8,128)(2,1)S(1)} %get-tuple-element.72.refs_1_), channel_id=1, source_target_pairs={{0,4},{1,5},{2,6},{3,7},{4,0},{5,1},{6,2},{7,3},{8,12},{9,13},{10,... | collective-permute-start | bytes 442376 | tf_op jit(solution)/shard_map/ppermute | solution.py:330
  111.6 11.0 %collective-permute-start.21 = (bf16[256,512]{1,0:T(8,128)(2,1)S(1)}, bf16[256,512]{1,0:T(8,128)(2,1)S(1)}, u32[]{:S(2)}, u32[]{:S(2)}) collective-permute-start(bf16[256,512]{1,0:T(8,128)(2,1)S(1)} %shard_map.140.refs_1_), channel_id=1, source_target_pairs={{0,1},{1,0},{2,3},{3,2},{4,5},{5,4},{6,7},{7,6},{8,9},{9,8},{10,11... | collective-permute-start | bytes 786440 | tf_op jit(solution)/shard_map/ppermute | solution.py:330
  111.6 10.9 %collective-permute-start.22 = (bf16[256,512]{1,0:T(8,128)(2,1)S(1)}, bf16[256,512]{1,0:T(8,128)(2,1)S(1)}, u32[]{:S(2)}, u32[]{:S(2)}) collective-permute-start(bf16[256,512]{1,0:T(8,128)(2,1)S(1)} %shard_map.140.refs_1_), channel_id=1, source_target_pairs={{0,16},{1,17},{2,18},{3,19},{4,20},{5,21},{6,22},{7,23},{8,24},{9,... | collective-permute-start | bytes 786440 | tf_op jit(solution)/shard_map/ppermute | solution.py:330
  112.3 12.0 %collective-permute-start.23 = (bf16[256,512]{1,0:T(8,128)(2,1)S(1)}, bf16[256,512]{1,0:T(8,128)(2,1)S(1)}, u32[]{:S(2)}, u32[]{:S(2)}) collective-permute-start(bf16[256,512]{1,0:T(8,128)(2,1)S(1)} %shard_map.140.refs_1_), channel_id=1, source_target_pairs={{0,17},{1,16},{2,19},{3,18},{4,21},{5,20},{6,23},{7,22},{8,25},{9,... | collective-permute-start | bytes 786440 | tf_op jit(solution)/shard_map/ppermute | solution.py:330
  116.9 5.0 %collective-permute-start.24 = (bf16[128,512]{1,0:T(8,128)(2,1)S(1)}, bf16[128,512]{1,0:T(8,128)(2,1)S(1)}, u32[]{:S(2)}, u32[]{:S(2)}) collective-permute-start(bf16[128,512]{1,0:T(8,128)(2,1)S(1)} %get-tuple-element.80.refs_1_), channel_id=1, source_target_pairs={{0,2},{1,3},{2,0},{3,1},{4,6},{5,7},{6,4},{7,5},{8,10},{9,11},{10,... | collective-permute-start | bytes 393224 | tf_op jit(solution)/shard_map/ppermute | solution.py:330
  124.9 12.8 %collective-permute-start.29 = (bf16[256,512]{1,0:T(8,128)(2,1)S(1)}, bf16[256,512]{1,0:T(8,128)(2,1)S(1)}, u32[]{:S(2)}, u32[]{:S(2)}) collective-permute-start(bf16[256,512]{1,0:T(8,128)(2,1)S(1)} %shard_map.141.refs_1_), channel_id=1, source_target_pairs={{0,1},{1,0},{2,3},{3,2},{4,5},{5,4},{6,7},{7,6},{8,9},{9,8},{10,11... | collective-permute-start | bytes 786440 | tf_op jit(solution)/shard_map/ppermute | solution.py:330
  125.2 10.4 %collective-permute-start.27 = (bf16[256,512]{1,0:T(8,128)(2,1)S(1)}, bf16[256,512]{1,0:T(8,128)(2,1)S(1)}, u32[]{:S(2)}, u32[]{:S(2)}) collective-permute-start(bf16[256,512]{1,0:T(8,128)(2,1)S(1)} %collective-permute-done.22.refs_3_), channel_id=1, source_target_pairs={{0,8},{1,9},{2,10},{3,11},{4,12},{5,13},{6,14},{7,15},{8,0},{9,1},... | collective-permute-start | bytes 786440 | tf_op jit(solution)/shard_map/ppermute | solution.py:330
  125.2 10.4 %collective-permute-start.28 = (bf16[256,512]{1,0:T(8,128)(2,1)S(1)}, bf16[256,512]{1,0:T(8,128)(2,1)S(1)}, u32[]{:S(2)}, u32[]{:S(2)}) collective-permute-start(bf16[256,512]{1,0:T(8,128)(2,1)S(1)} %collective-permute-done.23.refs_4_), channel_id=1, source_target_pairs={{0,8},{1,9},{2,10},{3,11},{4,12},{5,13},{6,14},{7,15},{8,0},{9,1},... | collective-permute-start | bytes 786440 | tf_op jit(solution)/shard_map/ppermute | solution.py:330
  125.9 11.7 %collective-permute-start.30 = (bf16[256,512]{1,0:T(8,128)(2,1)S(1)}, bf16[256,512]{1,0:T(8,128)(2,1)S(1)}, u32[]{:S(2)}, u32[]{:S(2)}) collective-permute-start(bf16[256,512]{1,0:T(8,128)(2,1)S(1)} %shard_map.141.refs_1_), channel_id=1, source_target_pairs={{0,16},{1,17},{2,18},{3,19},{4,20},{5,21},{6,22},{7,23},{8,24},{9,... | collective-permute-start | bytes 786440 | tf_op jit(solution)/shard_map/ppermute | solution.py:330
  126.8 13.9 %collective-permute-start.31 = (bf16[256,512]{1,0:T(8,128)(2,1)S(1)}, bf16[256,512]{1,0:T(8,128)(2,1)S(1)}, u32[]{:S(2)}, u32[]{:S(2)}) collective-permute-start(bf16[256,512]{1,0:T(8,128)(2,1)S(1)} %shard_map.141.refs_1_), channel_id=1, source_target_pairs={{0,17},{1,16},{2,19},{3,18},{4,21},{5,20},{6,23},{7,22},{8,25},{9,... | collective-permute-start | bytes 786440 | tf_op jit(solution)/shard_map/ppermute | solution.py:330
  (20 other events, 115.9 us)

commit v7 on v6

--- a/solution.py
+++ b/solution.py
@@ -278,7 +278,8 @@
     half = ins[0].shape[1]
     rows = ins[0].shape[0] // n_z
     for i, block in enumerate(ins):
-        core, k = divmod(i, n_xy)
+        core, at = divmod(i, n_xy)
+        k = (n_xy - at) % n_xy
         cols = pl.ds(pl.multiple_of((where[0] ^ core) * half, half), half)
         for j in range(n_z):
             at = pl.ds(pl.multiple_of(((where[1] ^ k) * n_z + (where[2] ^ j)) * rows, rows), rows)
@@ -398,8 +399,8 @@
     xy_rows = width // n_xy
     hub_xy = n_hubs // 2 // n_xy
 
-    def across(parts, bits, first=1):
-        return [swap(part, spread(bits, first + k)) for k, part in enumerate(parts)]
+    def across(parts, bits):
+        return [swap(parts[k - 1], spread(bits, k)) for k in range(len(parts), 0, -1)]
 
     def in_order(values, earlier):
         return list(lax.optimization_barrier((*values, *earlier))[: len(values)])

time: 146 us -> 143 us (0.979)
  starting transfers between devices: 49.6 us -> 45.8 us
  waiting for transfers between devices: 40 us -> 41.5 us
    ppermute x36, starting transfers between devices: 38.9 us -> 35.1 us  [swap(): return lax.ppermute(value, AXES, [(i, i ^ mask) for i in range(n_dev)])]
  transfers between devices with their start and end apart: 38 -> 38, of which waited for: 17 -> 16; matrix products, arithmetic and copies ran while one was open for 13% -> 14% of each run, Pallas kernels for 20% -> 20%
where the time goes in v7:
time: 143 us
  starting transfers between devices  45.8 us (32%)
  waiting for transfers between devices  41.5 us (29%)
  Pallas kernels  34.3 us (24%)
  other arithmetic  11.1 us (8%)
  matrix products  6.72 us (5%)
  local copies, waits for them, and re-layouts  2.46 us (2%)
    ppermute x36, waiting for transfers between devices, swap(): return lax.ppermute(value, AXES, [(i, i ^ mask) for i in range(n_dev)])  40.2 us
    ppermute x36, starting transfers between devices, swap(): return lax.ppermute(value, AXES, [(i, i ^ mask) for i in range(n_dev)])  35.1 us
    pallas_call x3, Pallas kernels, run(): pl.pallas_call(kernel, out_shape=outs, in_specs=[SMEM] + [HBM] * n_in, ou...  19.7 us
    pallas_call x12, Pallas kernels, run_inside(): pl.pallas_call(kernel, out_shape=outs, in_specs=[SMEM] + [VMEM] * n_in, o...  14.6 us
    convert_element_type x3, other arithmetic, count(): return (found.astype(BF16), found_t.astype(BF16))  10.7 us
    dot_general x2, matrix products, mul(): return jnp.dot(left, right, preferred_element_type=F32)  6.72 us
    all_to_all x1, starting transfers between devices, on_device(): lax.all_to_all(outgoing.reshape(n_dev, capacity, width), AXES, split_axis...  6.2 us
    all_to_all x1, starting transfers between devices, on_device(): lax.all_to_all(d_arrived.reshape(n_dev, capacity, width), AXES, split_axi...  4.46 us
  transfers between devices with their start and end apart: 38, of which 16 were waited for; matrix products, arithmetic and copies ran while one was open for 14% of the time, Pallas kernels for 20%

profile of v7, /device:TPU:0, one launch (start us, length us, event | category | flops | bytes accessed | tf_op | source)
XLA Modules:
  0.0 143.0 jit_solution(3528022728932881386)
XLA Ops:
  0.7 3.3 %shard_map.129 = (bf16[512,1024]{1,0:T(8,128)(2,1)}, bf16[8,1024]{1,0:T(8,128)(2,1)}, s32[1,512]{1,0:T(1,128)}) custom-call(s32[1]{0:T(128)} %bitcast.refs_0_, bf16[512,1024]{1,0:T(8,128)(2,1)} %refs_1_.2, s32[1,512]{1,0:T(1,128)} %refs_2_.1, s32[1,32]{1,0:T(1,128)} %refs_3_.1, s32[1,8]{1,0:T(1,128)} %bitcast.118), custom_call_target="tpu_custom_call" | custom-call | tf_op jit(solution)/shard_map/pallas_call | solution.py:60
  4.0 4.1 %collective-permute-start = (bf16[8,1024]{1,0:T(8,128)(2,1)}, bf16[8,1024]{1,0:T(8,128)(2,1)S(1)}, u32[]{:S(2)}, u32[]{:S(2)}) collective-permute-start(bf16[8,1024]{1,0:T(8,128)(2,1)} %get-tuple-element.48), channel_id=1, source_target_pairs={{0,4},{1,5},{2,6},{3,7},{4,0},{5,1},{6,2},{7,3},{8,12},{9,13},{10,... | collective-permute-start | bytes 49160 | tf_op jit(solution)/shard_map/ppermute | solution.py:331
  8.1 1.6 %collective-permute-start.1 = (bf16[8,1024]{1,0:T(8,128)(2,1)}, bf16[8,1024]{1,0:T(8,128)(2,1)S(1)}, u32[]{:S(2)}, u32[]{:S(2)}) collective-permute-start(bf16[8,1024]{1,0:T(8,128)(2,1)} %get-tuple-element.48), channel_id=1, source_target_pairs={{0,2},{1,3},{2,0},{3,1},{4,6},{5,7},{6,4},{7,5},{8,10},{9,11},{10,... | collective-permute-start | bytes 49160 | tf_op jit(solution)/shard_map/ppermute | solution.py:331
  9.6 6.2 %all-to-all-start = ((bf16[32,16,1024]{2,1,0:T(8,128)(2,1)}), bf16[32,16,1024]{2,1,0:T(8,128)(2,1)}, u32[]{:S(2)}, u32[]{:S(2)}) async-start(bf16[32,16,1024]{2,1,0:T(8,128)(2,1)} %bitcast.52), calls=%async_computation | async-start | bytes 2097152 | tf_op jit(solution)/shard_map/all_to_all | solution.py:345
  17.1 4.4 %add_convert_fusion.1.refs_1_ = bf16[512,768]{1,0:T(8,128)(2,1)} fusion(s32[768]{0:T(1024)S(1)} %iota_add_fusion, s32[512]{0:T(512)S(1)} %bitcast.87, s32[512]{0:T(512)S(1)} %bitcast.89, s32[512]{0:T(512)S(1)} %bitcast.91, s32[512]{0:T(512)S(1)} %bitcast.93, s32[512]{0:T(512)S(1)} %bitcast.95, s32[512]{0:T(512)S(1)} %bitcast.97, s32[512]{0:T(512)S(1)} %bitcast.99, ...), kind=kLoop, calls=%fused_computation.1 | loop fusion | flops 18874368 | bytes 822272 | tf_op jit(solution)/shard_map/convert_element_type | solution.py:366
  21.5 3.4 %add_convert_fusion.refs_9_ = bf16[768,512]{1,0:T(8,128)(2,1)} fusion(s32[512]{0:T(512)S(1)} %bitcast.55, s32[512]{0:T(512)S(1)} %bitcast.57, s32[512]{0:T(512)S(1)} %bitcast.59, s32[512]{0:T(512)S(1)} %bitcast.61, s32[512]{0:T(512)S(1)} %bitcast.63, s32[512]{0:T(512)S(1)} %bitcast.65, s32[512]{0:T(512)S(1)} %bitcast.67, s32[512]{0:T(512)S(1)} %bitcast.69, ...), kind=kLoop, calls=%fused_computation | loop fusion | flops 18874368 | bytes 822272 | tf_op jit(solution)/shard_map/convert_element_type | solution.py:366
  25.0 1.7 %collective-permute-start.3 = (bf16[32,1024]{1,0:T(8,128)(2,1)S(1)}, bf16[32,1024]{1,0:T(8,128)(2,1)S(1)}, u32[]{:S(2)}, u32[]{:S(2)}) collective-permute-start(bf16[32,1024]{1,0:T(8,128)(2,1)S(1)} %pad_maximum_fusion), channel_id=1, source_target_pairs={{0,1},{1,0},{2,3},{3,2},{4,5},{5,4},{6,7},{7,6},{8,9},{9,8},{10,11... | collective-permute-start | bytes 196616 | tf_op jit(solution)/shard_map/ppermute | solution.py:331
  26.7 5.2 %collective-permute-done.3 = bf16[32,1024]{1,0:T(8,128)(2,1)S(1)} collective-permute-done((bf16[32,1024]{1,0:T(8,128)(2,1)S(1)}, bf16[32,1024]{1,0:T(8,128)(2,1)S(1)}, u32[]{:S(2)}, u32[]{:S(2)}) %collective-permute-start.3) | collective-permute-done | bytes 65568 | tf_op jit(solution)/shard_map/ppermute | solution.py:331
  32.6 4.1 %fusion.refs_4_ = f32[512,1024]{1,0:T(8,128)} fusion(bf16[512,1024]{1,0:T(8,128)(2,1)S(1)} %copy-done.7, s32[512]{0:T(512)S(1)} %bitcast.88, s32[512]{0:T(512)S(1)} %bitcast.90, s32[512]{0:T(512)S(1)} %bitcast.92, s32[512]{0:T(512)S(1)} %bitcast.94, s32[512]{0:T(512)S(1)} %bitcast.96, s32[512]{0:T(512)S(1)} %bitcast.98, s32[512]{0:T(512)S(1)} %bitcast.100, ...), kind=kOutput, calls=%fused_computation.37 | convolution fusion | flops 549453824 | bytes 3178496 | tf_op jit(solution)/shard_map/dot_general | solution.py:21
  36.7 1.7 %collective-permute-done.4 = bf16[64,1024]{1,0:T(8,128)(2,1)S(1)} collective-permute-done((bf16[64,1024]{1,0:T(8,128)(2,1)S(1)}, bf16[64,1024]{1,0:T(8,128)(2,1)S(1)}, u32[]{:S(2)}, u32[]{:S(2)}) %collective-permute-start.4) | collective-permute-done | bytes 131104 | tf_op jit(solution)/shard_map/ppermute | solution.py:331
  38.6 2.6 %convolution_add_fusion.refs_7_ = f32[512,1024]{1,0:T(8,128)} fusion(bf16[512,1024]{1,0:T(8,128)(2,1)S(1)} %copy-done.7, bf16[1024,1024]{1,0:T(8,128)(2,1)S(1)} %copy-done.8, f32[1024]{0:T(1024)S(1)} %copy-done.13), kind=kOutput, calls=%fused_computation.2 | convolution fusion | flops 1074266112 | bytes 5246976 | tf_op jit(solution)/shard_map/dot_general | solution.py:21
  43.4 9.8 %shard_map.130 = (bf16[512,1024]{1,0:T(8,128)(2,1)}, bf16[512,512]{1,0:T(8,128)(2,1)}, bf16[512,1024]{1,0:T(8,128)(2,1)}, bf16[512,512]{1,0:T(8,128)(2,1)}, bf16...) custom-call(s32[1]{0:T(128)} %bitcast.refs_0_, ...), custom_call_target="tpu_custom_call" | custom-call | tf_op jit(solution)/shard_map/pallas_call | solution.py:60
  53.9 4.5 %all-to-all-start.1 = ((bf16[32,16,1024]{2,1,0:T(8,128)(2,1)}), bf16[32,16,1024]{2,1,0:T(8,128)(2,1)}, u32[]{:S(2)}, u32[]{:S(2)}) async-start(bf16[32,16,1024]{2,1,0:T(8,128)(2,1)} %bitcast.51), calls=%async_computation.1 | async-start | bytes 2097152 | tf_op jit(solution)/shard_map/all_to_all | solution.py:392
  58.5 2.1 %shard_map.131 = (f32[256,512]{1,0:T(8,128)S(1)}, bf16[256,512]{1,0:T(8,128)(2,1)}, bf16[256,512]{1,0:T(8,128)(2,1)}, bf16[256,512]{1,0:T(8,128)(2,1)S(1)}) custom-call(s32[1]{0:T(128)} %bitcast.42.refs_0_, bf16[1024,512]{1,0:T(8,128)(2,1)S(1)} %bitcast.50, bf16[1024,512]{1,0:T(8,128)(2,1)S(1)} %collective-permute-done.7.refs_2_, ...), custom_call_target="tpu_custom_call" | custom-call | tf_op jit(solution)/shard_map/pallas_call | solution.py:81
  61.4 2.6 %collective-permute-start.15 = (bf16[256,512]{1,0:T(8,128)(2,1)S(1)}, bf16[256,512]{1,0:T(8,128)(2,1)S(1)}, u32[]{:S(2)}, u32[]{:S(2)}) collective-permute-start(bf16[256,512]{1,0:T(8,128)(2,1)S(1)} %get-tuple-element.59), channel_id=1, source_target_pairs={{0,17},{1,16},{2,19},{3,18},{4,21},{5,20},{6,23},{7,22},{8,25},{9,... | collective-permute-start | bytes 786440 | tf_op jit(solution)/shard_map/ppermute | solution.py:331
  64.9 3.5 %shard_map.132 = (f32[256,512]{1,0:T(8,128)S(1)}, bf16[320,512]{1,0:T(8,128)(2,1)}, bf16[320,512]{1,0:T(8,128)(2,1)}, bf16[320,512]{1,0:T(8,128)(2,1)}, f32[2,32,512]{2,1,0:T(8,128)S(1)}) custom-call(s32[1]{0:T(128)} %bitcast.42.refs_0_, bf16[1024,512]{1,0:T(8,128)(2,1)S(1)} %copy-done.1, bf16[1024,512]{1,0:T(8,128)(2,1)} %collective-permute-done.6.refs_2_, ...), custom_call_target="tpu_custom_call" | custom-call | tf_op jit(solution)/shard_map/pallas_call | solution.py:81
  68.4 2.6 %collective-permute-start.10 = (bf16[320,512]{1,0:T(8,128)(2,1)}, bf16[320,512]{1,0:T(8,128)(2,1)S(1)}, u32[]{:S(2)}, u32[]{:S(2)}) collective-permute-start(bf16[320,512]{1,0:T(8,128)(2,1)} %get-tuple-element.66), channel_id=1, source_target_pairs={{0,17},{1,16},{2,19},{3,18},{4,21},{5,20},{6,23},{7,22},{8,25},{9,... | collective-permute-start | bytes 983048 | tf_op jit(solution)/shard_map/ppermute | solution.py:331
  71.6 8.3 %collective-permute-done.15.refs_2_ = bf16[256,512]{1,0:T(8,128)(2,1)S(1)} collective-permute-done((bf16[256,512]{1,0:T(8,128)(2,1)S(1)}, bf16[256,512]{1,0:T(8,128)(2,1)S(1)}, u32[]{:S(2)}, u32[]{:S(2)}) %collective-permute-start.15) | collective-permute-done | bytes 262176 | tf_op jit(solution)/shard_map/ppermute | solution.py:331
  79.9 2.8 %add_convert_fusion.2.refs_4_ = bf16[512,512]{1,0:T(8,128)(2,1)} fusion(s32[512]{0:T(512)S(1)} %bitcast.56, s32[512]{0:T(512)S(1)} %bitcast.58, s32[512]{0:T(512)S(1)} %bitcast.60, s32[512]{0:T(512)S(1)} %bitcast.62, s32[512]{0:T(512)S(1)} %bitcast.64, s32[512]{0:T(512)S(1)} %bitcast.66, s32[512]{0:T(512)S(1)} %bitcast.68, s32[512]{0:T(512)S(1)} %bitcast.70, ...), kind=kLoop, calls=%fused_computation.3 | loop fusion | flops 12582912 | bytes 557056 | tf_op jit(solution)/shard_map/convert_element_type | solution.py:366
  85.9 4.2 %collective-permute-done.18.refs_2_ = bf16[128,512]{1,0:T(8,128)(2,1)S(1)} collective-permute-done((bf16[128,512]{1,0:T(8,128)(2,1)S(1)}, bf16[128,512]{1,0:T(8,128)(2,1)S(1)}, u32[]{:S(2)}, u32[]{:S(2)}) %collective-permute-start.18) | collective-permute-done | bytes 131104 | tf_op jit(solution)/shard_map/ppermute | solution.py:331
  90.6 3.6 %collective-permute-start.19 = (bf16[128,512]{1,0:T(8,128)(2,1)S(1)}, bf16[128,512]{1,0:T(8,128)(2,1)S(1)}, u32[]{:S(2)}, u32[]{:S(2)}) collective-permute-start(bf16[128,512]{1,0:T(8,128)(2,1)S(1)} %shard_map.138.refs_1_), channel_id=1, source_target_pairs={{0,4},{1,5},{2,6},{3,7},{4,0},{5,1},{6,2},{7,3},{8,12},{9,13},{10,... | collective-permute-start | bytes 393224 | tf_op jit(solution)/shard_map/ppermute | solution.py:331
  94.3 4.3 %collective-permute-done.11.refs_4_ = bf16[320,512]{1,0:T(8,128)(2,1)S(1)} collective-permute-done((bf16[320,512]{1,0:T(8,128)(2,1)}, bf16[320,512]{1,0:T(8,128)(2,1)S(1)}, u32[]{:S(2)}, u32[]{:S(2)}) %collective-permute-start.11) | collective-permute-done | bytes 327712 | tf_op jit(solution)/shard_map/ppermute | solution.py:331
  100.3 1.7 %collective-permute-start.20 = (bf16[128,512]{1,0:T(8,128)(2,1)S(1)}, bf16[128,512]{1,0:T(8,128)(2,1)S(1)}, u32[]{:S(2)}, u32[]{:S(2)}) collective-permute-start(bf16[128,512]{1,0:T(8,128)(2,1)S(1)} %shard_map.139.refs_1_), channel_id=1, source_target_pairs={{0,2},{1,3},{2,0},{3,1},{4,6},{5,7},{6,4},{7,5},{8,10},{9,11},{10,... | collective-permute-start | bytes 393224 | tf_op jit(solution)/shard_map/ppermute | solution.py:331
  102.1 4.4 %collective-permute-done.13.refs_3_ = bf16[160,512]{1,0:T(8,128)(2,1)S(1)} collective-permute-done((bf16[160,512]{1,0:T(8,128)(2,1)S(1)}, bf16[160,512]{1,0:T(8,128)(2,1)S(1)}, u32[]{:S(2)}, u32[]{:S(2)}) %collective-permute-start.13) | collective-permute-done | bytes 163872 | tf_op jit(solution)/shard_map/ppermute | solution.py:331
  107.0 3.2 %collective-permute-start.14 = (bf16[144,512]{1,0:T(8,128)(2,1)S(1)}, bf16[144,512]{1,0:T(8,128)(2,1)S(1)}, u32[]{:S(2)}, u32[]{:S(2)}) collective-permute-start(bf16[144,512]{1,0:T(8,128)(2,1)S(1)} %get-tuple-element.72.refs_1_), channel_id=1, source_target_pairs={{0,4},{1,5},{2,6},{3,7},{4,0},{5,1},{6,2},{7,3},{8,12},{9,13},{10,... | collective-permute-start | bytes 442376 | tf_op jit(solution)/shard_map/ppermute | solution.py:331
  110.7 2.8 %collective-permute-start.21 = (bf16[256,512]{1,0:T(8,128)(2,1)S(1)}, bf16[256,512]{1,0:T(8,128)(2,1)S(1)}, u32[]{:S(2)}, u32[]{:S(2)}) collective-permute-start(bf16[256,512]{1,0:T(8,128)(2,1)S(1)} %shard_map.140.refs_1_), channel_id=1, source_target_pairs={{0,17},{1,16},{2,19},{3,18},{4,21},{5,20},{6,23},{7,22},{8,25},{9,... | collective-permute-start | bytes 786440 | tf_op jit(solution)/shard_map/ppermute | solution.py:331
  116.0 5.0 %collective-permute-done.24.refs_2_ = bf16[128,512]{1,0:T(8,128)(2,1)S(1)} collective-permute-done((bf16[128,512]{1,0:T(8,128)(2,1)S(1)}, bf16[128,512]{1,0:T(8,128)(2,1)S(1)}, u32[]{:S(2)}, u32[]{:S(2)}) %collective-permute-start.24) | collective-permute-done | bytes 131104 | tf_op jit(solution)/shard_map/ppermute | solution.py:331
  123.6 2.6 %collective-permute-start.29 = (bf16[256,512]{1,0:T(8,128)(2,1)S(1)}, bf16[256,512]{1,0:T(8,128)(2,1)S(1)}, u32[]{:S(2)}, u32[]{:S(2)}) collective-permute-start(bf16[256,512]{1,0:T(8,128)(2,1)S(1)} %shard_map.141.refs_1_), channel_id=1, source_target_pairs={{0,17},{1,16},{2,19},{3,18},{4,21},{5,20},{6,23},{7,22},{8,25},{9,... | collective-permute-start | bytes 786440 | tf_op jit(solution)/shard_map/ppermute | solution.py:331
  127.9 6.6 %shard_map.136 = bf16[512,1024]{1,0:T(8,128)(2,1)} custom-call(s32[1]{0:T(128)} %bitcast.refs_0_, bf16[1024,1024]{1,0:T(8,128)(2,1)} %refs_1_.3, bf16[512,512]{1,0:T(8,128)(2,1)} %get-tuple-element.50.refs_3_.refs_2_, bf16[512,512]{1,0:T(8,128)(2,1)} %get-tuple-element.51.refs_3_, bf16[512,512]{1,0:T(8,128)(2,1)} %add_convert_fusion.2.refs_4_, ...), custom_call_target="tpu_custom_call" | custom-call | tf_op jit(solution)/shard_map/pallas_call | solution.py:60
  134.5 2.0 %shard_map.142 = bf16[1024,1024]{1,0:T(8,128)(2,1)} custom-call(s32[3]{0:T(128)S(1)} %pad_add_fusion.1.refs_0_, bf16[256,512]{1,0:T(8,128)(2,1)S(1)} %shard_map.140.refs_1_, bf16[256,512]{1,0:T(8,128)(2,1)S(1)} %collective-permute-done.21.refs_2_, bf16[256,512]{1,0:T(8,128)(2,1)S(1)} %collective-permute-done.22.refs_3_, ...), custom_call_target="tpu_custom_call" | custom-call | tf_op jit(solution)/shard_map/pallas_call | solution.py:81
  136.6 1.7 %collective-permute-done.30.refs_3_ = bf16[256,512]{1,0:T(8,128)(2,1)S(1)} collective-permute-done((bf16[256,512]{1,0:T(8,128)(2,1)S(1)}, bf16[256,512]{1,0:T(8,128)(2,1)S(1)}, u32[]{:S(2)}, u32[]{:S(2)}) %collective-permute-start.30) | collective-permute-done | bytes 262176 | tf_op jit(solution)/shard_map/ppermute | solution.py:331
  141.0 2.0 %shard_map.143 = bf16[1024,1024]{1,0:T(8,128)(2,1)} custom-call(s32[3]{0:T(128)S(1)} %pad_add_fusion.1.refs_0_, bf16[256,512]{1,0:T(8,128)(2,1)S(1)} %shard_map.141.refs_1_, bf16[256,512]{1,0:T(8,128)(2,1)S(1)} %collective-permute-done.29.refs_2_, bf16[256,512]{1,0:T(8,128)(2,1)S(1)} %collective-permute-done.30.refs_3_, ...), custom_call_target="tpu_custom_call" | custom-call | tf_op jit(solution)/shard_map/pallas_call | solution.py:81
  (110 shorter events, 23.1 us)
Async XLA Ops:
  4.0 21.0 %collective-permute-start = (bf16[8,1024]{1,0:T(8,128)(2,1)}, bf16[8,1024]{1,0:T(8,128)(2,1)S(1)}, u32[]{:S(2)}, u32[]{:S(2)}) collective-permute-start(bf16[8,1024]{1,0:T(8,128)(2,1)} %get-tuple-element.48), channel_id=1, source_target_pairs={{0,4},{1,5},{2,6},{3,7},{4,0},{5,1},{6,2},{7,3},{8,12},{9,13},{10,... | collective-permute-start | bytes 49160 | tf_op jit(solution)/shard_map/ppermute | solution.py:331
  8.1 16.9 %collective-permute-start.1 = (bf16[8,1024]{1,0:T(8,128)(2,1)}, bf16[8,1024]{1,0:T(8,128)(2,1)S(1)}, u32[]{:S(2)}, u32[]{:S(2)}) collective-permute-start(bf16[8,1024]{1,0:T(8,128)(2,1)} %get-tuple-element.48), channel_id=1, source_target_pairs={{0,2},{1,3},{2,0},{3,1},{4,6},{5,7},{6,4},{7,5},{8,10},{9,11},{10,... | collective-permute-start | bytes 49160 | tf_op jit(solution)/shard_map/ppermute | solution.py:331
  9.6 15.3 %collective-permute-start.2 = (bf16[8,1024]{1,0:T(8,128)(2,1)}, bf16[8,1024]{1,0:T(8,128)(2,1)S(1)}, u32[]{:S(2)}, u32[]{:S(2)}) collective-permute-start(bf16[8,1024]{1,0:T(8,128)(2,1)} %get-tuple-element.48), channel_id=1, source_target_pairs={{0,6},{1,7},{2,4},{3,5},{4,2},{5,3},{6,0},{7,1},{8,14},{9,15},{10,... | collective-permute-start | bytes 49160 | tf_op jit(solution)/shard_map/ppermute | solution.py:331
  9.6 33.8 %all-to-all-start = ((bf16[32,16,1024]{2,1,0:T(8,128)(2,1)}), bf16[32,16,1024]{2,1,0:T(8,128)(2,1)}, u32[]{:S(2)}, u32[]{:S(2)}) async-start(bf16[32,16,1024]{2,1,0:T(8,128)(2,1)} %bitcast.52), calls=%async_computation | async-start | bytes 2097152 | tf_op jit(solution)/shard_map/all_to_all | solution.py:345
  16.5 42.0 %collective-permute-start.7 = (bf16[1024,512]{1,0:T(8,128)(2,1)S(1)}, bf16[1024,512]{1,0:T(8,128)(2,1)S(1)}, u32[]{:S(2)}, u32[]{:S(2)}) collective-permute-start(bf16[1024,512]{1,0:T(8,128)(2,1)S(1)} %bitcast.49), channel_id=1, source_target_pairs={{0,8},{1,9},{2,10},{3,11},{4,12},{5,13},{6,14},{7,15},{8,0},{9,1},... | collective-permute-start | bytes 3145736 | tf_op jit(solution)/shard_map/ppermute | solution.py:331
  25.0 6.9 %collective-permute-start.3 = (bf16[32,1024]{1,0:T(8,128)(2,1)S(1)}, bf16[32,1024]{1,0:T(8,128)(2,1)S(1)}, u32[]{:S(2)}, u32[]{:S(2)}) collective-permute-start(bf16[32,1024]{1,0:T(8,128)(2,1)S(1)} %pad_maximum_fusion), channel_id=1, source_target_pairs={{0,1},{1,0},{2,3},{3,2},{4,5},{5,4},{6,7},{7,6},{8,9},{9,8},{10,11... | collective-permute-start | bytes 196616 | tf_op jit(solution)/shard_map/ppermute | solution.py:331
  32.0 6.5 %collective-permute-start.4 = (bf16[64,1024]{1,0:T(8,128)(2,1)S(1)}, bf16[64,1024]{1,0:T(8,128)(2,1)S(1)}, u32[]{:S(2)}, u32[]{:S(2)}) collective-permute-start(bf16[64,1024]{1,0:T(8,128)(2,1)S(1)} %get-tuple-element.94), channel_id=1, source_target_pairs={{0,16},{1,17},{2,18},{3,19},{4,20},{5,21},{6,22},{7,23},{8,24},{9,... | collective-permute-start | bytes 393224 | tf_op jit(solution)/shard_map/ppermute | solution.py:331
  53.3 11.6 %collective-permute-start.6 = (bf16[1024,512]{1,0:T(8,128)(2,1)}, bf16[1024,512]{1,0:T(8,128)(2,1)}, u32[]{:S(2)}, u32[]{:S(2)}) collective-permute-start(bf16[1024,512]{1,0:T(8,128)(2,1)} %get-tuple-element.60.refs_1_), channel_id=1, source_target_pairs={{0,8},{1,9},{2,10},{3,11},{4,12},{5,13},{6,14},{7,15},{8,0},{9,1},... | collective-permute-start | bytes 3145736 | tf_op jit(solution)/shard_map/ppermute | solution.py:331
  53.4 5.1 %collective-permute-start.8 = (bf16[512,512]{1,0:T(8,128)(2,1)}, bf16[512,512]{1,0:T(8,128)(2,1)S(1)}, u32[]{:S(2)}, u32[]{:S(2)}) collective-permute-start(bf16[512,512]{1,0:T(8,128)(2,1)} %get-tuple-element.51.refs_3_), channel_id=1, source_target_pairs={{0,8},{1,9},{2,10},{3,11},{4,12},{5,13},{6,14},{7,15},{8,0},{9,1},... | collective-permute-start | bytes 1572872 | tf_op jit(solution)/shard_map/ppermute | solution.py:331
  53.9 74.0 %all-to-all-start.1 = ((bf16[32,16,1024]{2,1,0:T(8,128)(2,1)}), bf16[32,16,1024]{2,1,0:T(8,128)(2,1)}, u32[]{:S(2)}, u32[]{:S(2)}) async-start(bf16[32,16,1024]{2,1,0:T(8,128)(2,1)} %bitcast.51), calls=%async_computation.1 | async-start | bytes 2097152 | tf_op jit(solution)/shard_map/all_to_all | solution.py:392
  58.3 6.5 %collective-permute-start.9 = (bf16[2,128,512]{2,1,0:T(8,128)(2,1)}, bf16[2,128,512]{2,1,0:T(8,128)(2,1)S(1)}, u32[]{:S(2)}, u32[]{:S(2)}) collective-permute-start(bf16[2,128,512]{2,1,0:T(8,128)(2,1)} %get-tuple-element.63), channel_id=1, source_target_pairs={{0,8},{1,9},{2,10},{3,11},{4,12},{5,13},{6,14},{7,15},{8,0},{9,1},... | collective-permute-start | bytes 786440 | tf_op jit(solution)/shard_map/ppermute | solution.py:331
  61.4 18.5 %collective-permute-start.15 = (bf16[256,512]{1,0:T(8,128)(2,1)S(1)}, bf16[256,512]{1,0:T(8,128)(2,1)S(1)}, u32[]{:S(2)}, u32[]{:S(2)}) collective-permute-start(bf16[256,512]{1,0:T(8,128)(2,1)S(1)} %get-tuple-element.59), channel_id=1, source_target_pairs={{0,17},{1,16},{2,19},{3,18},{4,21},{5,20},{6,23},{7,22},{8,25},{9,... | collective-permute-start | bytes 786440 | tf_op jit(solution)/shard_map/ppermute | solution.py:331
  63.9 20.0 %collective-permute-start.16 = (bf16[256,512]{1,0:T(8,128)(2,1)}, bf16[256,512]{1,0:T(8,128)(2,1)S(1)}, u32[]{:S(2)}, u32[]{:S(2)}) collective-permute-start(bf16[256,512]{1,0:T(8,128)(2,1)} %get-tuple-element.58), channel_id=1, source_target_pairs={{0,16},{1,17},{2,18},{3,19},{4,20},{5,21},{6,22},{7,23},{8,24},{9,... | collective-permute-start | bytes 786440 | tf_op jit(solution)/shard_map/ppermute | solution.py:331
  64.5 19.4 %collective-permute-start.17 = (bf16[256,512]{1,0:T(8,128)(2,1)}, bf16[256,512]{1,0:T(8,128)(2,1)S(1)}, u32[]{:S(2)}, u32[]{:S(2)}) collective-permute-start(bf16[256,512]{1,0:T(8,128)(2,1)} %get-tuple-element.57), channel_id=1, source_target_pairs={{0,1},{1,0},{2,3},{3,2},{4,5},{5,4},{6,7},{7,6},{8,9},{9,8},{10,11... | collective-permute-start | bytes 786440 | tf_op jit(solution)/shard_map/ppermute | solution.py:331
  68.4 25.8 %collective-permute-start.10 = (bf16[320,512]{1,0:T(8,128)(2,1)}, bf16[320,512]{1,0:T(8,128)(2,1)S(1)}, u32[]{:S(2)}, u32[]{:S(2)}) collective-permute-start(bf16[320,512]{1,0:T(8,128)(2,1)} %get-tuple-element.66), channel_id=1, source_target_pairs={{0,17},{1,16},{2,19},{3,18},{4,21},{5,20},{6,23},{7,22},{8,25},{9,... | collective-permute-start | bytes 983048 | tf_op jit(solution)/shard_map/ppermute | solution.py:331
  71.0 27.6 %collective-permute-start.11 = (bf16[320,512]{1,0:T(8,128)(2,1)}, bf16[320,512]{1,0:T(8,128)(2,1)S(1)}, u32[]{:S(2)}, u32[]{:S(2)}) collective-permute-start(bf16[320,512]{1,0:T(8,128)(2,1)} %get-tuple-element.67), channel_id=1, source_target_pairs={{0,16},{1,17},{2,18},{3,19},{4,20},{5,21},{6,22},{7,23},{8,24},{9,... | collective-permute-start | bytes 983048 | tf_op jit(solution)/shard_map/ppermute | solution.py:331
  79.9 18.6 %collective-permute-start.12 = (bf16[320,512]{1,0:T(8,128)(2,1)}, bf16[320,512]{1,0:T(8,128)(2,1)S(1)}, u32[]{:S(2)}, u32[]{:S(2)}) collective-permute-start(bf16[320,512]{1,0:T(8,128)(2,1)} %get-tuple-element.68), channel_id=1, source_target_pairs={{0,1},{1,0},{2,3},{3,2},{4,5},{5,4},{6,7},{7,6},{8,9},{9,8},{10,11... | collective-permute-start | bytes 983048 | tf_op jit(solution)/shard_map/ppermute | solution.py:331
  84.7 5.4 %collective-permute-start.18 = (bf16[128,512]{1,0:T(8,128)(2,1)S(1)}, bf16[128,512]{1,0:T(8,128)(2,1)S(1)}, u32[]{:S(2)}, u32[]{:S(2)}) collective-permute-start(bf16[128,512]{1,0:T(8,128)(2,1)S(1)} %get-tuple-element.79), channel_id=1, source_target_pairs={{0,2},{1,3},{2,0},{3,1},{4,6},{5,7},{6,4},{7,5},{8,10},{9,11},{10,... | collective-permute-start | bytes 393224 | tf_op jit(solution)/shard_map/ppermute | solution.py:331
  90.6 9.1 %collective-permute-start.19 = (bf16[128,512]{1,0:T(8,128)(2,1)S(1)}, bf16[128,512]{1,0:T(8,128)(2,1)S(1)}, u32[]{:S(2)}, u32[]{:S(2)}) collective-permute-start(bf16[128,512]{1,0:T(8,128)(2,1)S(1)} %shard_map.138.refs_1_), channel_id=1, source_target_pairs={{0,4},{1,5},{2,6},{3,7},{4,0},{5,1},{6,2},{7,3},{8,12},{9,13},{10,... | collective-permute-start | bytes 393224 | tf_op jit(solution)/shard_map/ppermute | solution.py:331
  99.3 7.1 %collective-permute-start.13 = (bf16[160,512]{1,0:T(8,128)(2,1)S(1)}, bf16[160,512]{1,0:T(8,128)(2,1)S(1)}, u32[]{:S(2)}, u32[]{:S(2)}) collective-permute-start(bf16[160,512]{1,0:T(8,128)(2,1)S(1)} %get-tuple-element.71), channel_id=1, source_target_pairs={{0,2},{1,3},{2,0},{3,1},{4,6},{5,7},{6,4},{7,5},{8,10},{9,11},{10,... | collective-permute-start | bytes 491528 | tf_op jit(solution)/shard_map/ppermute | solution.py:331
  100.3 9.8 %collective-permute-start.20 = (bf16[128,512]{1,0:T(8,128)(2,1)S(1)}, bf16[128,512]{1,0:T(8,128)(2,1)S(1)}, u32[]{:S(2)}, u32[]{:S(2)}) collective-permute-start(bf16[128,512]{1,0:T(8,128)(2,1)S(1)} %shard_map.139.refs_1_), channel_id=1, source_target_pairs={{0,2},{1,3},{2,0},{3,1},{4,6},{5,7},{6,4},{7,5},{8,10},{9,11},{10,... | collective-permute-start | bytes 393224 | tf_op jit(solution)/shard_map/ppermute | solution.py:331
  107.0 8.3 %collective-permute-start.14 = (bf16[144,512]{1,0:T(8,128)(2,1)S(1)}, bf16[144,512]{1,0:T(8,128)(2,1)S(1)}, u32[]{:S(2)}, u32[]{:S(2)}) collective-permute-start(bf16[144,512]{1,0:T(8,128)(2,1)S(1)} %get-tuple-element.72.refs_1_), channel_id=1, source_target_pairs={{0,4},{1,5},{2,6},{3,7},{4,0},{5,1},{6,2},{7,3},{8,12},{9,13},{10,... | collective-permute-start | bytes 442376 | tf_op jit(solution)/shard_map/ppermute | solution.py:331
  110.7 10.8 %collective-permute-start.21 = (bf16[256,512]{1,0:T(8,128)(2,1)S(1)}, bf16[256,512]{1,0:T(8,128)(2,1)S(1)}, u32[]{:S(2)}, u32[]{:S(2)}) collective-permute-start(bf16[256,512]{1,0:T(8,128)(2,1)S(1)} %shard_map.140.refs_1_), channel_id=1, source_target_pairs={{0,17},{1,16},{2,19},{3,18},{4,21},{5,20},{6,23},{7,22},{8,25},{9,... | collective-permute-start | bytes 786440 | tf_op jit(solution)/shard_map/ppermute | solution.py:331
  113.5 9.5 %collective-permute-start.22 = (bf16[256,512]{1,0:T(8,128)(2,1)S(1)}, bf16[256,512]{1,0:T(8,128)(2,1)S(1)}, u32[]{:S(2)}, u32[]{:S(2)}) collective-permute-start(bf16[256,512]{1,0:T(8,128)(2,1)S(1)} %shard_map.140.refs_1_), channel_id=1, source_target_pairs={{0,16},{1,17},{2,18},{3,19},{4,20},{5,21},{6,22},{7,23},{8,24},{9,... | collective-permute-start | bytes 786440 | tf_op jit(solution)/shard_map/ppermute | solution.py:331
  113.5 9.6 %collective-permute-start.23 = (bf16[256,512]{1,0:T(8,128)(2,1)S(1)}, bf16[256,512]{1,0:T(8,128)(2,1)S(1)}, u32[]{:S(2)}, u32[]{:S(2)}) collective-permute-start(bf16[256,512]{1,0:T(8,128)(2,1)S(1)} %shard_map.140.refs_1_), channel_id=1, source_target_pairs={{0,1},{1,0},{2,3},{3,2},{4,5},{5,4},{6,7},{7,6},{8,9},{9,8},{10,11... | collective-permute-start | bytes 786440 | tf_op jit(solution)/shard_map/ppermute | solution.py:331
  115.9 5.0 %collective-permute-start.24 = (bf16[128,512]{1,0:T(8,128)(2,1)S(1)}, bf16[128,512]{1,0:T(8,128)(2,1)S(1)}, u32[]{:S(2)}, u32[]{:S(2)}) collective-permute-start(bf16[128,512]{1,0:T(8,128)(2,1)S(1)} %get-tuple-element.80.refs_1_), channel_id=1, source_target_pairs={{0,2},{1,3},{2,0},{3,1},{4,6},{5,7},{6,4},{7,5},{8,10},{9,11},{10,... | collective-permute-start | bytes 393224 | tf_op jit(solution)/shard_map/ppermute | solution.py:331
  123.1 3.9 %collective-permute-start.26 = (bf16[256,512]{1,0:T(8,128)(2,1)S(1)}, bf16[256,512]{1,0:T(8,128)(2,1)S(1)}, u32[]{:S(2)}, u32[]{:S(2)}) collective-permute-start(bf16[256,512]{1,0:T(8,128)(2,1)S(1)} %collective-permute-done.21.refs_2_), channel_id=1, source_target_pairs={{0,8},{1,9},{2,10},{3,11},{4,12},{5,13},{6,14},{7,15},{8,0},{9,1},... | collective-permute-start | bytes 786440 | tf_op jit(solution)/shard_map/ppermute | solution.py:331
  123.6 13.0 %collective-permute-start.29 = (bf16[256,512]{1,0:T(8,128)(2,1)S(1)}, bf16[256,512]{1,0:T(8,128)(2,1)S(1)}, u32[]{:S(2)}, u32[]{:S(2)}) collective-permute-start(bf16[256,512]{1,0:T(8,128)(2,1)S(1)} %shard_map.141.refs_1_), channel_id=1, source_target_pairs={{0,17},{1,16},{2,19},{3,18},{4,21},{5,20},{6,23},{7,22},{8,25},{9,... | collective-permute-start | bytes 786440 | tf_op jit(solution)/shard_map/ppermute | solution.py:331
  126.2 8.3 %collective-permute-start.27 = (bf16[256,512]{1,0:T(8,128)(2,1)S(1)}, bf16[256,512]{1,0:T(8,128)(2,1)S(1)}, u32[]{:S(2)}, u32[]{:S(2)}) collective-permute-start(bf16[256,512]{1,0:T(8,128)(2,1)S(1)} %collective-permute-done.22.refs_3_), channel_id=1, source_target_pairs={{0,8},{1,9},{2,10},{3,11},{4,12},{5,13},{6,14},{7,15},{8,0},{9,1},... | collective-permute-start | bytes 786440 | tf_op jit(solution)/shard_map/ppermute | solution.py:331
  126.2 8.3 %collective-permute-start.28 = (bf16[256,512]{1,0:T(8,128)(2,1)S(1)}, bf16[256,512]{1,0:T(8,128)(2,1)S(1)}, u32[]{:S(2)}, u32[]{:S(2)}) collective-permute-start(bf16[256,512]{1,0:T(8,128)(2,1)S(1)} %collective-permute-done.23.refs_4_), channel_id=1, source_target_pairs={{0,8},{1,9},{2,10},{3,11},{4,12},{5,13},{6,14},{7,15},{8,0},{9,1},... | collective-permute-start | bytes 786440 | tf_op jit(solution)/shard_map/ppermute | solution.py:331
  126.7 11.5 %collective-permute-start.30 = (bf16[256,512]{1,0:T(8,128)(2,1)S(1)}, bf16[256,512]{1,0:T(8,128)(2,1)S(1)}, u32[]{:S(2)}, u32[]{:S(2)}) collective-permute-start(bf16[256,512]{1,0:T(8,128)(2,1)S(1)} %shard_map.141.refs_1_), channel_id=1, source_target_pairs={{0,16},{1,17},{2,18},{3,19},{4,20},{5,21},{6,22},{7,23},{8,24},{9,... | collective-permute-start | bytes 786440 | tf_op jit(solution)/shard_map/ppermute | solution.py:331
  126.9 11.4 %collective-permute-start.31 = (bf16[256,512]{1,0:T(8,128)(2,1)S(1)}, bf16[256,512]{1,0:T(8,128)(2,1)S(1)}, u32[]{:S(2)}, u32[]{:S(2)}) collective-permute-start(bf16[256,512]{1,0:T(8,128)(2,1)S(1)} %shard_map.141.refs_1_), channel_id=1, source_target_pairs={{0,1},{1,0},{2,3},{3,2},{4,5},{5,4},{6,7},{7,6},{8,9},{9,8},{10,11... | collective-permute-start | bytes 786440 | tf_op jit(solution)/shard_map/ppermute | solution.py:331
  (20 other events, 120.0 us)

commit v8 on v7

--- a/solution.py
+++ b/solution.py
@@ -29,7 +29,7 @@
     return lax.dot_general(left, right, (((0,), (0,)), ((), ())), preferred_element_type=F32)
 
 
-def run(body, scalars, ins, outs, flops=0, scratch=(), limit=0):
+def run(body, scalars, ins, outs, flops=0, scratch=(), limit=0, halved=()):
     n_in, n_out = len(ins), len(outs)
     outs = [jax.ShapeDtypeStruct(shape, dtype) for shape, dtype in outs]
 
@@ -40,7 +40,17 @@
         in_buf, out_buf = refs[:n_in], refs[n_in : n_in + n_out]
         extra, (in_sem, out_sem) = refs[n_in + n_out : -2], refs[-2:]
         loads = [pltpu.make_async_copy(in_hbm[i], in_buf[i], in_sem.at[i]) for i in range(n_in)]
-        stores = [pltpu.make_async_copy(out_buf[i], out_hbm[i], out_sem.at[i]) for i in range(n_out)]
+        stores = {}
+        for i in range(n_out):
+            cut = out_buf[i].shape[-1] // 2
+            if i in halved:
+                for part in range(2):
+                    cols = slice(part * cut, (part + 1) * cut)
+                    stores[i, part] = pltpu.make_async_copy(
+                        out_buf[i].at[:, cols], out_hbm[i].at[:, cols], out_sem.at[i + part * n_out]
+                    )
+            else:
+                stores[i] = pltpu.make_async_copy(out_buf[i], out_hbm[i], out_sem.at[i])
         for load in loads:
             load.start()
 
@@ -53,7 +63,7 @@
                 stores[i].start()
 
         body(scalar_ref, in_buf, out_buf, need, emit, *extra)
-        for store in stores:
+        for store in stores.values():
             store.wait()
 
     held = sum(a.size * a.dtype.itemsize for a in [*ins, *outs])
@@ -64,7 +74,7 @@
         out_specs=[HBM] * n_out,
         scratch_shapes=[pltpu.VMEM(a.shape, a.dtype) for a in [*ins, *outs]]
         + list(scratch)
-        + [pltpu.SemaphoreType.DMA((n_in,)), pltpu.SemaphoreType.DMA((n_out,))],
+        + [pltpu.SemaphoreType.DMA((n_in,)), pltpu.SemaphoreType.DMA((2 * n_out,))],
         compiler_params=pltpu.CompilerParams(vmem_limit_bytes=limit or held + (8 << 20)),
         cost_estimate=pl.CostEstimate(flops=0, bytes_accessed=0, transcendentals=0),
     )(scalars, *ins)
@@ -84,7 +94,7 @@
         in_specs=[SMEM] + [VMEM] * n_in,
         out_specs=[VMEM] * n_out,
         scratch_shapes=list(scratch),
-        compiler_params=pltpu.CompilerParams(vmem_limit_bytes=held + (8 << 20)),
+        compiler_params=pltpu.CompilerParams(vmem_limit_bytes=held + (3 << 20)),
         cost_estimate=pl.CostEstimate(flops=0, bytes_accessed=0, transcendentals=0),
     )(scalars, *ins)
 
@@ -119,23 +129,23 @@
 
 
 def seed_body(side, ins, outs, need, emit, d_pre_all, aggregate):
-    counts, arrived, hubs, summed, inv_deg, w_neigh, own_pre, cotangent, counts_t = ins
+    counts, arrived, hubs, counts_own, features, inv_deg, w_neigh, own_pre, cotangent, counts_t = ins
     hidden, d_pre, d_agg, d_pre_other, aggregate_t, d_arrived, hub_keep, hub_send = outs
     n_local, width = cotangent.shape
     n_slots = arrived.shape[0]
     n_hubs = hubs.shape[0]
     half = width // 2
-    need(0, 1, 2, 3, 4)
+    need(3, 4, 0, 1, 2, 5)
     inv = inv_deg[...]
     for c in range(0, width, CHUNK):
         cols = slice(c, c + CHUNK)
-        total = summed[:, cols] + mul(counts[:, :n_slots], arrived[:, cols])
+        total = mul(counts_own[...], features[:, cols]) + mul(counts[:, :n_slots], arrived[:, cols])
         total = total + mul(counts[:, n_slots:], hubs[:, cols])
         mean = total * inv
         aggregate[:, cols] = mean.astype(BF16)
         aggregate_t[cols, :] = mean.T.astype(BF16)
     emit(4)
-    need(5, 6, 7)
+    need(6, 7, 8)
     for c in range(0, width, CHUNK):
         cols = slice(c, c + CHUNK)
         pre = own_pre[:, cols] + mul(aggregate[...], w_neigh[:, cols])
@@ -155,7 +165,7 @@
             d_pre_other[:, part] = grad
 
     emit(3, 1, 0)
-    need(8)
+    need(9)
     for c in range(0, width, CHUNK):
         cols = slice(c, c + CHUNK)
         grad = (mul_t(d_pre_all[...], w_neigh[cols, :]) * inv).astype(BF16)
@@ -165,7 +175,9 @@
         part = slice(c % half, c % half + CHUNK)
         hub_keep[c // half, :, part] = d_hubs[: n_hubs // 2]
         hub_send[c // half, :, part] = d_hubs[n_hubs // 2 :].astype(BF16)
-    emit(5, 7, 6, 2)
+        if c + CHUNK == half or c + CHUNK == width:
+            emit((5, c // half), (2, c // half))
+    emit(7, 6)
 
 
 def hub_rows_of(total, k, rows):
@@ -346,7 +358,8 @@
         outgoing.reshape(n_dev, capacity, width), AXES, split_axis=0, concat_axis=0, tiled=True
     ).reshape(n_slots, width)
 
-    hubs = jnp.concatenate([own_hubs] + [swap(own_hubs, spread(z_bits[::-1], k)) for k in range(1, n_z)], 0)
+    along = [swap(own_hubs, spread(z_bits[::-1], k)) for k in range(n_z - 1, 0, -1)]
+    hubs = jnp.concatenate([own_hubs] + along[::-1], 0)
     for mask in xy_bits + [core]:
         hubs = jnp.concatenate([hubs, swap(hubs, mask)], 0)
     feat_t = features.T
@@ -368,13 +381,12 @@
     counts_own, counts_own_t = count(0, n_local)
     counts_far, counts_far_t = count(n_local, hub_base + n_hubs)
     inv_deg = 1.0 / degrees.astype(F32)[:, None]
-    summed = mul(counts_own, features)
     own_pre = mul(features, w_self) + bias_term[None, :]
 
     hidden, d_pre, d_agg, d_other, agg_t, d_arrived, hub_keep, hub_send = run(
         seed_body,
         side[None],
-        [counts_far, arrived, hubs, summed, inv_deg, w_neigh, own_pre, cotangent, counts_far_t],
+        [counts_far, arrived, hubs, counts_own, features, inv_deg, w_neigh, own_pre, cotangent, counts_far_t],
         [
             (wide, BF16),
             ((n_local, half), BF16),
@@ -388,6 +400,7 @@
         flops=4 * n_local * width * (width + n_slots + n_hubs),
         scratch=[pltpu.VMEM(wide, BF16), pltpu.VMEM(wide, BF16)],
         limit=VMEM_LIMIT,
+        halved=(2, 5),
     )
     returned = lax.all_to_all(
         d_arrived.reshape(n_dev, capacity, width), AXES, split_axis=0, concat_axis=0, tiled=True

time: 143 us -> 143 us (level)
  other arithmetic: 11.1 us -> 14 us
  matrix products: 6.72 us -> 4.16 us
    convert_element_type x3 -> x4, other arithmetic: 10.7 us -> 13.5 us  [count(): return (found.astype(BF16), found_t.astype(BF16))]
    dot_general x2 -> x1, matrix products: 6.72 us -> 4.16 us  [mul(): return jnp.dot(left, right, preferred_element_type=F32)]
  transfers between devices with their start and end apart: 38 -> 38, of which waited for: 16 -> 18; matrix products, arithmetic and copies ran while one was open for 14% -> 14% of each run, Pallas kernels for 20% -> 20%
where the time goes in v8:
time: 143 us
  starting transfers between devices  46 us (32%)
  waiting for transfers between devices  41.3 us (29%)
  Pallas kernels  34 us (24%)
  other arithmetic  14 us (10%)
  matrix products  4.16 us (3%)
  local copies, waits for them, and re-layouts  2.41 us (2%)
    ppermute x36, waiting for transfers between devices, swap(): return lax.ppermute(value, AXES, [(i, i ^ mask) for i in range(n_dev)])  40.2 us
    ppermute x36, starting transfers between devices, swap(): return lax.ppermute(value, AXES, [(i, i ^ mask) for i in range(n_dev)])  35.1 us
    pallas_call x3, Pallas kernels, run(): pl.pallas_call(kernel, out_shape=outs, in_specs=[SMEM] + [HBM] * n_in, ou...  19.3 us
    pallas_call x12, Pallas kernels, run_inside(): pl.pallas_call(kernel, out_shape=outs, in_specs=[SMEM] + [VMEM] * n_in, o...  14.6 us
    convert_element_type x4, other arithmetic, count(): return (found.astype(BF16), found_t.astype(BF16))  13.5 us
    all_to_all x1, starting transfers between devices, on_device(): lax.all_to_all(outgoing.reshape(n_dev, capacity, width), AXES, split_axis...  6.2 us
    all_to_all x1, starting transfers between devices, on_device(): lax.all_to_all(d_arrived.reshape(n_dev, capacity, width), AXES, split_axi...  4.66 us
    dot_general x1, matrix products, mul(): return jnp.dot(left, right, preferred_element_type=F32)  4.16 us
  transfers between devices with their start and end apart: 38, of which 18 were waited for; matrix products, arithmetic and copies ran while one was open for 14% of the time, Pallas kernels for 20%

profile of v8, /device:TPU:0, one launch (start us, length us, event | category | flops | bytes accessed | tf_op | source)
XLA Modules:
  0.0 142.9 jit_solution(1601873003086239918)
XLA Ops:
  0.7 3.3 %shard_map.129 = (bf16[512,1024]{1,0:T(8,128)(2,1)}, bf16[8,1024]{1,0:T(8,128)(2,1)}, s32[1,512]{1,0:T(1,128)}) custom-call(s32[1]{0:T(128)} %bitcast.refs_0_, bf16[512,1024]{1,0:T(8,128)(2,1)} %refs_5_.1, s32[1,512]{1,0:T(1,128)} %refs_2_.1, s32[1,32]{1,0:T(1,128)} %refs_3_.1, s32[1,8]{1,0:T(1,128)} %bitcast.117), custom_call_target="tpu_custom_call" | custom-call | tf_op jit(solution)/shard_map/pallas_call | solution.py:70
  4.0 4.1 %collective-permute-start = (bf16[8,1024]{1,0:T(8,128)(2,1)}, bf16[8,1024]{1,0:T(8,128)(2,1)S(1)}, u32[]{:S(2)}, u32[]{:S(2)}) collective-permute-start(bf16[8,1024]{1,0:T(8,128)(2,1)} %get-tuple-element.48), channel_id=1, source_target_pairs={{0,4},{1,5},{2,6},{3,7},{4,0},{5,1},{6,2},{7,3},{8,12},{9,13},{10,... | collective-permute-start | bytes 49160 | tf_op jit(solution)/shard_map/ppermute | solution.py:343
  8.1 1.6 %collective-permute-start.1 = (bf16[8,1024]{1,0:T(8,128)(2,1)}, bf16[8,1024]{1,0:T(8,128)(2,1)S(1)}, u32[]{:S(2)}, u32[]{:S(2)}) collective-permute-start(bf16[8,1024]{1,0:T(8,128)(2,1)} %get-tuple-element.48), channel_id=1, source_target_pairs={{0,2},{1,3},{2,0},{3,1},{4,6},{5,7},{6,4},{7,5},{8,10},{9,11},{10,... | collective-permute-start | bytes 49160 | tf_op jit(solution)/shard_map/ppermute | solution.py:343
  9.7 6.2 %all-to-all-start = ((bf16[32,16,1024]{2,1,0:T(8,128)(2,1)}), bf16[32,16,1024]{2,1,0:T(8,128)(2,1)}, u32[]{:S(2)}, u32[]{:S(2)}) async-start(bf16[32,16,1024]{2,1,0:T(8,128)(2,1)} %bitcast.51), calls=%async_computation | async-start | bytes 2097152 | tf_op jit(solution)/shard_map/all_to_all | solution.py:357
  17.1 4.5 %add_convert_fusion.1.refs_1_ = bf16[512,768]{1,0:T(8,128)(2,1)} fusion(s32[768]{0:T(1024)S(1)} %iota_add_fusion, s32[512]{0:T(512)S(1)} %bitcast.86, s32[512]{0:T(512)S(1)} %bitcast.88, s32[512]{0:T(512)S(1)} %bitcast.90, s32[512]{0:T(512)S(1)} %bitcast.92, s32[512]{0:T(512)S(1)} %bitcast.94, s32[512]{0:T(512)S(1)} %bitcast.96, s32[512]{0:T(512)S(1)} %bitcast.98, ...), kind=kLoop, calls=%fused_computation.1 | loop fusion | flops 18874368 | bytes 822272 | tf_op jit(solution)/shard_map/convert_element_type | solution.py:379
  21.5 3.4 %add_convert_fusion.refs_10_ = bf16[768,512]{1,0:T(8,128)(2,1)} fusion(s32[512]{0:T(512)S(1)} %bitcast.54, s32[512]{0:T(512)S(1)} %bitcast.56, s32[512]{0:T(512)S(1)} %bitcast.58, s32[512]{0:T(512)S(1)} %bitcast.60, s32[512]{0:T(512)S(1)} %bitcast.62, s32[512]{0:T(512)S(1)} %bitcast.64, s32[512]{0:T(512)S(1)} %bitcast.66, s32[512]{0:T(512)S(1)} %bitcast.68, ...), kind=kLoop, calls=%fused_computation | loop fusion | flops 18874368 | bytes 822272 | tf_op jit(solution)/shard_map/convert_element_type | solution.py:379
  25.0 1.7 %collective-permute-start.3 = (bf16[32,1024]{1,0:T(8,128)(2,1)S(1)}, bf16[32,1024]{1,0:T(8,128)(2,1)S(1)}, u32[]{:S(2)}, u32[]{:S(2)}) collective-permute-start(bf16[32,1024]{1,0:T(8,128)(2,1)S(1)} %pad_maximum_fusion), channel_id=1, source_target_pairs={{0,1},{1,0},{2,3},{3,2},{4,5},{5,4},{6,7},{7,6},{8,9},{9,8},{10,11... | collective-permute-start | bytes 196616 | tf_op jit(solution)/shard_map/ppermute | solution.py:343
  26.8 5.1 %collective-permute-done.3 = bf16[32,1024]{1,0:T(8,128)(2,1)S(1)} collective-permute-done((bf16[32,1024]{1,0:T(8,128)(2,1)S(1)}, bf16[32,1024]{1,0:T(8,128)(2,1)S(1)}, u32[]{:S(2)}, u32[]{:S(2)}) %collective-permute-start.3) | collective-permute-done | bytes 65568 | tf_op jit(solution)/shard_map/ppermute | solution.py:343
  32.6 4.2 %convolution_add_fusion.refs_8_ = f32[512,1024]{1,0:T(8,128)} fusion(bf16[512,1024]{1,0:T(8,128)(2,1)S(1)} %copy-done.7, bf16[1024,1024]{1,0:T(8,128)(2,1)} %refs_1_.3, f32[1024]{0:T(1024)S(1)} %copy-done.12), kind=kOutput, calls=%fused_computation.2 | convolution fusion | flops 1074266112 | bytes 5246976 | tf_op jit(solution)/shard_map/dot_general | solution.py:21
  36.7 1.7 %collective-permute-done.4 = bf16[64,1024]{1,0:T(8,128)(2,1)S(1)} collective-permute-done((bf16[64,1024]{1,0:T(8,128)(2,1)S(1)}, bf16[64,1024]{1,0:T(8,128)(2,1)S(1)}, u32[]{:S(2)}, u32[]{:S(2)}) %collective-permute-start.4) | collective-permute-done | bytes 131104 | tf_op jit(solution)/shard_map/ppermute | solution.py:343
  38.6 2.8 %add_convert_fusion.3.refs_4_ = bf16[512,512]{1,0:T(8,128)(2,1)} fusion(s32[512]{0:T(512)S(1)} %bitcast.87, s32[512]{0:T(512)S(1)} %bitcast.89, s32[512]{0:T(512)S(1)} %bitcast.91, s32[512]{0:T(512)S(1)} %bitcast.93, s32[512]{0:T(512)S(1)} %bitcast.95, s32[512]{0:T(512)S(1)} %bitcast.97, s32[512]{0:T(512)S(1)} %bitcast.99, s32[512]{0:T(512)S(1)} %bitcast.101, ...), kind=kLoop, calls=%fused_computation.20 | loop fusion | flops 12582912 | bytes 557056 | tf_op jit(solution)/shard_map/convert_element_type | solution.py:379
  43.4 9.4 %shard_map.130 = (bf16[512,1024]{1,0:T(8,128)(2,1)}, bf16[512,512]{1,0:T(8,128)(2,1)}, bf16[512,1024]{1,0:T(8,128)(2,1)}, bf16[512,512]{1,0:T(8,128)(2,1)}, bf16...) custom-call(s32[1]{0:T(128)} %bitcast.refs_0_, ...), custom_call_target="tpu_custom_call" | custom-call | tf_op jit(solution)/shard_map/pallas_call | solution.py:70
  53.4 4.7 %all-to-all-start.1 = ((bf16[32,16,1024]{2,1,0:T(8,128)(2,1)}), bf16[32,16,1024]{2,1,0:T(8,128)(2,1)}, u32[]{:S(2)}, u32[]{:S(2)}) async-start(bf16[32,16,1024]{2,1,0:T(8,128)(2,1)} %bitcast.50), calls=%async_computation.1 | async-start | bytes 2097152 | tf_op jit(solution)/shard_map/all_to_all | solution.py:405
  58.3 2.1 %shard_map.131 = (f32[256,512]{1,0:T(8,128)S(1)}, bf16[256,512]{1,0:T(8,128)(2,1)}, bf16[256,512]{1,0:T(8,128)(2,1)}, bf16[256,512]{1,0:T(8,128)(2,1)S(1)}) custom-call(s32[1]{0:T(128)} %bitcast.42.refs_0_, bf16[1024,512]{1,0:T(8,128)(2,1)S(1)} %bitcast.49, bf16[1024,512]{1,0:T(8,128)(2,1)S(1)} %collective-permute-done.7.refs_2_, ...), custom_call_target="tpu_custom_call" | custom-call | tf_op jit(solution)/shard_map/pallas_call | solution.py:91
  61.2 2.6 %collective-permute-start.15 = (bf16[256,512]{1,0:T(8,128)(2,1)S(1)}, bf16[256,512]{1,0:T(8,128)(2,1)S(1)}, u32[]{:S(2)}, u32[]{:S(2)}) collective-permute-start(bf16[256,512]{1,0:T(8,128)(2,1)S(1)} %get-tuple-element.59), channel_id=1, source_target_pairs={{0,17},{1,16},{2,19},{3,18},{4,21},{5,20},{6,23},{7,22},{8,25},{9,... | collective-permute-start | bytes 786440 | tf_op jit(solution)/shard_map/ppermute | solution.py:343
  64.7 3.5 %shard_map.132 = (f32[256,512]{1,0:T(8,128)S(1)}, bf16[320,512]{1,0:T(8,128)(2,1)}, bf16[320,512]{1,0:T(8,128)(2,1)}, bf16[320,512]{1,0:T(8,128)(2,1)}, f32[2,32,512]{2,1,0:T(8,128)S(1)}) custom-call(s32[1]{0:T(128)} %bitcast.42.refs_0_, bf16[1024,512]{1,0:T(8,128)(2,1)S(1)} %copy-done.1, bf16[1024,512]{1,0:T(8,128)(2,1)} %collective-permute-done.6.refs_2_, ...), custom_call_target="tpu_custom_call" | custom-call | tf_op jit(solution)/shard_map/pallas_call | solution.py:91
  68.3 2.6 %collective-permute-start.10 = (bf16[320,512]{1,0:T(8,128)(2,1)}, bf16[320,512]{1,0:T(8,128)(2,1)S(1)}, u32[]{:S(2)}, u32[]{:S(2)}) collective-permute-start(bf16[320,512]{1,0:T(8,128)(2,1)} %get-tuple-element.66), channel_id=1, source_target_pairs={{0,17},{1,16},{2,19},{3,18},{4,21},{5,20},{6,23},{7,22},{8,25},{9,... | collective-permute-start | bytes 983048 | tf_op jit(solution)/shard_map/ppermute | solution.py:343
  71.4 8.3 %collective-permute-done.15.refs_2_ = bf16[256,512]{1,0:T(8,128)(2,1)S(1)} collective-permute-done((bf16[256,512]{1,0:T(8,128)(2,1)S(1)}, bf16[256,512]{1,0:T(8,128)(2,1)S(1)}, u32[]{:S(2)}, u32[]{:S(2)}) %collective-permute-start.15) | collective-permute-done | bytes 262176 | tf_op jit(solution)/shard_map/ppermute | solution.py:343
  79.7 2.8 %add_convert_fusion.2.refs_4_ = bf16[512,512]{1,0:T(8,128)(2,1)} fusion(s32[512]{0:T(512)S(1)} %bitcast.55, s32[512]{0:T(512)S(1)} %bitcast.57, s32[512]{0:T(512)S(1)} %bitcast.59, s32[512]{0:T(512)S(1)} %bitcast.61, s32[512]{0:T(512)S(1)} %bitcast.63, s32[512]{0:T(512)S(1)} %bitcast.65, s32[512]{0:T(512)S(1)} %bitcast.67, s32[512]{0:T(512)S(1)} %bitcast.69, ...), kind=kLoop, calls=%fused_computation.3 | loop fusion | flops 12582912 | bytes 557056 | tf_op jit(solution)/shard_map/convert_element_type | solution.py:379
  85.6 4.2 %collective-permute-done.18.refs_2_ = bf16[128,512]{1,0:T(8,128)(2,1)S(1)} collective-permute-done((bf16[128,512]{1,0:T(8,128)(2,1)S(1)}, bf16[128,512]{1,0:T(8,128)(2,1)S(1)}, u32[]{:S(2)}, u32[]{:S(2)}) %collective-permute-start.18) | collective-permute-done | bytes 131104 | tf_op jit(solution)/shard_map/ppermute | solution.py:343
  90.4 3.6 %collective-permute-start.19 = (bf16[128,512]{1,0:T(8,128)(2,1)S(1)}, bf16[128,512]{1,0:T(8,128)(2,1)S(1)}, u32[]{:S(2)}, u32[]{:S(2)}) collective-permute-start(bf16[128,512]{1,0:T(8,128)(2,1)S(1)} %shard_map.138.refs_1_), channel_id=1, source_target_pairs={{0,4},{1,5},{2,6},{3,7},{4,0},{5,1},{6,2},{7,3},{8,12},{9,13},{10,... | collective-permute-start | bytes 393224 | tf_op jit(solution)/shard_map/ppermute | solution.py:343
  94.1 4.3 %collective-permute-done.11.refs_4_ = bf16[320,512]{1,0:T(8,128)(2,1)S(1)} collective-permute-done((bf16[320,512]{1,0:T(8,128)(2,1)}, bf16[320,512]{1,0:T(8,128)(2,1)S(1)}, u32[]{:S(2)}, u32[]{:S(2)}) %collective-permute-start.11) | collective-permute-done | bytes 327712 | tf_op jit(solution)/shard_map/ppermute | solution.py:343
  100.1 1.7 %collective-permute-start.20 = (bf16[128,512]{1,0:T(8,128)(2,1)S(1)}, bf16[128,512]{1,0:T(8,128)(2,1)S(1)}, u32[]{:S(2)}, u32[]{:S(2)}) collective-permute-start(bf16[128,512]{1,0:T(8,128)(2,1)S(1)} %shard_map.139.refs_1_), channel_id=1, source_target_pairs={{0,2},{1,3},{2,0},{3,1},{4,6},{5,7},{6,4},{7,5},{8,10},{9,11},{10,... | collective-permute-start | bytes 393224 | tf_op jit(solution)/shard_map/ppermute | solution.py:343
  101.8 4.4 %collective-permute-done.13.refs_3_ = bf16[160,512]{1,0:T(8,128)(2,1)S(1)} collective-permute-done((bf16[160,512]{1,0:T(8,128)(2,1)S(1)}, bf16[160,512]{1,0:T(8,128)(2,1)S(1)}, u32[]{:S(2)}, u32[]{:S(2)}) %collective-permute-start.13) | collective-permute-done | bytes 163872 | tf_op jit(solution)/shard_map/ppermute | solution.py:343
  106.8 3.2 %collective-permute-start.14 = (bf16[144,512]{1,0:T(8,128)(2,1)S(1)}, bf16[144,512]{1,0:T(8,128)(2,1)S(1)}, u32[]{:S(2)}, u32[]{:S(2)}) collective-permute-start(bf16[144,512]{1,0:T(8,128)(2,1)S(1)} %get-tuple-element.72.refs_1_), channel_id=1, source_target_pairs={{0,4},{1,5},{2,6},{3,7},{4,0},{5,1},{6,2},{7,3},{8,12},{9,13},{10,... | collective-permute-start | bytes 442376 | tf_op jit(solution)/shard_map/ppermute | solution.py:343
  110.5 2.9 %collective-permute-start.21 = (bf16[256,512]{1,0:T(8,128)(2,1)S(1)}, bf16[256,512]{1,0:T(8,128)(2,1)S(1)}, u32[]{:S(2)}, u32[]{:S(2)}) collective-permute-start(bf16[256,512]{1,0:T(8,128)(2,1)S(1)} %shard_map.140.refs_1_), channel_id=1, source_target_pairs={{0,17},{1,16},{2,19},{3,18},{4,21},{5,20},{6,23},{7,22},{8,25},{9,... | collective-permute-start | bytes 786440 | tf_op jit(solution)/shard_map/ppermute | solution.py:343
  115.8 5.0 %collective-permute-done.24.refs_2_ = bf16[128,512]{1,0:T(8,128)(2,1)S(1)} collective-permute-done((bf16[128,512]{1,0:T(8,128)(2,1)S(1)}, bf16[128,512]{1,0:T(8,128)(2,1)S(1)}, u32[]{:S(2)}, u32[]{:S(2)}) %collective-permute-start.24) | collective-permute-done | bytes 131104 | tf_op jit(solution)/shard_map/ppermute | solution.py:343
  123.4 2.6 %collective-permute-start.29 = (bf16[256,512]{1,0:T(8,128)(2,1)S(1)}, bf16[256,512]{1,0:T(8,128)(2,1)S(1)}, u32[]{:S(2)}, u32[]{:S(2)}) collective-permute-start(bf16[256,512]{1,0:T(8,128)(2,1)S(1)} %shard_map.141.refs_1_), channel_id=1, source_target_pairs={{0,17},{1,16},{2,19},{3,18},{4,21},{5,20},{6,23},{7,22},{8,25},{9,... | collective-permute-start | bytes 786440 | tf_op jit(solution)/shard_map/ppermute | solution.py:343
  127.8 6.6 %shard_map.136 = bf16[512,1024]{1,0:T(8,128)(2,1)} custom-call(s32[1]{0:T(128)} %bitcast.refs_0_, bf16[1024,1024]{1,0:T(8,128)(2,1)} %refs_1_.3, bf16[512,512]{1,0:T(8,128)(2,1)} %get-tuple-element.50.refs_3_.refs_2_, bf16[512,512]{1,0:T(8,128)(2,1)} %get-tuple-element.51.refs_3_, bf16[512,512]{1,0:T(8,128)(2,1)} %add_convert_fusion.2.refs_4_, ...), custom_call_target="tpu_custom_call" | custom-call | tf_op jit(solution)/shard_map/pallas_call | solution.py:70
  134.4 2.0 %shard_map.142 = bf16[1024,1024]{1,0:T(8,128)(2,1)} custom-call(s32[3]{0:T(128)S(1)} %pad_add_fusion.1.refs_0_, bf16[256,512]{1,0:T(8,128)(2,1)S(1)} %shard_map.140.refs_1_, bf16[256,512]{1,0:T(8,128)(2,1)S(1)} %collective-permute-done.21.refs_2_, bf16[256,512]{1,0:T(8,128)(2,1)S(1)} %collective-permute-done.22.refs_3_, ...), custom_call_target="tpu_custom_call" | custom-call | tf_op jit(solution)/shard_map/pallas_call | solution.py:91
  136.4 1.6 %collective-permute-done.30.refs_3_ = bf16[256,512]{1,0:T(8,128)(2,1)S(1)} collective-permute-done((bf16[256,512]{1,0:T(8,128)(2,1)S(1)}, bf16[256,512]{1,0:T(8,128)(2,1)S(1)}, u32[]{:S(2)}, u32[]{:S(2)}) %collective-permute-start.30) | collective-permute-done | bytes 262176 | tf_op jit(solution)/shard_map/ppermute | solution.py:343
  140.8 2.0 %shard_map.143 = bf16[1024,1024]{1,0:T(8,128)(2,1)} custom-call(s32[3]{0:T(128)S(1)} %pad_add_fusion.1.refs_0_, bf16[256,512]{1,0:T(8,128)(2,1)S(1)} %shard_map.141.refs_1_, bf16[256,512]{1,0:T(8,128)(2,1)S(1)} %collective-permute-done.29.refs_2_, bf16[256,512]{1,0:T(8,128)(2,1)S(1)} %collective-permute-done.30.refs_3_, ...), custom_call_target="tpu_custom_call" | custom-call | tf_op jit(solution)/shard_map/pallas_call | solution.py:91
  (108 shorter events, 22.9 us)
Async XLA Ops:
  4.0 21.0 %collective-permute-start = (bf16[8,1024]{1,0:T(8,128)(2,1)}, bf16[8,1024]{1,0:T(8,128)(2,1)S(1)}, u32[]{:S(2)}, u32[]{:S(2)}) collective-permute-start(bf16[8,1024]{1,0:T(8,128)(2,1)} %get-tuple-element.48), channel_id=1, source_target_pairs={{0,4},{1,5},{2,6},{3,7},{4,0},{5,1},{6,2},{7,3},{8,12},{9,13},{10,... | collective-permute-start | bytes 49160 | tf_op jit(solution)/shard_map/ppermute | solution.py:343
  8.1 16.9 %collective-permute-start.1 = (bf16[8,1024]{1,0:T(8,128)(2,1)}, bf16[8,1024]{1,0:T(8,128)(2,1)S(1)}, u32[]{:S(2)}, u32[]{:S(2)}) collective-permute-start(bf16[8,1024]{1,0:T(8,128)(2,1)} %get-tuple-element.48), channel_id=1, source_target_pairs={{0,2},{1,3},{2,0},{3,1},{4,6},{5,7},{6,4},{7,5},{8,10},{9,11},{10,... | collective-permute-start | bytes 49160 | tf_op jit(solution)/shard_map/ppermute | solution.py:343
  9.7 15.3 %collective-permute-start.2 = (bf16[8,1024]{1,0:T(8,128)(2,1)}, bf16[8,1024]{1,0:T(8,128)(2,1)S(1)}, u32[]{:S(2)}, u32[]{:S(2)}) collective-permute-start(bf16[8,1024]{1,0:T(8,128)(2,1)} %get-tuple-element.48), channel_id=1, source_target_pairs={{0,6},{1,7},{2,4},{3,5},{4,2},{5,3},{6,0},{7,1},{8,14},{9,15},{10,... | collective-permute-start | bytes 49160 | tf_op jit(solution)/shard_map/ppermute | solution.py:343
  9.7 33.8 %all-to-all-start = ((bf16[32,16,1024]{2,1,0:T(8,128)(2,1)}), bf16[32,16,1024]{2,1,0:T(8,128)(2,1)}, u32[]{:S(2)}, u32[]{:S(2)}) async-start(bf16[32,16,1024]{2,1,0:T(8,128)(2,1)} %bitcast.51), calls=%async_computation | async-start | bytes 2097152 | tf_op jit(solution)/shard_map/all_to_all | solution.py:357
  16.5 41.7 %collective-permute-start.7 = (bf16[1024,512]{1,0:T(8,128)(2,1)S(1)}, bf16[1024,512]{1,0:T(8,128)(2,1)S(1)}, u32[]{:S(2)}, u32[]{:S(2)}) collective-permute-start(bf16[1024,512]{1,0:T(8,128)(2,1)S(1)} %bitcast.48), channel_id=1, source_target_pairs={{0,8},{1,9},{2,10},{3,11},{4,12},{5,13},{6,14},{7,15},{8,0},{9,1},... | collective-permute-start | bytes 3145736 | tf_op jit(solution)/shard_map/ppermute | solution.py:343
  25.0 6.9 %collective-permute-start.3 = (bf16[32,1024]{1,0:T(8,128)(2,1)S(1)}, bf16[32,1024]{1,0:T(8,128)(2,1)S(1)}, u32[]{:S(2)}, u32[]{:S(2)}) collective-permute-start(bf16[32,1024]{1,0:T(8,128)(2,1)S(1)} %pad_maximum_fusion), channel_id=1, source_target_pairs={{0,1},{1,0},{2,3},{3,2},{4,5},{5,4},{6,7},{7,6},{8,9},{9,8},{10,11... | collective-permute-start | bytes 196616 | tf_op jit(solution)/shard_map/ppermute | solution.py:343
  32.0 6.5 %collective-permute-start.4 = (bf16[64,1024]{1,0:T(8,128)(2,1)S(1)}, bf16[64,1024]{1,0:T(8,128)(2,1)S(1)}, u32[]{:S(2)}, u32[]{:S(2)}) collective-permute-start(bf16[64,1024]{1,0:T(8,128)(2,1)S(1)} %get-tuple-element.94), channel_id=1, source_target_pairs={{0,16},{1,17},{2,18},{3,19},{4,20},{5,21},{6,22},{7,23},{8,24},{9,... | collective-permute-start | bytes 393224 | tf_op jit(solution)/shard_map/ppermute | solution.py:343
  52.9 11.8 %collective-permute-start.6 = (bf16[1024,512]{1,0:T(8,128)(2,1)}, bf16[1024,512]{1,0:T(8,128)(2,1)}, u32[]{:S(2)}, u32[]{:S(2)}) collective-permute-start(bf16[1024,512]{1,0:T(8,128)(2,1)} %get-tuple-element.60.refs_1_), channel_id=1, source_target_pairs={{0,8},{1,9},{2,10},{3,11},{4,12},{5,13},{6,14},{7,15},{8,0},{9,1},... | collective-permute-start | bytes 3145736 | tf_op jit(solution)/shard_map/ppermute | solution.py:343
  53.1 5.2 %collective-permute-start.8 = (bf16[512,512]{1,0:T(8,128)(2,1)}, bf16[512,512]{1,0:T(8,128)(2,1)S(1)}, u32[]{:S(2)}, u32[]{:S(2)}) collective-permute-start(bf16[512,512]{1,0:T(8,128)(2,1)} %get-tuple-element.51.refs_3_), channel_id=1, source_target_pairs={{0,8},{1,9},{2,10},{3,11},{4,12},{5,13},{6,14},{7,15},{8,0},{9,1},... | collective-permute-start | bytes 1572872 | tf_op jit(solution)/shard_map/ppermute | solution.py:343
  53.4 74.3 %all-to-all-start.1 = ((bf16[32,16,1024]{2,1,0:T(8,128)(2,1)}), bf16[32,16,1024]{2,1,0:T(8,128)(2,1)}, u32[]{:S(2)}, u32[]{:S(2)}) async-start(bf16[32,16,1024]{2,1,0:T(8,128)(2,1)} %bitcast.50), calls=%async_computation.1 | async-start | bytes 2097152 | tf_op jit(solution)/shard_map/all_to_all | solution.py:405
  58.1 6.6 %collective-permute-start.9 = (bf16[2,128,512]{2,1,0:T(8,128)(2,1)}, bf16[2,128,512]{2,1,0:T(8,128)(2,1)S(1)}, u32[]{:S(2)}, u32[]{:S(2)}) collective-permute-start(bf16[2,128,512]{2,1,0:T(8,128)(2,1)} %get-tuple-element.63), channel_id=1, source_target_pairs={{0,8},{1,9},{2,10},{3,11},{4,12},{5,13},{6,14},{7,15},{8,0},{9,1},... | collective-permute-start | bytes 786440 | tf_op jit(solution)/shard_map/ppermute | solution.py:343
  61.2 18.5 %collective-permute-start.15 = (bf16[256,512]{1,0:T(8,128)(2,1)S(1)}, bf16[256,512]{1,0:T(8,128)(2,1)S(1)}, u32[]{:S(2)}, u32[]{:S(2)}) collective-permute-start(bf16[256,512]{1,0:T(8,128)(2,1)S(1)} %get-tuple-element.59), channel_id=1, source_target_pairs={{0,17},{1,16},{2,19},{3,18},{4,21},{5,20},{6,23},{7,22},{8,25},{9,... | collective-permute-start | bytes 786440 | tf_op jit(solution)/shard_map/ppermute | solution.py:343
  63.8 19.9 %collective-permute-start.16 = (bf16[256,512]{1,0:T(8,128)(2,1)}, bf16[256,512]{1,0:T(8,128)(2,1)S(1)}, u32[]{:S(2)}, u32[]{:S(2)}) collective-permute-start(bf16[256,512]{1,0:T(8,128)(2,1)} %get-tuple-element.58), channel_id=1, source_target_pairs={{0,16},{1,17},{2,18},{3,19},{4,20},{5,21},{6,22},{7,23},{8,24},{9,... | collective-permute-start | bytes 786440 | tf_op jit(solution)/shard_map/ppermute | solution.py:343
  64.3 19.4 %collective-permute-start.17 = (bf16[256,512]{1,0:T(8,128)(2,1)}, bf16[256,512]{1,0:T(8,128)(2,1)S(1)}, u32[]{:S(2)}, u32[]{:S(2)}) collective-permute-start(bf16[256,512]{1,0:T(8,128)(2,1)} %get-tuple-element.57), channel_id=1, source_target_pairs={{0,1},{1,0},{2,3},{3,2},{4,5},{5,4},{6,7},{7,6},{8,9},{9,8},{10,11... | collective-permute-start | bytes 786440 | tf_op jit(solution)/shard_map/ppermute | solution.py:343
  68.3 25.8 %collective-permute-start.10 = (bf16[320,512]{1,0:T(8,128)(2,1)}, bf16[320,512]{1,0:T(8,128)(2,1)S(1)}, u32[]{:S(2)}, u32[]{:S(2)}) collective-permute-start(bf16[320,512]{1,0:T(8,128)(2,1)} %get-tuple-element.66), channel_id=1, source_target_pairs={{0,17},{1,16},{2,19},{3,18},{4,21},{5,20},{6,23},{7,22},{8,25},{9,... | collective-permute-start | bytes 983048 | tf_op jit(solution)/shard_map/ppermute | solution.py:343
  70.8 27.5 %collective-permute-start.11 = (bf16[320,512]{1,0:T(8,128)(2,1)}, bf16[320,512]{1,0:T(8,128)(2,1)S(1)}, u32[]{:S(2)}, u32[]{:S(2)}) collective-permute-start(bf16[320,512]{1,0:T(8,128)(2,1)} %get-tuple-element.67), channel_id=1, source_target_pairs={{0,16},{1,17},{2,18},{3,19},{4,20},{5,21},{6,22},{7,23},{8,24},{9,... | collective-permute-start | bytes 983048 | tf_op jit(solution)/shard_map/ppermute | solution.py:343
  79.7 18.7 %collective-permute-start.12 = (bf16[320,512]{1,0:T(8,128)(2,1)}, bf16[320,512]{1,0:T(8,128)(2,1)S(1)}, u32[]{:S(2)}, u32[]{:S(2)}) collective-permute-start(bf16[320,512]{1,0:T(8,128)(2,1)} %get-tuple-element.68), channel_id=1, source_target_pairs={{0,1},{1,0},{2,3},{3,2},{4,5},{5,4},{6,7},{7,6},{8,9},{9,8},{10,11... | collective-permute-start | bytes 983048 | tf_op jit(solution)/shard_map/ppermute | solution.py:343
  84.5 5.4 %collective-permute-start.18 = (bf16[128,512]{1,0:T(8,128)(2,1)S(1)}, bf16[128,512]{1,0:T(8,128)(2,1)S(1)}, u32[]{:S(2)}, u32[]{:S(2)}) collective-permute-start(bf16[128,512]{1,0:T(8,128)(2,1)S(1)} %get-tuple-element.79), channel_id=1, source_target_pairs={{0,2},{1,3},{2,0},{3,1},{4,6},{5,7},{6,4},{7,5},{8,10},{9,11},{10,... | collective-permute-start | bytes 393224 | tf_op jit(solution)/shard_map/ppermute | solution.py:343
  90.4 9.1 %collective-permute-start.19 = (bf16[128,512]{1,0:T(8,128)(2,1)S(1)}, bf16[128,512]{1,0:T(8,128)(2,1)S(1)}, u32[]{:S(2)}, u32[]{:S(2)}) collective-permute-start(bf16[128,512]{1,0:T(8,128)(2,1)S(1)} %shard_map.138.refs_1_), channel_id=1, source_target_pairs={{0,4},{1,5},{2,6},{3,7},{4,0},{5,1},{6,2},{7,3},{8,12},{9,13},{10,... | collective-permute-start | bytes 393224 | tf_op jit(solution)/shard_map/ppermute | solution.py:343
  99.1 7.1 %collective-permute-start.13 = (bf16[160,512]{1,0:T(8,128)(2,1)S(1)}, bf16[160,512]{1,0:T(8,128)(2,1)S(1)}, u32[]{:S(2)}, u32[]{:S(2)}) collective-permute-start(bf16[160,512]{1,0:T(8,128)(2,1)S(1)} %get-tuple-element.71), channel_id=1, source_target_pairs={{0,2},{1,3},{2,0},{3,1},{4,6},{5,7},{6,4},{7,5},{8,10},{9,11},{10,... | collective-permute-start | bytes 491528 | tf_op jit(solution)/shard_map/ppermute | solution.py:343
  100.1 9.8 %collective-permute-start.20 = (bf16[128,512]{1,0:T(8,128)(2,1)S(1)}, bf16[128,512]{1,0:T(8,128)(2,1)S(1)}, u32[]{:S(2)}, u32[]{:S(2)}) collective-permute-start(bf16[128,512]{1,0:T(8,128)(2,1)S(1)} %shard_map.139.refs_1_), channel_id=1, source_target_pairs={{0,2},{1,3},{2,0},{3,1},{4,6},{5,7},{6,4},{7,5},{8,10},{9,11},{10,... | collective-permute-start | bytes 393224 | tf_op jit(solution)/shard_map/ppermute | solution.py:343
  106.8 8.3 %collective-permute-start.14 = (bf16[144,512]{1,0:T(8,128)(2,1)S(1)}, bf16[144,512]{1,0:T(8,128)(2,1)S(1)}, u32[]{:S(2)}, u32[]{:S(2)}) collective-permute-start(bf16[144,512]{1,0:T(8,128)(2,1)S(1)} %get-tuple-element.72.refs_1_), channel_id=1, source_target_pairs={{0,4},{1,5},{2,6},{3,7},{4,0},{5,1},{6,2},{7,3},{8,12},{9,13},{10,... | collective-permute-start | bytes 442376 | tf_op jit(solution)/shard_map/ppermute | solution.py:343
  110.5 10.8 %collective-permute-start.21 = (bf16[256,512]{1,0:T(8,128)(2,1)S(1)}, bf16[256,512]{1,0:T(8,128)(2,1)S(1)}, u32[]{:S(2)}, u32[]{:S(2)}) collective-permute-start(bf16[256,512]{1,0:T(8,128)(2,1)S(1)} %shard_map.140.refs_1_), channel_id=1, source_target_pairs={{0,17},{1,16},{2,19},{3,18},{4,21},{5,20},{6,23},{7,22},{8,25},{9,... | collective-permute-start | bytes 786440 | tf_op jit(solution)/shard_map/ppermute | solution.py:343
  113.4 9.4 %collective-permute-start.22 = (bf16[256,512]{1,0:T(8,128)(2,1)S(1)}, bf16[256,512]{1,0:T(8,128)(2,1)S(1)}, u32[]{:S(2)}, u32[]{:S(2)}) collective-permute-start(bf16[256,512]{1,0:T(8,128)(2,1)S(1)} %shard_map.140.refs_1_), channel_id=1, source_target_pairs={{0,16},{1,17},{2,18},{3,19},{4,20},{5,21},{6,22},{7,23},{8,24},{9,... | collective-permute-start | bytes 786440 | tf_op jit(solution)/shard_map/ppermute | solution.py:343
  113.4 9.5 %collective-permute-start.23 = (bf16[256,512]{1,0:T(8,128)(2,1)S(1)}, bf16[256,512]{1,0:T(8,128)(2,1)S(1)}, u32[]{:S(2)}, u32[]{:S(2)}) collective-permute-start(bf16[256,512]{1,0:T(8,128)(2,1)S(1)} %shard_map.140.refs_1_), channel_id=1, source_target_pairs={{0,1},{1,0},{2,3},{3,2},{4,5},{5,4},{6,7},{7,6},{8,9},{9,8},{10,11... | collective-permute-start | bytes 786440 | tf_op jit(solution)/shard_map/ppermute | solution.py:343
  115.7 5.0 %collective-permute-start.24 = (bf16[128,512]{1,0:T(8,128)(2,1)S(1)}, bf16[128,512]{1,0:T(8,128)(2,1)S(1)}, u32[]{:S(2)}, u32[]{:S(2)}) collective-permute-start(bf16[128,512]{1,0:T(8,128)(2,1)S(1)} %get-tuple-element.80.refs_1_), channel_id=1, source_target_pairs={{0,2},{1,3},{2,0},{3,1},{4,6},{5,7},{6,4},{7,5},{8,10},{9,11},{10,... | collective-permute-start | bytes 393224 | tf_op jit(solution)/shard_map/ppermute | solution.py:343
  122.9 3.8 %collective-permute-start.26 = (bf16[256,512]{1,0:T(8,128)(2,1)S(1)}, bf16[256,512]{1,0:T(8,128)(2,1)S(1)}, u32[]{:S(2)}, u32[]{:S(2)}) collective-permute-start(bf16[256,512]{1,0:T(8,128)(2,1)S(1)} %collective-permute-done.21.refs_2_), channel_id=1, source_target_pairs={{0,8},{1,9},{2,10},{3,11},{4,12},{5,13},{6,14},{7,15},{8,0},{9,1},... | collective-permute-start | bytes 786440 | tf_op jit(solution)/shard_map/ppermute | solution.py:343
  123.4 13.0 %collective-permute-start.29 = (bf16[256,512]{1,0:T(8,128)(2,1)S(1)}, bf16[256,512]{1,0:T(8,128)(2,1)S(1)}, u32[]{:S(2)}, u32[]{:S(2)}) collective-permute-start(bf16[256,512]{1,0:T(8,128)(2,1)S(1)} %shard_map.141.refs_1_), channel_id=1, source_target_pairs={{0,17},{1,16},{2,19},{3,18},{4,21},{5,20},{6,23},{7,22},{8,25},{9,... | collective-permute-start | bytes 786440 | tf_op jit(solution)/shard_map/ppermute | solution.py:343
  126.1 8.3 %collective-permute-start.27 = (bf16[256,512]{1,0:T(8,128)(2,1)S(1)}, bf16[256,512]{1,0:T(8,128)(2,1)S(1)}, u32[]{:S(2)}, u32[]{:S(2)}) collective-permute-start(bf16[256,512]{1,0:T(8,128)(2,1)S(1)} %collective-permute-done.22.refs_3_), channel_id=1, source_target_pairs={{0,8},{1,9},{2,10},{3,11},{4,12},{5,13},{6,14},{7,15},{8,0},{9,1},... | collective-permute-start | bytes 786440 | tf_op jit(solution)/shard_map/ppermute | solution.py:343
  126.1 8.3 %collective-permute-start.28 = (bf16[256,512]{1,0:T(8,128)(2,1)S(1)}, bf16[256,512]{1,0:T(8,128)(2,1)S(1)}, u32[]{:S(2)}, u32[]{:S(2)}) collective-permute-start(bf16[256,512]{1,0:T(8,128)(2,1)S(1)} %collective-permute-done.23.refs_4_), channel_id=1, source_target_pairs={{0,8},{1,9},{2,10},{3,11},{4,12},{5,13},{6,14},{7,15},{8,0},{9,1},... | collective-permute-start | bytes 786440 | tf_op jit(solution)/shard_map/ppermute | solution.py:343
  126.6 11.5 %collective-permute-start.30 = (bf16[256,512]{1,0:T(8,128)(2,1)S(1)}, bf16[256,512]{1,0:T(8,128)(2,1)S(1)}, u32[]{:S(2)}, u32[]{:S(2)}) collective-permute-start(bf16[256,512]{1,0:T(8,128)(2,1)S(1)} %shard_map.141.refs_1_), channel_id=1, source_target_pairs={{0,16},{1,17},{2,18},{3,19},{4,20},{5,21},{6,22},{7,23},{8,24},{9,... | collective-permute-start | bytes 786440 | tf_op jit(solution)/shard_map/ppermute | solution.py:343
  126.7 11.4 %collective-permute-start.31 = (bf16[256,512]{1,0:T(8,128)(2,1)S(1)}, bf16[256,512]{1,0:T(8,128)(2,1)S(1)}, u32[]{:S(2)}, u32[]{:S(2)}) collective-permute-start(bf16[256,512]{1,0:T(8,128)(2,1)S(1)} %shard_map.141.refs_1_), channel_id=1, source_target_pairs={{0,1},{1,0},{2,3},{3,2},{4,5},{5,4},{6,7},{7,6},{8,9},{9,8},{10,11... | collective-permute-start | bytes 786440 | tf_op jit(solution)/shard_map/ppermute | solution.py:343
  (19 other events, 123.2 us)
